TPU v7x, 128 devices: a whole 4x4x4 slice. The times are simulated.
128 devices in a mesh: seq: 8 (over y, core), exp: 16 (over z, x).
Axes of the slice: x: 4, y: 4, z: 4, core: 2. Of those that a mesh axis runs over, the one named last changes fastest.
Arguments:
- qkv_in: bfloat16 [16384, 6144], P('exp', 'seq'), may hold values from -6 to 6
- qkv_grad: bfloat16 [16384, 6144], P('exp', 'seq'), may hold values from -6 to 6
- conv_weight: float32 [4, 6144], P(None, 'seq'), may hold values from -3 to 3
- doc_ids: int32 [16384], replicated, may hold values from 0 to 15, never falling along the last dimension, each value on 1 to 4096 neighbouring positions
- qkv_weight: bfloat16 [6144, 2304], P('seq'), may hold values from -0.0078125 to 0.0078125
- resid: bfloat16 [16384, 2304], P(('exp', 'seq')), may hold values from -54 to 54
- norm_gain: float32 [2304], replicated, may hold values from 0.5 to 1.5
- out_grad: bfloat16 [16384, 2304], P(('exp', 'seq')), may hold values from -0.59765625 to 0.59765625
- routes: int32 [16384, 8], P(('exp', 'seq')), may hold values from 0 to 127, all different within a row; in each aligned block of 128 rows (0 to 127, 128 to 255, ...) at most 16 rows name the same one
- route_weights: float32 [16384, 8], P(('exp', 'seq')), may hold values from 0.05 to 1
- expert_weights: bfloat16 [128, 2304, 1536], P(('seq', 'exp')), may hold values from -0.125 to 0.125
Outputs:
- qkv_in_grad: bfloat16 [16384, 6144], P(('exp', 'seq'))
- expert_grads: bfloat16 [128, 2304, 1536], P(('seq', 'exp'))
Inputs may be any that keep to these rules, and one draw needn't show every extreme that they name: `routes`: each row names 8 different experts. In the rows of one device (aligned blocks of 128 rows) no expert is named more than 16 times, and in some block some expert is named exactly 16 times. `doc_ids`: document numbers never fall along the sequence; every document has 1 to 4096 positions, one exactly 4096.
All inputs are finite; a program needn't handle non-finite values.
Results may differ from a plain program's by a relative error of at most 0.019.
Values may be sent and summed in bfloat16 or wider, within the bound.
No kernel may reach another device: no remote copies, remote signals or barrier semaphores. Data moves between devices by JAX's collectives and lax.ppermute only.
A program may use at most 192 MiB of HBM per device.

v0:
```python
import jax
import jax.numpy as jnp
from jax import lax
from jax.sharding import PartitionSpec as P


def extended(block, sides, width):
    for axis, dim in sides:
        count = lax.axis_size(axis)
        forward = [(i, i + 1) for i in range(count - 1)]
        backward = [(target, source) for source, target in forward]
        low = lax.ppermute(
            lax.slice_in_dim(block, block.shape[dim] - width, None, axis=dim), axis, forward
        )
        high = lax.ppermute(lax.slice_in_dim(block, 0, width, axis=dim), axis, backward)
        block = jnp.concatenate([low, block, high], axis=dim)
    return block


def conv_local(ext_in, ext_grad, weight, ids_ext, head_rows):
    inputs_f = ext_in.astype(jnp.float32)
    grads_f = ext_grad.astype(jnp.float32)
    conv_rows = head_rows + 3
    summed = jnp.zeros((conv_rows, inputs_f.shape[1]), jnp.float32)
    for back_by in range(4):
        matches = (
            ids_ext[3 - back_by : 3 - back_by + conv_rows] == ids_ext[3 : 3 + conv_rows]
        ).astype(jnp.float32)
        summed = (
            summed
            + weight[back_by][None, :]
            * inputs_f[3 - back_by : 3 - back_by + conv_rows]
            * matches[:, None]
        )
    sigmoid_z = jax.nn.sigmoid(summed)
    pre_grad = grads_f[3 : 3 + conv_rows] * sigmoid_z * (1.0 + summed * (1.0 - sigmoid_z))
    result = jnp.zeros((head_rows, inputs_f.shape[1]), jnp.float32)
    for ahead_by in range(4):
        matches = (
            ids_ext[3 + ahead_by : 3 + ahead_by + head_rows] == ids_ext[3 : 3 + head_rows]
        ).astype(jnp.float32)
        result = (
            result
            + weight[ahead_by][None, :]
            * pre_grad[ahead_by : ahead_by + head_rows]
            * matches[:, None]
        )
    return result.astype(jnp.bfloat16)


def expert_terms(rows_h, rows_g, live_rows, own_weights, hidden):
    mixed_rows = jnp.dot(rows_h, own_weights[:, : 2 * hidden], preferred_element_type=jnp.float32)
    gate_pre = mixed_rows[:, :hidden]
    up_value = mixed_rows[:, hidden:]
    gate_sig = jax.nn.sigmoid(gate_pre)
    keep_rows = live_rows.astype(jnp.float32)[:, None]
    activated = (gate_pre * gate_sig * up_value * keep_rows).astype(jnp.bfloat16)
    act_grad = jnp.dot(rows_g, own_weights[:, 2 * hidden :], preferred_element_type=jnp.float32)
    hidden_grad = jnp.concatenate(
        [
            act_grad * up_value * gate_sig * (1.0 + gate_pre * (1.0 - gate_sig)),
            act_grad * gate_pre * gate_sig,
        ],
        1,
    )
    hidden_grad = (hidden_grad * keep_rows).astype(jnp.bfloat16)
    grad_gu = lax.dot_general(
        rows_h, hidden_grad, (((0,), (0,)), ((), ())), preferred_element_type=jnp.float32
    )
    grad_dn = lax.dot_general(
        rows_g, activated, (((0,), (0,)), ((), ())), preferred_element_type=jnp.float32
    )
    return (grad_gu, grad_dn)


def pack_slots(targets, bins, capacity):
    onehot = (targets[:, None] == jnp.arange(bins, dtype=jnp.int32)[None, :]).astype(jnp.int32)
    before = jnp.cumsum(onehot, axis=0) - onehot
    slot_in = jnp.sum(before * onehot, axis=1)
    dest = jnp.where(targets >= 0, targets * capacity + slot_in, bins * capacity)
    table = (
        jnp.zeros((bins * capacity + 1,), jnp.int32)
        .at[dest]
        .set(jnp.arange(targets.shape[0], dtype=jnp.int32))[: bins * capacity]
    )
    return (table, jnp.sum(onehot, axis=0))


def select_rows(token_of, normed, flow_grad, scales):
    picker = (token_of[:, None] == jnp.arange(normed.shape[0], dtype=jnp.int32)[None, :]).astype(
        jnp.bfloat16
    )
    rows_out = jnp.dot(picker, normed, preferred_element_type=jnp.float32).astype(jnp.bfloat16)
    flow_rows = jnp.dot(picker, flow_grad, preferred_element_type=jnp.float32)
    grads_out = (scales[:, None] * flow_rows).astype(jnp.bfloat16)
    return (rows_out, grads_out)


def per_device(
    qkv_in,
    qkv_grad,
    conv_weight,
    doc_ids,
    qkv_weight,
    resid,
    norm_gain,
    out_grad,
    routes,
    route_weights,
    expert_weights,
):
    head_rows = qkv_in.shape[0]
    ext_in, ext_grad = (extended(qkv_in, (("exp", 0),), 3), extended(qkv_grad, (("exp", 0),), 3))
    padded_ids = jnp.concatenate(
        [jnp.full((3,), -1, jnp.int32), doc_ids, jnp.full((3,), -1, jnp.int32)]
    )
    first_row = lax.axis_index("exp") * head_rows
    ids_ext = lax.dynamic_slice_in_dim(padded_ids, first_row, head_rows + 6)
    local_grad = conv_local(ext_in, ext_grad, conv_weight, ids_ext, head_rows)
    qkv_in_grad = lax.all_to_all(local_grad, "seq", split_axis=0, concat_axis=1, tiled=True)
    tokens = resid.shape[0]
    model_dim = resid.shape[1]
    per_token = routes.shape[1]
    hidden = expert_weights.shape[2] // 3
    n_seq = lax.axis_size("seq")
    n_exp = lax.axis_size("exp")
    experts = n_seq * n_exp
    capacity = 2 * tokens * per_token // experts
    proj_grad = lax.psum_scatter(
        jnp.dot(local_grad, qkv_weight, preferred_element_type=jnp.float32).astype(jnp.bfloat16),
        "seq",
        scatter_dimension=0,
        tiled=True,
    ).astype(jnp.float32)
    flow_grad = (out_grad.astype(jnp.float32) + proj_grad).astype(jnp.bfloat16)
    resid_f = resid.astype(jnp.float32)
    scale_rows = lax.rsqrt(jnp.mean(resid_f * resid_f, axis=1, keepdims=True) + 1e-06)
    normed = (resid_f * scale_rows * norm_gain[None, :]).astype(jnp.bfloat16)
    flat_routes = routes.reshape(-1)
    slot_table, counts = pack_slots(flat_routes, experts, capacity)
    counts = counts.reshape(experts, 1)
    token_of = slot_table // per_token
    send_rows, send_grads = select_rows(
        token_of, normed, flow_grad, route_weights.reshape(-1)[slot_table]
    )
    send_rows = send_rows.reshape(experts, capacity, model_dim)
    send_grads = send_grads.reshape(experts, capacity, model_dim)
    got_rows, got_grads, got_counts = (
        lax.all_to_all(send_rows, ("seq", "exp"), split_axis=0, concat_axis=0, tiled=True),
        lax.all_to_all(send_grads, ("seq", "exp"), split_axis=0, concat_axis=0, tiled=True),
        lax.all_to_all(counts, ("seq", "exp"), split_axis=0, concat_axis=0, tiled=True),
    )
    rows_all = got_rows.reshape(-1, model_dim)
    grads_all = got_grads.reshape(-1, model_dim)
    source_counts = got_counts.reshape(-1)
    valid_slots = (jnp.arange(capacity, dtype=jnp.int32)[None, :] < source_counts[:, None]).reshape(
        -1
    )
    own_weights = expert_weights[0]
    total_rows = rows_all.shape[0]
    tile_rows = 256
    live_total = jnp.sum(source_counts)
    position_live = jnp.cumsum(valid_slots.astype(jnp.int32)) - 1
    target = jnp.where(valid_slots, position_live, total_rows)
    live_order = (
        jnp.zeros((total_rows + 1,), jnp.int32)
        .at[target]
        .set(jnp.arange(total_rows, dtype=jnp.int32))[:total_rows]
    )

    def tile_step(tile_index, totals):
        picked = lax.dynamic_slice_in_dim(live_order, tile_index * tile_rows, tile_rows)
        live_rows = tile_index * tile_rows + jnp.arange(tile_rows, dtype=jnp.int32) < live_total
        part_gu, part_dn = expert_terms(
            rows_all[picked], grads_all[picked], live_rows, own_weights, hidden
        )
        return (totals[0] + part_gu, totals[1] + part_dn)

    tile_count = (live_total + tile_rows - 1) // tile_rows
    start_sums = (
        jnp.zeros((model_dim, 2 * hidden), jnp.float32),
        jnp.zeros((model_dim, hidden), jnp.float32),
    )
    grad_gu, grad_dn = lax.fori_loop(jnp.int32(0), tile_count, tile_step, start_sums)
    expert_grads = jnp.concatenate([grad_gu, grad_dn], 1).astype(jnp.bfloat16)[None]
    return (qkv_in_grad, expert_grads)


def solution(mesh):
    return jax.shard_map(
        per_device,
        mesh=mesh,
        in_specs=(
            P("exp", "seq"),
            P("exp", "seq"),
            P(None, "seq"),
            P(),
            P("seq", None),
            P(("exp", "seq"), None),
            P(),
            P(("exp", "seq"), None),
            P(("exp", "seq"), None),
            P(("exp", "seq"), None),
            P(("seq", "exp"), None, None),
        ),
        out_specs=(P(("exp", "seq"), None), P(("seq", "exp"), None, None)),
        check_vma=False,
    )
```

profile of v0, /device:TPU:26, one launch (start us, length us, event | category | flops | bytes accessed | tf_op | source)
XLA Modules:
  0.0 684.5 jit_solution(5728903150035396911)
XLA Ops:
  11.1 3.4 collective-permute-start.1
  15.8 3.0 collective-permute-start
  28.9 11.9 %all-to-all-start.1 = ((s32[128,1,1]{2,1,0:T(1,128)}), s32[128,1,1]{2,1,0:T(1,128)}, u32[]{:S(2)}, u32[]{:S(2)}) async-start(s32[128,1,1]{2,1,0:T(1,128)} %copy.32), calls=%async_computation.1 | async-start | bytes 131072 | tf_op jit(solution)/shard_map/all_to_all | solution.py:151
  49.7 4.9 scatter_custom_fusion.1
  61.0 11.3 %concatenate.29 = bf16[1030,768]{1,0:T(8,128)(2,1)} concatenate(bf16[3,768]{1,0:T(4,128)(2,1)} %collective-permute-done.1, bf16[1024,768]{1,0:T(8,128)(2,1)} %param.13, bf16[3,768]{1,0:T(4,128)(2,1)} %collective-permute-done.2), dimensions={0} | concatenate | bytes 3164160 | tf_op jit(solution)/shard_map/concatenate | solution.py:16
  74.3 4.1 add_multiply_fusion.1
  78.4 2.9 fusion.19
  81.3 4.7 all-to-all-start
  86.0 7.3 %convolution_convert_fusion.1 = bf16[1024,2304]{1,0:T(8,128)(2,1)} fusion(bf16[1024,768]{1,0:T(8,128)(2,1)} %fusion.19, bf16[768,2304]{1,0:T(8,128)(2,1)S(1)} %copy-done), kind=kOutput, calls=%fused_computation.28 | convolution fusion | flops 3626237952 | bytes 9830400 | tf_op jit(solution)/shard_map/dot_general | solution.py:130
  94.4 5.1 convolution_convert_fusion
  99.5 6.2 all-to-all-done
  105.7 10.0 %all-to-all-start.2 = ((bf16[128,16,2304]{2,1,0:T(8,128)(2,1)}), bf16[128,16,2304]{2,1,0:T(8,128)(2,1)}, u32[]{:S(2)}, u32[]{:S(2)}) async-start(bf16[128,16,2304]{2,1,0:T(8,128)(2,1)} %bitcast.43), calls=%async_computation.2 | async-start | bytes 18874368 | tf_op jit(solution)/shard_map/all_to_all | solution.py:149
  115.9 8.6 %gather_fusion.2 = f32[2048]{0:T(1024)S(1)} fusion(f32[1024]{0:T(1024)S(1)} %reshape.219, s32[2048]{0:T(1024)S(1)} %copy-done.13), kind=kCustom, calls=%fused_computation.2 | custom fusion | bytes 24576 | tf_op jit(solution)/shard_map/gather | solution.py:144
  124.5 115.1 %reduce-scatter.2.cloned.1.call-done = bf16[128,2304]{1,0:T(8,128)(2,1)} async-done(((bf16[1024,2304]{1,0:T(8,128)(2,1)}), bf16[128,2304]{1,0:T(8,128)(2,1)}) %reduce-scatter.2.cloned.1.call-update) | async-done | bytes 589840 | tf_op jit(solution)/shard_map/reduce_scatter | solution.py:129
  239.7 6.2 multiply_convert_fusion.2
  245.9 13.9 %all-to-all-start.3 = ((bf16[128,16,2304]{2,1,0:T(8,128)(2,1)}), bf16[128,16,2304]{2,1,0:T(8,128)(2,1)}, u32[]{:S(2)}, u32[]{:S(2)}) async-start(bf16[128,16,2304]{2,1,0:T(8,128)(2,1)} %bitcast.42), calls=%async_computation.4 | async-start | bytes 18874368 | tf_op jit(solution)/shard_map/all_to_all | solution.py:150
  259.9 3.9 fusion.50
  265.4 8.1 %scatter_custom_fusion = s32[2049]{0:T(1024)S(1)} fusion(s32[2048]{0:T(1024)S(1)} %bitcast.48, s32[2048]{0:T(1024)S(1)} %iota.26, s32[]{:T(128)} %constant.76.clone.1), kind=kCustom, calls=%fused_computation.97 | custom fusion | bytes 8200 | tf_op jit(solution)/shard_map/scatter | solution.py:168
  277.0 108.0 %all-to-all-done.3 = bf16[128,16,2304]{2,1,0:T(8,128)(2,1)} async-done(((bf16[128,16,2304]{2,1,0:T(8,128)(2,1)}), bf16[128,16,2304]{2,1,0:T(8,128)(2,1)}, u32[]{:S(2)}, u32[]{:S(2)}) %all-to-all-start.3) | async-done | bytes 9437216 | tf_op jit(solution)/shard_map/all_to_all | solution.py:150
  387.8 4.9 broadcast_in_dim.15
  392.7 267.4 %while.12 = (s32[]{:T(128)}, f32[2304,1024]{1,0:T(8,128)}, f32[2304,512]{1,0:T(8,128)}, s32[]{:T(128)}, s32[2048]{0:T(1024)S(1)}, /*index=5*/bf16[2048,2304]{1,0...) while((s32[]{:T(128)}, f32[2304,1024]{1,0:T(8,128)}, ...), condition=%wide.region_12.13_spmd, body=%wide.region_11.12_spmd.sunk | while | flops 3630565888 | bytes 116142360 | solution.py:184
  393.4 7.5 %gather_fusion.1 = bf16[256,2304]{1,0:T(8,128)(2,1)S(1)} fusion(bf16[2048,2304]{1,0:T(8,128)(2,1)} %get-tuple-element.185, s32[1024]{0:T(1024)S(1)} %pad_clamp_fusion.2), kind=kCustom, calls=%fused_computation.1.clone.1 | custom fusion | bytes 2360320 | tf_op jit(solution)/shard_map/while/body/gather | solution.py:175
  400.9 7.5 %gather_fusion = bf16[256,2304]{1,0:T(8,128)(2,1)S(1)} fusion(bf16[2048,2304]{1,0:T(8,128)(2,1)} %get-tuple-element.184, s32[1024]{0:T(1024)S(1)} %pad_clamp_fusion.2), kind=kCustom, calls=%fused_computation.clone.1 | custom fusion | bytes 2360320 | tf_op jit(solution)/shard_map/while/body/gather | solution.py:175
  408.4 3.7 fusion.71
  414.9 5.9 convolution_add_fusion.5
  422.4 3.7 copy-done.2
  426.9 7.5 %gather_fusion.1 = bf16[256,2304]{1,0:T(8,128)(2,1)S(1)} fusion(bf16[2048,2304]{1,0:T(8,128)(2,1)} %get-tuple-element.185, s32[1024]{0:T(1024)S(1)} %pad_clamp_fusion.2), kind=kCustom, calls=%fused_computation.1.clone.1 | custom fusion | bytes 2360320 | tf_op jit(solution)/shard_map/while/body/gather | solution.py:175
  434.3 7.5 %gather_fusion = bf16[256,2304]{1,0:T(8,128)(2,1)S(1)} fusion(bf16[2048,2304]{1,0:T(8,128)(2,1)} %get-tuple-element.184, s32[1024]{0:T(1024)S(1)} %pad_clamp_fusion.2), kind=kCustom, calls=%fused_computation.clone.1 | custom fusion | bytes 2360320 | tf_op jit(solution)/shard_map/while/body/gather | solution.py:175
  441.8 3.7 fusion.71
  448.3 5.9 convolution_add_fusion.5
  455.9 3.7 copy-done.2
  460.3 7.5 %gather_fusion.1 = bf16[256,2304]{1,0:T(8,128)(2,1)S(1)} fusion(bf16[2048,2304]{1,0:T(8,128)(2,1)} %get-tuple-element.185, s32[1024]{0:T(1024)S(1)} %pad_clamp_fusion.2), kind=kCustom, calls=%fused_computation.1.clone.1 | custom fusion | bytes 2360320 | tf_op jit(solution)/shard_map/while/body/gather | solution.py:175
  467.8 7.5 %gather_fusion = bf16[256,2304]{1,0:T(8,128)(2,1)S(1)} fusion(bf16[2048,2304]{1,0:T(8,128)(2,1)} %get-tuple-element.184, s32[1024]{0:T(1024)S(1)} %pad_clamp_fusion.2), kind=kCustom, calls=%fused_computation.clone.1 | custom fusion | bytes 2360320 | tf_op jit(solution)/shard_map/while/body/gather | solution.py:175
  475.2 3.7 fusion.71
  481.7 5.9 convolution_add_fusion.5
  489.3 3.7 copy-done.2
  493.7 7.5 %gather_fusion.1 = bf16[256,2304]{1,0:T(8,128)(2,1)S(1)} fusion(bf16[2048,2304]{1,0:T(8,128)(2,1)} %get-tuple-element.185, s32[1024]{0:T(1024)S(1)} %pad_clamp_fusion.2), kind=kCustom, calls=%fused_computation.1.clone.1 | custom fusion | bytes 2360320 | tf_op jit(solution)/shard_map/while/body/gather | solution.py:175
  501.2 7.5 %gather_fusion = bf16[256,2304]{1,0:T(8,128)(2,1)S(1)} fusion(bf16[2048,2304]{1,0:T(8,128)(2,1)} %get-tuple-element.184, s32[1024]{0:T(1024)S(1)} %pad_clamp_fusion.2), kind=kCustom, calls=%fused_computation.clone.1 | custom fusion | bytes 2360320 | tf_op jit(solution)/shard_map/while/body/gather | solution.py:175
  508.6 3.7 fusion.71
  515.1 5.9 convolution_add_fusion.5
  522.7 3.7 copy-done.2
  527.1 7.5 %gather_fusion.1 = bf16[256,2304]{1,0:T(8,128)(2,1)S(1)} fusion(bf16[2048,2304]{1,0:T(8,128)(2,1)} %get-tuple-element.185, s32[1024]{0:T(1024)S(1)} %pad_clamp_fusion.2), kind=kCustom, calls=%fused_computation.1.clone.1 | custom fusion | bytes 2360320 | tf_op jit(solution)/shard_map/while/body/gather | solution.py:175
  534.6 7.5 %gather_fusion = bf16[256,2304]{1,0:T(8,128)(2,1)S(1)} fusion(bf16[2048,2304]{1,0:T(8,128)(2,1)} %get-tuple-element.184, s32[1024]{0:T(1024)S(1)} %pad_clamp_fusion.2), kind=kCustom, calls=%fused_computation.clone.1 | custom fusion | bytes 2360320 | tf_op jit(solution)/shard_map/while/body/gather | solution.py:175
  542.1 3.7 fusion.71
  548.5 5.9 convolution_add_fusion.5
  556.1 3.7 copy-done.2
  560.5 7.5 %gather_fusion.1 = bf16[256,2304]{1,0:T(8,128)(2,1)S(1)} fusion(bf16[2048,2304]{1,0:T(8,128)(2,1)} %get-tuple-element.185, s32[1024]{0:T(1024)S(1)} %pad_clamp_fusion.2), kind=kCustom, calls=%fused_computation.1.clone.1 | custom fusion | bytes 2360320 | tf_op jit(solution)/shard_map/while/body/gather | solution.py:175
  568.0 7.5 %gather_fusion = bf16[256,2304]{1,0:T(8,128)(2,1)S(1)} fusion(bf16[2048,2304]{1,0:T(8,128)(2,1)} %get-tuple-element.184, s32[1024]{0:T(1024)S(1)} %pad_clamp_fusion.2), kind=kCustom, calls=%fused_computation.clone.1 | custom fusion | bytes 2360320 | tf_op jit(solution)/shard_map/while/body/gather | solution.py:175
  575.5 3.7 fusion.71
  582.0 5.9 convolution_add_fusion.5
  589.5 3.7 copy-done.2
  594.0 7.5 %gather_fusion.1 = bf16[256,2304]{1,0:T(8,128)(2,1)S(1)} fusion(bf16[2048,2304]{1,0:T(8,128)(2,1)} %get-tuple-element.185, s32[1024]{0:T(1024)S(1)} %pad_clamp_fusion.2), kind=kCustom, calls=%fused_computation.1.clone.1 | custom fusion | bytes 2360320 | tf_op jit(solution)/shard_map/while/body/gather | solution.py:175
  601.4 7.5 %gather_fusion = bf16[256,2304]{1,0:T(8,128)(2,1)S(1)} fusion(bf16[2048,2304]{1,0:T(8,128)(2,1)} %get-tuple-element.184, s32[1024]{0:T(1024)S(1)} %pad_clamp_fusion.2), kind=kCustom, calls=%fused_computation.clone.1 | custom fusion | bytes 2360320 | tf_op jit(solution)/shard_map/while/body/gather | solution.py:175
  608.9 3.7 fusion.71
  615.4 5.9 convolution_add_fusion.5
  622.9 3.7 copy-done.2
  627.4 7.5 %gather_fusion.1 = bf16[256,2304]{1,0:T(8,128)(2,1)S(1)} fusion(bf16[2048,2304]{1,0:T(8,128)(2,1)} %get-tuple-element.185, s32[1024]{0:T(1024)S(1)} %pad_clamp_fusion.2), kind=kCustom, calls=%fused_computation.1.clone.1 | custom fusion | bytes 2360320 | tf_op jit(solution)/shard_map/while/body/gather | solution.py:175
  634.8 7.5 %gather_fusion = bf16[256,2304]{1,0:T(8,128)(2,1)S(1)} fusion(bf16[2048,2304]{1,0:T(8,128)(2,1)} %get-tuple-element.184, s32[1024]{0:T(1024)S(1)} %pad_clamp_fusion.2), kind=kCustom, calls=%fused_computation.clone.1 | custom fusion | bytes 2360320 | tf_op jit(solution)/shard_map/while/body/gather | solution.py:175
  642.3 3.7 fusion.71
  648.8 5.9 convolution_add_fusion.5
  656.4 3.7 copy-done.2
  660.1 4.1 convert_bitcast_fusion.1
  664.2 6.6 convert_bitcast_fusion
  670.8 6.8 pad_maximum_fusion
  (202 shorter events, 81.3 us)
Async XLA Ops:
  7.2 78.8 %copy-start = (bf16[768,2304]{1,0:T(8,128)(2,1)S(1)}, bf16[768,2304]{1,0:T(8,128)(2,1)}, u32[]{:S(2)}) copy-start(bf16[768,2304]{1,0:T(8,128)(2,1)} %param.17) | copy-start | bytes 10616836
  7.2 33.5 %copy-start.9 = (s32[128,8]{0,1:T(8,128)S(1)}, s32[128,8]{0,1:T(8,128)}, u32[]{:S(2)}) copy-start(s32[128,8]{0,1:T(8,128)} %param.21) | copy-start | bytes 12292
  8.7 52.3 %collective-permute-start.2 = (bf16[3,768]{1,0:T(4,128)(2,1)}, bf16[3,768]{1,0:T(4,128)(2,1)}, u32[]{:S(2)}, u32[]{:S(2)}) collective-permute-start(bf16[3,768]{1,0:T(4,128)(2,1)} %get-tuple-element.83), channel_id=1, source_target_pairs={{1,0},{2,1},{3,2},{4,3},{5,4},{6,5},{7,6},{8,7},{9,8},{10,9},{11,1... | collective-permute-start | bytes 13832 | tf_op jit(solution)/shard_map/ppermute | solution.py:15
  11.1 49.9 %collective-permute-start.1 = (bf16[3,768]{1,0:T(4,128)(2,1)}, bf16[3,768]{1,0:T(4,128)(2,1)}, u32[]{:S(2)}, u32[]{:S(2)}) collective-permute-start(bf16[3,768]{1,0:T(4,128)(2,1)} %get-tuple-element.84), channel_id=1, source_target_pairs={{0,1},{1,2},{2,3},{3,4},{4,5},{5,6},{6,7},{7,8},{8,9},{9,10},{10,1... | collective-permute-start | bytes 13832 | tf_op jit(solution)/shard_map/ppermute | solution.py:12
  15.8 58.3 %collective-permute-start = (bf16[3,768]{1,0:T(4,128)(2,1)}, bf16[3,768]{1,0:T(4,128)(2,1)}, u32[]{:S(2)}, u32[]{:S(2)}) collective-permute-start(bf16[3,768]{1,0:T(4,128)(2,1)} %slice.119), channel_id=1, source_target_pairs={{1,0},{2,1},{3,2},{4,3},{5,4},{6,5},{7,6},{8,7},{9,8},{10,9},{11,1... | collective-permute-start | bytes 13832 | tf_op jit(solution)/shard_map/ppermute | solution.py:15
  23.9 0.8 copy-start.4
  28.9 52.4 %all-to-all-start.1 = ((s32[128,1,1]{2,1,0:T(1,128)}), s32[128,1,1]{2,1,0:T(1,128)}, u32[]{:S(2)}, u32[]{:S(2)}) async-start(s32[128,1,1]{2,1,0:T(1,128)} %copy.32), calls=%async_computation.1 | async-start | bytes 131072 | tf_op jit(solution)/shard_map/all_to_all | solution.py:151
  72.3 1.9 copy-start.5
  72.3 1.9 copy-start.7
  72.3 1.9 copy-start.8
  72.3 1.9 copy-start.10
  72.3 1.9 copy-start.11
  72.4 1.9 copy-start.12
  74.2 4.1 copy-start.14
  74.2 4.1 copy-start.15
  74.3 4.1 copy-start.16
  81.3 24.4 %all-to-all-start = ((bf16[8,128,768]{2,1,0:T(8,128)(2,1)}), bf16[8,128,768]{2,1,0:T(8,128)(2,1)}, u32[]{:S(2)}, u32[]{:S(2)}) async-start(bf16[8,128,768]{2,1,0:T(8,128)(2,1)} %bitcast.45), calls=%async_computation | async-start | bytes 3145728 | tf_op jit(solution)/shard_map/all_to_all | solution.py:120
  86.0 153.7 %reduce-scatter.2.cloned.1.call-start = ((), (), s32[]{:S(2)}) async-start(), calls=%async_computation.5 | async-start | bytes 5308416 | tf_op jit(solution)/shard_map/reduce_scatter | solution.py:129
  93.3 0.6 copy-start.19
  93.3 1.1 copy-start.3
  93.3 1.1 copy-start.17
  105.7 10.0 %copy-start.18 = (f32[128,8]{0,1:T(8,128)S(1)}, f32[128,8]{0,1:T(8,128)}, u32[]{:S(2)}) copy-start(f32[128,8]{0,1:T(8,128)} %param.22) | copy-start | bytes 12292
  105.7 10.2 %copy-start.13 = (s32[2048]{0:T(1024)S(1)}, s32[2048]{0:T(1024)}, u32[]{:S(2)}) copy-start(s32[2048]{0:T(1024)} %get-tuple-element.91) | copy-start | bytes 24580
  105.7 140.2 %all-to-all-start.2 = ((bf16[128,16,2304]{2,1,0:T(8,128)(2,1)}), bf16[128,16,2304]{2,1,0:T(8,128)(2,1)}, u32[]{:S(2)}, u32[]{:S(2)}) async-start(bf16[128,16,2304]{2,1,0:T(8,128)(2,1)} %bitcast.43), calls=%async_computation.2 | async-start | bytes 18874368 | tf_op jit(solution)/shard_map/all_to_all | solution.py:149
  115.9 123.7 %copy-start.6 = (bf16[128,2304]{1,0:T(8,128)(2,1)S(1)}, bf16[128,2304]{1,0:T(8,128)(2,1)}, u32[]{:S(2)}) copy-start(bf16[128,2304]{1,0:T(8,128)(2,1)} %param.20) | copy-start | bytes 1769476
  245.9 139.1 %all-to-all-start.3 = ((bf16[128,16,2304]{2,1,0:T(8,128)(2,1)}), bf16[128,16,2304]{2,1,0:T(8,128)(2,1)}, u32[]{:S(2)}, u32[]{:S(2)}) async-start(bf16[128,16,2304]{2,1,0:T(8,128)(2,1)} %bitcast.42), calls=%async_computation.4 | async-start | bytes 18874368 | tf_op jit(solution)/shard_map/all_to_all | solution.py:150
  412.1 8.7 %slice-start = ((s8[9437184]{0:T(1024)(128)(4,1)}), s8[4194304]{0:T(1024)(128)(4,1)S(1)}, s32[]{:S(2)}) async-start(s8[9437184]{0:T(1024)(128)(4,1)} %bitcast.40), calls=%async_computation.6 | async-start | bytes 8388608 | tf_op jit(solution)/shard_map/while
  412.1 8.7 %slice-start.1 = ((s8[9437184]{0:T(1024)(128)(4,1)}), s8[4194304]{0:T(1024)(128)(4,1)S(1)}, s32[]{:S(2)}) async-start(s8[9437184]{0:T(1024)(128)(4,1)} %bitcast.40), calls=%async_computation.7 | async-start | bytes 8388608 | tf_op jit(solution)/shard_map/while
  414.9 6.0 slice-start.2
  422.4 3.7 copy-start.2
  445.5 8.7 %slice-start = ((s8[9437184]{0:T(1024)(128)(4,1)}), s8[4194304]{0:T(1024)(128)(4,1)S(1)}, s32[]{:S(2)}) async-start(s8[9437184]{0:T(1024)(128)(4,1)} %bitcast.40), calls=%async_computation.6 | async-start | bytes 8388608 | tf_op jit(solution)/shard_map/while
  445.6 8.7 %slice-start.1 = ((s8[9437184]{0:T(1024)(128)(4,1)}), s8[4194304]{0:T(1024)(128)(4,1)S(1)}, s32[]{:S(2)}) async-start(s8[9437184]{0:T(1024)(128)(4,1)} %bitcast.40), calls=%async_computation.7 | async-start | bytes 8388608 | tf_op jit(solution)/shard_map/while
  448.3 6.0 slice-start.2
  455.8 3.7 copy-start.2
  479.0 8.7 %slice-start = ((s8[9437184]{0:T(1024)(128)(4,1)}), s8[4194304]{0:T(1024)(128)(4,1)S(1)}, s32[]{:S(2)}) async-start(s8[9437184]{0:T(1024)(128)(4,1)} %bitcast.40), calls=%async_computation.6 | async-start | bytes 8388608 | tf_op jit(solution)/shard_map/while
  479.0 8.7 %slice-start.1 = ((s8[9437184]{0:T(1024)(128)(4,1)}), s8[4194304]{0:T(1024)(128)(4,1)S(1)}, s32[]{:S(2)}) async-start(s8[9437184]{0:T(1024)(128)(4,1)} %bitcast.40), calls=%async_computation.7 | async-start | bytes 8388608 | tf_op jit(solution)/shard_map/while
  481.7 5.9 slice-start.2
  489.3 3.7 copy-start.2
  512.4 8.7 %slice-start = ((s8[9437184]{0:T(1024)(128)(4,1)}), s8[4194304]{0:T(1024)(128)(4,1)S(1)}, s32[]{:S(2)}) async-start(s8[9437184]{0:T(1024)(128)(4,1)} %bitcast.40), calls=%async_computation.6 | async-start | bytes 8388608 | tf_op jit(solution)/shard_map/while
  512.4 8.7 %slice-start.1 = ((s8[9437184]{0:T(1024)(128)(4,1)}), s8[4194304]{0:T(1024)(128)(4,1)S(1)}, s32[]{:S(2)}) async-start(s8[9437184]{0:T(1024)(128)(4,1)} %bitcast.40), calls=%async_computation.7 | async-start | bytes 8388608 | tf_op jit(solution)/shard_map/while
  515.1 6.0 slice-start.2
  522.7 3.7 copy-start.2
  545.8 8.7 %slice-start = ((s8[9437184]{0:T(1024)(128)(4,1)}), s8[4194304]{0:T(1024)(128)(4,1)S(1)}, s32[]{:S(2)}) async-start(s8[9437184]{0:T(1024)(128)(4,1)} %bitcast.40), calls=%async_computation.6 | async-start | bytes 8388608 | tf_op jit(solution)/shard_map/while
  545.8 8.7 %slice-start.1 = ((s8[9437184]{0:T(1024)(128)(4,1)}), s8[4194304]{0:T(1024)(128)(4,1)S(1)}, s32[]{:S(2)}) async-start(s8[9437184]{0:T(1024)(128)(4,1)} %bitcast.40), calls=%async_computation.7 | async-start | bytes 8388608 | tf_op jit(solution)/shard_map/while
  548.5 6.0 slice-start.2
  556.1 3.7 copy-start.2
  579.2 8.7 %slice-start = ((s8[9437184]{0:T(1024)(128)(4,1)}), s8[4194304]{0:T(1024)(128)(4,1)S(1)}, s32[]{:S(2)}) async-start(s8[9437184]{0:T(1024)(128)(4,1)} %bitcast.40), calls=%async_computation.6 | async-start | bytes 8388608 | tf_op jit(solution)/shard_map/while
  579.2 8.7 %slice-start.1 = ((s8[9437184]{0:T(1024)(128)(4,1)}), s8[4194304]{0:T(1024)(128)(4,1)S(1)}, s32[]{:S(2)}) async-start(s8[9437184]{0:T(1024)(128)(4,1)} %bitcast.40), calls=%async_computation.7 | async-start | bytes 8388608 | tf_op jit(solution)/shard_map/while
  582.0 6.0 slice-start.2
  589.5 3.7 copy-start.2
  612.6 8.7 %slice-start = ((s8[9437184]{0:T(1024)(128)(4,1)}), s8[4194304]{0:T(1024)(128)(4,1)S(1)}, s32[]{:S(2)}) async-start(s8[9437184]{0:T(1024)(128)(4,1)} %bitcast.40), calls=%async_computation.6 | async-start | bytes 8388608 | tf_op jit(solution)/shard_map/while
  612.6 8.7 %slice-start.1 = ((s8[9437184]{0:T(1024)(128)(4,1)}), s8[4194304]{0:T(1024)(128)(4,1)S(1)}, s32[]{:S(2)}) async-start(s8[9437184]{0:T(1024)(128)(4,1)} %bitcast.40), calls=%async_computation.7 | async-start | bytes 8388608 | tf_op jit(solution)/shard_map/while
  615.4 5.9 slice-start.2
  622.9 3.7 copy-start.2
  646.0 8.7 %slice-start = ((s8[9437184]{0:T(1024)(128)(4,1)}), s8[4194304]{0:T(1024)(128)(4,1)S(1)}, s32[]{:S(2)}) async-start(s8[9437184]{0:T(1024)(128)(4,1)} %bitcast.40), calls=%async_computation.6 | async-start | bytes 8388608 | tf_op jit(solution)/shard_map/while
  646.1 8.7 %slice-start.1 = ((s8[9437184]{0:T(1024)(128)(4,1)}), s8[4194304]{0:T(1024)(128)(4,1)S(1)}, s32[]{:S(2)}) async-start(s8[9437184]{0:T(1024)(128)(4,1)} %bitcast.40), calls=%async_computation.7 | async-start | bytes 8388608 | tf_op jit(solution)/shard_map/while
  648.8 6.0 slice-start.2
  656.4 3.7 copy-start.2
  670.8 6.8 copy-start.1
Sparse Core Ops, SparseCore 0:
  93.4 146.1 reduce-scatter.1
where the time goes:
time: 687 us; the launch traced here: 684 us
  waiting for transfers between devices  229 us (33%)
  local copies, waits for them, and re-layouts  212 us (31%)
  matrix products  130 us (19%)
  starting transfers between devices  49.3 us (7%)
  other arithmetic  48 us (7%)
  between operations  15 us (2%)
    reduce_scatter x1, waiting for transfers between devices, per_device(): lax.psum_scatter(jnp.dot(local_grad, qkv_weight, preferred_element_type=j...  115 us
    all_to_all x1, waiting for transfers between devices, per_device(): lax.all_to_all(send_grads, ('seq', 'exp'), split_axis=0, concat_axis=0, t...  108 us
    gather x8, local copies, waits for them, and re-layouts, tile_step(): rows_all[picked]  59.7 us
    gather x8, local copies, waits for them, and re-layouts, tile_step(): grads_all[picked]  59.7 us
    dot_general x8, matrix products, expert_terms(): lax.dot_general(rows_g, activated, (((0,), (0,)), ((), ())), preferred_el...  47.4 us
    while x64, local copies, waits for them, and re-layouts  30 us
    dot_general x8, matrix products, expert_terms(): jnp.dot(rows_h, own_weights[:, :2 * hidden], preferred_element_type=jnp.f...  29.7 us
    dot_general x8, matrix products, expert_terms(): jnp.dot(rows_g, own_weights[:, 2 * hidden:], preferred_element_type=jnp.f...  21.6 us
  transfers between devices with their start and end apart: 8, of which 3 were waited for; matrix products, arithmetic and copies ran while one was open for 14% of the time, Pallas kernels for 0%

commit v1 on v0

v1 whole, which is shorter than its diff:
```python
import functools

import jax
import jax.numpy as jnp
from jax import lax
from jax.experimental import pallas as pl
from jax.experimental.pallas import tpu as pltpu
from jax.sharding import PartitionSpec as P

BF16 = jnp.bfloat16
F32 = jnp.float32
HALO = 16
MIB = 1024 * 1024
VMEM_LIMIT = 60 * MIB
EXTRA = 128
RING = 4


def call_cost(flops, nbytes):
    return pl.CostEstimate(flops=int(flops), bytes_accessed=int(nbytes), transcendentals=0)


def norm_kernel(resid_ref, gain_ref, routes_ref, out_ref):
    rows = resid_ref[...].astype(F32)
    dim = rows.shape[1]
    scale = lax.rsqrt(jnp.mean(rows * rows, axis=1, keepdims=True) + 1e-06)
    out_ref[:, :dim] = (rows * scale * gain_ref[...]).astype(BF16)
    out_ref[:, dim:] = jnp.zeros((rows.shape[0], EXTRA), BF16)
    out_ref[:, dim : dim + routes_ref.shape[1]] = routes_ref[...].astype(F32).astype(BF16)


def norm_rows(resid, gain, routes):
    tokens, dim = resid.shape
    return pl.pallas_call(
        norm_kernel,
        out_shape=jax.ShapeDtypeStruct((tokens, dim + EXTRA), BF16),
        compiler_params=pltpu.CompilerParams(vmem_limit_bytes=VMEM_LIMIT),
        cost_estimate=call_cost(resid.size * 6, resid.size * 4),
        name="norm_rows",
    )(resid, gain.reshape(1, -1), routes)


def conv_kernel(
    tile,
    seq_ref,
    in_ref,
    in_low_ref,
    in_high_ref,
    grad_ref,
    grad_high_ref,
    ids_ref,
    taps_ref,
    weight_ref,
    flow_ref,
    local_ref,
    part_ref,
    in_ext,
    grad_ext,
):
    step = pl.program_id(0)
    rows = in_ref.shape[0]

    @pl.when(step == 0)
    def _():
        in_ext[:HALO] = in_low_ref[...].astype(F32)
        in_ext[HALO : HALO + rows] = in_ref[...].astype(F32)
        in_ext[HALO + rows :] = in_high_ref[...].astype(F32)
        grad_ext[:rows] = grad_ref[...].astype(F32)
        grad_ext[rows:] = grad_high_ref[...].astype(F32)

    first = pl.multiple_of(step * tile, tile)
    span = tile + 8
    taps = taps_ref[...]
    window = in_ext[pl.ds(first + HALO - 8, span + 8)]
    ids = ids_ref[pl.ds(first + HALO - 8, span + 8)]
    here = ids[8:]
    same = [None] + [(ids[8 - j : 8 - j + span] == here).astype(F32) for j in (1, 2, 3)]
    conv = taps[0:1] * window[8:]
    for j in (1, 2, 3):
        conv = conv + taps[j : j + 1] * window[8 - j : 8 - j + span] * same[j]
    gate = jax.nn.sigmoid(conv)
    pre = grad_ext[pl.ds(first, span)] * gate * (1.0 + conv * (1.0 - gate))
    result = taps[0:1] * pre[:tile]
    for j in (1, 2, 3):
        result = result + taps[j : j + 1] * (pre * same[j])[j : j + tile]
    local = result.astype(BF16)
    local_ref[...] = local
    part = jnp.dot(local, weight_ref[...], preferred_element_type=F32)
    part_ref[...] = part.astype(BF16)
    block = flow_ref.shape[0]
    per_tile = tile // block
    for inner in range(per_tile):

        @pl.when(step * per_tile + inner == seq_ref[0])
        def _():
            own = slice(inner * block, (inner + 1) * block)
            part_ref[own] = (part[own] + flow_ref[...].astype(F32)).astype(BF16)


def conv_project(seq_index, qkv_in, low, high, qkv_grad, grad_high, ids, taps, weight, out_grad):
    rows, width = qkv_in.shape
    dim = weight.shape[1]
    tile = 256
    whole = lambda shape: pl.BlockSpec(shape, lambda i, s: (0,) * len(shape))
    return pl.pallas_call(
        functools.partial(conv_kernel, tile),
        grid_spec=pltpu.PrefetchScalarGridSpec(
            num_scalar_prefetch=1,
            grid=(rows // tile,),
            in_specs=[
                whole(qkv_in.shape),
                whole(low.shape),
                whole(high.shape),
                whole(qkv_grad.shape),
                whole(grad_high.shape),
                whole(ids.shape),
                whole(taps.shape),
                whole(weight.shape),
                whole(out_grad.shape),
            ],
            out_specs=[
                pl.BlockSpec((tile, width), lambda i, s: (i, 0)),
                pl.BlockSpec((tile, dim), lambda i, s: (i, 0)),
            ],
            scratch_shapes=[
                pltpu.VMEM((rows + 2 * HALO, width), F32),
                pltpu.VMEM((rows + HALO, width), F32),
            ],
        ),
        out_shape=[
            jax.ShapeDtypeStruct((rows, width), BF16),
            jax.ShapeDtypeStruct((rows, dim), BF16),
        ],
        compiler_params=pltpu.CompilerParams(vmem_limit_bytes=VMEM_LIMIT),
        cost_estimate=call_cost(2 * rows * width * dim, 4 * rows * width * 2 + rows * dim * 2),
        name="conv_project",
    )(seq_index, qkv_in, low, high, qkv_grad, grad_high, ids, taps, weight, out_grad)


def seq_shift(s, dy, dc, sign):
    return (((s >> 1) + sign * dy) & (RING - 1)) * 2 + ((s & 1) ^ dc)


def exp_shift(e, dz, dx, sign):
    return (((e >> 2) + sign * dz) & (RING - 1)) * RING + ((e + sign * dx) & (RING - 1))


def slot_picker(names, own, capacity):
    count, tokens = own.shape
    match = [(names[k : k + 1] == own) for k in range(names.shape[0])]
    named = functools.reduce(jnp.logical_or, match)
    source = lax.broadcasted_iota(jnp.int32, (tokens, tokens), 0)
    target = lax.broadcasted_iota(jnp.int32, (tokens, tokens), 1)
    earlier = (source < target).astype(BF16)
    rank = jnp.dot(named.astype(BF16), earlier, preferred_element_type=F32).astype(jnp.int32)
    rank = jnp.where(named, rank, -1)
    slot = lax.broadcasted_iota(jnp.int32, (count, capacity, tokens), 1)
    picker = (rank[:, None, :] == slot).astype(F32)
    return picker, match


def pick_norm_kernel(per_token, capacity, place_ref, rows_ref, *out_refs):
    count = len(out_refs)
    tokens = rows_ref.shape[1]
    dim = out_refs[0].shape[2]
    names = rows_ref[0, :, dim:].astype(F32).T[:per_token].astype(jnp.int32)
    turn = lax.broadcasted_iota(jnp.int32, (count, tokens), 0)
    own = seq_shift(place_ref[0], turn >> 1, turn & 1, 1) * (RING * RING) + place_ref[1]
    picker, _ = slot_picker(names, own, capacity)
    picker = picker.reshape(count * capacity, tokens).astype(BF16)
    picked = jnp.dot(picker, rows_ref[0, :, :dim], preferred_element_type=F32).astype(BF16)
    for index, out_ref in enumerate(out_refs):
        out_ref[0] = picked[index * capacity : (index + 1) * capacity]


def pick_norm(place, rows, dim, per_token, capacity, count):
    blocks, tokens, width = rows.shape
    return pl.pallas_call(
        functools.partial(pick_norm_kernel, per_token, capacity),
        grid_spec=pltpu.PrefetchScalarGridSpec(
            num_scalar_prefetch=1,
            grid=(blocks,),
            in_specs=[
                pl.BlockSpec(
                    (1, tokens, width), lambda i, p: (exp_shift(p[1], i >> 2, i & 3, -1), 0, 0)
                )
            ],
            out_specs=[pl.BlockSpec((1, capacity, dim), lambda i, p: (i, 0, 0))] * count,
        ),
        out_shape=[jax.ShapeDtypeStruct((blocks, capacity, dim), BF16)] * count,
        compiler_params=pltpu.CompilerParams(vmem_limit_bytes=VMEM_LIMIT),
        cost_estimate=call_cost(
            2 * count * capacity * blocks * tokens * dim,
            2 * dim * blocks * (tokens + count * capacity),
        ),
        name="pick_norm",
    )(place, rows)


def pick_grad_kernel(per_token, capacity, place_ref, table_ref, rows_ref, *out_refs):
    count = len(out_refs)
    tokens = rows_ref.shape[1]
    names = table_ref[0, :per_token].astype(jnp.int32)
    turn = lax.broadcasted_iota(jnp.int32, (count, tokens), 0)
    own = place_ref[0] * (RING * RING) + exp_shift(place_ref[1], turn >> 2, turn & 3, 1)
    picker, match = slot_picker(names, own, capacity)
    weights = table_ref[0, per_token:]
    scale = functools.reduce(
        jnp.add, [jnp.where(match[k], weights[k : k + 1], 0.0) for k in range(per_token)]
    )
    scales = jnp.sum(picker * scale[:, None, :], axis=2, keepdims=True)
    picker = picker.reshape(count * capacity, tokens).astype(BF16)
    picked = jnp.dot(picker, rows_ref[0], preferred_element_type=F32)
    picked = (picked * scales.reshape(count * capacity, 1)).astype(BF16)
    for index, out_ref in enumerate(out_refs):
        out_ref[0] = picked[index * capacity : (index + 1) * capacity]


def pick_grad(place, table, rows, per_token, capacity, count):
    blocks, tokens, dim = rows.shape
    source = lambda i, p: (seq_shift(p[0], i >> 1, i & 1, -1), 0, 0)
    return pl.pallas_call(
        functools.partial(pick_grad_kernel, per_token, capacity),
        grid_spec=pltpu.PrefetchScalarGridSpec(
            num_scalar_prefetch=1,
            grid=(blocks,),
            in_specs=[
                pl.BlockSpec((1, 2 * per_token, tokens), source),
                pl.BlockSpec((1, tokens, dim), source),
            ],
            out_specs=[pl.BlockSpec((1, capacity, dim), lambda i, p: (i, 0, 0))] * count,
        ),
        out_shape=[jax.ShapeDtypeStruct((blocks, capacity, dim), BF16)] * count,
        compiler_params=pltpu.CompilerParams(vmem_limit_bytes=VMEM_LIMIT),
        cost_estimate=call_cost(
            2 * count * capacity * blocks * tokens * dim,
            2 * dim * blocks * (tokens + count * capacity),
        ),
        name="pick_grad",
    )(place, table, rows)


def forward_kernel(sources, *refs):
    row_refs = refs[:sources]
    weight_ref, rows_out, act_ref, gate_ref, up_ref = refs[sources:]
    pair, capacity, _ = row_refs[0].shape
    for inner in range(pair):
        for index in range(sources):
            at = (inner * sources + index) * capacity
            rows_out[at : at + capacity] = row_refs[index][inner]
    hidden = act_ref.shape[1]
    mixed = jnp.dot(rows_out[...], weight_ref[...], preferred_element_type=F32)
    gate = mixed[:, :hidden]
    up = mixed[:, hidden:]
    sig = jax.nn.sigmoid(gate)
    silu = gate * sig
    act_ref[...] = (silu * up).astype(BF16)
    gate_ref[...] = up * sig * (1.0 + gate * (1.0 - sig))
    up_ref[...] = silu


def expert_forward(rows, weight, hidden):
    sources = len(rows)
    blocks, capacity, dim = rows[0].shape
    pair = 2
    tile = sources * pair * capacity
    total = sources * blocks * capacity
    row_spec = lambda width: pl.BlockSpec((tile, width), lambda i: (i, 0))
    return pl.pallas_call(
        functools.partial(forward_kernel, sources),
        grid=(blocks // pair,),
        in_specs=[pl.BlockSpec((pair, capacity, dim), lambda i: (i, 0, 0))] * sources
        + [pl.BlockSpec((dim, 2 * hidden), lambda i: (0, 0))],
        out_specs=[row_spec(dim), row_spec(hidden), row_spec(hidden), row_spec(hidden)],
        out_shape=[
            jax.ShapeDtypeStruct((total, dim), BF16),
            jax.ShapeDtypeStruct((total, hidden), BF16),
            jax.ShapeDtypeStruct((total, hidden), F32),
            jax.ShapeDtypeStruct((total, hidden), F32),
        ],
        compiler_params=pltpu.CompilerParams(vmem_limit_bytes=VMEM_LIMIT),
        cost_estimate=call_cost(4 * total * dim * hidden, 4 * total * dim + 10 * total * hidden),
        name="expert_forward",
    )(*rows, weight)


def backward_kernel(sources, *refs):
    grad_refs = refs[:sources]
    gate_ref, up_ref, weight_ref, rows_ref, act_ref, out_ref = refs[sources : sources + 6]
    grads_all, hidden_all, sems = refs[sources + 6 :]
    step = pl.program_id(0)
    tile = gate_ref.shape[0]
    hidden = act_ref.shape[1]
    width = rows_ref.shape[1]
    size = grad_refs[0].shape[0]
    per_tile = tile // size
    row_steps = sources // per_tile
    copies = [
        pltpu.make_async_copy(
            grad_refs[index], grads_all.at[pl.ds(index * size, size)], sems.at[index]
        )
        for index in range(sources)
    ]

    @pl.when(step == 0)
    def _():
        for copy in copies:
            copy.start()

    for turn in range(row_steps):

        @pl.when(step == turn)
        def _():
            for copy in copies[turn * per_tile : (turn + 1) * per_tile]:
                copy.wait()

    @pl.when(step < row_steps)
    def _():
        where = pl.ds(pl.multiple_of(step * tile, tile), tile)
        act_grad = jnp.dot(grads_all[where], weight_ref[...], preferred_element_type=F32)
        hidden_all[where, :hidden] = (act_grad * gate_ref[...]).astype(BF16)
        hidden_all[where, hidden:] = (act_grad * up_ref[...]).astype(BF16)

    @pl.when(step >= row_steps)
    def _():
        columns = pl.ds(pl.multiple_of((step - row_steps) * width, width), width)
        over_rows = (((0,), (0,)), ((), ()))
        out_ref[:, : 2 * hidden] = lax.dot_general(
            rows_ref[...], hidden_all[...], over_rows, preferred_element_type=F32
        ).astype(BF16)
        out_ref[:, 2 * hidden :] = lax.dot_general(
            grads_all[:, columns], act_ref[...], over_rows, preferred_element_type=F32
        ).astype(BF16)


def expert_backward(grads, gate, up, weights, rows, act):
    sources = len(grads)
    total, dim = rows.shape
    hidden = act.shape[1]
    tile, width = 256, 256
    row_steps, column_steps = total // tile, dim // width
    row_spec = lambda cols: pl.BlockSpec(
        (tile, cols), lambda i: (jnp.minimum(i, row_steps - 1), 0)
    )
    column_of = lambda i: jnp.maximum(i - row_steps, 0)
    return pl.pallas_call(
        functools.partial(backward_kernel, sources),
        grid=(row_steps + column_steps,),
        in_specs=[pl.BlockSpec(memory_space=pl.ANY)] * sources
        + [
            row_spec(hidden),
            row_spec(hidden),
            pl.BlockSpec((dim, hidden), lambda i: (0, 2)),
            pl.BlockSpec((total, width), lambda i: (0, column_of(i))),
            pl.BlockSpec((total, hidden), lambda i: (0, 0)),
        ],
        out_specs=pl.BlockSpec((width, 3 * hidden), lambda i: (column_of(i), 0)),
        out_shape=jax.ShapeDtypeStruct((dim, 3 * hidden), BF16),
        scratch_shapes=[
            pltpu.VMEM((total, dim), BF16),
            pltpu.VMEM((total, 2 * hidden), BF16),
            pltpu.SemaphoreType.DMA((sources,)),
        ],
        compiler_params=pltpu.CompilerParams(vmem_limit_bytes=VMEM_LIMIT),
        cost_estimate=call_cost(8 * total * dim * hidden, 4 * total * dim + 20 * total * hidden),
        name="expert_backward",
    )(*grads, gate, up, weights, rows, act)


def exchange_seq(blocks, n_seq):
    got = [blocks[0]]
    for r in range(1, n_seq):
        pairs = [(s, seq_shift(s, r >> 1, r & 1, 1)) for s in range(n_seq)]
        got.append(lax.ppermute(blocks[r], "seq", pairs))
    return got


def exchange_exp(blocks, n_exp):
    got = [blocks[0]]
    for q in range(1, n_exp):
        pairs = [(e, exp_shift(e, q >> 2, q & 3, 1)) for e in range(n_exp)]
        got.append(lax.ppermute(blocks[q], "exp", pairs))
    return got


def per_device(
    qkv_in,
    qkv_grad,
    conv_weight,
    doc_ids,
    qkv_weight,
    resid,
    norm_gain,
    out_grad,
    routes,
    route_weights,
    expert_weights,
):
    rows, width = qkv_in.shape
    tokens, dim = resid.shape
    per_token = routes.shape[1]
    hidden = expert_weights.shape[2] // 3
    n_seq, n_exp = lax.axis_size("seq"), lax.axis_size("exp")
    experts = n_seq * n_exp
    capacity = 2 * tokens * per_token // experts
    seq_index, exp_index = lax.axis_index("seq"), lax.axis_index("exp")
    own_weights = expert_weights[0]

    forward = [(i, i + 1) for i in range(n_exp - 1)]
    backward = [(i + 1, i) for i in range(n_exp - 1)]
    low = lax.ppermute(qkv_in[-HALO:], "exp", forward)
    high = lax.ppermute(qkv_in[:HALO], "exp", backward)
    grad_high = lax.ppermute(qkv_grad[:HALO], "exp", backward)

    place = jnp.stack([seq_index, exp_index]).astype(jnp.int32)
    table = jnp.concatenate([routes.astype(F32), route_weights], 1).T
    tables = jnp.broadcast_to(table[None], (n_seq,) + table.shape)
    tables = lax.all_to_all(tables, "seq", split_axis=0, concat_axis=0, tiled=True)
    normed = norm_rows(resid, norm_gain, routes)
    exp_normed = lax.all_gather(normed, "exp")

    edge = jnp.full((HALO,), -1, jnp.int32)
    ids = lax.dynamic_slice_in_dim(
        jnp.concatenate([edge, doc_ids, edge]), exp_index * rows, rows + 2 * HALO
    )
    local_grad, partial = conv_project(
        seq_index.reshape(1),
        qkv_in,
        low,
        high,
        qkv_grad,
        grad_high,
        ids.reshape(-1, 1),
        conv_weight,
        qkv_weight,
        out_grad,
    )
    flow = lax.psum(partial, "seq")
    flow, local_grad = lax.optimization_barrier((flow, local_grad))
    qkv_in_grad = lax.all_to_all(local_grad, "seq", split_axis=0, concat_axis=1, tiled=True)

    send_rows = pick_norm(place, exp_normed, dim, per_token, capacity, n_seq)
    got_rows = exchange_seq(send_rows, n_seq)
    rows_all, act, gate, up = expert_forward(got_rows, own_weights, hidden)

    flow = flow.reshape(n_seq, tokens, dim)
    send_grads = pick_grad(place, tables, flow, per_token, capacity, n_exp)
    got_grads = [g.reshape(-1, dim) for g in exchange_exp(send_grads, n_exp)]
    expert_grads = expert_backward(got_grads, gate, up, own_weights, rows_all, act)
    return (qkv_in_grad, expert_grads[None])


def solution(mesh):
    return jax.shard_map(
        per_device,
        mesh=mesh,
        in_specs=(
            P("exp", "seq"),
            P("exp", "seq"),
            P(None, "seq"),
            P(),
            P("seq", None),
            P(("exp", "seq"), None),
            P(),
            P(("exp", "seq"), None),
            P(("exp", "seq"), None),
            P(("exp", "seq"), None),
            P(("seq", "exp"), None, None),
        ),
        out_specs=(P(("exp", "seq"), None), P(("seq", "exp"), None, None)),
        check_vma=False,
    )
```

time: 687 us -> 438 us (0.64)
  the two profiles are of different devices: /device:TPU:26 before, /device:TPU:1 now
where the time goes in v1:
time: 438 us; the launch traced here: 436 us
  waiting for transfers between devices  237 us (54%)
  Pallas kernels  91.3 us (21%)
  starting transfers between devices  80 us (18%)
  between operations  15.8 us (4%)
  local copies, waits for them, and re-layouts  11.2 us (3%)
    ppermute x7, waiting for transfers between devices, exchange_seq(): got.append(lax.ppermute(blocks[r], 'seq', pairs))  91 us
    ppermute x15, waiting for transfers between devices, exchange_exp(): got.append(lax.ppermute(blocks[q], 'exp', pairs))  74.7 us
    psum x1, waiting for transfers between devices, per_device(): flow = lax.psum(partial, 'seq')  69 us
    ppermute x7, starting transfers between devices, exchange_seq(): got.append(lax.ppermute(blocks[r], 'seq', pairs))  32.6 us
    pallas_call x1, Pallas kernels, expert_backward(): pl.pallas_call(functools.partial(backward_kernel, sources), grid=(row_ste...  31.4 us
    ppermute x15, starting transfers between devices, exchange_exp(): got.append(lax.ppermute(blocks[q], 'exp', pairs))  29.2 us
    pallas_call x1, Pallas kernels, expert_forward(): pl.pallas_call(functools.partial(forward_kernel, sources), grid=(blocks /...  17 us
    pallas_call x1, Pallas kernels, pick_norm(): pl.pallas_call(functools.partial(pick_norm_kernel, per_token, capacity),...  16.3 us
  transfers between devices with their start and end apart: 29, of which 9 were waited for; matrix products, arithmetic and copies ran while one was open for 2% of the time, Pallas kernels for 10%

profile of v1, /device:TPU:1, one launch (start us, length us, event | category | flops | bytes accessed | tf_op | source)
XLA Modules:
  0.0 435.5 jit_solution(11615730055345904102)
XLA Ops:
  8.0 0.0 all-reduce.2.cloned.1.call-start
  8.0 0.8 fusion
  8.8 3.9 collective-permute-start
  12.7 1.3 collective-permute-start.1
  14.0 0.7 slice.11
  14.8 1.3 collective-permute-start.2
  16.1 0.9 concatenate.6
  17.0 0.1 dynamic_slice.3
  17.1 1.0 reshape.89.ids_ref
  18.1 0.0 collective-permute-done.in_low_ref
  18.1 0.0 collective-permute-done.1.in_high_ref
  18.2 1.8 collective-permute-done.2.grad_high_ref
  20.0 0.6 copy-done.18
  20.6 14.3 %conv_project.1 = (bf16[1024,768]{1,0:T(8,128)(2,1)}, bf16[1024,2304]{1,0:T(8,128)(2,1)}) custom-call(s32[1]{0:T(128)} %bitcast.seq_ref, bf16[1024,768]{1,0:T(8,128)(2,1)} %in_ref.1, bf16[16,768]{1,0:T(8,128)(2,1)} %copy-done.16, bf16[16,768]{1,0:T(8,128)(2,1)} %copy-done.17, bf16[1024,768]{1,0:T(8,128)(2,1)} %grad_ref.1, bf16[16,768]{1,0:T(8,128)(2,1)} %copy-done.18, ...), custom_call_target="tpu_custom_call" | custom-call | flops 3623878656 | bytes 11010048 | tf_op jit(solution)/shard_map/conv_project/pallas_call | solution.py:105
  34.8 0.0 all-reduce.2.cloned.1.call-update
  34.9 0.0 copy-start.3
  34.9 0.0 all-gather.3.cloned.1.call-start
  34.9 0.6 copy-done.1
  35.5 0.7 copy.17.routes_ref
  36.3 0.6 reshape.87.gain_ref
  36.9 2.2 norm_rows.1
  39.0 0.0 all-gather.3.cloned.1.call-update
  39.1 0.6 broadcast_in_dim.4
  39.7 6.6 %all-to-all-start.1 = ((f32[8,16,128]{2,1,0:T(8,128)}), f32[8,16,128]{2,1,0:T(8,128)S(1)}, u32[]{:S(2)}, u32[]{:S(2)}) async-start(f32[8,16,128]{2,1,0:T(8,128)} %broadcast_in_dim.4), calls=%async_computation.1 | async-start | bytes 131072 | tf_op jit(solution)/shard_map/all_to_all | solution.py:418
  46.3 0.6 pad_add_fusion.place_ref
  46.9 69.0 %all-reduce.2.cloned.1.call-done = bf16[1024,2304]{1,0:T(8,128)(2,1)} async-done(((bf16[1024,2304]{1,0:T(8,128)(2,1)}), bf16[1024,2304]{1,0:T(8,128)(2,1)}) %all-reduce.2.cloned.1.call-update) | async-done | bytes 4718608 | tf_op jit(solution)/shard_map/psum | solution.py:438
  115.9 0.0 all-to-all-done.1.table_ref
  115.9 0.6 copy-done
  116.6 10.2 %pick_grad.1 = (bf16[8,16,2304]{2,1,0:T(8,128)(2,1)}, bf16[8,16,2304]{2,1,0:T(8,128)(2,1)}, bf16[8,16,2304]{2,1,0:T(8,128)(2,1)}, bf16[8,16,2304]{2,1,0:T(8,128)...) custom-call(s32[2]{0:T(128)} %pad_add_fusion.place_ref, ...), custom_call_target="tpu_custom_call" | custom-call | flops 1207959552 | bytes 14155776 | tf_op jit(solution)/shard_map/pick_grad/pallas_call | solution.py:222
  126.8 1.4 collective-permute-start.6
  128.1 1.6 collective-permute-start.7
  129.7 3.7 collective-permute-start.8
  133.4 1.0 collective-permute-start.9
  134.4 2.2 collective-permute-start.10
  136.6 41.8 %collective-permute-done.6 = bf16[8,16,2304]{2,1,0:T(8,128)(2,1)} collective-permute-done((bf16[8,16,2304]{2,1,0:T(8,128)(2,1)}, bf16[8,16,2304]{2,1,0:T(8,128)(2,1)}, u32[]{:S(2)}, u32[]{:S(2)}) %collective-permute-start.6) | collective-permute-done | bytes 589856 | tf_op jit(solution)/shard_map/ppermute | solution.py:382
  178.4 3.5 collective-permute-start.11
  181.9 3.5 collective-permute-start.12
  185.3 16.3 %pick_norm.1 = (bf16[16,16,2304]{2,1,0:T(8,128)(2,1)}, bf16[16,16,2304]{2,1,0:T(8,128)(2,1)}, bf16[16,16,2304]{2,1,0:T(8,128)(2,1)}, bf16[16,16,2304]{2,1,0:T(8,...) custom-call(s32[2]{0:T(128)} %pad_add_fusion.place_ref, ...), custom_call_target="tpu_custom_call" | custom-call | flops 1207959552 | bytes 18874368 | tf_op jit(solution)/shard_map/pick_norm/pallas_call | solution.py:178
  201.7 0.8 copy-done.6
  202.5 19.5 %collective-permute-start.18 = (bf16[16,16,2304]{2,1,0:T(8,128)(2,1)}, bf16[16,16,2304]{2,1,0:T(8,128)(2,1)S(1)}, u32[]{:S(2)}, u32[]{:S(2)}) collective-permute-start(bf16[16,16,2304]{2,1,0:T(8,128)(2,1)} %get-tuple-element.55), channel_id=1, source_target_pairs={{0,16},{16,0},{32,48},{48,32},{64,80},{80,64},{96,112},{112,96},{1... | collective-permute-start | bytes 3538952 | tf_op jit(solution)/shard_map/ppermute | solution.py:374
  222.0 0.0 collective-permute-done.10
  222.0 4.8 %collective-permute-start.13 = (bf16[8,16,2304]{2,1,0:T(8,128)(2,1)}, bf16[8,16,2304]{2,1,0:T(8,128)(2,1)}, u32[]{:S(2)}, u32[]{:S(2)}) collective-permute-start(bf16[8,16,2304]{2,1,0:T(8,128)(2,1)} %get-tuple-element.49), channel_id=1, source_target_pairs={{0,11},{1,8},{2,9},{3,10},{4,15},{5,12},{6,13},{7,14},{8,3},{9,0},... | collective-permute-start | bytes 1769480 | tf_op jit(solution)/shard_map/ppermute | solution.py:382
  226.8 0.0 collective-permute-done.11
  226.9 0.1 collective-permute-start.15
  227.0 0.7 copy-done.9
  227.7 0.2 copy-done.10
  227.8 5.1 %all-to-all-start = ((bf16[8,128,768]{2,1,0:T(8,128)(2,1)}), bf16[8,128,768]{2,1,0:T(8,128)(2,1)S(1)}, u32[]{:S(2)}, u32[]{:S(2)}) async-start(bf16[8,128,768]{2,1,0:T(8,128)(2,1)} %bitcast.1), calls=%async_computation | async-start | bytes 3145728 | tf_op jit(solution)/shard_map/all_to_all | solution.py:440
  232.9 6.9 %collective-permute-done.13 = bf16[8,16,2304]{2,1,0:T(8,128)(2,1)} collective-permute-done((bf16[8,16,2304]{2,1,0:T(8,128)(2,1)}, bf16[8,16,2304]{2,1,0:T(8,128)(2,1)}, u32[]{:S(2)}, u32[]{:S(2)}) %collective-permute-start.13) | collective-permute-done | bytes 589856 | tf_op jit(solution)/shard_map/ppermute | solution.py:382
  239.8 16.8 %collective-permute-done.14 = bf16[8,16,2304]{2,1,0:T(8,128)(2,1)} collective-permute-done((bf16[8,16,2304]{2,1,0:T(8,128)(2,1)}, bf16[8,16,2304]{2,1,0:T(8,128)(2,1)}, u32[]{:S(2)}, u32[]{:S(2)}) %collective-permute-start.14) | collective-permute-done | bytes 589856 | tf_op jit(solution)/shard_map/ppermute | solution.py:382
  256.6 8.3 %collective-permute-start.21 = (bf16[16,16,2304]{2,1,0:T(8,128)(2,1)}, bf16[16,16,2304]{2,1,0:T(8,128)(2,1)}, u32[]{:S(2)}, u32[]{:S(2)}) collective-permute-start(bf16[16,16,2304]{2,1,0:T(8,128)(2,1)} %get-tuple-element.58), channel_id=1, source_target_pairs={{0,64},{16,80},{32,96},{48,112},{64,0},{80,16},{96,32},{112,48},{1... | collective-permute-start | bytes 3538952 | tf_op jit(solution)/shard_map/ppermute | solution.py:374
  264.9 0.4 collective-permute-start.22
  265.3 4.4 %collective-permute-start.23 = (bf16[16,16,2304]{2,1,0:T(8,128)(2,1)}, bf16[16,16,2304]{2,1,0:T(8,128)(2,1)}, u32[]{:S(2)}, u32[]{:S(2)}) collective-permute-start(bf16[16,16,2304]{2,1,0:T(8,128)(2,1)} %get-tuple-element.60), channel_id=1, source_target_pairs={{0,96},{16,112},{32,0},{48,16},{64,32},{80,48},{96,64},{112,80},{1... | collective-permute-start | bytes 3538952 | tf_op jit(solution)/shard_map/ppermute | solution.py:374
  269.7 1.3 copy.18
  271.0 72.9 %collective-permute-done.20.refs_3_ = bf16[16,16,2304]{2,1,0:T(8,128)(2,1)} collective-permute-done((bf16[16,16,2304]{2,1,0:T(8,128)(2,1)}, bf16[16,16,2304]{2,1,0:T(8,128)(2,1)}, u32[]{:S(2)}, u32[]{:S(2)}) %collective-permute-start.20) | collective-permute-done | bytes 1179680 | tf_op jit(solution)/shard_map/ppermute | solution.py:374
  343.9 0.0 collective-permute-start.17
  343.9 1.2 collective-permute-start.3
  345.1 6.0 %collective-permute-start.4 = (bf16[8,16,2304]{2,1,0:T(8,128)(2,1)}, bf16[8,16,2304]{2,1,0:T(8,128)(2,1)S(1)}, u32[]{:S(2)}, u32[]{:S(2)}) collective-permute-start(bf16[8,16,2304]{2,1,0:T(8,128)(2,1)} %get-tuple-element.40), channel_id=1, source_target_pairs={{0,2},{1,3},{2,0},{3,1},{4,6},{5,7},{6,4},{7,5},{8,10},{9,11},{10,... | collective-permute-start | bytes 1769480 | tf_op jit(solution)/shard_map/ppermute | solution.py:382
  351.1 18.1 %collective-permute-done.24.refs_7_ = bf16[16,16,2304]{2,1,0:T(8,128)(2,1)} collective-permute-done((bf16[16,16,2304]{2,1,0:T(8,128)(2,1)}, bf16[16,16,2304]{2,1,0:T(8,128)(2,1)}, u32[]{:S(2)}, u32[]{:S(2)}) %collective-permute-start.24) | collective-permute-done | bytes 1179680 | tf_op jit(solution)/shard_map/ppermute | solution.py:374
  369.2 0.3 collective-permute-start.5
  369.6 17.0 %expert_forward.1 = (bf16[2048,2304]{1,0:T(8,128)(2,1)}, bf16[2048,512]{1,0:T(8,128)(2,1)}, f32[2048,512]{1,0:T(8,128)}, f32[2048,512]{1,0:T(8,128)}) custom-call(bf16[16,16,2304]{2,1,0:T(8,128)(2,1)} %get-tuple-element.54.refs_0_, bf16[16,16,2304]{2,1,0:T(8,128)(2,1)} %copy-done.4, bf16[16,16,2304]{2,1,0:T(8,128)(2,1)} %collective-permute-done.19.refs_2_, ...), custom_call_target="tpu_custom_call" | custom-call | flops 9663676416 | bytes 29360128 | tf_op jit(solution)/shard_map/expert_forward/pallas_call | solution.py:269
  386.6 3.9 collective-permute-done.4
  390.5 5.4 %collective-permute-done.5 = bf16[8,16,2304]{2,1,0:T(8,128)(2,1)S(1)} collective-permute-done((bf16[8,16,2304]{2,1,0:T(8,128)(2,1)S(1)}, bf16[8,16,2304]{2,1,0:T(8,128)(2,1)S(1)}, u32[]{:S(2)}, u32[]{:S(2)}) %collective-permute-start.5) | collective-permute-done | bytes 589856 | tf_op jit(solution)/shard_map/ppermute | solution.py:382
  395.9 0.8 copy-done.15
  396.7 31.4 %expert_backward.1 = bf16[2304,1536]{1,0:T(8,128)(2,1)} custom-call(bf16[128,2304]{1,0:T(8,128)(2,1)} %bitcast.34, bf16[128,2304]{1,0:T(8,128)(2,1)} %bitcast.42, bf16[128,2304]{1,0:T(8,128)(2,1)} %bitcast.43, bf16[128,2304]{1,0:T(8,128)(2,1)} %bitcast.44, bf16[128,2304]{1,0:T(8,128)(2,1)} %bitcast.10.refs_4_, bf16[128,2304]{1,0:T(8,128)(2,1)} %bitcast.11.refs_5_, ...), custom_call_target="tpu_custom_call" | custom-call | flops 19327352832 | bytes 39845888 | tf_op jit(solution)/shard_map/expert_backward/pallas_call | solution.py:346
  (53 shorter events, 0.1 us)
Async XLA Ops:
  8.0 107.9 %all-reduce.2.cloned.1.call-start = ((), (), s32[]{:S(2)}) async-start(), calls=%async_computation.2 | async-start | bytes 9437184 | tf_op jit(solution)/shard_map/psum | solution.py:438
  8.8 9.3 %collective-permute-start = (bf16[16,768]{1,0:T(8,128)(2,1)S(1)}, bf16[16,768]{1,0:T(8,128)(2,1)S(1)}, u32[]{:S(2)}, u32[]{:S(2)}) collective-permute-start(bf16[16,768]{1,0:T(8,128)(2,1)S(1)} %get-tuple-element.67), channel_id=1, source_target_pairs={{0,1},{1,2},{2,3},{3,4},{4,5},{5,6},{6,7},{7,8},{8,9},{9,10},{10,1... | collective-permute-start | bytes 73736 | tf_op jit(solution)/shard_map/ppermute | solution.py:411
  12.7 5.4 %collective-permute-start.1 = (bf16[16,768]{1,0:T(8,128)(2,1)S(1)}, bf16[16,768]{1,0:T(8,128)(2,1)S(1)}, u32[]{:S(2)}, u32[]{:S(2)}) collective-permute-start(bf16[16,768]{1,0:T(8,128)(2,1)S(1)} %get-tuple-element.66), channel_id=1, source_target_pairs={{1,0},{2,1},{3,2},{4,3},{5,4},{6,5},{7,6},{8,7},{9,8},{10,9},{11,1... | collective-permute-start | bytes 73736 | tf_op jit(solution)/shard_map/ppermute | solution.py:412
  14.8 5.2 %collective-permute-start.2 = (bf16[16,768]{1,0:T(8,128)(2,1)S(1)}, bf16[16,768]{1,0:T(8,128)(2,1)S(1)}, u32[]{:S(2)}, u32[]{:S(2)}) collective-permute-start(bf16[16,768]{1,0:T(8,128)(2,1)S(1)} %slice.11), channel_id=1, source_target_pairs={{1,0},{2,1},{3,2},{4,3},{5,4},{6,5},{7,6},{8,7},{9,8},{10,9},{11,1... | collective-permute-start | bytes 73736 | tf_op jit(solution)/shard_map/ppermute | solution.py:413
  18.1 1.8 copy-start.16
  18.1 1.8 copy-start.17
  20.0 0.6 copy-start.18
  34.8 0.7 copy-start.1
  34.8 1.4 copy-start.2
  34.9 4.2 copy-start.3
  34.9 150.4 %all-gather.3.cloned.1.call-start = ((), (), s32[]{:S(2)}) async-start(), calls=%async_computation.3 | async-start | bytes 10584064 | tf_op jit(solution)/shard_map/all_gather | solution.py:420
  39.7 76.2 %all-to-all-start.1 = ((f32[8,16,128]{2,1,0:T(8,128)}), f32[8,16,128]{2,1,0:T(8,128)S(1)}, u32[]{:S(2)}, u32[]{:S(2)}) async-start(f32[8,16,128]{2,1,0:T(8,128)} %broadcast_in_dim.4), calls=%async_computation.1 | async-start | bytes 131072 | tf_op jit(solution)/shard_map/all_to_all | solution.py:418
  115.9 0.6 copy-start
  126.8 51.6 %collective-permute-start.6 = (bf16[8,16,2304]{2,1,0:T(8,128)(2,1)}, bf16[8,16,2304]{2,1,0:T(8,128)(2,1)}, u32[]{:S(2)}, u32[]{:S(2)}) collective-permute-start(bf16[8,16,2304]{2,1,0:T(8,128)(2,1)} %get-tuple-element.42), channel_id=1, source_target_pairs={{0,4},{1,5},{2,6},{3,7},{4,8},{5,9},{6,10},{7,11},{8,12},{9,13},{1... | collective-permute-start | bytes 1769480 | tf_op jit(solution)/shard_map/ppermute | solution.py:382
  128.1 53.7 %collective-permute-start.7 = (bf16[8,16,2304]{2,1,0:T(8,128)(2,1)}, bf16[8,16,2304]{2,1,0:T(8,128)(2,1)}, u32[]{:S(2)}, u32[]{:S(2)}) collective-permute-start(bf16[8,16,2304]{2,1,0:T(8,128)(2,1)} %get-tuple-element.43), channel_id=1, source_target_pairs={{0,5},{1,6},{2,7},{3,4},{4,9},{5,10},{6,11},{7,8},{8,13},{9,14},{1... | collective-permute-start | bytes 1769480 | tf_op jit(solution)/shard_map/ppermute | solution.py:382
  129.7 71.9 %collective-permute-start.8 = (bf16[8,16,2304]{2,1,0:T(8,128)(2,1)}, bf16[8,16,2304]{2,1,0:T(8,128)(2,1)S(1)}, u32[]{:S(2)}, u32[]{:S(2)}) collective-permute-start(bf16[8,16,2304]{2,1,0:T(8,128)(2,1)} %get-tuple-element.44), channel_id=1, source_target_pairs={{0,6},{1,7},{2,4},{3,5},{4,10},{5,11},{6,8},{7,9},{8,14},{9,15},{1... | collective-permute-start | bytes 1769480 | tf_op jit(solution)/shard_map/ppermute | solution.py:382
  133.4 88.6 %collective-permute-start.9 = (bf16[8,16,2304]{2,1,0:T(8,128)(2,1)}, bf16[8,16,2304]{2,1,0:T(8,128)(2,1)S(1)}, u32[]{:S(2)}, u32[]{:S(2)}) collective-permute-start(bf16[8,16,2304]{2,1,0:T(8,128)(2,1)} %get-tuple-element.45), channel_id=1, source_target_pairs={{0,7},{1,4},{2,5},{3,6},{4,11},{5,8},{6,9},{7,10},{8,15},{9,12},{1... | collective-permute-start | bytes 1769480 | tf_op jit(solution)/shard_map/ppermute | solution.py:382
  134.4 87.6 %collective-permute-start.10 = (bf16[8,16,2304]{2,1,0:T(8,128)(2,1)}, bf16[8,16,2304]{2,1,0:T(8,128)(2,1)S(1)}, u32[]{:S(2)}, u32[]{:S(2)}) collective-permute-start(bf16[8,16,2304]{2,1,0:T(8,128)(2,1)} %get-tuple-element.46), channel_id=1, source_target_pairs={{0,8},{1,9},{2,10},{3,11},{4,12},{5,13},{6,14},{7,15},{8,0},{9,1},... | collective-permute-start | bytes 1769480 | tf_op jit(solution)/shard_map/ppermute | solution.py:382
  178.4 48.4 %collective-permute-start.11 = (bf16[8,16,2304]{2,1,0:T(8,128)(2,1)}, bf16[8,16,2304]{2,1,0:T(8,128)(2,1)S(1)}, u32[]{:S(2)}, u32[]{:S(2)}) collective-permute-start(bf16[8,16,2304]{2,1,0:T(8,128)(2,1)} %get-tuple-element.47), channel_id=1, source_target_pairs={{0,9},{1,10},{2,11},{3,8},{4,13},{5,14},{6,15},{7,12},{8,1},{9,2},... | collective-permute-start | bytes 1769480 | tf_op jit(solution)/shard_map/ppermute | solution.py:382
  181.9 45.0 %collective-permute-start.12 = (bf16[8,16,2304]{2,1,0:T(8,128)(2,1)}, bf16[8,16,2304]{2,1,0:T(8,128)(2,1)S(1)}, u32[]{:S(2)}, u32[]{:S(2)}) collective-permute-start(bf16[8,16,2304]{2,1,0:T(8,128)(2,1)} %get-tuple-element.48), channel_id=1, source_target_pairs={{0,10},{1,11},{2,8},{3,9},{4,14},{5,15},{6,12},{7,13},{8,2},{9,3},... | collective-permute-start | bytes 1769480 | tf_op jit(solution)/shard_map/ppermute | solution.py:382
  201.6 0.8 copy-start.6
  202.5 62.8 %collective-permute-start.18 = (bf16[16,16,2304]{2,1,0:T(8,128)(2,1)}, bf16[16,16,2304]{2,1,0:T(8,128)(2,1)S(1)}, u32[]{:S(2)}, u32[]{:S(2)}) collective-permute-start(bf16[16,16,2304]{2,1,0:T(8,128)(2,1)} %get-tuple-element.55), channel_id=1, source_target_pairs={{0,16},{16,0},{32,48},{48,32},{64,80},{80,64},{96,112},{112,96},{1... | collective-permute-start | bytes 3538952 | tf_op jit(solution)/shard_map/ppermute | solution.py:374
  222.0 5.0 %copy-start.7 = (bf16[8,16,2304]{2,1,0:T(8,128)(2,1)}, bf16[8,16,2304]{2,1,0:T(8,128)(2,1)S(1)}, u32[]{:S(2)}) copy-start(bf16[8,16,2304]{2,1,0:T(8,128)(2,1)S(1)} %collective-permute-done.9) | copy-start | bytes 1769476
  222.0 47.7 %collective-permute-start.19 = (bf16[16,16,2304]{2,1,0:T(8,128)(2,1)}, bf16[16,16,2304]{2,1,0:T(8,128)(2,1)}, u32[]{:S(2)}, u32[]{:S(2)}) collective-permute-start(bf16[16,16,2304]{2,1,0:T(8,128)(2,1)} %get-tuple-element.56), channel_id=1, source_target_pairs={{0,32},{16,48},{32,64},{48,80},{64,96},{80,112},{96,0},{112,16},{1... | collective-permute-start | bytes 3538952 | tf_op jit(solution)/shard_map/ppermute | solution.py:374
  222.0 5.0 %copy-start.8 = (bf16[8,16,2304]{2,1,0:T(8,128)(2,1)}, bf16[8,16,2304]{2,1,0:T(8,128)(2,1)S(1)}, u32[]{:S(2)}) copy-start(bf16[8,16,2304]{2,1,0:T(8,128)(2,1)S(1)} %collective-permute-done.10) | copy-start | bytes 1769476
  222.0 17.8 %collective-permute-start.13 = (bf16[8,16,2304]{2,1,0:T(8,128)(2,1)}, bf16[8,16,2304]{2,1,0:T(8,128)(2,1)}, u32[]{:S(2)}, u32[]{:S(2)}) collective-permute-start(bf16[8,16,2304]{2,1,0:T(8,128)(2,1)} %get-tuple-element.49), channel_id=1, source_target_pairs={{0,11},{1,8},{2,9},{3,10},{4,15},{5,12},{6,13},{7,14},{8,3},{9,0},... | collective-permute-start | bytes 1769480 | tf_op jit(solution)/shard_map/ppermute | solution.py:382
  226.8 0.8 copy-start.9
  226.8 29.8 %collective-permute-start.14 = (bf16[8,16,2304]{2,1,0:T(8,128)(2,1)}, bf16[8,16,2304]{2,1,0:T(8,128)(2,1)}, u32[]{:S(2)}, u32[]{:S(2)}) collective-permute-start(bf16[8,16,2304]{2,1,0:T(8,128)(2,1)} %get-tuple-element.50), channel_id=1, source_target_pairs={{0,12},{1,13},{2,14},{3,15},{4,0},{5,1},{6,2},{7,3},{8,4},{9,5},{1... | collective-permute-start | bytes 1769480 | tf_op jit(solution)/shard_map/ppermute | solution.py:382
  226.9 1.0 copy-start.10
  226.9 38.0 %collective-permute-start.15 = (bf16[8,16,2304]{2,1,0:T(8,128)(2,1)}, bf16[8,16,2304]{2,1,0:T(8,128)(2,1)}, u32[]{:S(2)}, u32[]{:S(2)}) collective-permute-start(bf16[8,16,2304]{2,1,0:T(8,128)(2,1)} %get-tuple-element.51), channel_id=1, source_target_pairs={{0,13},{1,14},{2,15},{3,12},{4,1},{5,2},{6,3},{7,0},{8,5},{9,6},{1... | collective-permute-start | bytes 1769480 | tf_op jit(solution)/shard_map/ppermute | solution.py:382
  227.8 41.8 %all-to-all-start = ((bf16[8,128,768]{2,1,0:T(8,128)(2,1)}), bf16[8,128,768]{2,1,0:T(8,128)(2,1)S(1)}, u32[]{:S(2)}, u32[]{:S(2)}) async-start(bf16[8,128,768]{2,1,0:T(8,128)(2,1)} %bitcast.1), calls=%async_computation | async-start | bytes 3145728 | tf_op jit(solution)/shard_map/all_to_all | solution.py:440
  239.8 104.1 %collective-permute-start.20 = (bf16[16,16,2304]{2,1,0:T(8,128)(2,1)}, bf16[16,16,2304]{2,1,0:T(8,128)(2,1)}, u32[]{:S(2)}, u32[]{:S(2)}) collective-permute-start(bf16[16,16,2304]{2,1,0:T(8,128)(2,1)} %get-tuple-element.57), channel_id=1, source_target_pairs={{0,48},{16,32},{32,80},{48,64},{64,112},{80,96},{96,16},{112,0},{1... | collective-permute-start | bytes 3538952 | tf_op jit(solution)/shard_map/ppermute | solution.py:374
  256.6 87.3 %collective-permute-start.21 = (bf16[16,16,2304]{2,1,0:T(8,128)(2,1)}, bf16[16,16,2304]{2,1,0:T(8,128)(2,1)}, u32[]{:S(2)}, u32[]{:S(2)}) collective-permute-start(bf16[16,16,2304]{2,1,0:T(8,128)(2,1)} %get-tuple-element.58), channel_id=1, source_target_pairs={{0,64},{16,80},{32,96},{48,112},{64,0},{80,16},{96,32},{112,48},{1... | collective-permute-start | bytes 3538952 | tf_op jit(solution)/shard_map/ppermute | solution.py:374
  264.9 79.0 %collective-permute-start.22 = (bf16[16,16,2304]{2,1,0:T(8,128)(2,1)}, bf16[16,16,2304]{2,1,0:T(8,128)(2,1)}, u32[]{:S(2)}, u32[]{:S(2)}) collective-permute-start(bf16[16,16,2304]{2,1,0:T(8,128)(2,1)} %get-tuple-element.59), channel_id=1, source_target_pairs={{0,80},{16,64},{32,112},{48,96},{64,16},{80,0},{96,48},{112,32},{1... | collective-permute-start | bytes 3538952 | tf_op jit(solution)/shard_map/ppermute | solution.py:374
  265.3 5.7 %copy-start.4 = (bf16[16,16,2304]{2,1,0:T(8,128)(2,1)}, bf16[16,16,2304]{2,1,0:T(8,128)(2,1)S(1)}, u32[]{:S(2)}) copy-start(bf16[16,16,2304]{2,1,0:T(8,128)(2,1)S(1)} %collective-permute-done.18.refs_1_) | copy-start | bytes 3538948
  265.3 79.8 %collective-permute-start.23 = (bf16[16,16,2304]{2,1,0:T(8,128)(2,1)}, bf16[16,16,2304]{2,1,0:T(8,128)(2,1)}, u32[]{:S(2)}, u32[]{:S(2)}) collective-permute-start(bf16[16,16,2304]{2,1,0:T(8,128)(2,1)} %get-tuple-element.60), channel_id=1, source_target_pairs={{0,96},{16,112},{32,0},{48,16},{64,32},{80,48},{96,64},{112,80},{1... | collective-permute-start | bytes 3538952 | tf_op jit(solution)/shard_map/ppermute | solution.py:374
  269.7 99.5 %collective-permute-start.24 = (bf16[16,16,2304]{2,1,0:T(8,128)(2,1)}, bf16[16,16,2304]{2,1,0:T(8,128)(2,1)}, u32[]{:S(2)}, u32[]{:S(2)}) collective-permute-start(bf16[16,16,2304]{2,1,0:T(8,128)(2,1)} %get-tuple-element.61), channel_id=1, source_target_pairs={{0,112},{16,96},{32,16},{48,0},{64,48},{80,32},{96,80},{112,64},{1... | collective-permute-start | bytes 3538952 | tf_op jit(solution)/shard_map/ppermute | solution.py:374
  269.7 99.5 %copy-start.5 = (bf16[8,16,2304]{2,1,0:T(8,128)(2,1)S(1)}, bf16[8,16,2304]{2,1,0:T(8,128)(2,1)}, u32[]{:S(2)}) copy-start(bf16[8,16,2304]{2,1,0:T(8,128)(2,1)} %get-tuple-element.41) | copy-start | bytes 1769476
  343.9 42.7 %collective-permute-start.16 = (bf16[8,16,2304]{2,1,0:T(8,128)(2,1)}, bf16[8,16,2304]{2,1,0:T(8,128)(2,1)S(1)}, u32[]{:S(2)}, u32[]{:S(2)}) collective-permute-start(bf16[8,16,2304]{2,1,0:T(8,128)(2,1)} %get-tuple-element.52), channel_id=1, source_target_pairs={{0,14},{1,15},{2,12},{3,13},{4,2},{5,3},{6,0},{7,1},{8,6},{9,7},{1... | collective-permute-start | bytes 1769480 | tf_op jit(solution)/shard_map/ppermute | solution.py:382
  343.9 42.7 %collective-permute-start.17 = (bf16[8,16,2304]{2,1,0:T(8,128)(2,1)}, bf16[8,16,2304]{2,1,0:T(8,128)(2,1)S(1)}, u32[]{:S(2)}, u32[]{:S(2)}) collective-permute-start(bf16[8,16,2304]{2,1,0:T(8,128)(2,1)} %get-tuple-element.53), channel_id=1, source_target_pairs={{0,15},{1,12},{2,13},{3,14},{4,3},{5,0},{6,1},{7,2},{8,7},{9,4},{1... | collective-permute-start | bytes 1769480 | tf_op jit(solution)/shard_map/ppermute | solution.py:382
  343.9 42.7 %collective-permute-start.3 = (bf16[8,16,2304]{2,1,0:T(8,128)(2,1)}, bf16[8,16,2304]{2,1,0:T(8,128)(2,1)S(1)}, u32[]{:S(2)}, u32[]{:S(2)}) collective-permute-start(bf16[8,16,2304]{2,1,0:T(8,128)(2,1)} %get-tuple-element.39), channel_id=1, source_target_pairs={{0,1},{1,2},{2,3},{3,0},{4,5},{5,6},{6,7},{7,4},{8,9},{9,10},{10,1... | collective-permute-start | bytes 1769480 | tf_op jit(solution)/shard_map/ppermute | solution.py:382
  345.1 45.4 %collective-permute-start.4 = (bf16[8,16,2304]{2,1,0:T(8,128)(2,1)}, bf16[8,16,2304]{2,1,0:T(8,128)(2,1)S(1)}, u32[]{:S(2)}, u32[]{:S(2)}) collective-permute-start(bf16[8,16,2304]{2,1,0:T(8,128)(2,1)} %get-tuple-element.40), channel_id=1, source_target_pairs={{0,2},{1,3},{2,0},{3,1},{4,6},{5,7},{6,4},{7,5},{8,10},{9,11},{10,... | collective-permute-start | bytes 1769480 | tf_op jit(solution)/shard_map/ppermute | solution.py:382
  369.2 26.7 %collective-permute-start.5 = (bf16[8,16,2304]{2,1,0:T(8,128)(2,1)S(1)}, bf16[8,16,2304]{2,1,0:T(8,128)(2,1)S(1)}, u32[]{:S(2)}, u32[]{:S(2)}) collective-permute-start(bf16[8,16,2304]{2,1,0:T(8,128)(2,1)S(1)} %copy-done.5), channel_id=1, source_target_pairs={{0,3},{1,0},{2,1},{3,2},{4,7},{5,4},{6,5},{7,6},{8,11},{9,8},{10,9... | collective-permute-start | bytes 1769480 | tf_op jit(solution)/shard_map/ppermute | solution.py:382
  386.6 9.3 %copy-start.11 = (bf16[8,16,2304]{2,1,0:T(8,128)(2,1)}, bf16[8,16,2304]{2,1,0:T(8,128)(2,1)S(1)}, u32[]{:S(2)}) copy-start(bf16[8,16,2304]{2,1,0:T(8,128)(2,1)S(1)} %collective-permute-done.16) | copy-start | bytes 1769476
  386.6 9.3 %copy-start.12 = (bf16[8,16,2304]{2,1,0:T(8,128)(2,1)}, bf16[8,16,2304]{2,1,0:T(8,128)(2,1)S(1)}, u32[]{:S(2)}) copy-start(bf16[8,16,2304]{2,1,0:T(8,128)(2,1)S(1)} %collective-permute-done.17) | copy-start | bytes 1769476
  386.6 9.3 %copy-start.13 = (bf16[8,16,2304]{2,1,0:T(8,128)(2,1)}, bf16[8,16,2304]{2,1,0:T(8,128)(2,1)S(1)}, u32[]{:S(2)}) copy-start(bf16[8,16,2304]{2,1,0:T(8,128)(2,1)S(1)} %collective-permute-done.3) | copy-start | bytes 1769476
  390.5 5.4 %copy-start.14 = (bf16[8,16,2304]{2,1,0:T(8,128)(2,1)}, bf16[8,16,2304]{2,1,0:T(8,128)(2,1)S(1)}, u32[]{:S(2)}) copy-start(bf16[8,16,2304]{2,1,0:T(8,128)(2,1)S(1)} %collective-permute-done.4) | copy-start | bytes 1769476
  395.9 0.8 copy-start.15
Sparse Core Ops, SparseCore 0:
  35.0 80.8 all-reduce.1
Sparse Core Ops, SparseCore 1:
  39.1 84.0 all-gather.2

commit v2 on v1

v2 whole, which is shorter than its diff:
```python
import functools

import jax
import jax.numpy as jnp
from jax import lax
from jax.experimental import pallas as pl
from jax.experimental.pallas import tpu as pltpu
from jax.sharding import PartitionSpec as P

BF16 = jnp.bfloat16
F32 = jnp.float32
HALO = 16
MIB = 1024 * 1024
VMEM_LIMIT = 60 * MIB
EXTRA = 128


def call_cost(flops, nbytes):
    return pl.CostEstimate(flops=int(flops), bytes_accessed=int(nbytes), transcendentals=0)


def norm_kernel(resid_ref, gain_ref, routes_ref, out_ref):
    rows = resid_ref[...].astype(F32)
    dim = rows.shape[1]
    scale = lax.rsqrt(jnp.mean(rows * rows, axis=1, keepdims=True) + 1e-06)
    out_ref[:, :dim] = (rows * scale * gain_ref[...]).astype(BF16)
    out_ref[:, dim:] = jnp.zeros((rows.shape[0], EXTRA), BF16)
    out_ref[:, dim : dim + routes_ref.shape[1]] = routes_ref[...].astype(F32).astype(BF16)


def norm_rows(resid, gain, routes):
    tokens, dim = resid.shape
    return pl.pallas_call(
        norm_kernel,
        out_shape=jax.ShapeDtypeStruct((tokens, dim + EXTRA), BF16),
        compiler_params=pltpu.CompilerParams(vmem_limit_bytes=VMEM_LIMIT),
        cost_estimate=call_cost(resid.size * 6, resid.size * 4),
        name="norm_rows",
    )(resid, gain.reshape(1, -1), routes)


def conv_kernel(
    tile,
    place_ref,
    in_ref,
    in_low_ref,
    in_high_ref,
    grad_ref,
    grad_high_ref,
    ids_ref,
    taps_ref,
    local_ref,
    keep_ref,
    send_ref,
    in_ext,
    grad_ext,
):
    step = pl.program_id(0)
    rows = in_ref.shape[0]

    @pl.when(step == 0)
    def _():
        in_ext[:HALO] = in_low_ref[...].astype(F32)
        in_ext[HALO : HALO + rows] = in_ref[...].astype(F32)
        in_ext[HALO + rows :] = in_high_ref[...].astype(F32)
        grad_ext[:rows] = grad_ref[...].astype(F32)
        grad_ext[rows:] = grad_high_ref[...].astype(F32)

    first = pl.multiple_of(step * tile, tile)
    span = tile + 8
    taps = taps_ref[...]
    window = in_ext[pl.ds(first + HALO - 8, span + 8)]
    ids = ids_ref[pl.ds(first + HALO - 8, span + 8)]
    here = ids[8:]
    same = [None] + [(ids[8 - j : 8 - j + span] == here).astype(F32) for j in (1, 2, 3)]
    conv = taps[0:1] * window[8:]
    for j in (1, 2, 3):
        conv = conv + taps[j : j + 1] * window[8 - j : 8 - j + span] * same[j]
    gate = jax.nn.sigmoid(conv)
    pre = grad_ext[pl.ds(first, span)] * gate * (1.0 + conv * (1.0 - gate))
    result = taps[0:1] * pre[:tile]
    for j in (1, 2, 3):
        result = result + taps[j : j + 1] * (pre * same[j])[j : j + tile]
    local = result.astype(BF16)
    local_ref[...] = local
    half = tile // 2
    core = place_ref[0] & 1

    @pl.when(core == 0)
    def _():
        keep_ref[...] = local[:half]
        send_ref[...] = local[half:]

    @pl.when(core == 1)
    def _():
        keep_ref[...] = local[half:]
        send_ref[...] = local[:half]


def conv_back(place, qkv_in, low, high, qkv_grad, grad_high, ids, taps, block):
    rows, width = qkv_in.shape
    tile = 2 * block
    whole = lambda shape: pl.BlockSpec(shape, lambda i, p: (0,) * len(shape))
    part = lambda size: pl.BlockSpec((size, width), lambda i, p: (i, 0))
    return pl.pallas_call(
        functools.partial(conv_kernel, tile),
        grid_spec=pltpu.PrefetchScalarGridSpec(
            num_scalar_prefetch=1,
            grid=(rows // tile,),
            in_specs=[
                whole(qkv_in.shape),
                whole(low.shape),
                whole(high.shape),
                whole(qkv_grad.shape),
                whole(grad_high.shape),
                whole(ids.shape),
                whole(taps.shape),
            ],
            out_specs=[part(tile), part(block), part(block)],
            scratch_shapes=[
                pltpu.VMEM((rows + 2 * HALO, width), F32),
                pltpu.VMEM((rows + HALO, width), F32),
            ],
        ),
        out_shape=[
            jax.ShapeDtypeStruct((rows, width), BF16),
            jax.ShapeDtypeStruct((rows // 2, width), BF16),
            jax.ShapeDtypeStruct((rows // 2, width), BF16),
        ],
        compiler_params=pltpu.CompilerParams(vmem_limit_bytes=VMEM_LIMIT),
        cost_estimate=call_cost(40 * rows * width, 8 * rows * width),
        name="conv_back",
    )(place, qkv_in, low, high, qkv_grad, grad_high, ids, taps)


def project_kernel(place_ref, own_ref, other_ref, own_weight, other_weight, flow_ref, out_ref):
    block = flow_ref.shape[0]
    total = jnp.dot(own_ref[...], own_weight[...], preferred_element_type=F32)
    total = total + jnp.dot(other_ref[...], other_weight[...], preferred_element_type=F32)
    out_ref[...] = total.astype(BF16)
    for index in range(out_ref.shape[0] // block):

        @pl.when(index == place_ref[0] >> 1)
        def _():
            own = slice(index * block, (index + 1) * block)
            out_ref[own] = (total[own] + flow_ref[...].astype(F32)).astype(BF16)


def project(place, own, other, own_weight, other_weight, out_grad):
    rows, width = own.shape
    dim = own_weight.shape[1]
    tile = dim // 3
    whole = pl.BlockSpec((rows, width), lambda i, p: (0, 0))
    columns = lambda size: pl.BlockSpec((size, tile), lambda i, p: (0, i))
    return pl.pallas_call(
        project_kernel,
        grid_spec=pltpu.PrefetchScalarGridSpec(
            num_scalar_prefetch=1,
            grid=(dim // tile,),
            in_specs=[whole, whole, columns(width), columns(width), columns(out_grad.shape[0])],
            out_specs=columns(rows),
        ),
        out_shape=jax.ShapeDtypeStruct((rows, dim), BF16),
        compiler_params=pltpu.CompilerParams(vmem_limit_bytes=VMEM_LIMIT),
        cost_estimate=call_cost(4 * rows * width * dim, 4 * (rows + dim) * width + 2 * rows * dim),
        name="project",
    )(place, own, other, own_weight, other_weight, out_grad)


def slot_picker(names, own, capacity):
    count, tokens = own.shape
    match = [(names[k : k + 1] == own) for k in range(names.shape[0])]
    named = functools.reduce(jnp.logical_or, match)
    source = lax.broadcasted_iota(jnp.int32, (tokens, tokens), 0)
    target = lax.broadcasted_iota(jnp.int32, (tokens, tokens), 1)
    earlier = (source < target).astype(BF16)
    rank = jnp.dot(named.astype(BF16), earlier, preferred_element_type=F32).astype(jnp.int32)
    rank = jnp.where(named, rank, -1)
    slot = lax.broadcasted_iota(jnp.int32, (count, capacity, tokens), 1)
    picker = (rank[:, None, :] == slot).astype(F32)
    return picker, match


def pick_norm_kernel(per_token, capacity, n_exp, turns, place_ref, rows_ref, *out_refs):
    tokens = rows_ref.shape[1]
    dim = out_refs[0].shape[3]
    names = rows_ref[0, :, dim:].astype(F32).T[:per_token].astype(jnp.int32)
    own = jnp.concatenate(
        [jnp.full((1, tokens), (place_ref[0] ^ t) * n_exp + place_ref[1], jnp.int32) for t in turns]
    )
    picker, _ = slot_picker(names, own, capacity)
    picker = picker.reshape(len(turns) * capacity, tokens).astype(BF16)
    picked = jnp.dot(picker, rows_ref[0, :, :dim], preferred_element_type=F32).astype(BF16)
    for index in range(len(turns)):
        out_refs[index // 2][index % 2, 0] = picked[index * capacity : (index + 1) * capacity]


def pick_norm(place, rows, turns, first, count, dim, per_token, capacity):
    blocks, tokens, width = rows.shape
    outs = len(turns) // 2
    return pl.pallas_call(
        functools.partial(pick_norm_kernel, per_token, capacity, blocks, turns),
        grid_spec=pltpu.PrefetchScalarGridSpec(
            num_scalar_prefetch=1,
            grid=(count,),
            in_specs=[pl.BlockSpec((1, tokens, width), lambda i, p: (p[1] ^ (i + first), 0, 0))],
            out_specs=[pl.BlockSpec((2, 1, capacity, dim), lambda i, p: (0, i, 0, 0))] * outs,
        ),
        out_shape=[jax.ShapeDtypeStruct((2, count, capacity, dim), BF16)] * outs,
        compiler_params=pltpu.CompilerParams(vmem_limit_bytes=VMEM_LIMIT),
        cost_estimate=call_cost(
            2 * len(turns) * capacity * count * tokens * dim,
            2 * dim * count * (tokens + len(turns) * capacity),
        ),
        name="pick_norm",
    )(place, rows)


def pick_grad_kernel(per_token, capacity, n_exp, turns, place_ref, *refs):
    out_ref = refs[-1]
    tokens = refs[0].shape[2]
    own = jnp.concatenate(
        [jnp.full((1, tokens), place_ref[0] * n_exp + (place_ref[1] ^ t), jnp.int32) for t in turns]
    )
    for core in range(2):
        table_ref, rows_ref = refs[2 * core : 2 * core + 2]
        names = table_ref[0, :per_token].astype(jnp.int32)
        picker, match = slot_picker(names, own, capacity)
        weights = table_ref[0, per_token:]
        scale = functools.reduce(
            jnp.add, [jnp.where(match[k], weights[k : k + 1], 0.0) for k in range(per_token)]
        )
        scales = jnp.sum(picker * scale[:, None, :], axis=2, keepdims=True)
        picker = picker.reshape(len(turns) * capacity, tokens).astype(BF16)
        picked = jnp.dot(picker, rows_ref[...], preferred_element_type=F32)
        picked = (picked * scales.reshape(len(turns) * capacity, 1)).astype(BF16)
        for index in range(len(turns)):
            out_ref[index, core * capacity : (core + 1) * capacity] = picked[
                index * capacity : (index + 1) * capacity
            ]


def pick_grad(place, tables, flows, turns, quarter, n_exp, per_token, capacity):
    tokens = tables.shape[2]
    dim = flows[0].shape[1]
    table_spec = lambda core: pl.BlockSpec(
        (1, 2 * per_token, tokens), lambda i, p: (p[0] ^ (2 * quarter + core), 0, 0)
    )
    flow_spec = pl.BlockSpec((tokens, dim), lambda i, p: ((p[0] >> 1) ^ quarter, 0))
    shape = (len(turns), 2 * capacity, dim)
    return pl.pallas_call(
        functools.partial(pick_grad_kernel, per_token, capacity, n_exp, turns),
        grid_spec=pltpu.PrefetchScalarGridSpec(
            num_scalar_prefetch=1,
            grid=(1,),
            in_specs=[table_spec(0), flow_spec, table_spec(1), flow_spec],
            out_specs=pl.BlockSpec(shape, lambda i, p: (0, 0, 0)),
        ),
        out_shape=jax.ShapeDtypeStruct(shape, BF16),
        compiler_params=pltpu.CompilerParams(vmem_limit_bytes=VMEM_LIMIT),
        cost_estimate=call_cost(
            4 * len(turns) * capacity * tokens * dim,
            4 * dim * (tokens + len(turns) * capacity),
        ),
        name="pick_grad",
    )(place, tables, flows[0], tables, flows[1])


def forward_kernel(sources, *refs):
    row_refs = refs[:sources]
    weight_ref = refs[sources]
    rows_out, act_ref, gate_ref, up_ref = refs[-4:]
    _, pair, capacity, _ = row_refs[0].shape
    for inner in range(pair):
        for index in range(sources):
            at = (inner * sources + index) * capacity
            rows_out[at : at + capacity] = row_refs[index][0, inner]
    hidden = act_ref.shape[1]
    mixed = jnp.dot(rows_out[...], weight_ref[...], preferred_element_type=F32)
    gate = mixed[:, :hidden]
    up = mixed[:, hidden:]
    sig = jax.nn.sigmoid(gate)
    silu = gate * sig
    act_ref[...] = (silu * up).astype(BF16)
    gate_ref[...] = up * sig * (1.0 + gate * (1.0 - sig))
    up_ref[...] = silu


def expert_forward(pieces, weight, hidden, parts, part, before):
    sources = len(pieces)
    _, blocks, capacity, dim = pieces[0][0].shape
    pair = 2
    tile = sources * pair * capacity
    steps = blocks // pair
    total = sources * blocks * capacity * parts
    row_spec = lambda width: pl.BlockSpec((tile, width), lambda i: (i + part * steps, 0))
    piece_spec = lambda unit: pl.BlockSpec(
        (1, pair, capacity, dim), lambda i: (unit, i, 0, 0)
    )
    return pl.pallas_call(
        functools.partial(forward_kernel, sources),
        grid=(steps,),
        in_specs=[piece_spec(unit) for _, unit in pieces]
        + [pl.BlockSpec((dim, 2 * hidden), lambda i: (0, 0))]
        + [pl.BlockSpec(memory_space=pl.ANY)] * len(before),
        out_specs=[row_spec(dim), row_spec(hidden), row_spec(hidden), row_spec(hidden)],
        out_shape=[
            jax.ShapeDtypeStruct((total, dim), BF16),
            jax.ShapeDtypeStruct((total, hidden), BF16),
            jax.ShapeDtypeStruct((total, hidden), F32),
            jax.ShapeDtypeStruct((total, hidden), F32),
        ],
        input_output_aliases={sources + 1 + i: i for i in range(len(before))},
        compiler_params=pltpu.CompilerParams(vmem_limit_bytes=VMEM_LIMIT),
        cost_estimate=call_cost(
            4 * total * dim * hidden // parts, (4 * total * dim + 10 * total * hidden) // parts
        ),
        name="expert_forward",
    )(*[array for array, _ in pieces], weight, *before)


def backward_kernel(places, arrays, *refs):
    grad_refs = refs[:arrays]
    gate_ref, up_ref, weight_ref, rows_ref, act_ref, out_ref = refs[arrays : arrays + 6]
    grads_all, hidden_all, sems = refs[arrays + 6 :]
    step = pl.program_id(0)
    tile = gate_ref.shape[0]
    hidden = act_ref.shape[1]
    width = rows_ref.shape[1]
    row_steps = grads_all.shape[0] // tile
    copies = []
    for index, (array, unit, row, size) in enumerate(places):
        copy = pltpu.make_async_copy(
            grad_refs[array].at[unit], grads_all.at[pl.ds(row, size)], sems.at[index]
        )
        copies.append((row // tile, copy))

    @pl.when(step == 0)
    def _():
        for turn in range(row_steps):
            for at, copy in copies:
                if at == turn:
                    copy.start()

    for turn in range(row_steps):

        @pl.when(step == turn)
        def _():
            for at, copy in copies:
                if at == turn:
                    copy.wait()

    @pl.when(step < row_steps)
    def _():
        where = pl.ds(pl.multiple_of(step * tile, tile), tile)
        act_grad = jnp.dot(grads_all[where], weight_ref[...], preferred_element_type=F32)
        hidden_all[where, :hidden] = (act_grad * gate_ref[...]).astype(BF16)
        hidden_all[where, hidden:] = (act_grad * up_ref[...]).astype(BF16)

    @pl.when(step >= row_steps)
    def _():
        columns = pl.ds(pl.multiple_of((step - row_steps) * width, width), width)
        over_rows = (((0,), (0,)), ((), ()))
        out_ref[:, : 2 * hidden] = lax.dot_general(
            rows_ref[...], hidden_all[...], over_rows, preferred_element_type=F32
        ).astype(BF16)
        out_ref[:, 2 * hidden :] = lax.dot_general(
            grads_all[:, columns], act_ref[...], over_rows, preferred_element_type=F32
        ).astype(BF16)


def expert_backward(arrays, places, gate, up, weights, rows, act):
    total, dim = rows.shape
    hidden = act.shape[1]
    tile, width = 256, 256
    row_steps, column_steps = total // tile, dim // width
    row_spec = lambda cols: pl.BlockSpec(
        (tile, cols), lambda i: (jnp.minimum(i, row_steps - 1), 0)
    )
    column_of = lambda i: jnp.maximum(i - row_steps, 0)
    return pl.pallas_call(
        functools.partial(backward_kernel, places, len(arrays)),
        grid=(row_steps + column_steps,),
        in_specs=[pl.BlockSpec(memory_space=pl.ANY)] * len(arrays)
        + [
            row_spec(hidden),
            row_spec(hidden),
            pl.BlockSpec((dim, hidden), lambda i: (0, 2)),
            pl.BlockSpec((total, width), lambda i: (0, column_of(i))),
            pl.BlockSpec((total, hidden), lambda i: (0, 0)),
        ],
        out_specs=pl.BlockSpec((width, 3 * hidden), lambda i: (column_of(i), 0)),
        out_shape=jax.ShapeDtypeStruct((dim, 3 * hidden), BF16),
        scratch_shapes=[
            pltpu.VMEM((total, dim), BF16),
            pltpu.VMEM((total, 2 * hidden), BF16),
            pltpu.SemaphoreType.DMA((len(places),)),
        ],
        compiler_params=pltpu.CompilerParams(vmem_limit_bytes=VMEM_LIMIT),
        cost_estimate=call_cost(8 * total * dim * hidden, 4 * total * dim + 20 * total * hidden),
        name="expert_backward",
    )(*arrays, gate, up, weights, rows, act)


def swap(array, axis, flip):
    count = lax.axis_size(axis)
    return lax.ppermute(array, axis, [(i, i ^ flip) for i in range(count)])


def swap_gather(array, axis, flip):
    count, index = lax.axis_size(axis), lax.axis_index(axis)
    groups = [[i, i ^ flip] for i in range(count) if i < i ^ flip]
    both = lax.all_gather(array, axis, axis_index_groups=groups)
    other = (index < (index ^ flip)).astype(jnp.int32)
    return lax.dynamic_index_in_dim(both, other, 0, keepdims=False)


def mask_of(flips, bits):
    return functools.reduce(lambda a, b: a ^ b, [f for f, bit in zip(flips, bits) if bit], 0)


def exchange_rows(half, picks, exchange):
    keep, send, keep_far, send_far = picks
    flips = (1, 3) if half == 0 else (3, 1)
    send_got, keep_got = swap(send_far, "seq", 1), swap(keep_far, "seq", 1)
    first = exchange(jnp.concatenate([send, send_got]), "seq", 2 * flips[0])
    second = exchange(
        jnp.concatenate([keep[1:], keep_got[1:], first[1:2], first[3:4]]), "seq", 2 * flips[1]
    )
    found = {
        0: [(keep, 0), (keep_got, 0)],
        flips[0]: [(first, 0), (first, 2)],
        flips[1]: [(second, 0), (second, 1)],
        flips[0] ^ flips[1]: [(second, 2), (second, 3)],
    }
    return [found[r >> 1][r & 1] for r in range(8)]


def exchange_grads(flips, keep, send):
    first = swap(send, "exp", flips[0])
    second = swap(jnp.concatenate([keep[4:8], first[4:8]]), "exp", flips[1])
    third = swap(
        jnp.concatenate([keep[2:4], first[2:4], second[2:4], second[6:8]]), "exp", flips[2]
    )
    odd = lambda a: [a[i : i + 1] for i in (1, 3, 5, 7)]
    fourth = swap(
        jnp.concatenate(
            [keep[1:2], first[1:2], second[1:2], second[5:6]] + odd(third)
        ),
        "exp",
        flips[3],
    )
    arrays = [keep, first, second, third, fourth]
    found = {}
    found[0, 0, 0, 0] = (0, 0)
    found[1, 0, 0, 0] = (1, 0)
    found[0, 1, 0, 0] = (2, 0)
    found[1, 1, 0, 0] = (2, 4)
    for index, start in enumerate([(0, 0), (1, 0), (0, 1), (1, 1)]):
        found[start + (1, 0)] = (3, 2 * index)
    for index, start in enumerate([(0, 0), (1, 0), (0, 1), (1, 1)]):
        found[start + (0, 1)] = (4, index)
        found[start + (1, 1)] = (4, 4 + index)
    return arrays, {mask_of(flips, bits): at for bits, at in found.items()}


def per_device(
    qkv_in,
    qkv_grad,
    conv_weight,
    doc_ids,
    qkv_weight,
    resid,
    norm_gain,
    out_grad,
    routes,
    route_weights,
    expert_weights,
):
    rows, width = qkv_in.shape
    tokens, dim = resid.shape
    per_token = routes.shape[1]
    hidden = expert_weights.shape[2] // 3
    n_seq, n_exp = lax.axis_size("seq"), lax.axis_size("exp")
    experts = n_seq * n_exp
    capacity = 2 * tokens * per_token // experts
    seq_index, exp_index = lax.axis_index("seq"), lax.axis_index("exp")
    own_weights = expert_weights[0]

    place = jnp.stack([seq_index, exp_index]).astype(jnp.int32)
    normed = norm_rows(resid, norm_gain, routes)
    normed, qkv_grad = lax.optimization_barrier((normed, qkv_grad))
    exp_normed = lax.all_gather(normed, "exp")

    forward = [(i, i + 1) for i in range(n_exp - 1)]
    backward = [(i + 1, i) for i in range(n_exp - 1)]
    low = lax.ppermute(qkv_in[-HALO:], "exp", forward)
    high = lax.ppermute(qkv_in[:HALO], "exp", backward)
    grad_high = lax.ppermute(qkv_grad[:HALO], "exp", backward)
    weight_far = swap(qkv_weight, "seq", 1)

    table = jnp.concatenate([routes.astype(F32), route_weights], 1).T
    tables = jnp.broadcast_to(table[None], (n_seq,) + table.shape)
    tables = lax.all_to_all(tables, "seq", split_axis=0, concat_axis=0, tiled=True)

    edge = jnp.full((HALO,), -1, jnp.int32)
    ids = lax.dynamic_slice_in_dim(
        jnp.concatenate([edge, doc_ids, edge]), exp_index * rows, rows + 2 * HALO
    )
    local_grad, local_keep, local_send = conv_back(
        place, qkv_in, low, high, qkv_grad, grad_high, ids.reshape(-1, 1), conv_weight, tokens
    )
    local_got = swap(local_send, "seq", 1)
    partial = project(place, local_keep, local_got, qkv_weight, weight_far, out_grad)
    same_core = [[s for s in range(n_seq) if s % 2 == core] for core in range(2)]
    flow = lax.psum(partial, "seq", axis_index_groups=same_core)
    flow, local_grad = lax.optimization_barrier((flow, local_grad))
    flow_far = swap(flow, "seq", 1)
    qkv_in_grad = lax.all_to_all(local_grad, "seq", split_axis=0, concat_axis=1, tiled=True)

    halves = []
    for half in range(2):
        near = (0, 3, 1, 2) if half == 0 else (0, 1, 3, 2)
        turns = tuple(2 * m for m in near) + tuple(2 * m + 1 for m in near)
        picks = pick_norm(
            place, exp_normed, turns, half * n_exp // 2, n_exp // 2, dim, per_token, capacity
        )
        halves.append(exchange_rows(half, picks, swap if half == 0 else swap_gather))
    results = ()
    for half in range(2):
        results = expert_forward(halves[half], own_weights, hidden, 2, half, results)
    rows_all, act, gate, up = results

    flips = (1, 3, 4, 12)
    quarters = len(flips)
    orders = [flips[k:] + flips[:k] for k in range(quarters)]
    bit_rows = [tuple((j >> (2 - b)) & 1 for b in range(3)) for j in range(8)]
    turns_of = lambda k, bit: tuple(mask_of(orders[k], (bit,) + bits) for bits in bit_rows)
    picks = [
        [
            pick_grad(
                place, tables, (flow, flow_far), turns_of(k, bit), k, n_exp, per_token, capacity
            )
            for k in range(quarters)
        ]
        for bit in (1, 0)
    ]
    arrays, places = [], []
    for k in range(quarters):
        got, found = exchange_grads(orders[k], picks[1][k], picks[0][k])
        size = 2 * capacity
        for mask, (array, unit) in sorted(found.items()):
            row = mask * n_seq * capacity + k * size
            places.append((len(arrays) + array, unit, row, size))
        arrays += got
    expert_grads = expert_backward(arrays, tuple(places), gate, up, own_weights, rows_all, act)
    return (qkv_in_grad, expert_grads[None])


def solution(mesh):
    return jax.shard_map(
        per_device,
        mesh=mesh,
        in_specs=(
            P("exp", "seq"),
            P("exp", "seq"),
            P(None, "seq"),
            P(),
            P("seq", None),
            P(("exp", "seq"), None),
            P(),
            P(("exp", "seq"), None),
            P(("exp", "seq"), None),
            P(("exp", "seq"), None),
            P(("seq", "exp"), None, None),
        ),
        out_specs=(P(("exp", "seq"), None), P(("seq", "exp"), None, None)),
        check_vma=False,
    )
```

time: 438 us -> 532 us (1.21)
  local copies, waits for them, and re-layouts: 11.2 us -> 74 us
  starting transfers between devices: 80 us -> 36.9 us
  Pallas kernels: 91.3 us -> 125 us
  waiting for transfers between devices: 237 us -> 265 us
  other arithmetic: 0.64 us -> 11.6 us
    ppermute x22 -> x25, starting transfers between devices: 61.7 us -> 21.7 us  [swap(): return lax.ppermute(array, axis, [(i, i ^ flip) for i in range(count)])]
    unnamed x39 -> x87, local copies, waits for them, and re-layouts: 5.08 us -> 41.6 us
    pallas_call x5 -> x15, Pallas kernels: 89.1 us -> 123 us  [the longest x1 32.2 us: expert_backward(): pl.pallas_call(functools.partial(backward_kernel, places, len(arrays)), g...]
    all_gather x0 -> x2, waiting for transfers between devices: none -> 33.1 us  [swap_gather(): both = lax.all_gather(array, axis, axis_index_groups=groups)]
    ppermute x22 -> x25, waiting for transfers between devices: 166 us -> 139 us  [swap(): return lax.ppermute(array, axis, [(i, i ^ flip) for i in range(count)])]
    all_to_all x1, waiting for transfers between devices: 0.01 us -> 20.7 us  [per_device(): lax.all_to_all(local_grad, 'seq', split_axis=0, concat_axis=1, tiled=True)]
    slice x0 -> x36, local copies, waits for them, and re-layouts: none -> 12.3 us  [the longest x12 3.38 us: exchange_grads(): second = swap(jnp.concatenate([keep[4:8], first[4:8]]), 'exp', flips[1])]
    concatenate x0 -> x12, other arithmetic: none -> 11 us  [the longest x2 5.89 us: exchange_rows(): first = exchange(jnp.concatenate([send, send_got]), 'seq', 2 * flips[0])]
  transfers between devices with their start and end apart: 29 -> 34, of which waited for: 9 -> 15; matrix products, arithmetic and copies ran while one was open for 2% -> 14% of each run, Pallas kernels for 10% -> 16%
where the time goes in v2:
time: 532 us; the launch traced here: 529 us
  waiting for transfers between devices  265 us (50%)
  Pallas kernels  125 us (23%)
  local copies, waits for them, and re-layouts  74 us (14%)
  starting transfers between devices  36.9 us (7%)
  between operations  16.1 us (3%)
  other arithmetic  11.6 us (2%)
    ppermute x25, waiting for transfers between devices, swap(): return lax.ppermute(array, axis, [(i, i ^ flip) for i in range(count)])  139 us
    psum x1, waiting for transfers between devices, per_device(): flow = lax.psum(partial, 'seq', axis_index_groups=same_core)  69.1 us
    unnamed x87, local copies, waits for them, and re-layouts  41.6 us
    all_gather x2, waiting for transfers between devices, swap_gather(): both = lax.all_gather(array, axis, axis_index_groups=groups)  33.1 us
    pallas_call x1, Pallas kernels, expert_backward(): pl.pallas_call(functools.partial(backward_kernel, places, len(arrays)), g...  32.2 us
    pallas_call x8, Pallas kernels, pick_grad(): pl.pallas_call(functools.partial(pick_grad_kernel, per_token, capacity, n...  29.8 us
    ppermute x25, starting transfers between devices, swap(): return lax.ppermute(array, axis, [(i, i ^ flip) for i in range(count)])  21.7 us
    all_to_all x1, waiting for transfers between devices, per_device(): lax.all_to_all(local_grad, 'seq', split_axis=0, concat_axis=1, tiled=True)  20.7 us
  transfers between devices with their start and end apart: 34, of which 15 were waited for; matrix products, arithmetic and copies ran while one was open for 14% of the time, Pallas kernels for 16%

profile of v2, /device:TPU:1, one launch (start us, length us, event | category | flops | bytes accessed | tf_op | source)
XLA Modules:
  0.0 529.0 jit_solution(11198299557101271861)
XLA Ops:
  8.1 1.5 collective-permute-start.4
  9.6 1.4 copy.22.routes_ref
  12.3 2.2 norm_rows.1
  17.2 4.0 collective-permute-start
  26.4 12.6 %conv_back.1 = (bf16[1024,768]{1,0:T(8,128)(2,1)}, bf16[512,768]{1,0:T(8,128)(2,1)}, bf16[512,768]{1,0:T(8,128)(2,1)}) custom-call(s32[2]{0:T(128)} %pad_add_fusion.place_ref, bf16[1024,768]{1,0:T(8,128)(2,1)} %in_ref.1, bf16[16,768]{1,0:T(8,128)(2,1)} %copy-done.21, bf16[16,768]{1,0:T(8,128)(2,1)} %copy-done.22, bf16[1024,768]{1,0:T(8,128)(2,1)} %grad_ref, ...), custom_call_target="tpu_custom_call" | custom-call | flops 31457280 | bytes 6291456 | tf_op jit(solution)/shard_map/conv_back/pallas_call | solution.py:105
  39.0 1.7 collective-permute-start.3
  40.7 2.1 collective-permute-done.3.other_ref
  43.7 8.9 %project.1 = bf16[512,2304]{1,0:T(8,128)(2,1)} custom-call(s32[2]{0:T(128)} %pad_add_fusion.place_ref, bf16[512,768]{1,0:T(8,128)(2,1)} %get-tuple-element.26.own_ref, bf16[512,768]{1,0:T(8,128)(2,1)} %copy-done.28, bf16[768,2304]{1,0:T(8,128)(2,1)} %own_weight.1, bf16[768,2304]{1,0:T(8,128)(2,1)} %collective-permute-done.4.other_weight, ...), custom_call_target="tpu_custom_call" | custom-call | flops 3623878656 | bytes 11010048 | tf_op jit(solution)/shard_map/project/pallas_call | solution.py:155
  52.7 69.1 %all-reduce.2.cloned.1.call-done.refs_1_ = bf16[512,2304]{1,0:T(8,128)(2,1)} async-done(((bf16[512,2304]{1,0:T(8,128)(2,1)}), bf16[512,2304]{1,0:T(8,128)(2,1)}) %all-reduce.2.cloned.1.call-update) | async-done | bytes 2359312 | tf_op jit(solution)/shard_map/psum | solution.py:516
  122.4 4.4 all-to-all-start
  126.8 20.7 %all-to-all-done = bf16[8,128,768]{2,1,0:T(8,128)(2,1)} async-done(((bf16[8,128,768]{2,1,0:T(8,128)(2,1)}), bf16[8,128,768]{2,1,0:T(8,128)(2,1)}, u32[]{:S(2)}, u32[]{:S(2)}) %all-to-all-start) | async-done | bytes 1572896 | tf_op jit(solution)/shard_map/all_to_all | solution.py:519
  148.2 4.1 all-to-all-start.1
  152.9 2.7 copy.25
  155.7 1.5 all-to-all-done.1.refs_0_.refs_2_
  157.8 1.4 copy-done
  159.2 3.7 pick_grad.15
  162.9 2.7 collective-permute-start.18
  165.6 3.7 pick_grad.13
  169.3 3.7 pick_grad.11
  173.0 2.4 collective-permute-start.10
  175.5 3.7 pick_grad.14.refs_15_
  179.2 3.7 pick_grad.12.refs_10_
  182.9 3.8 pick_grad.10.refs_5_
  188.1 1.6 slice_dynamic-update-slice_fusion.23
  189.6 3.7 pick_grad.9
  193.4 3.7 pick_grad.8.refs_0_
  197.1 1.6 slice_dynamic-update-slice_fusion.31
  198.6 3.8 collective-permute-done.18.refs_16_
  204.3 2.3 collective-permute-done.14.refs_11_
  207.9 2.5 collective-permute-start.15
  210.4 1.5 collective-permute-done.10.refs_6_
  213.2 25.0 %collective-permute-done.6.refs_1_ = bf16[8,32,2304]{2,1,0:T(8,128)(2,1)S(1)} collective-permute-done((bf16[8,32,2304]{2,1,0:T(8,128)(2,1)}, bf16[8,32,2304]{2,1,0:T(8,128)(2,1)S(1)}, u32[]{:S(2)}, u32[]{:S(2)}) %collective-permute-start.6) | collective-permute-done | bytes 1179680 | tf_op jit(solution)/shard_map/ppermute | solution.py:407
  238.5 1.7 slice_dynamic-update-slice_fusion.6
  240.2 1.6 slice_dynamic-update-slice_fusion.14
  241.8 1.6 slice_dynamic-update-slice_fusion.22
  247.1 37.8 %collective-permute-done.19.refs_17_ = bf16[8,32,2304]{2,1,0:T(8,128)(2,1)S(1)} collective-permute-done((bf16[8,32,2304]{2,1,0:T(8,128)(2,1)S(1)}, bf16[8,32,2304]{2,1,0:T(8,128)(2,1)S(1)}, u32[]{:S(2)}, u32[]{:S(2)}) %collective-permute-start.19) | collective-permute-done | bytes 1179680 | tf_op jit(solution)/shard_map/ppermute | solution.py:407
  297.7 13.8 %collective-permute-done.20.refs_18_ = bf16[8,32,2304]{2,1,0:T(8,128)(2,1)S(1)} collective-permute-done((bf16[8,32,2304]{2,1,0:T(8,128)(2,1)S(1)}, bf16[8,32,2304]{2,1,0:T(8,128)(2,1)S(1)}, u32[]{:S(2)}, u32[]{:S(2)}) %collective-permute-start.20) | collective-permute-done | bytes 1179680 | tf_op jit(solution)/shard_map/ppermute | solution.py:407
  313.5 9.2 %pick_norm.2 = (bf16[2,8,16,2304]{3,2,1,0:T(8,128)(2,1)}, bf16[2,8,16,2304]{3,2,1,0:T(8,128)(2,1)}, bf16[2,8,16,2304]{3,2,1,0:T(8,128)(2,1)}, bf16[2,8,16,2304]{3,2,1,0:T(8,128)(2,1)}) custom-call(s32[2]{0:T(128)} %pad_add_fusion.place_ref, bf16[16,128,2432]{2,1,0:T(8,128)(2,1)} %bitcast.21), custom_call_target="tpu_custom_call" | custom-call | flops 603979776 | bytes 9437184 | tf_op jit(solution)/shard_map/pick_norm/pallas_call | solution.py:201
  322.7 3.3 collective-permute-start.23
  326.1 1.6 slice_dynamic-update-slice_fusion
  328.9 1.6 slice_dynamic-update-slice_fusion.11
  330.5 2.9 pad_maximum_fusion
  333.5 1.6 slice_dynamic-update-slice_fusion.10
  335.1 1.6 slice_dynamic-update-slice_fusion.9
  336.6 9.6 %pick_norm.3 = (bf16[2,8,16,2304]{3,2,1,0:T(8,128)(2,1)}, bf16[2,8,16,2304]{3,2,1,0:T(8,128)(2,1)}, bf16[2,8,16,2304]{3,2,1,0:T(8,128)(2,1)}, bf16[2,8,16,2304]{3,2,1,0:T(8,128)(2,1)}) custom-call(s32[2]{0:T(128)} %pad_add_fusion.place_ref, bf16[16,128,2432]{2,1,0:T(8,128)(2,1)} %bitcast.22), custom_call_target="tpu_custom_call" | custom-call | flops 603979776 | bytes 9437184 | tf_op jit(solution)/shard_map/pick_norm/pallas_call | solution.py:201
  346.4 1.6 slice_dynamic-update-slice_fusion.8
  349.3 3.0 pad_maximum_fusion.2
  352.4 1.6 slice_dynamic-update-slice_fusion.18
  354.6 1.6 slice_dynamic-update-slice_fusion.17
  356.2 1.6 slice_dynamic-update-slice_fusion.16
  361.6 33.1 %all-gather.9.cloned.1.call-done = bf16[8,8,16,2304]{3,2,1,0:T(8,128)(2,1)} async-done(((bf16[4,8,16,2304]{3,2,1,0:T(8,128)(2,1)}), bf16[8,8,16,2304]{3,2,1,0:T(8,128)(2,1)}) %all-gather.9.cloned.1.call-update) | async-done | bytes 4718608 | tf_op jit(solution)/shard_map/all_gather | solution.py:413
  394.7 1.4 dynamic-slice_bitcast_fusion.3
  396.3 1.7 pad_maximum_fusion.1
  398.0 7.1 %collective-permute-done.26.refs_2_.refs_3_ = bf16[4,8,16,2304]{3,2,1,0:T(8,128)(2,1)S(1)} collective-permute-done((bf16[4,8,16,2304]{3,2,1,0:T(8,128)(2,1)}, bf16[4,8,16,2304]{3,2,1,0:T(8,128)(2,1)S(1)}, u32[]{:S(2)}, u32[]{:S(2)}) %collective-permute-start.26) | collective-permute-done | bytes 2359328 | tf_op jit(solution)/shard_map/ppermute | solution.py:407
  408.1 1.6 slice_dynamic-update-slice_fusion.27
  409.8 1.6 slice_dynamic-update-slice_fusion.26
  411.4 1.6 slice_dynamic-update-slice_fusion.25
  413.0 1.6 slice_dynamic-update-slice_fusion.24
  414.7 45.1 %collective-permute-done.27.refs_4_.refs_5_.refs_6_.refs_7_ = bf16[4,8,16,2304]{3,2,1,0:T(8,128)(2,1)S(1)} collective-permute-done((bf16[4,8,16,2304]{3,2,1,0:T(8,128)(2,1)S(1)}, bf16[4,8,16,2304]{3,2,1,0:T(8,128)(2,1)S(1)}, u32[]{:S(2)}, u32[]{:S(2)}) %collective-permute-start.27) | collective-permute-done | bytes 2359328 | tf_op jit(solution)/shard_map/ppermute | solution.py:407
  461.2 10.2 %expert_forward.2 = (bf16[2048,2304]{1,0:T(8,128)(2,1)}, bf16[2048,512]{1,0:T(8,128)(2,1)}, f32[2048,512]{1,0:T(8,128)}, f32[2048,512]{1,0:T(8,128)}) custom-call(bf16[2,8,16,2304]{3,2,1,0:T(8,128)(2,1)} %get-tuple-element.36.refs_0_, bf16[2,8,16,2304]{3,2,1,0:T(8,128)(2,1)} %copy-done.7, bf16[4,8,16,2304]{3,2,1,0:T(8,128)(2,1)} %copy-done.3, ...), custom_call_target="tpu_custom_call" | custom-call | flops 4831838208 | bytes 14680064 | tf_op jit(solution)/shard_map/expert_forward/pallas_call | solution.py:300
  471.4 3.2 dynamic-slice_bitcast_fusion.1.refs_6_.refs_7_
  474.6 3.2 dynamic-slice_bitcast_fusion.refs_2_.refs_3_.refs_4_.refs_5_
  477.9 10.2 %expert_forward.3 = (bf16[2048,2304]{1,0:T(8,128)(2,1)}, bf16[2048,512]{1,0:T(8,128)(2,1)}, f32[2048,512]{1,0:T(8,128)}, f32[2048,512]{1,0:T(8,128)}) custom-call(bf16[2,8,16,2304]{3,2,1,0:T(8,128)(2,1)} %get-tuple-element.32.refs_0_, bf16[2,8,16,2304]{3,2,1,0:T(8,128)(2,1)} %copy-done.9, ...), custom_call_target="tpu_custom_call", output_to_operand_aliasing={{0}: (9, {}), {1}: (10, {}), {2}: (11, {}), {3}: (12, {})} | custom-call | flops 4831838208 | bytes 14680064 | tf_op jit(solution)/shard_map/expert_forward/pallas_call | solution.py:300
  489.2 32.2 %expert_backward.1 = bf16[2304,1536]{1,0:T(8,128)(2,1)} custom-call(bf16[8,32,2304]{2,1,0:T(8,128)(2,1)} %pick_grad.8.refs_0_, bf16[8,32,2304]{2,1,0:T(8,128)(2,1)} %copy-done.12, bf16[8,32,2304]{2,1,0:T(8,128)(2,1)} %copy-done.16, bf16[8,32,2304]{2,1,0:T(8,128)(2,1)} %collective-permute-done.8.refs_3_, bf16[8,32,2304]{2,1,0:T(8,128)(2,1)} %copy-done.26, ...), custom_call_target="tpu_custom_call" | custom-call | flops 19327352832 | bytes 39845888 | tf_op jit(solution)/shard_map/expert_backward/pallas_call | solution.py:381
  (177 shorter events, 50.3 us)
Async XLA Ops:
  8.0 15.2 %copy-start.19 = (s32[16384]{0:T(1024)S(1)}, s32[16384]{0:T(1024)}, u32[]{:S(2)}) copy-start(s32[16384]{0:T(1024)} %param.14) | copy-start | bytes 196612
  8.0 113.7 %all-reduce.2.cloned.1.call-start = ((), (), s32[]{:S(2)}) async-start(), calls=%async_computation.2 | async-start | bytes 4718592 | tf_op jit(solution)/shard_map/psum | solution.py:516
  8.1 34.8 %collective-permute-start.4 = (bf16[768,2304]{1,0:T(8,128)(2,1)}, bf16[768,2304]{1,0:T(8,128)(2,1)}, u32[]{:S(2)}, u32[]{:S(2)}) collective-permute-start(bf16[768,2304]{1,0:T(8,128)(2,1)} %own_weight.1), channel_id=1, source_target_pairs={{0,16},{16,0},{32,48},{48,32},{64,80},{80,64},{96,112},{112,96},{1... | collective-permute-start | bytes 10616840 | tf_op jit(solution)/shard_map/ppermute | solution.py:407
  15.2 9.2 %collective-permute-start.2 = (bf16[16,768]{1,0:T(8,128)(2,1)S(1)}, bf16[16,768]{1,0:T(8,128)(2,1)S(1)}, u32[]{:S(2)}, u32[]{:S(2)}) collective-permute-start(bf16[16,768]{1,0:T(8,128)(2,1)S(1)} %slice.209), channel_id=1, source_target_pairs={{1,0},{2,1},{3,2},{4,3},{5,4},{6,5},{7,6},{8,7},{9,8},{10,9},{11,1... | collective-permute-start | bytes 73736 | tf_op jit(solution)/shard_map/ppermute | solution.py:499
  17.2 7.1 %collective-permute-start = (bf16[16,768]{1,0:T(8,128)(2,1)S(1)}, bf16[16,768]{1,0:T(8,128)(2,1)S(1)}, u32[]{:S(2)}, u32[]{:S(2)}) collective-permute-start(bf16[16,768]{1,0:T(8,128)(2,1)S(1)} %get-tuple-element.53), channel_id=1, source_target_pairs={{0,1},{1,2},{2,3},{3,4},{4,5},{5,6},{6,7},{7,8},{8,9},{9,10},{10,1... | collective-permute-start | bytes 73736 | tf_op jit(solution)/shard_map/ppermute | solution.py:497
  21.2 4.6 collective-permute-start.1
  24.4 1.4 copy-start.20
  24.4 1.4 copy-start.21
  39.0 3.9 collective-permute-start.3
  121.7 35.5 %collective-permute-start.5 = (bf16[512,2304]{1,0:T(8,128)(2,1)}, bf16[512,2304]{1,0:T(8,128)(2,1)S(1)}, u32[]{:S(2)}, u32[]{:S(2)}) collective-permute-start(bf16[512,2304]{1,0:T(8,128)(2,1)} %all-reduce.2.cloned.1.call-done.refs_1_), channel_id=1, source_target_pairs={{0,16},{16,0},{32,48},{48,32},{64,80},{80,64},{96,112},{112,96},{1... | collective-permute-start | bytes 7077896 | tf_op jit(solution)/shard_map/ppermute | solution.py:407
  122.4 4.4 copy-start.23
  122.4 4.4 copy-start.24
  122.4 25.1 %all-to-all-start = ((bf16[8,128,768]{2,1,0:T(8,128)(2,1)}), bf16[8,128,768]{2,1,0:T(8,128)(2,1)}, u32[]{:S(2)}, u32[]{:S(2)}) async-start(bf16[8,128,768]{2,1,0:T(8,128)(2,1)} %bitcast.29), calls=%async_computation | async-start | bytes 3145728 | tf_op jit(solution)/shard_map/all_to_all | solution.py:519
  148.2 9.0 %all-to-all-start.1 = ((f32[8,16,128]{2,1,0:T(8,128)}), f32[8,16,128]{2,1,0:T(8,128)S(1)}, u32[]{:S(2)}, u32[]{:S(2)}) async-start(f32[8,16,128]{2,1,0:T(8,128)} %broadcast_in_dim.4), calls=%async_computation.1 | async-start | bytes 131072 | tf_op jit(solution)/shard_map/all_to_all | solution.py:504
  152.3 161.2 %all-gather.7.cloned.1.call-start = ((), (), s32[]{:S(2)}) async-start(), calls=%async_computation.3 | async-start | bytes 10584064 | tf_op jit(solution)/shard_map/all_gather | solution.py:493
  152.9 241.8 %all-gather.9.cloned.1.call-start = ((), (), s32[]{:S(2)}) async-start(), calls=%async_computation.4 | async-start | bytes 7077888 | tf_op jit(solution)/shard_map/all_gather | solution.py:413
  157.8 1.4 copy-start
  162.9 39.5 %collective-permute-start.18 = (bf16[8,32,2304]{2,1,0:T(8,128)(2,1)}, bf16[8,32,2304]{2,1,0:T(8,128)(2,1)}, u32[]{:S(2)}, u32[]{:S(2)}) collective-permute-start(bf16[8,32,2304]{2,1,0:T(8,128)(2,1)} %pick_grad.15), channel_id=1, source_target_pairs={{0,12},{1,13},{2,14},{3,15},{4,8},{5,9},{6,10},{7,11},{8,4},{9,5},... | collective-permute-start | bytes 3538952 | tf_op jit(solution)/shard_map/ppermute | solution.py:407
  169.3 37.4 %collective-permute-start.14 = (bf16[8,32,2304]{2,1,0:T(8,128)(2,1)}, bf16[8,32,2304]{2,1,0:T(8,128)(2,1)}, u32[]{:S(2)}, u32[]{:S(2)}) collective-permute-start(bf16[8,32,2304]{2,1,0:T(8,128)(2,1)} %pick_grad.13), channel_id=1, source_target_pairs={{0,4},{1,5},{2,6},{3,7},{4,0},{5,1},{6,2},{7,3},{8,12},{9,13},{10,... | collective-permute-start | bytes 3538952 | tf_op jit(solution)/shard_map/ppermute | solution.py:407
  173.0 38.9 %collective-permute-start.10 = (bf16[8,32,2304]{2,1,0:T(8,128)(2,1)}, bf16[8,32,2304]{2,1,0:T(8,128)(2,1)}, u32[]{:S(2)}, u32[]{:S(2)}) collective-permute-start(bf16[8,32,2304]{2,1,0:T(8,128)(2,1)} %pick_grad.11), channel_id=1, source_target_pairs={{0,3},{1,2},{2,1},{3,0},{4,7},{5,6},{6,5},{7,4},{8,11},{9,10},{10,... | collective-permute-start | bytes 3538952 | tf_op jit(solution)/shard_map/ppermute | solution.py:407
  182.9 3.8 copy-start.4
  182.9 4.5 copy-start.5
  193.4 44.9 %collective-permute-start.6 = (bf16[8,32,2304]{2,1,0:T(8,128)(2,1)}, bf16[8,32,2304]{2,1,0:T(8,128)(2,1)S(1)}, u32[]{:S(2)}, u32[]{:S(2)}) collective-permute-start(bf16[8,32,2304]{2,1,0:T(8,128)(2,1)} %pick_grad.9), channel_id=1, source_target_pairs={{0,1},{1,0},{2,3},{3,2},{4,5},{5,4},{6,7},{7,6},{8,9},{9,8},{10,11... | collective-permute-start | bytes 3538952 | tf_op jit(solution)/shard_map/ppermute | solution.py:407
  198.6 4.9 slice-start
  203.6 4.2 slice-start.2
  203.6 81.2 %collective-permute-start.19 = (bf16[8,32,2304]{2,1,0:T(8,128)(2,1)S(1)}, bf16[8,32,2304]{2,1,0:T(8,128)(2,1)S(1)}, u32[]{:S(2)}, u32[]{:S(2)}) collective-permute-start(bf16[8,32,2304]{2,1,0:T(8,128)(2,1)S(1)} %pad_maximum_fusion.10), channel_id=1, source_target_pairs={{0,1},{1,0},{2,3},{3,2},{4,5},{5,4},{6,7},{7,6},{8,9},{9,8},{10,11... | collective-permute-start | bytes 3538952 | tf_op jit(solution)/shard_map/ppermute | solution.py:407
  207.9 5.1 slice-start.4
  207.9 77.4 %collective-permute-start.15 = (bf16[8,32,2304]{2,1,0:T(8,128)(2,1)S(1)}, bf16[8,32,2304]{2,1,0:T(8,128)(2,1)S(1)}, u32[]{:S(2)}, u32[]{:S(2)}) collective-permute-start(bf16[8,32,2304]{2,1,0:T(8,128)(2,1)S(1)} %pad_maximum_fusion.8), channel_id=1, source_target_pairs={{0,12},{1,13},{2,14},{3,15},{4,8},{5,9},{6,10},{7,11},{8,4},{9,5},... | collective-permute-start | bytes 3538952 | tf_op jit(solution)/shard_map/ppermute | solution.py:407
  213.1 25.2 %slice-start.6 = ((bf16[8,32,2304]{2,1,0:T(8,128)(2,1)}), bf16[4,32,2304]{2,1,0:T(8,128)(2,1)S(1)}, s32[]{:S(2)}) async-start(bf16[8,32,2304]{2,1,0:T(8,128)(2,1)} %pick_grad.8.refs_0_), calls=%async_computation.12 | async-start | bytes 1179648 | tf_op jit(solution)/shard_map/slice | solution.py:441
  213.1 74.3 %collective-permute-start.11 = (bf16[8,32,2304]{2,1,0:T(8,128)(2,1)S(1)}, bf16[8,32,2304]{2,1,0:T(8,128)(2,1)S(1)}, u32[]{:S(2)}, u32[]{:S(2)}) collective-permute-start(bf16[8,32,2304]{2,1,0:T(8,128)(2,1)S(1)} %pad_maximum_fusion.6), channel_id=1, source_target_pairs={{0,4},{1,5},{2,6},{3,7},{4,0},{5,1},{6,2},{7,3},{8,12},{9,13},{10,... | collective-permute-start | bytes 3538952 | tf_op jit(solution)/shard_map/ppermute | solution.py:407
  238.2 8.8 %copy-start.12 = (bf16[8,32,2304]{2,1,0:T(8,128)(2,1)}, bf16[8,32,2304]{2,1,0:T(8,128)(2,1)S(1)}, u32[]{:S(2)}) copy-start(bf16[8,32,2304]{2,1,0:T(8,128)(2,1)S(1)} %collective-permute-done.6.refs_1_) | copy-start | bytes 3538948
  238.4 50.7 %collective-permute-start.7 = (bf16[8,32,2304]{2,1,0:T(8,128)(2,1)S(1)}, bf16[8,32,2304]{2,1,0:T(8,128)(2,1)S(1)}, u32[]{:S(2)}, u32[]{:S(2)}) collective-permute-start(bf16[8,32,2304]{2,1,0:T(8,128)(2,1)S(1)} %pad_maximum_fusion.4), channel_id=1, source_target_pairs={{0,3},{1,2},{2,1},{3,0},{4,7},{5,6},{6,5},{7,4},{8,11},{9,10},{10,... | collective-permute-start | bytes 3538952 | tf_op jit(solution)/shard_map/ppermute | solution.py:407
  246.0 38.9 %slice-start.1 = ((bf16[8,32,2304]{2,1,0:T(8,128)(2,1)}), bf16[2,32,2304]{2,1,0:T(8,128)(2,1)S(1)}, s32[]{:S(2)}) async-start(bf16[8,32,2304]{2,1,0:T(8,128)(2,1)} %pick_grad.14.refs_15_), calls=%async_computation.7 | async-start | bytes 589824 | tf_op jit(solution)/shard_map/slice | solution.py:443
  284.9 8.1 %copy-start.13 = (bf16[8,32,2304]{2,1,0:T(8,128)(2,1)}, bf16[8,32,2304]{2,1,0:T(8,128)(2,1)S(1)}, u32[]{:S(2)}) copy-start(bf16[8,32,2304]{2,1,0:T(8,128)(2,1)S(1)} %collective-permute-done.19.refs_17_) | copy-start | bytes 3538948
  285.1 1.2 slice-start.3
  285.1 26.4 %collective-permute-start.20 = (bf16[8,32,2304]{2,1,0:T(8,128)(2,1)S(1)}, bf16[8,32,2304]{2,1,0:T(8,128)(2,1)S(1)}, u32[]{:S(2)}, u32[]{:S(2)}) collective-permute-start(bf16[8,32,2304]{2,1,0:T(8,128)(2,1)S(1)} %pad_maximum_fusion.11), channel_id=1, source_target_pairs={{0,3},{1,2},{2,1},{3,0},{4,7},{5,6},{6,5},{7,4},{8,11},{9,10},{10,... | collective-permute-start | bytes 3538952 | tf_op jit(solution)/shard_map/ppermute | solution.py:407
  285.3 9.0 %copy-start.14 = (bf16[8,32,2304]{2,1,0:T(8,128)(2,1)}, bf16[8,32,2304]{2,1,0:T(8,128)(2,1)S(1)}, u32[]{:S(2)}) copy-start(bf16[8,32,2304]{2,1,0:T(8,128)(2,1)S(1)} %collective-permute-done.15.refs_12_) | copy-start | bytes 3538948
  287.4 41.5 %collective-permute-start.16 = (bf16[8,32,2304]{2,1,0:T(8,128)(2,1)}, bf16[8,32,2304]{2,1,0:T(8,128)(2,1)}, u32[]{:S(2)}, u32[]{:S(2)}) collective-permute-start(bf16[8,32,2304]{2,1,0:T(8,128)(2,1)} %pad_maximum_fusion.9), channel_id=1, source_target_pairs={{0,1},{1,0},{2,3},{3,2},{4,5},{5,4},{6,7},{7,6},{8,9},{9,8},{10,11... | collective-permute-start | bytes 3538952 | tf_op jit(solution)/shard_map/ppermute | solution.py:407
  287.4 8.3 %copy-start.15 = (bf16[8,32,2304]{2,1,0:T(8,128)(2,1)}, bf16[8,32,2304]{2,1,0:T(8,128)(2,1)S(1)}, u32[]{:S(2)}) copy-start(bf16[8,32,2304]{2,1,0:T(8,128)(2,1)S(1)} %collective-permute-done.11.refs_7_) | copy-start | bytes 3538948
  288.7 59.3 %collective-permute-start.12 = (bf16[8,32,2304]{2,1,0:T(8,128)(2,1)S(1)}, bf16[8,32,2304]{2,1,0:T(8,128)(2,1)S(1)}, u32[]{:S(2)}, u32[]{:S(2)}) collective-permute-start(bf16[8,32,2304]{2,1,0:T(8,128)(2,1)S(1)} %pad_maximum_fusion.7), channel_id=1, source_target_pairs={{0,12},{1,13},{2,14},{3,15},{4,8},{5,9},{6,10},{7,11},{8,4},{9,5},... | collective-permute-start | bytes 3538952 | tf_op jit(solution)/shard_map/ppermute | solution.py:407
  289.1 7.9 %copy-start.16 = (bf16[8,32,2304]{2,1,0:T(8,128)(2,1)}, bf16[8,32,2304]{2,1,0:T(8,128)(2,1)S(1)}, u32[]{:S(2)}) copy-start(bf16[8,32,2304]{2,1,0:T(8,128)(2,1)S(1)} %collective-permute-done.7.refs_2_) | copy-start | bytes 3538948
  290.9 117.2 %collective-permute-start.8 = (bf16[8,32,2304]{2,1,0:T(8,128)(2,1)}, bf16[8,32,2304]{2,1,0:T(8,128)(2,1)}, u32[]{:S(2)}, u32[]{:S(2)}) collective-permute-start(bf16[8,32,2304]{2,1,0:T(8,128)(2,1)} %pad_maximum_fusion.5), channel_id=1, source_target_pairs={{0,4},{1,5},{2,6},{3,7},{4,0},{5,1},{6,2},{7,3},{8,12},{9,13},{10,... | collective-permute-start | bytes 3538952 | tf_op jit(solution)/shard_map/ppermute | solution.py:407
  311.5 1.4 copy-start.17
  322.7 7.8 %collective-permute-start.23 = (bf16[2,8,16,2304]{3,2,1,0:T(8,128)(2,1)}, bf16[2,8,16,2304]{3,2,1,0:T(8,128)(2,1)S(1)}, u32[]{:S(2)}, u32[]{:S(2)}) collective-permute-start(bf16[2,8,16,2304]{3,2,1,0:T(8,128)(2,1)} %get-tuple-element.35), channel_id=1, source_target_pairs={{0,16},{16,0},{32,48},{48,32},{64,80},{80,64},{96,112},{112,96},{1... | collective-permute-start | bytes 3538952 | tf_op jit(solution)/shard_map/ppermute | solution.py:407
  327.6 160.5 %collective-permute-start.21 = (bf16[8,32,2304]{2,1,0:T(8,128)(2,1)}, bf16[8,32,2304]{2,1,0:T(8,128)(2,1)}, u32[]{:S(2)}, u32[]{:S(2)}) collective-permute-start(bf16[8,32,2304]{2,1,0:T(8,128)(2,1)} %slice_dynamic-update-slice_fusion), channel_id=1, source_target_pairs={{0,4},{1,5},{2,6},{3,7},{4,0},{5,1},{6,2},{7,3},{8,12},{9,13},{10,... | collective-permute-start | bytes 3538952 | tf_op jit(solution)/shard_map/ppermute | solution.py:407
  333.4 141.2 %all-gather.11.cloned.1.call-start = ((), (), s32[]{:S(2)}) async-start(), calls=%async_computation.5 | async-start | bytes 7077888 | tf_op jit(solution)/shard_map/all_gather | solution.py:413
  346.2 3.1 collective-permute-start.25
  348.0 1.2 copy-start.18
  349.3 4.8 copy-start.25
  349.3 5.3 copy-start.27
  349.3 8.5 %copy-start.8 = (bf16[2,8,16,2304]{3,2,1,0:T(8,128)(2,1)S(1)}, bf16[2,8,16,2304]{3,2,1,0:T(8,128)(2,1)}, u32[]{:S(2)}) copy-start(bf16[2,8,16,2304]{3,2,1,0:T(8,128)(2,1)} %get-tuple-element.32.refs_0_) | copy-start | bytes 3538948
  352.3 6.4 %copy-start.6 = (bf16[2,8,16,2304]{3,2,1,0:T(8,128)(2,1)S(1)}, bf16[2,8,16,2304]{3,2,1,0:T(8,128)(2,1)}, u32[]{:S(2)}) copy-start(bf16[2,8,16,2304]{3,2,1,0:T(8,128)(2,1)} %get-tuple-element.36.refs_0_) | copy-start | bytes 3538948
  352.3 52.8 %collective-permute-start.26 = (bf16[4,8,16,2304]{3,2,1,0:T(8,128)(2,1)}, bf16[4,8,16,2304]{3,2,1,0:T(8,128)(2,1)S(1)}, u32[]{:S(2)}, u32[]{:S(2)}) collective-permute-start(bf16[4,8,16,2304]{3,2,1,0:T(8,128)(2,1)} %pad_maximum_fusion.2), channel_id=1, source_target_pairs={{0,32},{16,48},{32,0},{48,16},{64,96},{80,112},{96,64},{112,80},{1... | collective-permute-start | bytes 7077896 | tf_op jit(solution)/shard_map/ppermute | solution.py:407
  354.1 5.5 %collective-permute-start.22 = (bf16[2,8,16,2304]{3,2,1,0:T(8,128)(2,1)S(1)}, bf16[2,8,16,2304]{3,2,1,0:T(8,128)(2,1)S(1)}, u32[]{:S(2)}, u32[]{:S(2)}) collective-permute-start(bf16[2,8,16,2304]{3,2,1,0:T(8,128)(2,1)S(1)} %copy-done.25), channel_id=1, source_target_pairs={{0,16},{16,0},{32,48},{48,32},{64,80},{80,64},{96,112},{112,96},{1... | collective-permute-start | bytes 3538952 | tf_op jit(solution)/shard_map/ppermute | solution.py:407
  354.5 5.4 %collective-permute-start.24 = (bf16[2,8,16,2304]{3,2,1,0:T(8,128)(2,1)S(1)}, bf16[2,8,16,2304]{3,2,1,0:T(8,128)(2,1)S(1)}, u32[]{:S(2)}, u32[]{:S(2)}) collective-permute-start(bf16[2,8,16,2304]{3,2,1,0:T(8,128)(2,1)S(1)} %copy-done.27), channel_id=1, source_target_pairs={{0,16},{16,0},{32,48},{48,32},{64,80},{80,64},{96,112},{112,96},{1... | collective-permute-start | bytes 3538952 | tf_op jit(solution)/shard_map/ppermute | solution.py:407
  359.5 128.6 %collective-permute-start.17 = (bf16[8,32,2304]{2,1,0:T(8,128)(2,1)}, bf16[8,32,2304]{2,1,0:T(8,128)(2,1)}, u32[]{:S(2)}, u32[]{:S(2)}) collective-permute-start(bf16[8,32,2304]{2,1,0:T(8,128)(2,1)} %slice_dynamic-update-slice_fusion.8), channel_id=1, source_target_pairs={{0,3},{1,2},{2,1},{3,0},{4,7},{5,6},{6,5},{7,4},{8,11},{9,10},{10,... | collective-permute-start | bytes 3538952 | tf_op jit(solution)/shard_map/ppermute | solution.py:407
  360.5 127.6 %collective-permute-start.13 = (bf16[8,32,2304]{2,1,0:T(8,128)(2,1)}, bf16[8,32,2304]{2,1,0:T(8,128)(2,1)}, u32[]{:S(2)}, u32[]{:S(2)}) collective-permute-start(bf16[8,32,2304]{2,1,0:T(8,128)(2,1)} %slice_dynamic-update-slice_fusion.16), channel_id=1, source_target_pairs={{0,1},{1,0},{2,3},{3,2},{4,5},{5,4},{6,7},{7,6},{8,9},{9,8},{10,11... | collective-permute-start | bytes 3538952 | tf_op jit(solution)/shard_map/ppermute | solution.py:407
  394.7 1.4 slice-start.8
  394.7 1.6 copy-start.11
  398.0 8.5 %copy-start.10 = (bf16[1,8,16,2304]{3,2,1,0:T(8,128)(2,1)S(1)}, bf16[1,8,16,2304]{3,2,1,0:T(8,128)(2,1)}, u32[]{:S(2)}) copy-start(bf16[1,8,16,2304]{3,2,1,0:T(8,128)(2,1)} %slice.272) | copy-start | bytes 1769476
  405.1 1.4 copy-start.3
  406.8 53.0 %collective-permute-start.27 = (bf16[4,8,16,2304]{3,2,1,0:T(8,128)(2,1)S(1)}, bf16[4,8,16,2304]{3,2,1,0:T(8,128)(2,1)S(1)}, u32[]{:S(2)}, u32[]{:S(2)}) collective-permute-start(bf16[4,8,16,2304]{3,2,1,0:T(8,128)(2,1)S(1)} %pad_maximum_fusion.3), channel_id=1, source_target_pairs={{0,96},{16,112},{32,64},{48,80},{64,32},{80,48},{96,0},{112,16},{1... | collective-permute-start | bytes 7077896 | tf_op jit(solution)/shard_map/ppermute | solution.py:407
  414.6 73.6 %collective-permute-start.9 = (bf16[8,32,2304]{2,1,0:T(8,128)(2,1)}, bf16[8,32,2304]{2,1,0:T(8,128)(2,1)S(1)}, u32[]{:S(2)}, u32[]{:S(2)}) collective-permute-start(bf16[8,32,2304]{2,1,0:T(8,128)(2,1)} %slice_dynamic-update-slice_fusion.24), channel_id=1, source_target_pairs={{0,12},{1,13},{2,14},{3,15},{4,8},{5,9},{6,10},{7,11},{8,4},{9,5},... | collective-permute-start | bytes 3538952 | tf_op jit(solution)/shard_map/ppermute | solution.py:407
  459.8 1.4 copy-start.1
  (9 other events, 8.3 us)
Sparse Core Ops, SparseCore 0:
  52.8 68.9 all-reduce.1
Sparse Core Ops, SparseCore 1:
  154.9 126.4 all-gather.6
  333.5 61.1 all-gather.8
  398.1 64.1 all-gather.10

commit v3 on v2

--- a/solution.py
+++ b/solution.py
@@ -25,10 +25,12 @@
     scale = lax.rsqrt(jnp.mean(rows * rows, axis=1, keepdims=True) + 1e-06)
     out_ref[:, :dim] = (rows * scale * gain_ref[...]).astype(BF16)
     out_ref[:, dim:] = jnp.zeros((rows.shape[0], EXTRA), BF16)
-    out_ref[:, dim : dim + routes_ref.shape[1]] = routes_ref[...].astype(F32).astype(BF16)
-
-
-def norm_rows(resid, gain, routes):
+    names = routes_ref[...].astype(F32)
+    pad = jnp.zeros((HALO - names.shape[0], EXTRA), F32)
+    out_ref[:HALO, dim:] = jnp.concatenate([names, pad]).astype(BF16)
+
+
+def norm_rows(resid, gain, names):
     tokens, dim = resid.shape
     return pl.pallas_call(
         norm_kernel,
@@ -36,7 +38,7 @@
         compiler_params=pltpu.CompilerParams(vmem_limit_bytes=VMEM_LIMIT),
         cost_estimate=call_cost(resid.size * 6, resid.size * 4),
         name="norm_rows",
-    )(resid, gain.reshape(1, -1), routes)
+    )(resid, gain.reshape(1, -1), names)
 
 
 def conv_kernel(
@@ -184,7 +186,7 @@
 def pick_norm_kernel(per_token, capacity, n_exp, turns, place_ref, rows_ref, *out_refs):
     tokens = rows_ref.shape[1]
     dim = out_refs[0].shape[3]
-    names = rows_ref[0, :, dim:].astype(F32).T[:per_token].astype(jnp.int32)
+    names = rows_ref[0, :HALO, dim:].astype(F32)[:per_token].astype(jnp.int32)
     own = jnp.concatenate(
         [jnp.full((1, tokens), (place_ref[0] ^ t) * n_exp + place_ref[1], jnp.int32) for t in turns]
     )
@@ -216,107 +218,140 @@
     )(place, rows)
 
 
-def pick_grad_kernel(per_token, capacity, n_exp, turns, place_ref, *refs):
-    out_ref = refs[-1]
-    tokens = refs[0].shape[2]
-    own = jnp.concatenate(
-        [jnp.full((1, tokens), place_ref[0] * n_exp + (place_ref[1] ^ t), jnp.int32) for t in turns]
-    )
-    for core in range(2):
-        table_ref, rows_ref = refs[2 * core : 2 * core + 2]
-        names = table_ref[0, :per_token].astype(jnp.int32)
-        picker, match = slot_picker(names, own, capacity)
-        weights = table_ref[0, per_token:]
-        scale = functools.reduce(
-            jnp.add, [jnp.where(match[k], weights[k : k + 1], 0.0) for k in range(per_token)]
+def pick_grad_kernel(per_token, capacity, n_exp, turns, place_ref, tables_ref, *refs):
+    flow_refs, out_refs = refs[:2], refs[2:-2]
+    buffer, sems = refs[-2:]
+    tokens = tables_ref.shape[2]
+    copies = []
+    for quarter, turn in enumerate(turns):
+        count = len(turn)
+        own = jnp.concatenate(
+            [
+                jnp.full((1, tokens), place_ref[0] * n_exp + (place_ref[1] ^ t), jnp.int32)
+                for t in turn
+            ]
         )
-        scales = jnp.sum(picker * scale[:, None, :], axis=2, keepdims=True)
-        picker = picker.reshape(len(turns) * capacity, tokens).astype(BF16)
-        picked = jnp.dot(picker, rows_ref[...], preferred_element_type=F32)
-        picked = (picked * scales.reshape(len(turns) * capacity, 1)).astype(BF16)
-        for index in range(len(turns)):
-            out_ref[index, core * capacity : (core + 1) * capacity] = picked[
-                index * capacity : (index + 1) * capacity
-            ]
-
-
-def pick_grad(place, tables, flows, turns, quarter, n_exp, per_token, capacity):
-    tokens = tables.shape[2]
+        first = pl.multiple_of(((place_ref[0] >> 1) ^ quarter) * tokens, tokens)
+        for core in range(2):
+            table = tables_ref[place_ref[0] ^ (2 * quarter + core)]
+            names = table[:per_token].astype(jnp.int32)
+            picker, match = slot_picker(names, own, capacity)
+            weights = table[per_token:]
+            scale = functools.reduce(
+                jnp.add, [jnp.where(match[k], weights[k : k + 1], 0.0) for k in range(per_token)]
+            )
+            scales = jnp.sum(picker * scale[:, None, :], axis=2, keepdims=True)
+            picker = picker.reshape(count * capacity, tokens).astype(BF16)
+            picked = jnp.dot(
+                picker, flow_refs[core][pl.ds(first, tokens)], preferred_element_type=F32
+            )
+            picked = (picked * scales.reshape(count * capacity, 1)).astype(BF16)
+            for index in range(count):
+                buffer[quarter, index, core * capacity : (core + 1) * capacity] = picked[
+                    index * capacity : (index + 1) * capacity
+                ]
+        for part in range(2):
+            at = 2 * quarter + part
+            copy = pltpu.make_async_copy(
+                buffer.at[quarter, pl.ds(part * count // 2, count // 2)],
+                out_refs[at],
+                sems.at[at],
+            )
+            copy.start()
+            copies.append(copy)
+    for copy in copies:
+        copy.wait()
+
+
+def pick_grad(place, tables, flows, turns, n_exp, per_token, capacity):
     dim = flows[0].shape[1]
-    table_spec = lambda core: pl.BlockSpec(
-        (1, 2 * per_token, tokens), lambda i, p: (p[0] ^ (2 * quarter + core), 0, 0)
-    )
-    flow_spec = pl.BlockSpec((tokens, dim), lambda i, p: ((p[0] >> 1) ^ quarter, 0))
-    shape = (len(turns), 2 * capacity, dim)
+    rows, count = 2 * capacity, len(turns[0])
+    whole = lambda array: pl.BlockSpec(array.shape, lambda i, p: (0,) * array.ndim)
+    outs = 2 * len(turns)
     return pl.pallas_call(
         functools.partial(pick_grad_kernel, per_token, capacity, n_exp, turns),
         grid_spec=pltpu.PrefetchScalarGridSpec(
             num_scalar_prefetch=1,
             grid=(1,),
-            in_specs=[table_spec(0), flow_spec, table_spec(1), flow_spec],
-            out_specs=pl.BlockSpec(shape, lambda i, p: (0, 0, 0)),
-        ),
-        out_shape=jax.ShapeDtypeStruct(shape, BF16),
+            in_specs=[whole(tables), whole(flows[0]), whole(flows[1])],
+            out_specs=[pl.BlockSpec(memory_space=pl.ANY)] * outs,
+            scratch_shapes=[
+                pltpu.VMEM((len(turns), count, rows, dim), BF16),
+                pltpu.SemaphoreType.DMA((outs,)),
+            ],
+        ),
+        out_shape=[jax.ShapeDtypeStruct((count // 2, rows, dim), BF16)] * outs,
         compiler_params=pltpu.CompilerParams(vmem_limit_bytes=VMEM_LIMIT),
         cost_estimate=call_cost(
-            4 * len(turns) * capacity * tokens * dim,
-            4 * dim * (tokens + len(turns) * capacity),
+            2 * len(turns) * count * rows * tables.shape[2] * dim,
+            4 * dim * (flows[0].shape[0] + len(turns) * count * rows // 2),
         ),
         name="pick_grad",
-    )(place, tables, flows[0], tables, flows[1])
+    )(place, tables, *flows)
 
 
 def forward_kernel(sources, *refs):
-    row_refs = refs[:sources]
-    weight_ref = refs[sources]
-    rows_out, act_ref, gate_ref, up_ref = refs[-4:]
-    _, pair, capacity, _ = row_refs[0].shape
-    for inner in range(pair):
+    row_refs = refs[1 : 1 + sources]
+    weight_ref = refs[1 + sources]
+    rows_out, act_ref, gate_ref, up_ref, rows = refs[-5:]
+    _, group, capacity, _ = row_refs[0].shape
+    for inner in range(group):
         for index in range(sources):
             at = (inner * sources + index) * capacity
-            rows_out[at : at + capacity] = row_refs[index][0, inner]
-    hidden = act_ref.shape[1]
-    mixed = jnp.dot(rows_out[...], weight_ref[...], preferred_element_type=F32)
+            rows[at : at + capacity] = row_refs[index][0, inner]
+    hidden = act_ref.shape[0]
+    mixed = jnp.dot(rows[...], weight_ref[...], preferred_element_type=F32)
+    rows_out[...] = rows[...].T
     gate = mixed[:, :hidden]
     up = mixed[:, hidden:]
     sig = jax.nn.sigmoid(gate)
     silu = gate * sig
-    act_ref[...] = (silu * up).astype(BF16)
+    act_ref[...] = (silu * up).astype(BF16).T
     gate_ref[...] = up * sig * (1.0 + gate * (1.0 - sig))
     up_ref[...] = silu
 
 
-def expert_forward(pieces, weight, hidden, parts, part, before):
+def expert_forward(pieces, weight, hidden, shifts, parts, part, before):
     sources = len(pieces)
     _, blocks, capacity, dim = pieces[0][0].shape
-    pair = 2
-    tile = sources * pair * capacity
-    steps = blocks // pair
-    total = sources * blocks * capacity * parts
-    row_spec = lambda width: pl.BlockSpec((tile, width), lambda i: (i + part * steps, 0))
-    piece_spec = lambda unit: pl.BlockSpec(
-        (1, pair, capacity, dim), lambda i: (unit, i, 0, 0)
-    )
+    group = 16 // sources
+    tile = sources * group * capacity
+    steps = blocks // group
+    total = tile * steps * parts
+    at = lambda i: i + part * steps
+    row_spec = lambda width: pl.BlockSpec((tile, width), lambda i, p: (at(i), 0))
+    column_spec = lambda height: pl.BlockSpec((height, tile), lambda i, p: (0, at(i)))
+
+    def piece_spec(unit, shift):
+        return pl.BlockSpec(
+            (1, group, capacity, dim),
+            lambda i, p: (unit if shift is None else unit + p[shift], i, 0, 0),
+        )
+
     return pl.pallas_call(
         functools.partial(forward_kernel, sources),
-        grid=(steps,),
-        in_specs=[piece_spec(unit) for _, unit in pieces]
-        + [pl.BlockSpec((dim, 2 * hidden), lambda i: (0, 0))]
-        + [pl.BlockSpec(memory_space=pl.ANY)] * len(before),
-        out_specs=[row_spec(dim), row_spec(hidden), row_spec(hidden), row_spec(hidden)],
+        grid_spec=pltpu.PrefetchScalarGridSpec(
+            num_scalar_prefetch=1,
+            grid=(steps,),
+            in_specs=[piece_spec(unit, shift) for _, unit, shift in pieces]
+            + [pl.BlockSpec((dim, 2 * hidden), lambda i, p: (0, 0))]
+            + [pl.BlockSpec(memory_space=pl.ANY)] * len(before),
+            out_specs=[column_spec(dim), column_spec(hidden), row_spec(hidden), row_spec(hidden)],
+            scratch_shapes=[pltpu.VMEM((tile, dim), BF16)],
+        ),
         out_shape=[
-            jax.ShapeDtypeStruct((total, dim), BF16),
-            jax.ShapeDtypeStruct((total, hidden), BF16),
+            jax.ShapeDtypeStruct((dim, total), BF16),
+            jax.ShapeDtypeStruct((hidden, total), BF16),
             jax.ShapeDtypeStruct((total, hidden), F32),
             jax.ShapeDtypeStruct((total, hidden), F32),
         ],
-        input_output_aliases={sources + 1 + i: i for i in range(len(before))},
+        input_output_aliases={sources + 2 + i: i for i in range(len(before))},
         compiler_params=pltpu.CompilerParams(vmem_limit_bytes=VMEM_LIMIT),
         cost_estimate=call_cost(
             4 * total * dim * hidden // parts, (4 * total * dim + 10 * total * hidden) // parts
         ),
         name="expert_forward",
-    )(*[array for array, _ in pieces], weight, *before)
+    )(shifts, *[array for array, _, _ in pieces], weight, *before)
 
 
 def backward_kernel(places, arrays, *refs):
@@ -325,8 +360,8 @@
     grads_all, hidden_all, sems = refs[arrays + 6 :]
     step = pl.program_id(0)
     tile = gate_ref.shape[0]
-    hidden = act_ref.shape[1]
-    width = rows_ref.shape[1]
+    hidden = act_ref.shape[0]
+    width = rows_ref.shape[0]
     row_steps = grads_all.shape[0] // tile
     copies = []
     for index, (array, unit, row, size) in enumerate(places):
@@ -360,18 +395,16 @@
     @pl.when(step >= row_steps)
     def _():
         columns = pl.ds(pl.multiple_of((step - row_steps) * width, width), width)
-        over_rows = (((0,), (0,)), ((), ()))
-        out_ref[:, : 2 * hidden] = lax.dot_general(
-            rows_ref[...], hidden_all[...], over_rows, preferred_element_type=F32
+        out_ref[:, : 2 * hidden] = jnp.dot(
+            rows_ref[...], hidden_all[...], preferred_element_type=F32
         ).astype(BF16)
-        out_ref[:, 2 * hidden :] = lax.dot_general(
-            grads_all[:, columns], act_ref[...], over_rows, preferred_element_type=F32
-        ).astype(BF16)
+        down = jnp.dot(act_ref[...], grads_all[:, columns], preferred_element_type=F32)
+        out_ref[:, 2 * hidden :] = down.T.astype(BF16)
 
 
 def expert_backward(arrays, places, gate, up, weights, rows, act):
-    total, dim = rows.shape
-    hidden = act.shape[1]
+    dim, total = rows.shape
+    hidden = act.shape[0]
     tile, width = 256, 256
     row_steps, column_steps = total // tile, dim // width
     row_spec = lambda cols: pl.BlockSpec(
@@ -386,8 +419,8 @@
             row_spec(hidden),
             row_spec(hidden),
             pl.BlockSpec((dim, hidden), lambda i: (0, 2)),
-            pl.BlockSpec((total, width), lambda i: (0, column_of(i))),
-            pl.BlockSpec((total, hidden), lambda i: (0, 0)),
+            pl.BlockSpec((width, total), lambda i: (column_of(i), 0)),
+            pl.BlockSpec((hidden, total), lambda i: (0, 0)),
         ],
         out_specs=pl.BlockSpec((width, 3 * hidden), lambda i: (column_of(i), 0)),
         out_shape=jax.ShapeDtypeStruct((dim, 3 * hidden), BF16),
@@ -407,46 +440,40 @@
     return lax.ppermute(array, axis, [(i, i ^ flip) for i in range(count)])
 
 
+def mask_of(flips, bits):
+    return functools.reduce(lambda a, b: a ^ b, [f for f, bit in zip(flips, bits) if bit], 0)
+
+
+def flips_of(half):
+    return (1, 3) if half == 0 else (3, 1)
+
+
+def sibling_rows(picks):
+    keep, send, keep_far, send_far = picks
+    send_got, keep_got = swap(send_far, "seq", 1), swap(keep_far, "seq", 1)
+    return keep, keep_got, jnp.concatenate([send, send_got])
+
+
 def swap_gather(array, axis, flip):
-    count, index = lax.axis_size(axis), lax.axis_index(axis)
+    count = lax.axis_size(axis)
     groups = [[i, i ^ flip] for i in range(count) if i < i ^ flip]
     both = lax.all_gather(array, axis, axis_index_groups=groups)
-    other = (index < (index ^ flip)).astype(jnp.int32)
-    return lax.dynamic_index_in_dim(both, other, 0, keepdims=False)
-
-
-def mask_of(flips, bits):
-    return functools.reduce(lambda a, b: a ^ b, [f for f, bit in zip(flips, bits) if bit], 0)
-
-
-def exchange_rows(half, picks, exchange):
-    keep, send, keep_far, send_far = picks
-    flips = (1, 3) if half == 0 else (3, 1)
-    send_got, keep_got = swap(send_far, "seq", 1), swap(keep_far, "seq", 1)
-    first = exchange(jnp.concatenate([send, send_got]), "seq", 2 * flips[0])
-    second = exchange(
-        jnp.concatenate([keep[1:], keep_got[1:], first[1:2], first[3:4]]), "seq", 2 * flips[1]
-    )
-    found = {
-        0: [(keep, 0), (keep_got, 0)],
-        flips[0]: [(first, 0), (first, 2)],
-        flips[1]: [(second, 0), (second, 1)],
-        flips[0] ^ flips[1]: [(second, 2), (second, 3)],
-    }
-    return [found[r >> 1][r & 1] for r in range(8)]
+    return both.reshape((-1,) + array.shape[1:])
 
 
 def exchange_grads(flips, keep, send):
     first = swap(send, "exp", flips[0])
     second = swap(jnp.concatenate([keep[4:8], first[4:8]]), "exp", flips[1])
+    return keep, first, second
+
+
+def finish_grads(flips, keep, first, second):
     third = swap(
         jnp.concatenate([keep[2:4], first[2:4], second[2:4], second[6:8]]), "exp", flips[2]
     )
     odd = lambda a: [a[i : i + 1] for i in (1, 3, 5, 7)]
     fourth = swap(
-        jnp.concatenate(
-            [keep[1:2], first[1:2], second[1:2], second[5:6]] + odd(third)
-        ),
+        jnp.concatenate([keep[1:2], first[1:2], second[1:2], second[5:6]] + odd(third)),
         "exp",
         flips[3],
     )
@@ -458,7 +485,6 @@
     found[1, 1, 0, 0] = (2, 4)
     for index, start in enumerate([(0, 0), (1, 0), (0, 1), (1, 1)]):
         found[start + (1, 0)] = (3, 2 * index)
-    for index, start in enumerate([(0, 0), (1, 0), (0, 1), (1, 1)]):
         found[start + (0, 1)] = (4, index)
         found[start + (1, 1)] = (4, 4 + index)
     return arrays, {mask_of(flips, bits): at for bits, at in found.items()}
@@ -488,10 +514,6 @@
     own_weights = expert_weights[0]
 
     place = jnp.stack([seq_index, exp_index]).astype(jnp.int32)
-    normed = norm_rows(resid, norm_gain, routes)
-    normed, qkv_grad = lax.optimization_barrier((normed, qkv_grad))
-    exp_normed = lax.all_gather(normed, "exp")
-
     forward = [(i, i + 1) for i in range(n_exp - 1)]
     backward = [(i + 1, i) for i in range(n_exp - 1)]
     low = lax.ppermute(qkv_in[-HALO:], "exp", forward)
@@ -502,6 +524,9 @@
     table = jnp.concatenate([routes.astype(F32), route_weights], 1).T
     tables = jnp.broadcast_to(table[None], (n_seq,) + table.shape)
     tables = lax.all_to_all(tables, "seq", split_axis=0, concat_axis=0, tiled=True)
+    normed = norm_rows(resid, norm_gain, routes.T)
+    normed, tables, conv_weight = lax.optimization_barrier((normed, tables, conv_weight))
+    exp_normed = lax.all_gather(normed, "exp")
 
     edge = jnp.full((HALO,), -1, jnp.int32)
     ids = lax.dynamic_slice_in_dim(
@@ -514,44 +539,73 @@
     partial = project(place, local_keep, local_got, qkv_weight, weight_far, out_grad)
     same_core = [[s for s in range(n_seq) if s % 2 == core] for core in range(2)]
     flow = lax.psum(partial, "seq", axis_index_groups=same_core)
-    flow, local_grad = lax.optimization_barrier((flow, local_grad))
-    flow_far = swap(flow, "seq", 1)
-    qkv_in_grad = lax.all_to_all(local_grad, "seq", split_axis=0, concat_axis=1, tiled=True)
 
     halves = []
     for half in range(2):
-        near = (0, 3, 1, 2) if half == 0 else (0, 1, 3, 2)
+        flips = flips_of(half)
+        near = (0, flips[1], flips[0], flips[0] ^ flips[1])
         turns = tuple(2 * m for m in near) + tuple(2 * m + 1 for m in near)
         picks = pick_norm(
             place, exp_normed, turns, half * n_exp // 2, n_exp // 2, dim, per_token, capacity
         )
-        halves.append(exchange_rows(half, picks, swap if half == 0 else swap_gather))
-    results = ()
-    for half in range(2):
-        results = expert_forward(halves[half], own_weights, hidden, 2, half, results)
-    rows_all, act, gate, up = results
+        halves.append(sibling_rows(picks))
+    (keep_a, far_a, message_a), (keep_b, far_b, message_b) = halves
+    flow, far_a, far_b = lax.optimization_barrier((flow, far_a, far_b))
+    flow_far = swap(flow, "seq", 1)
 
     flips = (1, 3, 4, 12)
     quarters = len(flips)
     orders = [flips[k:] + flips[:k] for k in range(quarters)]
-    bit_rows = [tuple((j >> (2 - b)) & 1 for b in range(3)) for j in range(8)]
-    turns_of = lambda k, bit: tuple(mask_of(orders[k], (bit,) + bits) for bits in bit_rows)
-    picks = [
-        [
-            pick_grad(
-                place, tables, (flow, flow_far), turns_of(k, bit), k, n_exp, per_token, capacity
-            )
-            for k in range(quarters)
-        ]
-        for bit in (1, 0)
+    bit_rows = [tuple((j >> (3 - b)) & 1 for b in range(4)) for j in range(n_exp)]
+    turns = tuple(tuple(mask_of(order, bits) for bits in bit_rows) for order in orders)
+    sends = pick_grad(place, tables, (flow, flow_far), turns, n_exp, per_token, capacity)
+
+    flips_a, flips_b = flips_of(0), flips_of(1)
+    shifts = [(seq_index < seq_index ^ 2 * f).astype(jnp.int32) * 4 for f in flips_b]
+    first_a = swap(message_a, "seq", 2 * flips_a[0])
+    first_b = swap_gather(message_b, "seq", 2 * flips_b[0])
+    states = [
+        exchange_grads(orders[k], sends[2 * k], sends[2 * k + 1]) for k in range(quarters)
     ]
+    first_a, first_b, states = lax.optimization_barrier((first_a, first_b, states))
+    piece = lambda i: lax.dynamic_slice_in_dim(first_b, shifts[0] + i, 1, 0)
+    second_a = swap(
+        jnp.concatenate([keep_a[1:], far_a[1:], first_a[1:2], first_a[3:4]]),
+        "seq",
+        2 * flips_a[1],
+    )
+    second_b = swap_gather(
+        jnp.concatenate([keep_b[1:], far_b[1:], piece(1), piece(3)]), "seq", 2 * flips_b[1]
+    )
+    local_grad, second_a, second_b = lax.optimization_barrier((local_grad, second_a, second_b))
+    qkv_in_grad = lax.all_to_all(local_grad, "seq", split_axis=0, concat_axis=1, tiled=True)
+    calls = [
+        [(keep_a, 0, None), (far_a, 0, None), (first_a, 0, None), (first_a, 2, None)],
+        [(keep_b, 0, None), (far_b, 0, None), (first_b, 0, 0), (first_b, 2, 0)],
+        [(second_a, i, None) for i in range(4)],
+        [(second_b, i, 1) for i in range(4)],
+    ]
+    results = ()
+    for part, pieces in enumerate(calls):
+        results = expert_forward(
+            pieces, own_weights, hidden, jnp.stack(shifts), len(calls), part, results
+        )
+    rows_all, act, gate, up = results
+
+    def row_of(mask, quarter):
+        half, inner = mask >> 3, mask & 7
+        flips = flips_of(half)
+        order = (0, flips[0], flips[1], flips[0] ^ flips[1])
+        spot = order.index(quarter)
+        call = (spot >> 1) * 2 + half
+        tile = call * 2 + (inner >> 2)
+        return tile * n_exp * capacity + (inner & 3) * 4 * capacity + (spot & 1) * 2 * capacity
+
     arrays, places = [], []
     for k in range(quarters):
-        got, found = exchange_grads(orders[k], picks[1][k], picks[0][k])
-        size = 2 * capacity
+        got, found = finish_grads(orders[k], *states[k])
         for mask, (array, unit) in sorted(found.items()):
-            row = mask * n_seq * capacity + k * size
-            places.append((len(arrays) + array, unit, row, size))
+            places.append((len(arrays) + array, unit, row_of(mask, k), 2 * capacity))
         arrays += got
     expert_grads = expert_backward(arrays, tuple(places), gate, up, own_weights, rows_all, act)
     return (qkv_in_grad, expert_grads[None])

time: 532 us -> 367 us (0.69)
  waiting for transfers between devices: 265 us -> 109 us
  local copies, waits for them, and re-layouts: 74 us -> 63.5 us
  Pallas kernels: 125 us -> 115 us
  starting transfers between devices: 36.9 us -> 45.9 us
    ppermute x25, waiting for transfers between devices: 139 us -> 59.2 us  [swap(): return lax.ppermute(array, axis, [(i, i ^ flip) for i in range(count)])]
    psum x1, waiting for transfers between devices: 69.1 us -> 6.58 us  [per_device(): flow = lax.psum(partial, 'seq', axis_index_groups=same_core)]
    all_gather x1, waiting for transfers between devices: 0.01 us -> 39.4 us  [per_device(): exp_normed = lax.all_gather(normed, 'exp')]
    all_gather x2, waiting for transfers between devices: 33.1 us -> 0.03 us  [swap_gather(): both = lax.all_gather(array, axis, axis_index_groups=groups)]
    pallas_call x8 -> x1, Pallas kernels: 29.8 us -> 8.24 us  [pick_grad(): pl.pallas_call(functools.partial(pick_grad_kernel, per_token, capacity, n...]
    all_to_all x1, waiting for transfers between devices: 20.7 us -> 0.01 us  [per_device(): lax.all_to_all(local_grad, 'seq', split_axis=0, concat_axis=1, tiled=True)]
    pallas_call x2 -> x4, Pallas kernels: 20.4 us -> 31.3 us  [expert_forward(): pl.pallas_call(functools.partial(forward_kernel, sources), grid_spec=pltp...]
    all_to_all x1, starting transfers between devices: 4.38 us -> 12.2 us  [per_device(): lax.all_to_all(local_grad, 'seq', split_axis=0, concat_axis=1, tiled=True)]
  transfers between devices with their start and end apart: 34 -> 34, of which waited for: 15 -> 14; matrix products, arithmetic and copies ran while one was open for 14% -> 13% of each run, Pallas kernels for 16% -> 31%
where the time goes in v3:
time: 367 us; the launch traced here: 365 us
  Pallas kernels  115 us (31%)
  waiting for transfers between devices  109 us (30%)
  local copies, waits for them, and re-layouts  63.5 us (17%)
  starting transfers between devices  45.9 us (13%)
  other arithmetic  16 us (4%)
  between operations  15.9 us (4%)
    ppermute x25, waiting for transfers between devices, swap(): return lax.ppermute(array, axis, [(i, i ^ flip) for i in range(count)])  59.2 us
    all_gather x1, waiting for transfers between devices, per_device(): exp_normed = lax.all_gather(normed, 'exp')  39.4 us
    unnamed x100, local copies, waits for them, and re-layouts  36.6 us
    pallas_call x1, Pallas kernels, expert_backward(): pl.pallas_call(functools.partial(backward_kernel, places, len(arrays)), g...  32.6 us
    pallas_call x4, Pallas kernels, expert_forward(): pl.pallas_call(functools.partial(forward_kernel, sources), grid_spec=pltp...  31.3 us
    ppermute x25, starting transfers between devices, swap(): return lax.ppermute(array, axis, [(i, i ^ flip) for i in range(count)])  21.9 us
    pallas_call x2, Pallas kernels, pick_norm(): pl.pallas_call(functools.partial(pick_norm_kernel, per_token, capacity, b...  18.2 us
    pallas_call x1, Pallas kernels, conv_back(): pl.pallas_call(functools.partial(conv_kernel, tile), grid_spec=pltpu.Pref...  12.6 us
  transfers between devices with their start and end apart: 34, of which 14 were waited for; matrix products, arithmetic and copies ran while one was open for 13% of the time, Pallas kernels for 31%

profile of v3, /device:TPU:1, one launch (start us, length us, event | category | flops | bytes accessed | tf_op | source)
XLA Modules:
  0.0 364.8 jit_solution(2132069040038863750)
XLA Ops:
  10.1 6.0 %all-to-all-start = ((f32[8,16,128]{2,1,0:T(8,128)}), f32[8,16,128]{2,1,0:T(8,128)S(1)}, u32[]{:S(2)}, u32[]{:S(2)}) async-start(f32[8,16,128]{2,1,0:T(8,128)} %broadcast_in_dim.4), calls=%async_computation | async-start | bytes 131072 | tf_op jit(solution)/shard_map/all_to_all | solution.py:526
  16.0 1.3 reshape.21.gain_ref
  17.3 2.2 norm_rows.1
  19.5 1.4 all-to-all-done.tables_ref
  22.6 3.1 collective-permute-start
  25.7 1.3 collective-permute-start.1
  27.7 1.3 collective-permute-start.2
  30.9 2.0 collective-permute-done.2.grad_high_ref
  33.5 12.6 %conv_back.1 = (bf16[1024,768]{1,0:T(8,128)(2,1)}, bf16[512,768]{1,0:T(8,128)(2,1)}, bf16[512,768]{1,0:T(8,128)(2,1)}) custom-call(s32[2]{0:T(128)} %pad_add_fusion.place_ref, bf16[1024,768]{1,0:T(8,128)(2,1)} %in_ref.1, bf16[16,768]{1,0:T(8,128)(2,1)} %copy-done.32, bf16[16,768]{1,0:T(8,128)(2,1)} %copy-done.33, bf16[1024,768]{1,0:T(8,128)(2,1)} %grad_ref.1, ...), custom_call_target="tpu_custom_call" | custom-call | flops 31457280 | bytes 6291456 | tf_op jit(solution)/shard_map/conv_back/pallas_call | solution.py:107
  46.1 1.5 collective-permute-start.3
  47.6 2.1 collective-permute-done.3.other_ref
  50.6 9.8 %project.1 = bf16[512,2304]{1,0:T(8,128)(2,1)} custom-call(s32[2]{0:T(128)} %pad_add_fusion.place_ref, bf16[512,768]{1,0:T(8,128)(2,1)} %get-tuple-element.64.own_ref, bf16[512,768]{1,0:T(8,128)(2,1)} %copy-done.36, bf16[768,2304]{1,0:T(8,128)(2,1)} %own_weight.1, bf16[768,2304]{1,0:T(8,128)(2,1)} %collective-permute-done.4.other_weight, ...), custom_call_target="tpu_custom_call" | custom-call | flops 3623878656 | bytes 11010048 | tf_op jit(solution)/shard_map/project/pallas_call | solution.py:157
  60.5 39.4 %all-gather.7.cloned.1.call-done = bf16[2048,2432]{1,0:T(8,128)(2,1)} async-done(((bf16[128,2432]{1,0:T(8,128)(2,1)}), bf16[2048,2432]{1,0:T(8,128)(2,1)}) %all-gather.7.cloned.1.call-update) | async-done | bytes 9961488 | tf_op jit(solution)/shard_map/all_gather | solution.py:529
  99.9 9.1 %pick_norm.2 = (bf16[2,8,16,2304]{3,2,1,0:T(8,128)(2,1)}, bf16[2,8,16,2304]{3,2,1,0:T(8,128)(2,1)}, bf16[2,8,16,2304]{3,2,1,0:T(8,128)(2,1)}, bf16[2,8,16,2304]{3,2,1,0:T(8,128)(2,1)}) custom-call(s32[2]{0:T(128)} %pad_add_fusion.place_ref, bf16[16,128,2432]{2,1,0:T(8,128)(2,1)} %bitcast.19), custom_call_target="tpu_custom_call" | custom-call | flops 603979776 | bytes 9437184 | tf_op jit(solution)/shard_map/pick_norm/pallas_call | solution.py:203
  109.7 9.1 %pick_norm.3 = (bf16[2,8,16,2304]{3,2,1,0:T(8,128)(2,1)}, bf16[2,8,16,2304]{3,2,1,0:T(8,128)(2,1)}, bf16[2,8,16,2304]{3,2,1,0:T(8,128)(2,1)}, bf16[2,8,16,2304]{3,2,1,0:T(8,128)(2,1)}) custom-call(s32[2]{0:T(128)} %pad_add_fusion.place_ref, bf16[16,128,2432]{2,1,0:T(8,128)(2,1)} %bitcast.20), custom_call_target="tpu_custom_call" | custom-call | flops 603979776 | bytes 9437184 | tf_op jit(solution)/shard_map/pick_norm/pallas_call | solution.py:203
  118.8 6.6 %all-reduce.2.cloned.1.call-done.refs_0_ = bf16[512,2304]{1,0:T(8,128)(2,1)} async-done(((bf16[512,2304]{1,0:T(8,128)(2,1)}), bf16[512,2304]{1,0:T(8,128)(2,1)}) %all-reduce.2.cloned.1.call-update) | async-done | bytes 2359312 | tf_op jit(solution)/shard_map/psum | solution.py:541
  126.3 5.8 %collective-permute-done.9 = bf16[2,8,16,2304]{3,2,1,0:T(8,128)(2,1)S(1)} collective-permute-done((bf16[2,8,16,2304]{3,2,1,0:T(8,128)(2,1)}, bf16[2,8,16,2304]{3,2,1,0:T(8,128)(2,1)S(1)}, u32[]{:S(2)}, u32[]{:S(2)}) %collective-permute-start.9) | collective-permute-done | bytes 1179680 | tf_op jit(solution)/shard_map/ppermute | solution.py:440
  132.1 2.9 pad_maximum_fusion.1
  136.4 8.2 %pick_grad.1 = (bf16[8,32,2304]{2,1,0:T(8,128)(2,1)}, bf16[8,32,2304]{2,1,0:T(8,128)(2,1)}, bf16[8,32,2304]{2,1,0:T(8,128)(2,1)}, bf16[8,32,2304]{2,1,0:T(8,128)...) custom-call(s32[2]{0:T(128)} %pad_add_fusion.place_ref, ...), custom_call_target="tpu_custom_call" | custom-call | flops 1207959552 | bytes 14155776 | tf_op jit(solution)/shard_map/pick_grad/pallas_call | solution.py:271
  144.7 2.8 collective-permute-start.17
  147.4 2.4 collective-permute-start.13
  149.9 1.6 pad_maximum_fusion
  154.2 19.4 %collective-permute-done.17.refs_16_ = bf16[8,32,2304]{2,1,0:T(8,128)(2,1)S(1)} collective-permute-done((bf16[8,32,2304]{2,1,0:T(8,128)(2,1)}, bf16[8,32,2304]{2,1,0:T(8,128)(2,1)S(1)}, u32[]{:S(2)}, u32[]{:S(2)}) %collective-permute-start.17) | collective-permute-done | bytes 1179680 | tf_op jit(solution)/shard_map/ppermute | solution.py:440
  173.7 1.2 pad_maximum_fusion.7
  175.0 1.3 collective-permute-start.18
  176.3 1.2 pad_maximum_fusion.6
  177.7 2.6 collective-permute-start.16
  180.4 1.3 pad_maximum_fusion.5
  183.2 1.7 collective-permute-start.12
  187.3 16.0 %collective-permute-done.8.refs_3_.refs_4_ = bf16[4,8,16,2304]{3,2,1,0:T(8,128)(2,1)S(1)} collective-permute-done((bf16[4,8,16,2304]{3,2,1,0:T(8,128)(2,1)}, bf16[4,8,16,2304]{3,2,1,0:T(8,128)(2,1)S(1)}, u32[]{:S(2)}, u32[]{:S(2)}) %collective-permute-start.8) | collective-permute-done | bytes 2359328 | tf_op jit(solution)/shard_map/ppermute | solution.py:440
  203.3 2.2 collective-permute-done.16.refs_12_
  205.5 2.6 collective-permute-done.14.refs_7_
  208.1 2.6 collective-permute-done.12.refs_2_
  210.7 1.7 slice.248
  212.5 1.6 slice_dynamic-update-slice_fusion.19
  214.0 1.6 slice_dynamic-update-slice_fusion.23
  215.6 1.7 slice.236
  217.3 1.7 slice.224
  219.0 1.6 slice_dynamic-update-slice_fusion.27
  220.6 1.6 slice_dynamic-update-slice_fusion.31
  222.2 1.7 slice.212
  223.9 2.3 constant_dynamic-slice_fusion.1
  226.2 1.7 pad_maximum_fusion.3
  229.3 1.7 pad_maximum_fusion.2
  232.8 1.9 collective-permute-start.26
  236.5 1.6 slice_dynamic-update-slice_fusion.21
  238.8 1.6 slice_dynamic-update-slice_fusion.17
  240.7 1.3 fusion.4
  245.1 1.6 slice_dynamic-update-slice_fusion.29
  247.5 1.3 collective-permute-start.20
  248.8 1.7 slice_dynamic-update-slice_fusion.16
  250.5 1.6 slice_dynamic-update-slice_fusion.25
  252.1 1.7 slice_dynamic-update-slice_fusion.24
  253.8 5.0 %collective-permute-done.26.refs_18_ = bf16[8,32,2304]{2,1,0:T(8,128)(2,1)S(1)} collective-permute-done((bf16[8,32,2304]{2,1,0:T(8,128)(2,1)S(1)}, bf16[8,32,2304]{2,1,0:T(8,128)(2,1)S(1)}, u32[]{:S(2)}, u32[]{:S(2)}) %collective-permute-start.26) | collective-permute-done | bytes 1179680 | tf_op jit(solution)/shard_map/ppermute | solution.py:440
  262.4 2.8 collective-permute-done.24.refs_13_
  275.1 1.3 collective-permute-start.21
  277.0 7.8 %expert_forward.4 = (bf16[2304,2048]{1,0:T(8,128)(2,1)}, bf16[512,2048]{1,0:T(8,128)(2,1)}, f32[2048,512]{1,0:T(8,128)}, f32[2048,512]{1,0:T(8,128)}) custom-call(s32[2]{0:T(128)} %pad_add_fusion.1.refs_0_, bf16[2,8,16,2304]{3,2,1,0:T(8,128)(2,1)} %get-tuple-element.63.refs_1_, bf16[2,8,16,2304]{3,2,1,0:T(8,128)(2,1)} %copy-done.5, ...), custom_call_target="tpu_custom_call" | custom-call | flops 2415919104 | bytes 7340032 | tf_op jit(solution)/shard_map/expert_forward/pallas_call | solution.py:331
  284.8 7.9 %expert_forward.5 = (bf16[2304,2048]{1,0:T(8,128)(2,1)}, bf16[512,2048]{1,0:T(8,128)(2,1)}, f32[2048,512]{1,0:T(8,128)}, f32[2048,512]{1,0:T(8,128)}) custom-call(s32[2]{0:T(128)} %pad_add_fusion.1.refs_0_, bf16[2,8,16,2304]{3,2,1,0:T(8,128)(2,1)} %get-tuple-element.84.refs_1_, ...), custom_call_target="tpu_custom_call", output_to_operand_aliasing={{0}: (6, {}), {1}: (7, {}), {2}: (8, {}), {3}: (9, {})} | custom-call | flops 2415919104 | bytes 7340032 | tf_op jit(solution)/shard_map/expert_forward/pallas_call | solution.py:331
  292.8 1.5 copy-done
  294.2 12.2 %all-to-all-start.1 = ((bf16[8,128,768]{2,1,0:T(8,128)(2,1)}), bf16[8,128,768]{2,1,0:T(8,128)(2,1)}, u32[]{:S(2)}, u32[]{:S(2)}) async-start(bf16[8,128,768]{2,1,0:T(8,128)(2,1)} %bitcast.21), calls=%async_computation.1 | async-start | bytes 3145728 | tf_op jit(solution)/shard_map/all_to_all | solution.py:581
  306.4 7.8 %expert_forward.6 = (bf16[2304,2048]{1,0:T(8,128)(2,1)}, bf16[512,2048]{1,0:T(8,128)(2,1)}, f32[2048,512]{1,0:T(8,128)}, f32[2048,512]{1,0:T(8,128)}) custom-call(s32[2]{0:T(128)} %pad_add_fusion.1.refs_0_, bf16[4,8,16,2304]{3,2,1,0:T(8,128)(2,1)} %copy-done, ...), custom_call_target="tpu_custom_call", output_to_operand_aliasing={{0}: (6, {}), {1}: (7, {}), {2}: (8, {}), {3}: (9, {})} | custom-call | flops 2415919104 | bytes 7340032 | tf_op jit(solution)/shard_map/expert_forward/pallas_call | solution.py:331
  314.2 7.8 %expert_forward.7 = (bf16[2304,2048]{1,0:T(8,128)(2,1)}, bf16[512,2048]{1,0:T(8,128)(2,1)}, f32[2048,512]{1,0:T(8,128)}, f32[2048,512]{1,0:T(8,128)}) custom-call(s32[2]{0:T(128)} %pad_add_fusion.1.refs_0_, ...), custom_call_target="tpu_custom_call", output_to_operand_aliasing={{0}: (6, {}), {1}: (7, {}), {2}: (8, {}), {3}: (9, {})} | custom-call | flops 2415919104 | bytes 7340032 | tf_op jit(solution)/shard_map/expert_forward/pallas_call | solution.py:331
  322.0 32.6 %expert_backward.1 = bf16[2304,1536]{1,0:T(8,128)(2,1)} custom-call(bf16[8,32,2304]{2,1,0:T(8,128)(2,1)} %get-tuple-element.88.refs_0_, bf16[8,32,2304]{2,1,0:T(8,128)(2,1)} %copy-done.15, bf16[8,32,2304]{2,1,0:T(8,128)(2,1)} %collective-permute-done.12.refs_2_, bf16[8,32,2304]{2,1,0:T(8,128)(2,1)} %copy-done.29, ...), custom_call_target="tpu_custom_call" | custom-call | flops 19327352832 | bytes 39845888 | tf_op jit(solution)/shard_map/expert_backward/pallas_call | solution.py:414
  354.6 2.7 copy.30
  (179 shorter events, 42.0 us)
Async XLA Ops:
  8.0 21.7 %copy-start.31 = (s32[16384]{0:T(1024)S(1)}, s32[16384]{0:T(1024)}, u32[]{:S(2)}) copy-start(s32[16384]{0:T(1024)} %param.14) | copy-start | bytes 196612
  10.1 10.8 %all-to-all-start = ((f32[8,16,128]{2,1,0:T(8,128)}), f32[8,16,128]{2,1,0:T(8,128)S(1)}, u32[]{:S(2)}, u32[]{:S(2)}) async-start(f32[8,16,128]{2,1,0:T(8,128)} %broadcast_in_dim.4), calls=%async_computation | async-start | bytes 131072 | tf_op jit(solution)/shard_map/all_to_all | solution.py:526
  16.0 83.9 %all-gather.7.cloned.1.call-start = ((), (), s32[]{:S(2)}) async-start(), calls=%async_computation.3 | async-start | bytes 10584064 | tf_op jit(solution)/shard_map/all_gather | solution.py:529
  20.9 25.2 %copy-start.30 = (f32[8,16,128]{2,1,0:T(8,128)}, f32[8,16,128]{2,1,0:T(8,128)S(1)}, u32[]{:S(2)}) copy-start(f32[8,16,128]{2,1,0:T(8,128)S(1)} %all-to-all-done.tables_ref) | copy-start | bytes 196612
  20.9 104.4 %all-reduce.2.cloned.1.call-start = ((), (), s32[]{:S(2)}) async-start(), calls=%async_computation.2 | async-start | bytes 4718592 | tf_op jit(solution)/shard_map/psum | solution.py:541
  21.0 28.8 %collective-permute-start.4 = (bf16[768,2304]{1,0:T(8,128)(2,1)}, bf16[768,2304]{1,0:T(8,128)(2,1)}, u32[]{:S(2)}, u32[]{:S(2)}) collective-permute-start(bf16[768,2304]{1,0:T(8,128)(2,1)} %own_weight.1), channel_id=1, source_target_pairs={{0,16},{16,0},{32,48},{48,32},{64,80},{80,64},{96,112},{112,96},{1... | collective-permute-start | bytes 10616840 | tf_op jit(solution)/shard_map/ppermute | solution.py:440
  22.6 8.3 %collective-permute-start = (bf16[16,768]{1,0:T(8,128)(2,1)S(1)}, bf16[16,768]{1,0:T(8,128)(2,1)S(1)}, u32[]{:S(2)}, u32[]{:S(2)}) collective-permute-start(bf16[16,768]{1,0:T(8,128)(2,1)S(1)} %get-tuple-element.123), channel_id=1, source_target_pairs={{0,1},{1,2},{2,3},{3,4},{4,5},{5,6},{6,7},{7,8},{8,9},{9,10},{10,1... | collective-permute-start | bytes 73736 | tf_op jit(solution)/shard_map/ppermute | solution.py:519
  25.7 5.2 %collective-permute-start.1 = (bf16[16,768]{1,0:T(8,128)(2,1)S(1)}, bf16[16,768]{1,0:T(8,128)(2,1)S(1)}, u32[]{:S(2)}, u32[]{:S(2)}) collective-permute-start(bf16[16,768]{1,0:T(8,128)(2,1)S(1)} %get-tuple-element.122), channel_id=1, source_target_pairs={{1,0},{2,1},{3,2},{4,3},{5,4},{6,5},{7,6},{8,7},{9,8},{10,9},{11,1... | collective-permute-start | bytes 73736 | tf_op jit(solution)/shard_map/ppermute | solution.py:520
  27.7 5.2 %collective-permute-start.2 = (bf16[16,768]{1,0:T(8,128)(2,1)S(1)}, bf16[16,768]{1,0:T(8,128)(2,1)S(1)}, u32[]{:S(2)}, u32[]{:S(2)}) collective-permute-start(bf16[16,768]{1,0:T(8,128)(2,1)S(1)} %slice.197), channel_id=1, source_target_pairs={{1,0},{2,1},{3,2},{4,3},{5,4},{6,5},{7,6},{8,7},{9,8},{10,9},{11,1... | collective-permute-start | bytes 73736 | tf_op jit(solution)/shard_map/ppermute | solution.py:521
  30.9 2.0 copy-start.32
  30.9 2.0 copy-start.33
  46.1 3.6 collective-permute-start.3
  60.4 150.3 %all-gather.9.cloned.1.call-start = ((), (), s32[]{:S(2)}) async-start(), calls=%async_computation.4 | async-start | bytes 7077888 | tf_op jit(solution)/shard_map/all_gather | solution.py:460
  109.0 16.4 %collective-permute-start.5 = (bf16[2,8,16,2304]{3,2,1,0:T(8,128)(2,1)}, bf16[2,8,16,2304]{3,2,1,0:T(8,128)(2,1)S(1)}, u32[]{:S(2)}, u32[]{:S(2)}) collective-permute-start(bf16[2,8,16,2304]{3,2,1,0:T(8,128)(2,1)} %get-tuple-element.66), channel_id=1, source_target_pairs={{0,16},{16,0},{32,48},{48,32},{64,80},{80,64},{96,112},{112,96},{1... | collective-permute-start | bytes 3538952 | tf_op jit(solution)/shard_map/ppermute | solution.py:440
  118.7 6.6 %collective-permute-start.6 = (bf16[2,8,16,2304]{3,2,1,0:T(8,128)(2,1)}, bf16[2,8,16,2304]{3,2,1,0:T(8,128)(2,1)S(1)}, u32[]{:S(2)}, u32[]{:S(2)}) collective-permute-start(bf16[2,8,16,2304]{3,2,1,0:T(8,128)(2,1)} %get-tuple-element.67), channel_id=1, source_target_pairs={{0,16},{16,0},{32,48},{48,32},{64,80},{80,64},{96,112},{112,96},{1... | collective-permute-start | bytes 3538952 | tf_op jit(solution)/shard_map/ppermute | solution.py:440
  125.3 9.7 %copy-start.5 = (bf16[2,8,16,2304]{3,2,1,0:T(8,128)(2,1)}, bf16[2,8,16,2304]{3,2,1,0:T(8,128)(2,1)S(1)}, u32[]{:S(2)}) copy-start(bf16[2,8,16,2304]{3,2,1,0:T(8,128)(2,1)S(1)} %collective-permute-done.5.refs_2_) | copy-start | bytes 3538948
  125.3 9.7 %copy-start.3 = (bf16[2,8,16,2304]{3,2,1,0:T(8,128)(2,1)}, bf16[2,8,16,2304]{3,2,1,0:T(8,128)(2,1)S(1)}, u32[]{:S(2)}) copy-start(bf16[2,8,16,2304]{3,2,1,0:T(8,128)(2,1)S(1)} %collective-permute-done.6.refs_2_) | copy-start | bytes 3538948
  125.3 11.1 %collective-permute-start.10 = (bf16[512,2304]{1,0:T(8,128)(2,1)}, bf16[512,2304]{1,0:T(8,128)(2,1)}, u32[]{:S(2)}, u32[]{:S(2)}) collective-permute-start(bf16[512,2304]{1,0:T(8,128)(2,1)} %all-reduce.2.cloned.1.call-done.refs_0_), channel_id=1, source_target_pairs={{0,16},{16,0},{32,48},{48,32},{64,80},{80,64},{96,112},{112,96},{1... | collective-permute-start | bytes 7077896 | tf_op jit(solution)/shard_map/ppermute | solution.py:440
  126.2 5.9 %collective-permute-start.9 = (bf16[2,8,16,2304]{3,2,1,0:T(8,128)(2,1)}, bf16[2,8,16,2304]{3,2,1,0:T(8,128)(2,1)S(1)}, u32[]{:S(2)}, u32[]{:S(2)}) collective-permute-start(bf16[2,8,16,2304]{3,2,1,0:T(8,128)(2,1)} %get-tuple-element.72), channel_id=1, source_target_pairs={{0,16},{16,0},{32,48},{48,32},{64,80},{80,64},{96,112},{112,96},{1... | collective-permute-start | bytes 3538952 | tf_op jit(solution)/shard_map/ppermute | solution.py:440
  135.0 157.7 %all-gather.11.cloned.1.call-start = ((), (), s32[]{:S(2)}) async-start(), calls=%async_computation.5 | async-start | bytes 7077888 | tf_op jit(solution)/shard_map/all_gather | solution.py:460
  136.3 13.6 %copy-start.21 = (bf16[2,8,16,2304]{3,2,1,0:T(8,128)(2,1)S(1)}, bf16[2,8,16,2304]{3,2,1,0:T(8,128)(2,1)}, u32[]{:S(2)}) copy-start(bf16[2,8,16,2304]{3,2,1,0:T(8,128)(2,1)} %get-tuple-element.69) | copy-start | bytes 3538948
  136.3 13.6 %collective-permute-start.7 = (bf16[2,8,16,2304]{3,2,1,0:T(8,128)(2,1)S(1)}, bf16[2,8,16,2304]{3,2,1,0:T(8,128)(2,1)S(1)}, u32[]{:S(2)}, u32[]{:S(2)}) collective-permute-start(bf16[2,8,16,2304]{3,2,1,0:T(8,128)(2,1)S(1)} %copy-done.35), channel_id=1, source_target_pairs={{0,16},{16,0},{32,48},{48,32},{64,80},{80,64},{96,112},{112,96},{1... | collective-permute-start | bytes 3538952 | tf_op jit(solution)/shard_map/ppermute | solution.py:440
  144.7 28.9 %collective-permute-start.17 = (bf16[8,32,2304]{2,1,0:T(8,128)(2,1)}, bf16[8,32,2304]{2,1,0:T(8,128)(2,1)S(1)}, u32[]{:S(2)}, u32[]{:S(2)}) collective-permute-start(bf16[8,32,2304]{2,1,0:T(8,128)(2,1)} %get-tuple-element.82), channel_id=1, source_target_pairs={{0,12},{1,13},{2,14},{3,15},{4,8},{5,9},{6,10},{7,11},{8,4},{9,5},... | collective-permute-start | bytes 3538952 | tf_op jit(solution)/shard_map/ppermute | solution.py:440
  147.4 28.9 %collective-permute-start.15 = (bf16[8,32,2304]{2,1,0:T(8,128)(2,1)}, bf16[8,32,2304]{2,1,0:T(8,128)(2,1)S(1)}, u32[]{:S(2)}, u32[]{:S(2)}) collective-permute-start(bf16[8,32,2304]{2,1,0:T(8,128)(2,1)} %get-tuple-element.80), channel_id=1, source_target_pairs={{0,4},{1,5},{2,6},{3,7},{4,0},{5,1},{6,2},{7,3},{8,12},{9,13},{10,... | collective-permute-start | bytes 3538952 | tf_op jit(solution)/shard_map/ppermute | solution.py:440
  147.4 32.9 %collective-permute-start.13 = (bf16[8,32,2304]{2,1,0:T(8,128)(2,1)}, bf16[8,32,2304]{2,1,0:T(8,128)(2,1)S(1)}, u32[]{:S(2)}, u32[]{:S(2)}) collective-permute-start(bf16[8,32,2304]{2,1,0:T(8,128)(2,1)} %get-tuple-element.78), channel_id=1, source_target_pairs={{0,3},{1,2},{2,1},{3,0},{4,7},{5,6},{6,5},{7,4},{8,11},{9,10},{10,... | collective-permute-start | bytes 3538952 | tf_op jit(solution)/shard_map/ppermute | solution.py:440
  149.9 32.0 %collective-permute-start.11 = (bf16[8,32,2304]{2,1,0:T(8,128)(2,1)}, bf16[8,32,2304]{2,1,0:T(8,128)(2,1)S(1)}, u32[]{:S(2)}, u32[]{:S(2)}) collective-permute-start(bf16[8,32,2304]{2,1,0:T(8,128)(2,1)} %get-tuple-element.76), channel_id=1, source_target_pairs={{0,1},{1,0},{2,3},{3,2},{4,5},{5,4},{6,7},{7,6},{8,9},{9,8},{10,11... | collective-permute-start | bytes 3538952 | tf_op jit(solution)/shard_map/ppermute | solution.py:440
  149.9 1.8 copy-start.25
  151.5 51.9 %collective-permute-start.8 = (bf16[4,8,16,2304]{3,2,1,0:T(8,128)(2,1)}, bf16[4,8,16,2304]{3,2,1,0:T(8,128)(2,1)S(1)}, u32[]{:S(2)}, u32[]{:S(2)}) collective-permute-start(bf16[4,8,16,2304]{3,2,1,0:T(8,128)(2,1)} %pad_maximum_fusion), channel_id=1, source_target_pairs={{0,32},{16,48},{32,0},{48,16},{64,96},{80,112},{96,64},{112,80},{1... | collective-permute-start | bytes 7077896 | tf_op jit(solution)/shard_map/ppermute | solution.py:440
  151.7 1.4 copy-start.23
  175.0 28.3 %collective-permute-start.18 = (bf16[8,32,2304]{2,1,0:T(8,128)(2,1)}, bf16[8,32,2304]{2,1,0:T(8,128)(2,1)}, u32[]{:S(2)}, u32[]{:S(2)}) collective-permute-start(bf16[8,32,2304]{2,1,0:T(8,128)(2,1)} %pad_maximum_fusion.7), channel_id=1, source_target_pairs={{0,1},{1,0},{2,3},{3,2},{4,5},{5,4},{6,7},{7,6},{8,9},{9,8},{10,11... | collective-permute-start | bytes 3538952 | tf_op jit(solution)/shard_map/ppermute | solution.py:440
  176.3 1.4 copy-start.13
  177.7 27.8 %collective-permute-start.16 = (bf16[8,32,2304]{2,1,0:T(8,128)(2,1)}, bf16[8,32,2304]{2,1,0:T(8,128)(2,1)}, u32[]{:S(2)}, u32[]{:S(2)}) collective-permute-start(bf16[8,32,2304]{2,1,0:T(8,128)(2,1)} %pad_maximum_fusion.6), channel_id=1, source_target_pairs={{0,12},{1,13},{2,14},{3,15},{4,8},{5,9},{6,10},{7,11},{8,4},{9,5},... | collective-permute-start | bytes 3538952 | tf_op jit(solution)/shard_map/ppermute | solution.py:440
  180.4 1.4 copy-start.19
  181.8 26.3 %collective-permute-start.14 = (bf16[8,32,2304]{2,1,0:T(8,128)(2,1)}, bf16[8,32,2304]{2,1,0:T(8,128)(2,1)}, u32[]{:S(2)}, u32[]{:S(2)}) collective-permute-start(bf16[8,32,2304]{2,1,0:T(8,128)(2,1)} %pad_maximum_fusion.5), channel_id=1, source_target_pairs={{0,4},{1,5},{2,6},{3,7},{4,0},{5,1},{6,2},{7,3},{8,12},{9,13},{10,... | collective-permute-start | bytes 3538952 | tf_op jit(solution)/shard_map/ppermute | solution.py:440
  181.9 3.1 copy-start.2
  183.2 27.5 %collective-permute-start.12 = (bf16[8,32,2304]{2,1,0:T(8,128)(2,1)}, bf16[8,32,2304]{2,1,0:T(8,128)(2,1)}, u32[]{:S(2)}, u32[]{:S(2)}) collective-permute-start(bf16[8,32,2304]{2,1,0:T(8,128)(2,1)} %pad_maximum_fusion.4), channel_id=1, source_target_pairs={{0,3},{1,2},{2,1},{3,0},{4,7},{5,6},{6,5},{7,4},{8,11},{9,10},{10,... | collective-permute-start | bytes 3538952 | tf_op jit(solution)/shard_map/ppermute | solution.py:440
  185.0 1.5 copy-start.4
  203.3 20.6 %copy-start.1 = (bf16[4,8,16,2304]{3,2,1,0:T(8,128)(2,1)}, bf16[4,8,16,2304]{3,2,1,0:T(8,128)(2,1)S(1)}, u32[]{:S(2)}) copy-start(bf16[4,8,16,2304]{3,2,1,0:T(8,128)(2,1)S(1)} %collective-permute-done.8.refs_3_.refs_4_) | copy-start | bytes 7077892
  223.9 2.3 slice-start
  223.9 2.3 copy-start.8
  231.0 1.6 copy-start.12
  231.0 1.6 slice-start.4
  231.0 61.7 %collective-permute-start.19 = (bf16[4,8,16,2304]{3,2,1,0:T(8,128)(2,1)}, bf16[4,8,16,2304]{3,2,1,0:T(8,128)(2,1)S(1)}, u32[]{:S(2)}, u32[]{:S(2)}) collective-permute-start(bf16[4,8,16,2304]{3,2,1,0:T(8,128)(2,1)} %pad_maximum_fusion.2), channel_id=1, source_target_pairs={{0,96},{16,112},{32,64},{48,80},{64,32},{80,48},{96,0},{112,16},{1... | collective-permute-start | bytes 7077896 | tf_op jit(solution)/shard_map/ppermute | solution.py:440
  232.6 2.1 copy-start.14
  232.8 5.4 %copy-start.18 = (bf16[8,32,2304]{2,1,0:T(8,128)(2,1)S(1)}, bf16[8,32,2304]{2,1,0:T(8,128)(2,1)}, u32[]{:S(2)}) copy-start(bf16[8,32,2304]{2,1,0:T(8,128)(2,1)} %copy-done.17) | copy-start | bytes 3538948
  232.8 26.0 %collective-permute-start.26 = (bf16[8,32,2304]{2,1,0:T(8,128)(2,1)S(1)}, bf16[8,32,2304]{2,1,0:T(8,128)(2,1)S(1)}, u32[]{:S(2)}, u32[]{:S(2)}) collective-permute-start(bf16[8,32,2304]{2,1,0:T(8,128)(2,1)S(1)} %pad_maximum_fusion.11), channel_id=1, source_target_pairs={{0,3},{1,2},{2,1},{3,0},{4,7},{5,6},{6,5},{7,4},{8,11},{9,10},{10,... | collective-permute-start | bytes 3538952 | tf_op jit(solution)/shard_map/ppermute | solution.py:440
  234.7 5.8 %copy-start.11 = (bf16[2,32,2304]{2,1,0:T(8,128)(2,1)S(1)}, bf16[2,32,2304]{2,1,0:T(8,128)(2,1)}, u32[]{:S(2)}) copy-start(bf16[2,32,2304]{2,1,0:T(8,128)(2,1)} %slice.236) | copy-start | bytes 884740
  234.7 5.8 %slice-start.2 = ((bf16[8,32,2304]{2,1,0:T(8,128)(2,1)}), bf16[2,32,2304]{2,1,0:T(8,128)(2,1)S(1)}, s32[]{:S(2)}) async-start(bf16[8,32,2304]{2,1,0:T(8,128)(2,1)} %copy-done.13), calls=%async_computation.8 | async-start | bytes 589824 | tf_op jit(solution)/shard_map/slice | solution.py:472
  240.6 24.7 %collective-permute-start.24 = (bf16[8,32,2304]{2,1,0:T(8,128)(2,1)S(1)}, bf16[8,32,2304]{2,1,0:T(8,128)(2,1)S(1)}, u32[]{:S(2)}, u32[]{:S(2)}) collective-permute-start(bf16[8,32,2304]{2,1,0:T(8,128)(2,1)S(1)} %pad_maximum_fusion.10), channel_id=1, source_target_pairs={{0,1},{1,0},{2,3},{3,2},{4,5},{5,4},{6,7},{7,6},{8,9},{9,8},{10,11... | collective-permute-start | bytes 3538952 | tf_op jit(solution)/shard_map/ppermute | solution.py:440
  242.1 4.6 %copy-start.20 = (bf16[8,32,2304]{2,1,0:T(8,128)(2,1)S(1)}, bf16[8,32,2304]{2,1,0:T(8,128)(2,1)}, u32[]{:S(2)}) copy-start(bf16[8,32,2304]{2,1,0:T(8,128)(2,1)} %copy-done.19) | copy-start | bytes 3538948
  242.2 26.8 %collective-permute-start.22 = (bf16[8,32,2304]{2,1,0:T(8,128)(2,1)S(1)}, bf16[8,32,2304]{2,1,0:T(8,128)(2,1)S(1)}, u32[]{:S(2)}, u32[]{:S(2)}) collective-permute-start(bf16[8,32,2304]{2,1,0:T(8,128)(2,1)S(1)} %pad_maximum_fusion.9), channel_id=1, source_target_pairs={{0,12},{1,13},{2,14},{3,15},{4,8},{5,9},{6,10},{7,11},{8,4},{9,5},... | collective-permute-start | bytes 3538952 | tf_op jit(solution)/shard_map/ppermute | solution.py:440
  243.4 4.0 %copy-start.9 = (bf16[2,32,2304]{2,1,0:T(8,128)(2,1)S(1)}, bf16[2,32,2304]{2,1,0:T(8,128)(2,1)}, u32[]{:S(2)}) copy-start(bf16[2,32,2304]{2,1,0:T(8,128)(2,1)} %slice.212) | copy-start | bytes 884740
  243.4 4.0 %slice-start.3 = ((bf16[8,32,2304]{2,1,0:T(8,128)(2,1)}), bf16[2,32,2304]{2,1,0:T(8,128)(2,1)S(1)}, s32[]{:S(2)}) async-start(bf16[8,32,2304]{2,1,0:T(8,128)(2,1)} %copy-done.15), calls=%async_computation.9 | async-start | bytes 589824 | tf_op jit(solution)/shard_map/slice | solution.py:472
  247.5 24.8 %collective-permute-start.20 = (bf16[8,32,2304]{2,1,0:T(8,128)(2,1)S(1)}, bf16[8,32,2304]{2,1,0:T(8,128)(2,1)S(1)}, u32[]{:S(2)}, u32[]{:S(2)}) collective-permute-start(bf16[8,32,2304]{2,1,0:T(8,128)(2,1)S(1)} %pad_maximum_fusion.8), channel_id=1, source_target_pairs={{0,4},{1,5},{2,6},{3,7},{4,0},{5,1},{6,2},{7,3},{8,12},{9,13},{10,... | collective-permute-start | bytes 3538952 | tf_op jit(solution)/shard_map/ppermute | solution.py:440
  258.8 9.2 %copy-start.26 = (bf16[8,32,2304]{2,1,0:T(8,128)(2,1)}, bf16[8,32,2304]{2,1,0:T(8,128)(2,1)S(1)}, u32[]{:S(2)}) copy-start(bf16[8,32,2304]{2,1,0:T(8,128)(2,1)S(1)} %collective-permute-done.26.refs_18_) | copy-start | bytes 3538948
  261.5 60.5 %collective-permute-start.27 = (bf16[8,32,2304]{2,1,0:T(8,128)(2,1)}, bf16[8,32,2304]{2,1,0:T(8,128)(2,1)}, u32[]{:S(2)}, u32[]{:S(2)}) collective-permute-start(bf16[8,32,2304]{2,1,0:T(8,128)(2,1)} %slice_dynamic-update-slice_fusion), channel_id=1, source_target_pairs={{0,4},{1,5},{2,6},{3,7},{4,0},{5,1},{6,2},{7,3},{8,12},{9,13},{10,... | collective-permute-start | bytes 3538952 | tf_op jit(solution)/shard_map/ppermute | solution.py:440
  265.3 6.4 %copy-start.27 = (bf16[8,32,2304]{2,1,0:T(8,128)(2,1)}, bf16[8,32,2304]{2,1,0:T(8,128)(2,1)S(1)}, u32[]{:S(2)}) copy-start(bf16[8,32,2304]{2,1,0:T(8,128)(2,1)S(1)} %collective-permute-done.24.refs_13_) | copy-start | bytes 3538948
  268.0 54.0 %collective-permute-start.25 = (bf16[8,32,2304]{2,1,0:T(8,128)(2,1)}, bf16[8,32,2304]{2,1,0:T(8,128)(2,1)}, u32[]{:S(2)}, u32[]{:S(2)}) collective-permute-start(bf16[8,32,2304]{2,1,0:T(8,128)(2,1)} %slice_dynamic-update-slice_fusion.4), channel_id=1, source_target_pairs={{0,3},{1,2},{2,1},{3,0},{4,7},{5,6},{6,5},{7,4},{8,11},{9,10},{10,... | collective-permute-start | bytes 3538952 | tf_op jit(solution)/shard_map/ppermute | solution.py:440
  269.0 6.1 %copy-start.28 = (bf16[8,32,2304]{2,1,0:T(8,128)(2,1)}, bf16[8,32,2304]{2,1,0:T(8,128)(2,1)S(1)}, u32[]{:S(2)}) copy-start(bf16[8,32,2304]{2,1,0:T(8,128)(2,1)S(1)} %collective-permute-done.22.refs_8_) | copy-start | bytes 3538948
  271.7 50.3 %collective-permute-start.23 = (bf16[8,32,2304]{2,1,0:T(8,128)(2,1)}, bf16[8,32,2304]{2,1,0:T(8,128)(2,1)}, u32[]{:S(2)}, u32[]{:S(2)}) collective-permute-start(bf16[8,32,2304]{2,1,0:T(8,128)(2,1)} %slice_dynamic-update-slice_fusion.8), channel_id=1, source_target_pairs={{0,1},{1,0},{2,3},{3,2},{4,5},{5,4},{6,7},{7,6},{8,9},{9,8},{10,11... | collective-permute-start | bytes 3538952 | tf_op jit(solution)/shard_map/ppermute | solution.py:440
  272.3 12.5 %copy-start.29 = (bf16[8,32,2304]{2,1,0:T(8,128)(2,1)}, bf16[8,32,2304]{2,1,0:T(8,128)(2,1)S(1)}, u32[]{:S(2)}) copy-start(bf16[8,32,2304]{2,1,0:T(8,128)(2,1)S(1)} %collective-permute-done.20.refs_3_) | copy-start | bytes 3538948
  275.1 47.0 %collective-permute-start.21 = (bf16[8,32,2304]{2,1,0:T(8,128)(2,1)}, bf16[8,32,2304]{2,1,0:T(8,128)(2,1)}, u32[]{:S(2)}, u32[]{:S(2)}) collective-permute-start(bf16[8,32,2304]{2,1,0:T(8,128)(2,1)} %slice_dynamic-update-slice_fusion.12), channel_id=1, source_target_pairs={{0,12},{1,13},{2,14},{3,15},{4,8},{5,9},{6,10},{7,11},{8,4},{9,5},... | collective-permute-start | bytes 3538952 | tf_op jit(solution)/shard_map/ppermute | solution.py:440
  292.7 1.5 copy-start
  294.2 60.4 %all-to-all-start.1 = ((bf16[8,128,768]{2,1,0:T(8,128)(2,1)}), bf16[8,128,768]{2,1,0:T(8,128)(2,1)}, u32[]{:S(2)}, u32[]{:S(2)}) async-start(bf16[8,128,768]{2,1,0:T(8,128)(2,1)} %bitcast.21), calls=%async_computation.1 | async-start | bytes 3145728 | tf_op jit(solution)/shard_map/all_to_all | solution.py:581
  (13 other events, 16.1 us)
Sparse Core Ops, SparseCore 0:
  21.0 78.8 all-gather.6
  135.2 65.7 all-gather.8
Sparse Core Ops, SparseCore 1:
  60.5 64.8 all-reduce.1
  228.0 64.0 all-gather.10

commit v4 on v3

--- a/solution.py
+++ b/solution.py
@@ -183,39 +183,55 @@
     return picker, match
 
 
-def pick_norm_kernel(per_token, capacity, n_exp, turns, place_ref, rows_ref, *out_refs):
-    tokens = rows_ref.shape[1]
-    dim = out_refs[0].shape[3]
-    names = rows_ref[0, :HALO, dim:].astype(F32)[:per_token].astype(jnp.int32)
-    own = jnp.concatenate(
-        [jnp.full((1, tokens), (place_ref[0] ^ t) * n_exp + place_ref[1], jnp.int32) for t in turns]
+def pick_norm_kernel(per_token, capacity, n_exp, turns, place_ref, *refs):
+    halves = len(turns)
+    out_refs = refs[halves:]
+    outs = len(out_refs) // halves
+    for half in range(halves):
+        rows_ref = refs[half]
+        tokens = rows_ref.shape[1]
+        dim = out_refs[0].shape[3]
+        count = len(turns[half])
+        names = rows_ref[0, :HALO, dim:].astype(F32)[:per_token].astype(jnp.int32)
+        own = jnp.concatenate(
+            [
+                jnp.full((1, tokens), (place_ref[0] ^ t) * n_exp + place_ref[1], jnp.int32)
+                for t in turns[half]
+            ]
+        )
+        picker, _ = slot_picker(names, own, capacity)
+        picker = picker.reshape(count * capacity, tokens).astype(BF16)
+        picked = jnp.dot(picker, rows_ref[0, :, :dim], preferred_element_type=F32).astype(BF16)
+        for index in range(count):
+            out_refs[half * outs + index // 2][index % 2, 0] = picked[
+                index * capacity : (index + 1) * capacity
+            ]
+
+
+def pick_norm(place, rows, turns, dim, per_token, capacity):
+    blocks, tokens, width = rows.shape
+    halves = len(turns)
+    count = blocks // halves
+    outs = len(turns[0]) // 2 * halves
+    row_spec = lambda first: pl.BlockSpec(
+        (1, tokens, width), lambda i, p: (p[1] ^ (i + first), 0, 0)
     )
-    picker, _ = slot_picker(names, own, capacity)
-    picker = picker.reshape(len(turns) * capacity, tokens).astype(BF16)
-    picked = jnp.dot(picker, rows_ref[0, :, :dim], preferred_element_type=F32).astype(BF16)
-    for index in range(len(turns)):
-        out_refs[index // 2][index % 2, 0] = picked[index * capacity : (index + 1) * capacity]
-
-
-def pick_norm(place, rows, turns, first, count, dim, per_token, capacity):
-    blocks, tokens, width = rows.shape
-    outs = len(turns) // 2
     return pl.pallas_call(
         functools.partial(pick_norm_kernel, per_token, capacity, blocks, turns),
         grid_spec=pltpu.PrefetchScalarGridSpec(
             num_scalar_prefetch=1,
             grid=(count,),
-            in_specs=[pl.BlockSpec((1, tokens, width), lambda i, p: (p[1] ^ (i + first), 0, 0))],
+            in_specs=[row_spec(half * count) for half in range(halves)],
             out_specs=[pl.BlockSpec((2, 1, capacity, dim), lambda i, p: (0, i, 0, 0))] * outs,
         ),
         out_shape=[jax.ShapeDtypeStruct((2, count, capacity, dim), BF16)] * outs,
         compiler_params=pltpu.CompilerParams(vmem_limit_bytes=VMEM_LIMIT),
         cost_estimate=call_cost(
-            2 * len(turns) * capacity * count * tokens * dim,
-            2 * dim * count * (tokens + len(turns) * capacity),
+            2 * len(turns[0]) * capacity * blocks * tokens * dim,
+            2 * dim * blocks * (tokens + len(turns[0]) * capacity),
         ),
         name="pick_norm",
-    )(place, rows)
+    )(place, *[rows] * halves)
 
 
 def pick_grad_kernel(per_token, capacity, n_exp, turns, place_ref, tables_ref, *refs):
@@ -405,7 +421,7 @@
 def expert_backward(arrays, places, gate, up, weights, rows, act):
     dim, total = rows.shape
     hidden = act.shape[0]
-    tile, width = 256, 256
+    tile, width = 512, 768
     row_steps, column_steps = total // tile, dim // width
     row_spec = lambda cols: pl.BlockSpec(
         (tile, cols), lambda i: (jnp.minimum(i, row_steps - 1), 0)
@@ -435,6 +451,52 @@
     )(*arrays, gate, up, weights, rows, act)
 
 
+def merge_kernel(parts, arrays, shift_ref, *refs):
+    out_ref, sems = refs[arrays], refs[arrays + 1]
+    copies = []
+    for at, (array, unit, shift) in enumerate(parts):
+        source = refs[array]
+        first = unit if shift is None else unit + shift_ref[shift]
+        half = source.shape[1] // 2
+        for piece in range(2):
+            rows = pl.ds(piece * half, half)
+            copies.append(
+                pltpu.make_async_copy(
+                    source.at[first, rows], out_ref.at[at, rows], sems.at[2 * at + piece]
+                )
+            )
+    for copy in copies:
+        copy.start()
+    for copy in copies:
+        copy.wait()
+
+
+def merge(shifts, parts):
+    arrays, list_of = [], []
+    for array, units, shift in parts:
+        known = [i for i, other in enumerate(arrays) if other is array]
+        if not known:
+            arrays.append(array)
+            known = [len(arrays) - 1]
+        list_of += [(known[0], unit, shift) for unit in units]
+    shape = (len(list_of),) + arrays[0].shape[1:]
+    size = functools.reduce(lambda a, b: a * b, shape, 1)
+    return pl.pallas_call(
+        functools.partial(merge_kernel, tuple(list_of), len(arrays)),
+        grid_spec=pltpu.PrefetchScalarGridSpec(
+            num_scalar_prefetch=1,
+            grid=(1,),
+            in_specs=[pl.BlockSpec(memory_space=pl.ANY)] * len(arrays),
+            out_specs=pl.BlockSpec(shape, lambda i, s: (0,) * len(shape)),
+            scratch_shapes=[pltpu.SemaphoreType.DMA((2 * len(list_of),))],
+        ),
+        out_shape=jax.ShapeDtypeStruct(shape, BF16),
+        compiler_params=pltpu.CompilerParams(vmem_limit_bytes=VMEM_LIMIT),
+        cost_estimate=call_cost(0, 4 * size),
+        name="merge_rows",
+    )(shifts, *arrays)
+
+
 def swap(array, axis, flip):
     count = lax.axis_size(axis)
     return lax.ppermute(array, axis, [(i, i ^ flip) for i in range(count)])
@@ -446,12 +508,6 @@
 
 def flips_of(half):
     return (1, 3) if half == 0 else (3, 1)
-
-
-def sibling_rows(picks):
-    keep, send, keep_far, send_far = picks
-    send_got, keep_got = swap(send_far, "seq", 1), swap(keep_far, "seq", 1)
-    return keep, keep_got, jnp.concatenate([send, send_got])
 
 
 def swap_gather(array, axis, flip):
@@ -461,23 +517,17 @@
     return both.reshape((-1,) + array.shape[1:])
 
 
-def exchange_grads(flips, keep, send):
-    first = swap(send, "exp", flips[0])
-    second = swap(jnp.concatenate([keep[4:8], first[4:8]]), "exp", flips[1])
-    return keep, first, second
-
-
-def finish_grads(flips, keep, first, second):
-    third = swap(
-        jnp.concatenate([keep[2:4], first[2:4], second[2:4], second[6:8]]), "exp", flips[2]
-    )
-    odd = lambda a: [a[i : i + 1] for i in (1, 3, 5, 7)]
-    fourth = swap(
-        jnp.concatenate([keep[1:2], first[1:2], second[1:2], second[5:6]] + odd(third)),
-        "exp",
-        flips[3],
-    )
-    arrays = [keep, first, second, third, fourth]
+def third_message(shifts, keep, first, second):
+    parts = [(keep, (2, 3)), (first, (2, 3)), (second, (2, 3)), (second, (6, 7))]
+    return merge(shifts, [(array, units, None) for array, units in parts])
+
+
+def fourth_message(shifts, keep, first, second, third):
+    parts = [(keep, (1,)), (first, (1,)), (second, (1, 5)), (third, (1, 3, 5, 7))]
+    return merge(shifts, [(array, units, None) for array, units in parts])
+
+
+def grad_places(flips):
     found = {}
     found[0, 0, 0, 0] = (0, 0)
     found[1, 0, 0, 0] = (1, 0)
@@ -487,7 +537,7 @@
         found[start + (1, 0)] = (3, 2 * index)
         found[start + (0, 1)] = (4, index)
         found[start + (1, 1)] = (4, 4 + index)
-    return arrays, {mask_of(flips, bits): at for bits, at in found.items()}
+    return {mask_of(flips, bits): at for bits, at in found.items()}
 
 
 def per_device(
@@ -525,7 +575,7 @@
     tables = jnp.broadcast_to(table[None], (n_seq,) + table.shape)
     tables = lax.all_to_all(tables, "seq", split_axis=0, concat_axis=0, tiled=True)
     normed = norm_rows(resid, norm_gain, routes.T)
-    normed, tables, conv_weight = lax.optimization_barrier((normed, tables, conv_weight))
+    normed, conv_weight = lax.optimization_barrier((normed, conv_weight))
     exp_normed = lax.all_gather(normed, "exp")
 
     edge = jnp.full((HALO,), -1, jnp.int32)
@@ -535,22 +585,33 @@
     local_grad, local_keep, local_send = conv_back(
         place, qkv_in, low, high, qkv_grad, grad_high, ids.reshape(-1, 1), conv_weight, tokens
     )
+    local_send, tables = lax.optimization_barrier((local_send, tables))
     local_got = swap(local_send, "seq", 1)
     partial = project(place, local_keep, local_got, qkv_weight, weight_far, out_grad)
     same_core = [[s for s in range(n_seq) if s % 2 == core] for core in range(2)]
     flow = lax.psum(partial, "seq", axis_index_groups=same_core)
 
-    halves = []
-    for half in range(2):
-        flips = flips_of(half)
-        near = (0, flips[1], flips[0], flips[0] ^ flips[1])
-        turns = tuple(2 * m for m in near) + tuple(2 * m + 1 for m in near)
-        picks = pick_norm(
-            place, exp_normed, turns, half * n_exp // 2, n_exp // 2, dim, per_token, capacity
-        )
-        halves.append(sibling_rows(picks))
-    (keep_a, far_a, message_a), (keep_b, far_b, message_b) = halves
-    flow, far_a, far_b = lax.optimization_barrier((flow, far_a, far_b))
+    flips_a, flips_b = flips_of(0), flips_of(1)
+    shifts = [(seq_index < seq_index ^ 2 * f).astype(jnp.int32) * 4 for f in flips_b]
+    shifts = jnp.stack(shifts)
+    turns = []
+    for near in (flips_a, flips_b):
+        near = (0, near[1], near[0], near[0] ^ near[1])
+        turns.append(tuple(2 * m for m in near) + tuple(2 * m + 1 for m in near))
+    picks = pick_norm(place, exp_normed, tuple(turns), dim, per_token, capacity)
+    (keep_a, send_a, keep_far_a, send_far_a) = picks[:4]
+    (keep_b, send_b, keep_far_b, send_far_b) = picks[4:]
+    got_a, got_b = swap(send_far_a, "seq", 1), swap(send_far_b, "seq", 1)
+    message_a = merge(shifts, [(send_a, (0, 1), None), (got_a, (0, 1), None)])
+    message_a, got_b = lax.optimization_barrier((message_a, got_b))
+    first_a = swap(message_a, "seq", 2 * flips_a[0])
+    message_b = merge(shifts, [(send_b, (0, 1), None), (got_b, (0, 1), None)])
+    far_a, far_b = swap(keep_far_a, "seq", 1), swap(keep_far_b, "seq", 1)
+    flow, far_a, far_b, message_b, local_grad = lax.optimization_barrier(
+        (flow, far_a, far_b, message_b, local_grad)
+    )
+    first_b = swap_gather(message_b, "seq", 2 * flips_b[0])
+    qkv_in_grad = lax.all_to_all(local_grad, "seq", split_axis=0, concat_axis=1, tiled=True)
     flow_far = swap(flow, "seq", 1)
 
     flips = (1, 3, 4, 12)
@@ -560,36 +621,39 @@
     turns = tuple(tuple(mask_of(order, bits) for bits in bit_rows) for order in orders)
     sends = pick_grad(place, tables, (flow, flow_far), turns, n_exp, per_token, capacity)
 
-    flips_a, flips_b = flips_of(0), flips_of(1)
-    shifts = [(seq_index < seq_index ^ 2 * f).astype(jnp.int32) * 4 for f in flips_b]
-    first_a = swap(message_a, "seq", 2 * flips_a[0])
-    first_b = swap_gather(message_b, "seq", 2 * flips_b[0])
-    states = [
-        exchange_grads(orders[k], sends[2 * k], sends[2 * k + 1]) for k in range(quarters)
+    firsts = [swap(sends[2 * k + 1], "exp", orders[k][0]) for k in range(quarters)]
+    seconds = [
+        swap(
+            merge(shifts, [(sends[2 * k], range(4, 8), None), (firsts[k], range(4, 8), None)]),
+            "exp",
+            orders[k][1],
+        )
+        for k in range(quarters)
     ]
-    first_a, first_b, states = lax.optimization_barrier((first_a, first_b, states))
-    piece = lambda i: lax.dynamic_slice_in_dim(first_b, shifts[0] + i, 1, 0)
-    second_a = swap(
-        jnp.concatenate([keep_a[1:], far_a[1:], first_a[1:2], first_a[3:4]]),
-        "seq",
-        2 * flips_a[1],
+    first_a, first_b, firsts = lax.optimization_barrier((first_a, first_b, firsts))
+    message_a = merge(
+        shifts, [(keep_a, (1,), None), (far_a, (1,), None), (first_a, (1, 3), None)]
     )
-    second_b = swap_gather(
-        jnp.concatenate([keep_b[1:], far_b[1:], piece(1), piece(3)]), "seq", 2 * flips_b[1]
-    )
-    local_grad, second_a, second_b = lax.optimization_barrier((local_grad, second_a, second_b))
-    qkv_in_grad = lax.all_to_all(local_grad, "seq", split_axis=0, concat_axis=1, tiled=True)
+    message_b = merge(shifts, [(keep_b, (1,), None), (far_b, (1,), None), (first_b, (1, 3), 0)])
+    second_a = swap(message_a, "seq", 2 * flips_a[1])
+    second_b = swap_gather(message_b, "seq", 2 * flips_b[1])
     calls = [
         [(keep_a, 0, None), (far_a, 0, None), (first_a, 0, None), (first_a, 2, None)],
         [(keep_b, 0, None), (far_b, 0, None), (first_b, 0, 0), (first_b, 2, 0)],
         [(second_a, i, None) for i in range(4)],
         [(second_b, i, 1) for i in range(4)],
     ]
+    thirds = []
+    for k in range(quarters):
+        message = third_message(shifts, sends[2 * k], firsts[k], seconds[k])
+        thirds.append(swap(message, "exp", orders[k][2]))
     results = ()
     for part, pieces in enumerate(calls):
         results = expert_forward(
-            pieces, own_weights, hidden, jnp.stack(shifts), len(calls), part, results
+            pieces, own_weights, hidden, shifts, len(calls), part, results
         )
+        if part == 1:
+            results, thirds = lax.optimization_barrier((results, thirds))
     rows_all, act, gate, up = results
 
     def row_of(mask, quarter):
@@ -603,8 +667,10 @@
 
     arrays, places = [], []
     for k in range(quarters):
-        got, found = finish_grads(orders[k], *states[k])
-        for mask, (array, unit) in sorted(found.items()):
+        got = [sends[2 * k], firsts[k], seconds[k], thirds[k]]
+        message = fourth_message(shifts, *got)
+        got.append(swap(message, "exp", orders[k][3]))
+        for mask, (array, unit) in sorted(grad_places(orders[k]).items()):
             places.append((len(arrays) + array, unit, row_of(mask, k), 2 * capacity))
         arrays += got
     expert_grads = expert_backward(arrays, tuple(places), gate, up, own_weights, rows_all, act)

time: 367 us -> 351 us (0.956)
  local copies, waits for them, and re-layouts: 63.5 us -> 14.3 us
  Pallas kernels: 115 us -> 159 us
  other arithmetic: 16 us -> 1.17 us
    pallas_call x0 -> x16, Pallas kernels: none -> 53.3 us  [merge(): pl.pallas_call(functools.partial(merge_kernel, tuple(list_of), len(arrays...]
    unnamed x100 -> x34, local copies, waits for them, and re-layouts: 36.6 us -> 6.96 us
    slice x30 -> x0, local copies, waits for them, and re-layouts: 14.5 us -> none  [the longest x4 6.81 us: finish_grads(): keep[2:4]]
    concatenate x12 -> x0, other arithmetic: 13.3 us -> none  [the longest x4 4.84 us: exchange_grads(): second = swap(jnp.concatenate([keep[4:8], first[4:8]]), 'exp', flips[1])]
    all_gather x2, waiting for transfers between devices: 0.03 us -> 12.2 us  [swap_gather(): both = lax.all_gather(array, axis, axis_index_groups=groups)]
    pallas_call x2 -> x1, Pallas kernels: 18.2 us -> 12.2 us  [pick_norm(): pl.pallas_call(functools.partial(pick_norm_kernel, per_token, capacity, b...]
    all_to_all x1, starting transfers between devices: 12.2 us -> 6.67 us  [per_device(): lax.all_to_all(local_grad, 'seq', split_axis=0, concat_axis=1, tiled=True)]
    ppermute x25, starting transfers between devices: 21.9 us -> 26.1 us  [swap(): return lax.ppermute(array, axis, [(i, i ^ flip) for i in range(count)])]
  transfers between devices with their start and end apart: 34 -> 34, of which waited for: 14 -> 11; matrix products, arithmetic and copies ran while one was open for 13% -> 2% of each run, Pallas kernels for 31% -> 36%
where the time goes in v4:
time: 351 us; the launch traced here: 346 us
  Pallas kernels  159 us (45%)
  waiting for transfers between devices  112 us (32%)
  starting transfers between devices  43.4 us (12%)
  between operations  16.1 us (5%)
  local copies, waits for them, and re-layouts  14.3 us (4%)
    ppermute x25, waiting for transfers between devices, swap(): return lax.ppermute(array, axis, [(i, i ^ flip) for i in range(count)])  57.1 us
    pallas_call x16, Pallas kernels, merge(): pl.pallas_call(functools.partial(merge_kernel, tuple(list_of), len(arrays...  53.3 us
    all_gather x1, waiting for transfers between devices, per_device(): exp_normed = lax.all_gather(normed, 'exp')  39 us
    pallas_call x4, Pallas kernels, expert_forward(): pl.pallas_call(functools.partial(forward_kernel, sources), grid_spec=pltp...  31.4 us
    pallas_call x1, Pallas kernels, expert_backward(): pl.pallas_call(functools.partial(backward_kernel, places, len(arrays)), g...  29.6 us
    ppermute x25, starting transfers between devices, swap(): return lax.ppermute(array, axis, [(i, i ^ flip) for i in range(count)])  26.1 us
    pallas_call x1, Pallas kernels, conv_back(): pl.pallas_call(functools.partial(conv_kernel, tile), grid_spec=pltpu.Pref...  12.6 us
    pallas_call x1, Pallas kernels, pick_norm(): pl.pallas_call(functools.partial(pick_norm_kernel, per_token, capacity, b...  12.2 us
  transfers between devices with their start and end apart: 34, of which 11 were waited for; matrix products, arithmetic and copies ran while one was open for 2% of the time, Pallas kernels for 36%

profile of v4, /device:TPU:1, one launch (start us, length us, event | category | flops | bytes accessed | tf_op | source)
XLA Modules:
  0.0 345.7 jit_solution(4047218336941788491)
XLA Ops:
  8.1 1.3 reshape.21.gain_ref
  9.4 2.2 norm_rows.1
  11.6 1.5 collective-permute-start.4
  13.1 0.8 fusion
  13.8 3.2 collective-permute-start
  17.0 1.3 collective-permute-start.1
  19.1 1.3 collective-permute-start.2
  21.0 4.8 %all-to-all-start = ((f32[8,16,128]{2,1,0:T(8,128)}), f32[8,16,128]{2,1,0:T(8,128)S(1)}, u32[]{:S(2)}, u32[]{:S(2)}) async-start(f32[8,16,128]{2,1,0:T(8,128)} %broadcast_in_dim.4), calls=%async_computation | async-start | bytes 131072 | tf_op jit(solution)/shard_map/all_to_all | solution.py:576
  26.6 1.0 reshape.29.ids_ref
  28.8 12.6 %conv_back.1 = (bf16[1024,768]{1,0:T(8,128)(2,1)}, bf16[512,768]{1,0:T(8,128)(2,1)}, bf16[512,768]{1,0:T(8,128)(2,1)}) custom-call(s32[2]{0:T(128)} %pad_add_fusion.place_ref, bf16[1024,768]{1,0:T(8,128)(2,1)} %in_ref.1, bf16[16,768]{1,0:T(8,128)(2,1)} %copy-done.10, bf16[16,768]{1,0:T(8,128)(2,1)} %copy-done.11, bf16[1024,768]{1,0:T(8,128)(2,1)} %grad_ref.1, ...), custom_call_target="tpu_custom_call" | custom-call | flops 31457280 | bytes 6291456 | tf_op jit(solution)/shard_map/conv_back/pallas_call | solution.py:107
  41.5 2.5 collective-permute-done.3.other_ref
  44.0 0.9 copy-done.16
  44.9 9.2 %project.1 = bf16[512,2304]{1,0:T(8,128)(2,1)} custom-call(s32[2]{0:T(128)} %pad_add_fusion.place_ref, bf16[512,768]{1,0:T(8,128)(2,1)} %get-tuple-element.63.own_ref, bf16[512,768]{1,0:T(8,128)(2,1)} %copy-done.16, bf16[768,2304]{1,0:T(8,128)(2,1)} %own_weight.1, bf16[768,2304]{1,0:T(8,128)(2,1)} %collective-permute-done.4.other_weight, ...), custom_call_target="tpu_custom_call" | custom-call | flops 3623878656 | bytes 11010048 | tf_op jit(solution)/shard_map/project/pallas_call | solution.py:157
  54.1 39.0 %all-gather.7.cloned.1.call-done = bf16[2048,2432]{1,0:T(8,128)(2,1)} async-done(((bf16[128,2432]{1,0:T(8,128)(2,1)}), bf16[2048,2432]{1,0:T(8,128)(2,1)}) %all-gather.7.cloned.1.call-update) | async-done | bytes 9961488 | tf_op jit(solution)/shard_map/all_gather | solution.py:579
  93.1 12.2 %pick_norm.1 = (bf16[2,8,16,2304]{3,2,1,0:T(8,128)(2,1)}, bf16[2,8,16,2304]{3,2,1,0:T(8,128)(2,1)}, bf16[2,8,16,2304]{3,2,1,0:T(8,128)(2,1)}, bf16[2,8,16,2304]{...) custom-call(s32[2]{0:T(128)} %pad_add_fusion.place_ref, ...), custom_call_target="tpu_custom_call" | custom-call | flops 1207959552 | bytes 18874368 | tf_op jit(solution)/shard_map/pick_norm/pallas_call | solution.py:219
  107.2 2.4 collective-permute-done.7.refs_1_
  109.6 3.8 %merge_rows.16 = bf16[4,8,16,2304]{3,2,1,0:T(8,128)(2,1)} custom-call(s32[2]{0:T(128)} %pad_add_fusion.1.shift_ref.refs_0_, bf16[2,8,16,2304]{3,2,1,0:T(8,128)(2,1)} %get-tuple-element.70.refs_0_, bf16[2,8,16,2304]{3,2,1,0:T(8,128)(2,1)} %collective-permute-done.7.refs_1_), custom_call_target="tpu_custom_call" | custom-call | bytes 4718592 | tf_op jit(solution)/shard_map/merge_rows/pallas_call | solution.py:484
  113.4 1.0 copy-done.6
  114.4 3.8 %merge_rows.17 = bf16[4,8,16,2304]{3,2,1,0:T(8,128)(2,1)} custom-call(s32[2]{0:T(128)} %pad_add_fusion.1.shift_ref.refs_0_, bf16[2,8,16,2304]{3,2,1,0:T(8,128)(2,1)} %get-tuple-element.69.refs_0_, bf16[2,8,16,2304]{3,2,1,0:T(8,128)(2,1)} %copy-done.6), custom_call_target="tpu_custom_call" | custom-call | bytes 4718592 | tf_op jit(solution)/shard_map/merge_rows/pallas_call | solution.py:484
  118.2 3.5 %all-reduce.2.cloned.1.call-done.refs_0_ = bf16[512,2304]{1,0:T(8,128)(2,1)} async-done(((bf16[512,2304]{1,0:T(8,128)(2,1)}), bf16[512,2304]{1,0:T(8,128)(2,1)}) %all-reduce.2.cloned.1.call-update) | async-done | bytes 2359312 | tf_op jit(solution)/shard_map/psum | solution.py:592
  121.7 1.1 copy-done.4
  123.1 0.8 collective-permute-start.9
  123.9 4.5 %collective-permute-done.9.refs_1_ = bf16[512,2304]{1,0:T(8,128)(2,1)} collective-permute-done((bf16[512,2304]{1,0:T(8,128)(2,1)}, bf16[512,2304]{1,0:T(8,128)(2,1)}, u32[]{:S(2)}, u32[]{:S(2)}) %collective-permute-start.9) | collective-permute-done | bytes 2359328 | tf_op jit(solution)/shard_map/ppermute | solution.py:502
  128.4 8.4 %pick_grad.1 = (bf16[8,32,2304]{2,1,0:T(8,128)(2,1)}, bf16[8,32,2304]{2,1,0:T(8,128)(2,1)}, bf16[8,32,2304]{2,1,0:T(8,128)(2,1)}, bf16[8,32,2304]{2,1,0:T(8,128)...) custom-call(s32[2]{0:T(128)} %pad_add_fusion.place_ref, ...), custom_call_target="tpu_custom_call" | custom-call | flops 1207959552 | bytes 14155776 | tf_op jit(solution)/shard_map/pick_grad/pallas_call | solution.py:287
  136.8 1.3 collective-permute-start.11
  138.1 1.8 collective-permute-start.12
  139.9 1.3 collective-permute-start.13
  141.2 1.9 collective-permute-start.14
  143.0 34.0 %collective-permute-done.10.refs_3_.refs_4_.refs_2_ = bf16[4,8,16,2304]{3,2,1,0:T(8,128)(2,1)S(1)} collective-permute-done((bf16[4,8,16,2304]{3,2,1,0:T(8,128)(2,1)}, bf16[4,8,16,2304]{3,2,1,0:T(8,128)(2,1)S(1)}, u32[]{:S(2)}, u32[]{:S(2)}) %collective-permute-start.10) | collective-permute-done | bytes 2359328 | tf_op jit(solution)/shard_map/ppermute | solution.py:502
  177.1 12.2 %all-gather.9.cloned.1.call-done.refs_3_.refs_4_.refs_2_ = bf16[8,8,16,2304]{3,2,1,0:T(8,128)(2,1)} async-done(((bf16[4,8,16,2304]{3,2,1,0:T(8,128)(2,1)}), bf16[8,8,16,2304]{3,2,1,0:T(8,128)(2,1)}) %all-gather.9.cloned.1.call-update) | async-done | bytes 4718608 | tf_op jit(solution)/shard_map/all_gather | solution.py:516
  189.3 3.7 %merge_rows.30 = bf16[4,8,16,2304]{3,2,1,0:T(8,128)(2,1)} custom-call(s32[2]{0:T(128)} %pad_add_fusion.1.shift_ref.refs_0_, bf16[2,8,16,2304]{3,2,1,0:T(8,128)(2,1)} %get-tuple-element.86.refs_1_.refs_0_, bf16[2,8,16,2304]{3,2,1,0:T(8,128)(2,1)} %copy-done.3, bf16[8,8,16,2304]{3,2,1,0:T(8,128)(2,1)} %all-gather.9.cloned.1.call-done.refs_3_.refs_4_.refs_2_), custom_call_target="tpu_custom_call" | custom-call | bytes 4718592 | tf_op jit(solution)/shard_map/merge_rows/pallas_call | solution.py:484
  193.1 3.2 merge_rows.18
  196.2 2.5 collective-permute-start.15
  198.7 3.1 merge_rows.20
  201.9 1.4 collective-permute-start.17
  203.2 3.4 merge_rows.22
  206.6 2.0 collective-permute-start.19
  208.6 3.1 merge_rows.24
  211.9 3.8 %merge_rows.31 = bf16[4,8,16,2304]{3,2,1,0:T(8,128)(2,1)} custom-call(s32[2]{0:T(128)} %pad_add_fusion.1.shift_ref.refs_0_, bf16[2,8,16,2304]{3,2,1,0:T(8,128)(2,1)} %get-tuple-element.89.refs_1_.refs_0_, bf16[2,8,16,2304]{3,2,1,0:T(8,128)(2,1)} %copy-done.4, bf16[4,8,16,2304]{3,2,1,0:T(8,128)(2,1)} %copy-done.1), custom_call_target="tpu_custom_call" | custom-call | bytes 4718592 | tf_op jit(solution)/shard_map/merge_rows/pallas_call | solution.py:484
  216.2 8.4 %collective-permute-done.15.refs_2_ = bf16[8,32,2304]{2,1,0:T(8,128)(2,1)S(1)} collective-permute-done((bf16[8,32,2304]{2,1,0:T(8,128)(2,1)}, bf16[8,32,2304]{2,1,0:T(8,128)(2,1)S(1)}, u32[]{:S(2)}, u32[]{:S(2)}) %collective-permute-start.15) | collective-permute-done | bytes 1179680 | tf_op jit(solution)/shard_map/ppermute | solution.py:502
  224.6 1.1 copy-done.5
  225.6 3.1 merge_rows.19
  228.8 1.2 collective-permute-start.16
  230.0 3.2 merge_rows.21
  233.2 2.0 collective-permute-start.18
  235.2 3.2 merge_rows.23
  238.5 3.2 merge_rows.25
  241.7 2.4 collective-permute-start.22
  244.1 6.7 %all-to-all-start.1 = ((bf16[8,128,768]{2,1,0:T(8,128)(2,1)}), bf16[8,128,768]{2,1,0:T(8,128)(2,1)}, u32[]{:S(2)}, u32[]{:S(2)}) async-start(bf16[8,128,768]{2,1,0:T(8,128)(2,1)} %bitcast.21), calls=%async_computation.1 | async-start | bytes 3145728 | tf_op jit(solution)/shard_map/all_to_all | solution.py:614
  250.8 7.7 %expert_forward.4 = (bf16[2304,2048]{1,0:T(8,128)(2,1)}, bf16[512,2048]{1,0:T(8,128)(2,1)}, f32[2048,512]{1,0:T(8,128)}, f32[2048,512]{1,0:T(8,128)}) custom-call(s32[2]{0:T(128)} %pad_add_fusion.1.shift_ref.refs_0_, bf16[2,8,16,2304]{3,2,1,0:T(8,128)(2,1)} %get-tuple-element.89.refs_1_.refs_0_, bf16[2,8,16,2304]{3,2,1,0:T(8,128)(2,1)} %copy-done.4, ...), custom_call_target="tpu_custom_call" | custom-call | flops 2415919104 | bytes 7340032 | tf_op jit(solution)/shard_map/expert_forward/pallas_call | solution.py:347
  258.5 7.9 %expert_forward.5 = (bf16[2304,2048]{1,0:T(8,128)(2,1)}, bf16[512,2048]{1,0:T(8,128)(2,1)}, f32[2048,512]{1,0:T(8,128)}, f32[2048,512]{1,0:T(8,128)}) custom-call(s32[2]{0:T(128)} %pad_add_fusion.1.shift_ref.refs_0_, ...), custom_call_target="tpu_custom_call", output_to_operand_aliasing={{0}: (6, {}), {1}: (7, {}), {2}: (8, {}), {3}: (9, {})} | custom-call | flops 2415919104 | bytes 7340032 | tf_op jit(solution)/shard_map/expert_forward/pallas_call | solution.py:347
  266.5 1.9 collective-permute-done.22.refs_3_.refs_18_
  268.4 3.1 merge_rows.26
  271.5 1.1 collective-permute-start.23
  272.6 3.2 merge_rows.27
  276.0 3.2 merge_rows.28
  279.2 2.2 collective-permute-start.25
  281.4 3.2 merge_rows.29
  285.3 2.7 copy.30
  288.0 1.4 copy-done
  289.4 7.9 %expert_forward.6 = (bf16[2304,2048]{1,0:T(8,128)(2,1)}, bf16[512,2048]{1,0:T(8,128)(2,1)}, f32[2048,512]{1,0:T(8,128)}, f32[2048,512]{1,0:T(8,128)}) custom-call(s32[2]{0:T(128)} %pad_add_fusion.1.shift_ref.refs_0_, bf16[4,8,16,2304]{3,2,1,0:T(8,128)(2,1)} %copy-done, ...), custom_call_target="tpu_custom_call", output_to_operand_aliasing={{0}: (6, {}), {1}: (7, {}), {2}: (8, {}), {3}: (9, {})} | custom-call | flops 2415919104 | bytes 7340032 | tf_op jit(solution)/shard_map/expert_forward/pallas_call | solution.py:347
  297.3 7.8 %expert_forward.7 = (bf16[2304,2048]{1,0:T(8,128)(2,1)}, bf16[512,2048]{1,0:T(8,128)(2,1)}, f32[2048,512]{1,0:T(8,128)}, f32[2048,512]{1,0:T(8,128)}) custom-call(s32[2]{0:T(128)} %pad_add_fusion.1.shift_ref.refs_0_, ...), custom_call_target="tpu_custom_call", output_to_operand_aliasing={{0}: (6, {}), {1}: (7, {}), {2}: (8, {}), {3}: (9, {})} | custom-call | flops 2415919104 | bytes 7340032 | tf_op jit(solution)/shard_map/expert_forward/pallas_call | solution.py:347
  305.2 3.4 collective-permute-done.26.refs_19_
  308.5 29.6 %expert_backward.1 = bf16[2304,1536]{1,0:T(8,128)(2,1)} custom-call(bf16[8,32,2304]{2,1,0:T(8,128)(2,1)} %get-tuple-element.78.refs_0_, bf16[8,32,2304]{2,1,0:T(8,128)(2,1)} %copy-done.2, bf16[8,32,2304]{2,1,0:T(8,128)(2,1)} %copy-done.5, bf16[8,32,2304]{2,1,0:T(8,128)(2,1)} %copy-done.7, bf16[8,32,2304]{2,1,0:T(8,128)(2,1)} %copy-done.15, ...), custom_call_target="tpu_custom_call" | custom-call | flops 19327352832 | bytes 39845888 | tf_op jit(solution)/shard_map/expert_backward/pallas_call | solution.py:430
  (81 shorter events, 7.6 us)
Async XLA Ops:
  8.0 12.4 %copy-start.13 = (s32[128,8]{0,1:T(8,128)S(1)}, s32[128,8]{0,1:T(8,128)}, u32[]{:S(2)}) copy-start(s32[128,8]{0,1:T(8,128)} %param.19) | copy-start | bytes 12292
  8.0 12.4 %copy-start.14 = (f32[128,8]{0,1:T(8,128)S(1)}, f32[128,8]{0,1:T(8,128)}, u32[]{:S(2)}) copy-start(f32[128,8]{0,1:T(8,128)} %param.20) | copy-start | bytes 12292
  8.0 18.3 %copy-start.9 = (s32[16384]{0:T(1024)S(1)}, s32[16384]{0:T(1024)}, u32[]{:S(2)}) copy-start(s32[16384]{0:T(1024)} %param.14) | copy-start | bytes 196612
  8.0 85.1 %all-gather.7.cloned.1.call-start = ((), (), s32[]{:S(2)}) async-start(), calls=%async_computation.3 | async-start | bytes 10584064 | tf_op jit(solution)/shard_map/all_gather | solution.py:579
  11.6 32.4 %collective-permute-start.4 = (bf16[768,2304]{1,0:T(8,128)(2,1)}, bf16[768,2304]{1,0:T(8,128)(2,1)}, u32[]{:S(2)}, u32[]{:S(2)}) collective-permute-start(bf16[768,2304]{1,0:T(8,128)(2,1)} %own_weight.1), channel_id=1, source_target_pairs={{0,16},{16,0},{32,48},{48,32},{64,80},{80,64},{96,112},{112,96},{1... | collective-permute-start | bytes 10616840 | tf_op jit(solution)/shard_map/ppermute | solution.py:502
  13.8 13.7 %collective-permute-start = (bf16[16,768]{1,0:T(8,128)(2,1)S(1)}, bf16[16,768]{1,0:T(8,128)(2,1)S(1)}, u32[]{:S(2)}, u32[]{:S(2)}) collective-permute-start(bf16[16,768]{1,0:T(8,128)(2,1)S(1)} %get-tuple-element.123), channel_id=1, source_target_pairs={{0,1},{1,2},{2,3},{3,4},{4,5},{5,6},{6,7},{7,8},{8,9},{9,10},{10,1... | collective-permute-start | bytes 73736 | tf_op jit(solution)/shard_map/ppermute | solution.py:569
  17.0 10.6 %collective-permute-start.1 = (bf16[16,768]{1,0:T(8,128)(2,1)S(1)}, bf16[16,768]{1,0:T(8,128)(2,1)S(1)}, u32[]{:S(2)}, u32[]{:S(2)}) collective-permute-start(bf16[16,768]{1,0:T(8,128)(2,1)S(1)} %get-tuple-element.122), channel_id=1, source_target_pairs={{1,0},{2,1},{3,2},{4,3},{5,4},{6,5},{7,6},{8,7},{9,8},{10,9},{11,1... | collective-permute-start | bytes 73736 | tf_op jit(solution)/shard_map/ppermute | solution.py:570
  19.1 8.5 %collective-permute-start.2 = (bf16[16,768]{1,0:T(8,128)(2,1)S(1)}, bf16[16,768]{1,0:T(8,128)(2,1)S(1)}, u32[]{:S(2)}, u32[]{:S(2)}) collective-permute-start(bf16[16,768]{1,0:T(8,128)(2,1)S(1)} %slice.11), channel_id=1, source_target_pairs={{1,0},{2,1},{3,2},{4,3},{5,4},{6,5},{7,6},{8,7},{9,8},{10,9},{11,1... | collective-permute-start | bytes 73736 | tf_op jit(solution)/shard_map/ppermute | solution.py:571
  21.0 20.4 %all-to-all-start = ((f32[8,16,128]{2,1,0:T(8,128)}), f32[8,16,128]{2,1,0:T(8,128)S(1)}, u32[]{:S(2)}, u32[]{:S(2)}) async-start(f32[8,16,128]{2,1,0:T(8,128)} %broadcast_in_dim.4), calls=%async_computation | async-start | bytes 131072 | tf_op jit(solution)/shard_map/all_to_all | solution.py:576
  25.8 95.9 %all-reduce.2.cloned.1.call-start = ((), (), s32[]{:S(2)}) async-start(), calls=%async_computation.2 | async-start | bytes 4718592 | tf_op jit(solution)/shard_map/psum | solution.py:592
  27.6 0.6 copy-start.10
  27.6 0.6 copy-start.11
  28.2 0.6 copy-start.12
  41.4 12.7 %copy-start.8 = (f32[8,16,128]{2,1,0:T(8,128)}, f32[8,16,128]{2,1,0:T(8,128)S(1)}, u32[]{:S(2)}) copy-start(f32[8,16,128]{2,1,0:T(8,128)S(1)} %all-to-all-done.tables_ref) | copy-start | bytes 196612
  41.4 2.6 collective-permute-start.3
  44.0 0.9 copy-start.16
  54.1 135.2 %all-gather.9.cloned.1.call-start = ((), (), s32[]{:S(2)}) async-start(), calls=%async_computation.4 | async-start | bytes 7077888 | tf_op jit(solution)/shard_map/all_gather | solution.py:516
  105.3 4.3 %collective-permute-start.7 = (bf16[2,8,16,2304]{3,2,1,0:T(8,128)(2,1)}, bf16[2,8,16,2304]{3,2,1,0:T(8,128)(2,1)}, u32[]{:S(2)}, u32[]{:S(2)}) collective-permute-start(bf16[2,8,16,2304]{3,2,1,0:T(8,128)(2,1)} %get-tuple-element.71), channel_id=1, source_target_pairs={{0,16},{16,0},{32,48},{48,32},{64,80},{80,64},{96,112},{112,96},{1... | collective-permute-start | bytes 3538952 | tf_op jit(solution)/shard_map/ppermute | solution.py:502
  106.0 7.4 %collective-permute-start.8 = (bf16[2,8,16,2304]{3,2,1,0:T(8,128)(2,1)}, bf16[2,8,16,2304]{3,2,1,0:T(8,128)(2,1)S(1)}, u32[]{:S(2)}, u32[]{:S(2)}) collective-permute-start(bf16[2,8,16,2304]{3,2,1,0:T(8,128)(2,1)} %get-tuple-element.72), channel_id=1, source_target_pairs={{0,16},{16,0},{32,48},{48,32},{64,80},{80,64},{96,112},{112,96},{1... | collective-permute-start | bytes 3538952 | tf_op jit(solution)/shard_map/ppermute | solution.py:502
  106.1 15.5 %collective-permute-start.5 = (bf16[2,8,16,2304]{3,2,1,0:T(8,128)(2,1)}, bf16[2,8,16,2304]{3,2,1,0:T(8,128)(2,1)S(1)}, u32[]{:S(2)}, u32[]{:S(2)}) collective-permute-start(bf16[2,8,16,2304]{3,2,1,0:T(8,128)(2,1)} %get-tuple-element.67), channel_id=1, source_target_pairs={{0,16},{16,0},{32,48},{48,32},{64,80},{80,64},{96,112},{112,96},{1... | collective-permute-start | bytes 3538952 | tf_op jit(solution)/shard_map/ppermute | solution.py:502
  106.6 15.1 %collective-permute-start.6 = (bf16[2,8,16,2304]{3,2,1,0:T(8,128)(2,1)}, bf16[2,8,16,2304]{3,2,1,0:T(8,128)(2,1)S(1)}, u32[]{:S(2)}, u32[]{:S(2)}) collective-permute-start(bf16[2,8,16,2304]{3,2,1,0:T(8,128)(2,1)} %get-tuple-element.68), channel_id=1, source_target_pairs={{0,16},{16,0},{32,48},{48,32},{64,80},{80,64},{96,112},{112,96},{1... | collective-permute-start | bytes 3538952 | tf_op jit(solution)/shard_map/ppermute | solution.py:502
  113.4 1.0 copy-start.6
  121.7 1.1 copy-start.4
  121.7 1.4 copy-start.3
  123.1 174.2 %all-gather.11.cloned.1.call-start = ((), (), s32[]{:S(2)}) async-start(), calls=%async_computation.5 | async-start | bytes 7077888 | tf_op jit(solution)/shard_map/all_gather | solution.py:516
  123.1 5.3 %collective-permute-start.9 = (bf16[512,2304]{1,0:T(8,128)(2,1)}, bf16[512,2304]{1,0:T(8,128)(2,1)}, u32[]{:S(2)}, u32[]{:S(2)}) collective-permute-start(bf16[512,2304]{1,0:T(8,128)(2,1)} %all-reduce.2.cloned.1.call-done.refs_0_), channel_id=1, source_target_pairs={{0,16},{16,0},{32,48},{48,32},{64,80},{80,64},{96,112},{112,96},{1... | collective-permute-start | bytes 7077896 | tf_op jit(solution)/shard_map/ppermute | solution.py:502
  123.9 53.2 %collective-permute-start.10 = (bf16[4,8,16,2304]{3,2,1,0:T(8,128)(2,1)}, bf16[4,8,16,2304]{3,2,1,0:T(8,128)(2,1)S(1)}, u32[]{:S(2)}, u32[]{:S(2)}) collective-permute-start(bf16[4,8,16,2304]{3,2,1,0:T(8,128)(2,1)} %merge_rows.16), channel_id=1, source_target_pairs={{0,32},{16,48},{32,0},{48,16},{64,96},{80,112},{96,64},{112,80},{1... | collective-permute-start | bytes 7077896 | tf_op jit(solution)/shard_map/ppermute | solution.py:502
  136.8 40.3 %collective-permute-start.11 = (bf16[8,32,2304]{2,1,0:T(8,128)(2,1)}, bf16[8,32,2304]{2,1,0:T(8,128)(2,1)S(1)}, u32[]{:S(2)}, u32[]{:S(2)}) collective-permute-start(bf16[8,32,2304]{2,1,0:T(8,128)(2,1)} %get-tuple-element.81), channel_id=1, source_target_pairs={{0,1},{1,0},{2,3},{3,2},{4,5},{5,4},{6,7},{7,6},{8,9},{9,8},{10,11... | collective-permute-start | bytes 3538952 | tf_op jit(solution)/shard_map/ppermute | solution.py:502
  138.1 39.0 %collective-permute-start.12 = (bf16[8,32,2304]{2,1,0:T(8,128)(2,1)}, bf16[8,32,2304]{2,1,0:T(8,128)(2,1)}, u32[]{:S(2)}, u32[]{:S(2)}) collective-permute-start(bf16[8,32,2304]{2,1,0:T(8,128)(2,1)} %get-tuple-element.82), channel_id=1, source_target_pairs={{0,3},{1,2},{2,1},{3,0},{4,7},{5,6},{6,5},{7,4},{8,11},{9,10},{10,... | collective-permute-start | bytes 3538952 | tf_op jit(solution)/shard_map/ppermute | solution.py:502
  139.9 37.2 %collective-permute-start.13 = (bf16[8,32,2304]{2,1,0:T(8,128)(2,1)}, bf16[8,32,2304]{2,1,0:T(8,128)(2,1)}, u32[]{:S(2)}, u32[]{:S(2)}) collective-permute-start(bf16[8,32,2304]{2,1,0:T(8,128)(2,1)} %get-tuple-element.83), channel_id=1, source_target_pairs={{0,4},{1,5},{2,6},{3,7},{4,0},{5,1},{6,2},{7,3},{8,12},{9,13},{10,... | collective-permute-start | bytes 3538952 | tf_op jit(solution)/shard_map/ppermute | solution.py:502
  141.2 35.9 %collective-permute-start.14 = (bf16[8,32,2304]{2,1,0:T(8,128)(2,1)}, bf16[8,32,2304]{2,1,0:T(8,128)(2,1)}, u32[]{:S(2)}, u32[]{:S(2)}) collective-permute-start(bf16[8,32,2304]{2,1,0:T(8,128)(2,1)} %get-tuple-element.84), channel_id=1, source_target_pairs={{0,12},{1,13},{2,14},{3,15},{4,8},{5,9},{6,10},{7,11},{8,4},{9,5},... | collective-permute-start | bytes 3538952 | tf_op jit(solution)/shard_map/ppermute | solution.py:502
  177.1 15.9 %copy-start.1 = (bf16[4,8,16,2304]{3,2,1,0:T(8,128)(2,1)}, bf16[4,8,16,2304]{3,2,1,0:T(8,128)(2,1)S(1)}, u32[]{:S(2)}) copy-start(bf16[4,8,16,2304]{3,2,1,0:T(8,128)(2,1)S(1)} %collective-permute-done.10.refs_3_.refs_4_.refs_2_) | copy-start | bytes 7077892
  177.1 15.9 %copy-start.2 = (bf16[8,32,2304]{2,1,0:T(8,128)(2,1)}, bf16[8,32,2304]{2,1,0:T(8,128)(2,1)S(1)}, u32[]{:S(2)}) copy-start(bf16[8,32,2304]{2,1,0:T(8,128)(2,1)S(1)} %collective-permute-done.11.refs_1_) | copy-start | bytes 3538948
  196.2 28.3 %collective-permute-start.15 = (bf16[8,32,2304]{2,1,0:T(8,128)(2,1)}, bf16[8,32,2304]{2,1,0:T(8,128)(2,1)S(1)}, u32[]{:S(2)}, u32[]{:S(2)}) collective-permute-start(bf16[8,32,2304]{2,1,0:T(8,128)(2,1)} %merge_rows.18), channel_id=1, source_target_pairs={{0,3},{1,2},{2,1},{3,0},{4,7},{5,6},{6,5},{7,4},{8,11},{9,10},{10,... | collective-permute-start | bytes 3538952 | tf_op jit(solution)/shard_map/ppermute | solution.py:502
  201.9 28.2 %collective-permute-start.17 = (bf16[8,32,2304]{2,1,0:T(8,128)(2,1)}, bf16[8,32,2304]{2,1,0:T(8,128)(2,1)}, u32[]{:S(2)}, u32[]{:S(2)}) collective-permute-start(bf16[8,32,2304]{2,1,0:T(8,128)(2,1)} %merge_rows.20), channel_id=1, source_target_pairs={{0,4},{1,5},{2,6},{3,7},{4,0},{5,1},{6,2},{7,3},{8,12},{9,13},{10,... | collective-permute-start | bytes 3538952 | tf_op jit(solution)/shard_map/ppermute | solution.py:502
  206.6 28.6 %collective-permute-start.19 = (bf16[8,32,2304]{2,1,0:T(8,128)(2,1)}, bf16[8,32,2304]{2,1,0:T(8,128)(2,1)}, u32[]{:S(2)}, u32[]{:S(2)}) collective-permute-start(bf16[8,32,2304]{2,1,0:T(8,128)(2,1)} %merge_rows.22), channel_id=1, source_target_pairs={{0,12},{1,13},{2,14},{3,15},{4,8},{5,9},{6,10},{7,11},{8,4},{9,5},... | collective-permute-start | bytes 3538952 | tf_op jit(solution)/shard_map/ppermute | solution.py:502
  211.8 26.7 %collective-permute-start.21 = (bf16[8,32,2304]{2,1,0:T(8,128)(2,1)}, bf16[8,32,2304]{2,1,0:T(8,128)(2,1)}, u32[]{:S(2)}, u32[]{:S(2)}) collective-permute-start(bf16[8,32,2304]{2,1,0:T(8,128)(2,1)} %merge_rows.24), channel_id=1, source_target_pairs={{0,1},{1,0},{2,3},{3,2},{4,5},{5,4},{6,7},{7,6},{8,9},{9,8},{10,11... | collective-permute-start | bytes 3538952 | tf_op jit(solution)/shard_map/ppermute | solution.py:502
  215.8 72.2 %collective-permute-start.27 = (bf16[4,8,16,2304]{3,2,1,0:T(8,128)(2,1)}, bf16[4,8,16,2304]{3,2,1,0:T(8,128)(2,1)S(1)}, u32[]{:S(2)}, u32[]{:S(2)}) collective-permute-start(bf16[4,8,16,2304]{3,2,1,0:T(8,128)(2,1)} %merge_rows.31), channel_id=1, source_target_pairs={{0,96},{16,112},{32,64},{48,80},{64,32},{80,48},{96,0},{112,16},{1... | collective-permute-start | bytes 7077896 | tf_op jit(solution)/shard_map/ppermute | solution.py:502
  224.6 1.1 copy-start.5
  228.8 37.7 %collective-permute-start.16 = (bf16[8,32,2304]{2,1,0:T(8,128)(2,1)}, bf16[8,32,2304]{2,1,0:T(8,128)(2,1)S(1)}, u32[]{:S(2)}, u32[]{:S(2)}) collective-permute-start(bf16[8,32,2304]{2,1,0:T(8,128)(2,1)} %merge_rows.19), channel_id=1, source_target_pairs={{0,4},{1,5},{2,6},{3,7},{4,0},{5,1},{6,2},{7,3},{8,12},{9,13},{10,... | collective-permute-start | bytes 3538952 | tf_op jit(solution)/shard_map/ppermute | solution.py:502
  233.2 33.3 %collective-permute-start.18 = (bf16[8,32,2304]{2,1,0:T(8,128)(2,1)}, bf16[8,32,2304]{2,1,0:T(8,128)(2,1)}, u32[]{:S(2)}, u32[]{:S(2)}) collective-permute-start(bf16[8,32,2304]{2,1,0:T(8,128)(2,1)} %merge_rows.21), channel_id=1, source_target_pairs={{0,12},{1,13},{2,14},{3,15},{4,8},{5,9},{6,10},{7,11},{8,4},{9,5},... | collective-permute-start | bytes 3538952 | tf_op jit(solution)/shard_map/ppermute | solution.py:502
  238.3 28.1 %collective-permute-start.20 = (bf16[8,32,2304]{2,1,0:T(8,128)(2,1)}, bf16[8,32,2304]{2,1,0:T(8,128)(2,1)}, u32[]{:S(2)}, u32[]{:S(2)}) collective-permute-start(bf16[8,32,2304]{2,1,0:T(8,128)(2,1)} %merge_rows.23), channel_id=1, source_target_pairs={{0,1},{1,0},{2,3},{3,2},{4,5},{5,4},{6,7},{7,6},{8,9},{9,8},{10,11... | collective-permute-start | bytes 3538952 | tf_op jit(solution)/shard_map/ppermute | solution.py:502
  241.7 26.7 %collective-permute-start.22 = (bf16[8,32,2304]{2,1,0:T(8,128)(2,1)}, bf16[8,32,2304]{2,1,0:T(8,128)(2,1)}, u32[]{:S(2)}, u32[]{:S(2)}) collective-permute-start(bf16[8,32,2304]{2,1,0:T(8,128)(2,1)} %merge_rows.25), channel_id=1, source_target_pairs={{0,3},{1,2},{2,1},{3,0},{4,7},{5,6},{6,5},{7,4},{8,11},{9,10},{10,... | collective-permute-start | bytes 3538952 | tf_op jit(solution)/shard_map/ppermute | solution.py:502
  244.1 41.2 %all-to-all-start.1 = ((bf16[8,128,768]{2,1,0:T(8,128)(2,1)}), bf16[8,128,768]{2,1,0:T(8,128)(2,1)}, u32[]{:S(2)}, u32[]{:S(2)}) async-start(bf16[8,128,768]{2,1,0:T(8,128)(2,1)} %bitcast.21), calls=%async_computation.1 | async-start | bytes 3145728 | tf_op jit(solution)/shard_map/all_to_all | solution.py:614
  266.5 1.9 copy-start.7
  271.5 33.6 %collective-permute-start.23 = (bf16[8,32,2304]{2,1,0:T(8,128)(2,1)}, bf16[8,32,2304]{2,1,0:T(8,128)(2,1)S(1)}, u32[]{:S(2)}, u32[]{:S(2)}) collective-permute-start(bf16[8,32,2304]{2,1,0:T(8,128)(2,1)} %merge_rows.26), channel_id=1, source_target_pairs={{0,12},{1,13},{2,14},{3,15},{4,8},{5,9},{6,10},{7,11},{8,4},{9,5},... | collective-permute-start | bytes 3538952 | tf_op jit(solution)/shard_map/ppermute | solution.py:502
  275.7 29.4 %collective-permute-start.24 = (bf16[8,32,2304]{2,1,0:T(8,128)(2,1)}, bf16[8,32,2304]{2,1,0:T(8,128)(2,1)}, u32[]{:S(2)}, u32[]{:S(2)}) collective-permute-start(bf16[8,32,2304]{2,1,0:T(8,128)(2,1)} %merge_rows.27), channel_id=1, source_target_pairs={{0,1},{1,0},{2,3},{3,2},{4,5},{5,4},{6,7},{7,6},{8,9},{9,8},{10,11... | collective-permute-start | bytes 3538952 | tf_op jit(solution)/shard_map/ppermute | solution.py:502
  279.2 26.0 %collective-permute-start.25 = (bf16[8,32,2304]{2,1,0:T(8,128)(2,1)}, bf16[8,32,2304]{2,1,0:T(8,128)(2,1)}, u32[]{:S(2)}, u32[]{:S(2)}) collective-permute-start(bf16[8,32,2304]{2,1,0:T(8,128)(2,1)} %merge_rows.28), channel_id=1, source_target_pairs={{0,3},{1,2},{2,1},{3,0},{4,7},{5,6},{6,5},{7,4},{8,11},{9,10},{10,... | collective-permute-start | bytes 3538952 | tf_op jit(solution)/shard_map/ppermute | solution.py:502
  284.7 23.9 %collective-permute-start.26 = (bf16[8,32,2304]{2,1,0:T(8,128)(2,1)}, bf16[8,32,2304]{2,1,0:T(8,128)(2,1)}, u32[]{:S(2)}, u32[]{:S(2)}) collective-permute-start(bf16[8,32,2304]{2,1,0:T(8,128)(2,1)} %merge_rows.29), channel_id=1, source_target_pairs={{0,4},{1,5},{2,6},{3,7},{4,0},{5,1},{6,2},{7,3},{8,12},{9,13},{10,... | collective-permute-start | bytes 3538952 | tf_op jit(solution)/shard_map/ppermute | solution.py:502
  288.0 1.4 copy-start
  305.1 3.4 copy-start.15
Sparse Core Ops, SparseCore 0:
  11.7 81.3 all-gather.6
Sparse Core Ops, SparseCore 1:
  54.2 67.5 all-reduce.1
  123.2 66.0 all-gather.8
  193.1 67.4 all-gather.10

commit v5 on v4

--- a/solution.py
+++ b/solution.py
@@ -451,50 +451,74 @@
     )(*arrays, gate, up, weights, rows, act)
 
 
-def merge_kernel(parts, arrays, shift_ref, *refs):
-    out_ref, sems = refs[arrays], refs[arrays + 1]
-    copies = []
-    for at, (array, unit, shift) in enumerate(parts):
-        source = refs[array]
-        first = unit if shift is None else unit + shift_ref[shift]
-        half = source.shape[1] // 2
-        for piece in range(2):
-            rows = pl.ds(piece * half, half)
-            copies.append(
-                pltpu.make_async_copy(
-                    source.at[first, rows], out_ref.at[at, rows], sems.at[2 * at + piece]
+def merge_kernel(plans, arrays, shift_ref, *refs):
+    sources, refs = refs[:arrays], refs[arrays + refs_after(refs, arrays, plans) :]
+    outs, buffers = refs[: len(plans)], refs[len(plans) : 2 * len(plans)]
+    in_sems, out_sems = refs[2 * len(plans) :]
+    reads, count = [], 0
+    for plan, buffer in zip(plans, buffers):
+        copies = []
+        for at, (array, unit, shift) in enumerate(plan):
+            first = unit if shift is None else unit + shift_ref[shift]
+            half = buffer.shape[1] // 2
+            for piece in range(2):
+                rows = pl.ds(piece * half, half)
+                copies.append(
+                    pltpu.make_async_copy(
+                        sources[array].at[first, rows], buffer.at[at, rows], in_sems.at[count]
+                    )
                 )
-            )
-    for copy in copies:
-        copy.start()
-    for copy in copies:
+                count += 1
+        reads.append(copies)
+    for copies in reads:
+        for copy in copies:
+            copy.start()
+    writes = []
+    for index, copies in enumerate(reads):
+        for copy in copies:
+            copy.wait()
+        writes.append(pltpu.make_async_copy(buffers[index], outs[index], out_sems.at[index]))
+        writes[-1].start()
+    for copy in writes:
         copy.wait()
 
 
-def merge(shifts, parts):
-    arrays, list_of = [], []
-    for array, units, shift in parts:
-        known = [i for i, other in enumerate(arrays) if other is array]
-        if not known:
-            arrays.append(array)
-            known = [len(arrays) - 1]
-        list_of += [(known[0], unit, shift) for unit in units]
-    shape = (len(list_of),) + arrays[0].shape[1:]
-    size = functools.reduce(lambda a, b: a * b, shape, 1)
+def refs_after(refs, arrays, plans):
+    return len(refs) - arrays - 2 * len(plans) - 2
+
+
+def merge(shifts, messages, after=()):
+    arrays, plans = [], []
+    for parts in messages:
+        plan = []
+        for array, units, shift in parts:
+            known = [i for i, other in enumerate(arrays) if other is array]
+            if not known:
+                arrays.append(array)
+                known = [len(arrays) - 1]
+            plan += [(known[0], unit, shift) for unit in units]
+        plans.append(tuple(plan))
+    shapes = [(len(plan),) + arrays[plan[0][0]].shape[1:] for plan in plans]
+    size = sum(functools.reduce(lambda a, b: a * b, shape, 1) for shape in shapes)
+    any_spec = pl.BlockSpec(memory_space=pl.ANY)
     return pl.pallas_call(
-        functools.partial(merge_kernel, tuple(list_of), len(arrays)),
+        functools.partial(merge_kernel, tuple(plans), len(arrays)),
         grid_spec=pltpu.PrefetchScalarGridSpec(
             num_scalar_prefetch=1,
             grid=(1,),
-            in_specs=[pl.BlockSpec(memory_space=pl.ANY)] * len(arrays),
-            out_specs=pl.BlockSpec(shape, lambda i, s: (0,) * len(shape)),
-            scratch_shapes=[pltpu.SemaphoreType.DMA((2 * len(list_of),))],
-        ),
-        out_shape=jax.ShapeDtypeStruct(shape, BF16),
+            in_specs=[any_spec] * (len(arrays) + len(after)),
+            out_specs=[any_spec] * len(plans),
+            scratch_shapes=[pltpu.VMEM(shape, BF16) for shape in shapes]
+            + [
+                pltpu.SemaphoreType.DMA((2 * sum(len(plan) for plan in plans),)),
+                pltpu.SemaphoreType.DMA((len(plans),)),
+            ],
+        ),
+        out_shape=[jax.ShapeDtypeStruct(shape, BF16) for shape in shapes],
         compiler_params=pltpu.CompilerParams(vmem_limit_bytes=VMEM_LIMIT),
         cost_estimate=call_cost(0, 4 * size),
         name="merge_rows",
-    )(shifts, *arrays)
+    )(shifts, *arrays, *after)
 
 
 def swap(array, axis, flip):
@@ -517,14 +541,25 @@
     return both.reshape((-1,) + array.shape[1:])
 
 
-def third_message(shifts, keep, first, second):
-    parts = [(keep, (2, 3)), (first, (2, 3)), (second, (2, 3)), (second, (6, 7))]
-    return merge(shifts, [(array, units, None) for array, units in parts])
-
-
-def fourth_message(shifts, keep, first, second, third):
-    parts = [(keep, (1,)), (first, (1,)), (second, (1, 5)), (third, (1, 3, 5, 7))]
-    return merge(shifts, [(array, units, None) for array, units in parts])
+def second_parts(keep, first):
+    return [(keep, range(4, 8), None), (first, range(4, 8), None)]
+
+
+def third_parts(keep, first, second):
+    return [
+        (keep, (2, 3), None),
+        (first, (2, 3), None),
+        (second, (2, 3, 6, 7), None),
+    ]
+
+
+def fourth_parts(keep, first, second, third):
+    return [
+        (keep, (1,), None),
+        (first, (1,), None),
+        (second, (1, 5), None),
+        (third, (1, 3, 5, 7), None),
+    ]
 
 
 def grad_places(flips):
@@ -602,10 +637,14 @@
     (keep_a, send_a, keep_far_a, send_far_a) = picks[:4]
     (keep_b, send_b, keep_far_b, send_far_b) = picks[4:]
     got_a, got_b = swap(send_far_a, "seq", 1), swap(send_far_b, "seq", 1)
-    message_a = merge(shifts, [(send_a, (0, 1), None), (got_a, (0, 1), None)])
-    message_a, got_b = lax.optimization_barrier((message_a, got_b))
+    message_a, message_b = merge(
+        shifts,
+        [
+            [(send_a, (0, 1), None), (got_a, (0, 1), None)],
+            [(send_b, (0, 1), None), (got_b, (0, 1), None)],
+        ],
+    )
     first_a = swap(message_a, "seq", 2 * flips_a[0])
-    message_b = merge(shifts, [(send_b, (0, 1), None), (got_b, (0, 1), None)])
     far_a, far_b = swap(keep_far_a, "seq", 1), swap(keep_far_b, "seq", 1)
     flow, far_a, far_b, message_b, local_grad = lax.optimization_barrier(
         (flow, far_a, far_b, message_b, local_grad)
@@ -621,20 +660,21 @@
     turns = tuple(tuple(mask_of(order, bits) for bits in bit_rows) for order in orders)
     sends = pick_grad(place, tables, (flow, flow_far), turns, n_exp, per_token, capacity)
 
-    firsts = [swap(sends[2 * k + 1], "exp", orders[k][0]) for k in range(quarters)]
-    seconds = [
-        swap(
-            merge(shifts, [(sends[2 * k], range(4, 8), None), (firsts[k], range(4, 8), None)]),
-            "exp",
-            orders[k][1],
-        )
-        for k in range(quarters)
-    ]
-    first_a, first_b, firsts = lax.optimization_barrier((first_a, first_b, firsts))
-    message_a = merge(
-        shifts, [(keep_a, (1,), None), (far_a, (1,), None), (first_a, (1, 3), None)]
-    )
-    message_b = merge(shifts, [(keep_b, (1,), None), (far_b, (1,), None), (first_b, (1, 3), 0)])
+    streams = range(quarters)
+    keeps = [sends[2 * k] for k in streams]
+    firsts = [swap(sends[2 * k + 1], "exp", orders[k][0]) for k in streams]
+    messages = merge(shifts, [second_parts(keeps[k], firsts[k]) for k in streams])
+    seconds = [swap(messages[k], "exp", orders[k][1]) for k in streams]
+    (message_a,) = merge(
+        shifts,
+        [[(keep_a, (1,), None), (far_a, (1,), None), (first_a, (1, 3), None)]],
+        messages,
+    )
+    (message_b,) = merge(
+        shifts,
+        [[(keep_b, (1,), None), (far_b, (1,), None), (first_b, (1, 3), 0)]],
+        messages,
+    )
     second_a = swap(message_a, "seq", 2 * flips_a[1])
     second_b = swap_gather(message_b, "seq", 2 * flips_b[1])
     calls = [
@@ -643,10 +683,8 @@
         [(second_a, i, None) for i in range(4)],
         [(second_b, i, 1) for i in range(4)],
     ]
-    thirds = []
-    for k in range(quarters):
-        message = third_message(shifts, sends[2 * k], firsts[k], seconds[k])
-        thirds.append(swap(message, "exp", orders[k][2]))
+    messages = merge(shifts, [third_parts(keeps[k], firsts[k], seconds[k]) for k in streams])
+    thirds = [swap(messages[k], "exp", orders[k][2]) for k in streams]
     results = ()
     for part, pieces in enumerate(calls):
         results = expert_forward(
@@ -665,11 +703,13 @@
         tile = call * 2 + (inner >> 2)
         return tile * n_exp * capacity + (inner & 3) * 4 * capacity + (spot & 1) * 2 * capacity
 
+    messages = merge(
+        shifts, [fourth_parts(keeps[k], firsts[k], seconds[k], thirds[k]) for k in streams]
+    )
+    fourths = [swap(messages[k], "exp", orders[k][3]) for k in streams]
     arrays, places = [], []
-    for k in range(quarters):
-        got = [sends[2 * k], firsts[k], seconds[k], thirds[k]]
-        message = fourth_message(shifts, *got)
-        got.append(swap(message, "exp", orders[k][3]))
+    for k in streams:
+        got = [keeps[k], firsts[k], seconds[k], thirds[k], fourths[k]]
         for mask, (array, unit) in sorted(grad_places(orders[k]).items()):
             places.append((len(arrays) + array, unit, row_of(mask, k), 2 * capacity))
         arrays += got

time: 351 us -> 335 us (0.954); the launches traced: 346 us -> 334 us
  Pallas kernels: 159 us -> 134 us
  waiting for transfers between devices: 112 us -> 127 us
  starting transfers between devices: 43.4 us -> 39.4 us
    pallas_call x16 -> x6, Pallas kernels: 53.3 us -> 28 us  [merge(): pl.pallas_call(functools.partial(merge_kernel, tuple(plans), len(arrays))...]
    all_to_all x1, waiting for transfers between devices: 0.24 us -> 9.41 us  [per_device(): lax.all_to_all(local_grad, 'seq', split_axis=0, concat_axis=1, tiled=True)]
    ppermute x25, starting transfers between devices: 26.1 us -> 21.6 us  [swap(): return lax.ppermute(array, axis, [(i, i ^ flip) for i in range(count)])]
    unnamed x34 -> x36, local copies, waits for them, and re-layouts: 6.96 us -> 8.64 us
  transfers between devices with their start and end apart: 34 -> 34, of which waited for: 11 -> 19; matrix products, arithmetic and copies ran while one was open for 2% -> 2% of each run, Pallas kernels for 36% -> 31%
where the time goes in v5:
time: 335 us; the launch traced here: 334 us
  Pallas kernels  134 us (40%)
  waiting for transfers between devices  127 us (38%)
  starting transfers between devices  39.4 us (12%)
  local copies, waits for them, and re-layouts  16 us (5%)
  between operations  16 us (5%)
    ppermute x25, waiting for transfers between devices, swap(): return lax.ppermute(array, axis, [(i, i ^ flip) for i in range(count)])  60.2 us
    all_gather x1, waiting for transfers between devices, per_device(): exp_normed = lax.all_gather(normed, 'exp')  38.9 us
    pallas_call x4, Pallas kernels, expert_forward(): pl.pallas_call(functools.partial(forward_kernel, sources), grid_spec=pltp...  31.3 us
    pallas_call x1, Pallas kernels, expert_backward(): pl.pallas_call(functools.partial(backward_kernel, places, len(arrays)), g...  29.6 us
    pallas_call x6, Pallas kernels, merge(): pl.pallas_call(functools.partial(merge_kernel, tuple(plans), len(arrays))...  28 us
    ppermute x25, starting transfers between devices, swap(): return lax.ppermute(array, axis, [(i, i ^ flip) for i in range(count)])  21.6 us
    all_gather x2, waiting for transfers between devices, swap_gather(): both = lax.all_gather(array, axis, axis_index_groups=groups)  13.8 us
    pallas_call x1, Pallas kernels, conv_back(): pl.pallas_call(functools.partial(conv_kernel, tile), grid_spec=pltpu.Pref...  12.6 us
  transfers between devices with their start and end apart: 34, of which 19 were waited for; matrix products, arithmetic and copies ran while one was open for 2% of the time, Pallas kernels for 31%

profile of v5, /device:TPU:1, one launch (start us, length us, event | category | flops | bytes accessed | tf_op | source)
XLA Modules:
  0.0 333.7 jit_solution(1780106579480480976)
XLA Ops:
  8.1 1.3 reshape.21.gain_ref
  9.4 2.1 norm_rows.1
  11.6 1.5 collective-permute-start.4
  13.1 0.8 fusion
  13.8 3.2 collective-permute-start
  17.0 1.3 collective-permute-start.1
  18.3 0.7 slice.11
  19.1 1.3 collective-permute-start.2
  20.4 0.6 broadcast_in_dim.4
  21.0 4.8 %all-to-all-start = ((f32[8,16,128]{2,1,0:T(8,128)}), f32[8,16,128]{2,1,0:T(8,128)S(1)}, u32[]{:S(2)}, u32[]{:S(2)}) async-start(f32[8,16,128]{2,1,0:T(8,128)} %broadcast_in_dim.4), calls=%async_computation | async-start | bytes 131072 | tf_op jit(solution)/shard_map/all_to_all | solution.py:611
  25.8 0.6 pad_add_fusion.place_ref
  26.6 1.0 reshape.29.ids_ref
  28.9 12.6 %conv_back.1 = (bf16[1024,768]{1,0:T(8,128)(2,1)}, bf16[512,768]{1,0:T(8,128)(2,1)}, bf16[512,768]{1,0:T(8,128)(2,1)}) custom-call(s32[2]{0:T(128)} %pad_add_fusion.place_ref, bf16[1024,768]{1,0:T(8,128)(2,1)} %in_ref.1, bf16[16,768]{1,0:T(8,128)(2,1)} %copy-done.11, bf16[16,768]{1,0:T(8,128)(2,1)} %copy-done.12, bf16[1024,768]{1,0:T(8,128)(2,1)} %grad_ref.1, ...), custom_call_target="tpu_custom_call" | custom-call | flops 31457280 | bytes 6291456 | tf_op jit(solution)/shard_map/conv_back/pallas_call | solution.py:107
  41.6 2.5 collective-permute-done.3.other_ref
  44.1 0.9 copy-done.17
  45.0 9.1 %project.1 = bf16[512,2304]{1,0:T(8,128)(2,1)} custom-call(s32[2]{0:T(128)} %pad_add_fusion.place_ref, bf16[512,768]{1,0:T(8,128)(2,1)} %get-tuple-element.69.own_ref, bf16[512,768]{1,0:T(8,128)(2,1)} %copy-done.17, bf16[768,2304]{1,0:T(8,128)(2,1)} %own_weight.1, bf16[768,2304]{1,0:T(8,128)(2,1)} %collective-permute-done.4.other_weight, ...), custom_call_target="tpu_custom_call" | custom-call | flops 3623878656 | bytes 11010048 | tf_op jit(solution)/shard_map/project/pallas_call | solution.py:157
  54.2 38.9 %all-gather.7.cloned.1.call-done = bf16[2048,2432]{1,0:T(8,128)(2,1)} async-done(((bf16[128,2432]{1,0:T(8,128)(2,1)}), bf16[2048,2432]{1,0:T(8,128)(2,1)}) %all-gather.7.cloned.1.call-update) | async-done | bytes 9961488 | tf_op jit(solution)/shard_map/all_gather | solution.py:614
  93.1 12.2 %pick_norm.1 = (bf16[2,8,16,2304]{3,2,1,0:T(8,128)(2,1)}, bf16[2,8,16,2304]{3,2,1,0:T(8,128)(2,1)}, bf16[2,8,16,2304]{3,2,1,0:T(8,128)(2,1)}, bf16[2,8,16,2304]{...) custom-call(s32[2]{0:T(128)} %pad_add_fusion.place_ref, ...), custom_call_target="tpu_custom_call" | custom-call | flops 1207959552 | bytes 18874368 | tf_op jit(solution)/shard_map/pick_norm/pallas_call | solution.py:219
  105.3 0.7 collective-permute-start.7
  107.2 2.2 collective-permute-done.7.refs_1_
  109.5 2.6 collective-permute-done.8.refs_3_
  112.1 4.6 %merge_rows.6 = (bf16[4,8,16,2304]{3,2,1,0:T(8,128)(2,1)}, bf16[4,8,16,2304]{3,2,1,0:T(8,128)(2,1)}) custom-call(s32[2]{0:T(128)} %pad_add_fusion.1.shift_ref.refs_0_, bf16[2,8,16,2304]{3,2,1,0:T(8,128)(2,1)} %get-tuple-element.75.refs_0_, bf16[2,8,16,2304]{3,2,1,0:T(8,128)(2,1)} %copy-done.7, bf16[2,8,16,2304]{3,2,1,0:T(8,128)(2,1)} %get-tuple-element.77.refs_2_, ...), custom_call_target="tpu_custom_call" | custom-call | bytes 9437184 | tf_op jit(solution)/shard_map/merge_rows/pallas_call | solution.py:504
  116.7 5.0 %all-reduce.2.cloned.1.call-done.refs_0_ = bf16[512,2304]{1,0:T(8,128)(2,1)} async-done(((bf16[512,2304]{1,0:T(8,128)(2,1)}), bf16[512,2304]{1,0:T(8,128)(2,1)}) %all-reduce.2.cloned.1.call-update) | async-done | bytes 2359312 | tf_op jit(solution)/shard_map/psum | solution.py:627
  121.8 1.1 copy-done.4
  123.1 0.8 collective-permute-start.9
  123.9 4.4 %collective-permute-done.9.refs_1_ = bf16[512,2304]{1,0:T(8,128)(2,1)S(1)} collective-permute-done((bf16[512,2304]{1,0:T(8,128)(2,1)}, bf16[512,2304]{1,0:T(8,128)(2,1)S(1)}, u32[]{:S(2)}, u32[]{:S(2)}) %collective-permute-start.9) | collective-permute-done | bytes 2359328 | tf_op jit(solution)/shard_map/ppermute | solution.py:526
  128.3 1.4 copy-done.6
  129.7 8.6 %pick_grad.1 = (bf16[8,32,2304]{2,1,0:T(8,128)(2,1)}, bf16[8,32,2304]{2,1,0:T(8,128)(2,1)}, bf16[8,32,2304]{2,1,0:T(8,128)(2,1)}, bf16[8,32,2304]{2,1,0:T(8,128)...) custom-call(s32[2]{0:T(128)} %pad_add_fusion.place_ref, ...), custom_call_target="tpu_custom_call" | custom-call | flops 1207959552 | bytes 14155776 | tf_op jit(solution)/shard_map/pick_grad/pallas_call | solution.py:287
  138.3 1.2 collective-permute-start.10
  139.5 1.8 collective-permute-start.11
  141.3 1.3 collective-permute-start.12
  142.6 1.9 collective-permute-start.13
  144.5 21.5 %collective-permute-done.10.refs_1_ = bf16[8,32,2304]{2,1,0:T(8,128)(2,1)S(1)} collective-permute-done((bf16[8,32,2304]{2,1,0:T(8,128)(2,1)}, bf16[8,32,2304]{2,1,0:T(8,128)(2,1)S(1)}, u32[]{:S(2)}, u32[]{:S(2)}) %collective-permute-start.10) | collective-permute-done | bytes 1179680 | tf_op jit(solution)/shard_map/ppermute | solution.py:526
  165.9 2.0 collective-permute-done.11.refs_3_.refs_4_.refs_5_.refs_6_
  168.2 2.2 collective-permute-done.13.refs_7_.refs_10_.refs_13_.refs_16_
  170.4 5.2 %merge_rows.7 = (bf16[8,32,2304]{2,1,0:T(8,128)(2,1)}, bf16[8,32,2304]{2,1,0:T(8,128)(2,1)}, bf16[8,32,2304]{2,1,0:T(8,128)(2,1)}, bf16[8,32,2304]{2,1,0:T(8,128)(2,1)}) custom-call(s32[2]{0:T(128)} %pad_add_fusion.1.shift_ref.refs_0_, bf16[8,32,2304]{2,1,0:T(8,128)(2,1)} %get-tuple-element.84.refs_0_, bf16[8,32,2304]{2,1,0:T(8,128)(2,1)} %copy-done.2, ...), custom_call_target="tpu_custom_call" | custom-call | bytes 9437184 | tf_op jit(solution)/shard_map/merge_rows/pallas_call | solution.py:504
  175.6 13.8 %all-gather.9.cloned.1.call-done.refs_3_.refs_4_.refs_2_ = bf16[8,8,16,2304]{3,2,1,0:T(8,128)(2,1)} async-done(((bf16[4,8,16,2304]{3,2,1,0:T(8,128)(2,1)}), bf16[8,8,16,2304]{3,2,1,0:T(8,128)(2,1)}) %all-gather.9.cloned.1.call-update) | async-done | bytes 4718608 | tf_op jit(solution)/shard_map/all_gather | solution.py:540
  189.3 3.7 %merge_rows.10 = bf16[4,8,16,2304]{3,2,1,0:T(8,128)(2,1)} custom-call(s32[2]{0:T(128)} %pad_add_fusion.1.shift_ref.refs_0_, bf16[2,8,16,2304]{3,2,1,0:T(8,128)(2,1)} %get-tuple-element.93.refs_1_.refs_0_, bf16[2,8,16,2304]{3,2,1,0:T(8,128)(2,1)} %copy-done.3, bf16[8,8,16,2304]{3,2,1,0:T(8,128)(2,1)} %all-gather.9.cloned.1.call-done.refs_3_.refs_4_.refs_2_, ...), custom_call_target="tpu_custom_call" | custom-call | bytes 4718592 | tf_op jit(solution)/shard_map/merge_rows/pallas_call | solution.py:504
  193.1 2.5 collective-permute-start.14
  195.6 1.3 collective-permute-start.16
  196.9 1.9 collective-permute-start.17
  198.8 1.4 copy-done.1
  200.2 4.2 %merge_rows.11 = bf16[4,8,16,2304]{3,2,1,0:T(8,128)(2,1)} custom-call(s32[2]{0:T(128)} %pad_add_fusion.1.shift_ref.refs_0_, bf16[2,8,16,2304]{3,2,1,0:T(8,128)(2,1)} %get-tuple-element.96.refs_1_.refs_0_, bf16[2,8,16,2304]{3,2,1,0:T(8,128)(2,1)} %copy-done.4, bf16[4,8,16,2304]{3,2,1,0:T(8,128)(2,1)} %copy-done.1, ...), custom_call_target="tpu_custom_call" | custom-call | bytes 4718592 | tf_op jit(solution)/shard_map/merge_rows/pallas_call | solution.py:504
  204.4 17.0 %collective-permute-done.14.refs_2_ = bf16[8,32,2304]{2,1,0:T(8,128)(2,1)} collective-permute-done((bf16[8,32,2304]{2,1,0:T(8,128)(2,1)}, bf16[8,32,2304]{2,1,0:T(8,128)(2,1)}, u32[]{:S(2)}, u32[]{:S(2)}) %collective-permute-start.14) | collective-permute-done | bytes 1179680 | tf_op jit(solution)/shard_map/ppermute | solution.py:526
  221.4 0.9 collective-permute-done.16.refs_5_.refs_6_.refs_7_
  222.3 2.2 collective-permute-done.17.refs_8_.refs_10_.refs_12_
  224.7 5.2 %merge_rows.8 = (bf16[8,32,2304]{2,1,0:T(8,128)(2,1)}, bf16[8,32,2304]{2,1,0:T(8,128)(2,1)}, bf16[8,32,2304]{2,1,0:T(8,128)(2,1)}, bf16[8,32,2304]{2,1,0:T(8,128)(2,1)}) custom-call(s32[2]{0:T(128)} %pad_add_fusion.1.shift_ref.refs_0_, bf16[8,32,2304]{2,1,0:T(8,128)(2,1)} %get-tuple-element.84.refs_0_, bf16[8,32,2304]{2,1,0:T(8,128)(2,1)} %copy-done.2, ...), custom_call_target="tpu_custom_call" | custom-call | bytes 9437184 | tf_op jit(solution)/shard_map/merge_rows/pallas_call | solution.py:504
  230.3 1.4 collective-permute-start.20
  231.8 0.8 collective-permute-start.22
  232.6 7.3 %all-to-all-start.1 = ((bf16[8,128,768]{2,1,0:T(8,128)(2,1)}), bf16[8,128,768]{2,1,0:T(8,128)(2,1)}, u32[]{:S(2)}, u32[]{:S(2)}) async-start(bf16[8,128,768]{2,1,0:T(8,128)(2,1)} %bitcast.21), calls=%async_computation.1 | async-start | bytes 3145728 | tf_op jit(solution)/shard_map/all_to_all | solution.py:653
  239.9 7.8 %expert_forward.4 = (bf16[2304,2048]{1,0:T(8,128)(2,1)}, bf16[512,2048]{1,0:T(8,128)(2,1)}, f32[2048,512]{1,0:T(8,128)}, f32[2048,512]{1,0:T(8,128)}) custom-call(s32[2]{0:T(128)} %pad_add_fusion.1.shift_ref.refs_0_, bf16[2,8,16,2304]{3,2,1,0:T(8,128)(2,1)} %get-tuple-element.96.refs_1_.refs_0_, bf16[2,8,16,2304]{3,2,1,0:T(8,128)(2,1)} %copy-done.4, ...), custom_call_target="tpu_custom_call" | custom-call | flops 2415919104 | bytes 7340032 | tf_op jit(solution)/shard_map/expert_forward/pallas_call | solution.py:347
  247.7 7.9 %expert_forward.5 = (bf16[2304,2048]{1,0:T(8,128)(2,1)}, bf16[512,2048]{1,0:T(8,128)(2,1)}, f32[2048,512]{1,0:T(8,128)}, f32[2048,512]{1,0:T(8,128)}) custom-call(s32[2]{0:T(128)} %pad_add_fusion.1.shift_ref.refs_0_, ...), custom_call_target="tpu_custom_call", output_to_operand_aliasing={{0}: (6, {}), {1}: (7, {}), {2}: (8, {}), {3}: (9, {})} | custom-call | flops 2415919104 | bytes 7340032 | tf_op jit(solution)/shard_map/expert_forward/pallas_call | solution.py:347
  255.6 0.9 collective-permute-done.20.refs_7_.refs_8_
  257.0 1.0 collective-permute-done.22.refs_15_.refs_18_
  258.0 5.2 %merge_rows.9 = (bf16[8,32,2304]{2,1,0:T(8,128)(2,1)}, bf16[8,32,2304]{2,1,0:T(8,128)(2,1)}, bf16[8,32,2304]{2,1,0:T(8,128)(2,1)}, bf16[8,32,2304]{2,1,0:T(8,128)(2,1)}) custom-call(s32[2]{0:T(128)} %pad_add_fusion.1.shift_ref.refs_0_, bf16[8,32,2304]{2,1,0:T(8,128)(2,1)} %get-tuple-element.84.refs_0_, bf16[8,32,2304]{2,1,0:T(8,128)(2,1)} %copy-done.2, ...), custom_call_target="tpu_custom_call" | custom-call | bytes 9437184 | tf_op jit(solution)/shard_map/merge_rows/pallas_call | solution.py:504
  263.1 0.8 collective-permute-start.23
  264.1 2.2 collective-permute-start.25
  266.4 9.4 %all-to-all-done.1 = bf16[8,128,768]{2,1,0:T(8,128)(2,1)} async-done(((bf16[8,128,768]{2,1,0:T(8,128)(2,1)}), bf16[8,128,768]{2,1,0:T(8,128)(2,1)}, u32[]{:S(2)}, u32[]{:S(2)}) %all-to-all-start.1) | async-done | bytes 1572896 | tf_op jit(solution)/shard_map/all_to_all | solution.py:653
  275.8 2.7 copy.30
  278.5 1.4 copy-done
  279.9 7.8 %expert_forward.6 = (bf16[2304,2048]{1,0:T(8,128)(2,1)}, bf16[512,2048]{1,0:T(8,128)(2,1)}, f32[2048,512]{1,0:T(8,128)}, f32[2048,512]{1,0:T(8,128)}) custom-call(s32[2]{0:T(128)} %pad_add_fusion.1.shift_ref.refs_0_, bf16[4,8,16,2304]{3,2,1,0:T(8,128)(2,1)} %copy-done, ...), custom_call_target="tpu_custom_call", output_to_operand_aliasing={{0}: (6, {}), {1}: (7, {}), {2}: (8, {}), {3}: (9, {})} | custom-call | flops 2415919104 | bytes 7340032 | tf_op jit(solution)/shard_map/expert_forward/pallas_call | solution.py:347
  287.7 7.8 %expert_forward.7 = (bf16[2304,2048]{1,0:T(8,128)(2,1)}, bf16[512,2048]{1,0:T(8,128)(2,1)}, f32[2048,512]{1,0:T(8,128)}, f32[2048,512]{1,0:T(8,128)}) custom-call(s32[2]{0:T(128)} %pad_add_fusion.1.shift_ref.refs_0_, ...), custom_call_target="tpu_custom_call", output_to_operand_aliasing={{0}: (6, {}), {1}: (7, {}), {2}: (8, {}), {3}: (9, {})} | custom-call | flops 2415919104 | bytes 7340032 | tf_op jit(solution)/shard_map/expert_forward/pallas_call | solution.py:347
  295.5 1.0 copy-done.16
  296.5 29.6 %expert_backward.1 = bf16[2304,1536]{1,0:T(8,128)(2,1)} custom-call(bf16[8,32,2304]{2,1,0:T(8,128)(2,1)} %get-tuple-element.84.refs_0_, bf16[8,32,2304]{2,1,0:T(8,128)(2,1)} %copy-done.2, bf16[8,32,2304]{2,1,0:T(8,128)(2,1)} %collective-permute-done.14.refs_2_, bf16[8,32,2304]{2,1,0:T(8,128)(2,1)} %copy-done.8, bf16[8,32,2304]{2,1,0:T(8,128)(2,1)} %copy-done.16, ...), custom_call_target="tpu_custom_call" | custom-call | flops 19327352832 | bytes 39845888 | tf_op jit(solution)/shard_map/expert_backward/pallas_call | solution.py:430
  (73 shorter events, 5.0 us)
Async XLA Ops:
  8.0 12.4 %copy-start.14 = (s32[128,8]{0,1:T(8,128)S(1)}, s32[128,8]{0,1:T(8,128)}, u32[]{:S(2)}) copy-start(s32[128,8]{0,1:T(8,128)} %param.19) | copy-start | bytes 12292
  8.0 12.4 %copy-start.15 = (f32[128,8]{0,1:T(8,128)S(1)}, f32[128,8]{0,1:T(8,128)}, u32[]{:S(2)}) copy-start(f32[128,8]{0,1:T(8,128)} %param.20) | copy-start | bytes 12292
  8.0 18.4 %copy-start.10 = (s32[16384]{0:T(1024)S(1)}, s32[16384]{0:T(1024)}, u32[]{:S(2)}) copy-start(s32[16384]{0:T(1024)} %param.14) | copy-start | bytes 196612
  8.0 85.1 %all-gather.7.cloned.1.call-start = ((), (), s32[]{:S(2)}) async-start(), calls=%async_computation.3 | async-start | bytes 10584064 | tf_op jit(solution)/shard_map/all_gather | solution.py:614
  11.6 32.5 %collective-permute-start.4 = (bf16[768,2304]{1,0:T(8,128)(2,1)}, bf16[768,2304]{1,0:T(8,128)(2,1)}, u32[]{:S(2)}, u32[]{:S(2)}) collective-permute-start(bf16[768,2304]{1,0:T(8,128)(2,1)} %own_weight.1), channel_id=1, source_target_pairs={{0,16},{16,0},{32,48},{48,32},{64,80},{80,64},{96,112},{112,96},{1... | collective-permute-start | bytes 10616840 | tf_op jit(solution)/shard_map/ppermute | solution.py:526
  13.8 13.8 %collective-permute-start = (bf16[16,768]{1,0:T(8,128)(2,1)S(1)}, bf16[16,768]{1,0:T(8,128)(2,1)S(1)}, u32[]{:S(2)}, u32[]{:S(2)}) collective-permute-start(bf16[16,768]{1,0:T(8,128)(2,1)S(1)} %get-tuple-element.135), channel_id=1, source_target_pairs={{0,1},{1,2},{2,3},{3,4},{4,5},{5,6},{6,7},{7,8},{8,9},{9,10},{10,1... | collective-permute-start | bytes 73736 | tf_op jit(solution)/shard_map/ppermute | solution.py:604
  17.0 10.7 %collective-permute-start.1 = (bf16[16,768]{1,0:T(8,128)(2,1)S(1)}, bf16[16,768]{1,0:T(8,128)(2,1)S(1)}, u32[]{:S(2)}, u32[]{:S(2)}) collective-permute-start(bf16[16,768]{1,0:T(8,128)(2,1)S(1)} %get-tuple-element.134), channel_id=1, source_target_pairs={{1,0},{2,1},{3,2},{4,3},{5,4},{6,5},{7,6},{8,7},{9,8},{10,9},{11,1... | collective-permute-start | bytes 73736 | tf_op jit(solution)/shard_map/ppermute | solution.py:605
  19.1 8.6 %collective-permute-start.2 = (bf16[16,768]{1,0:T(8,128)(2,1)S(1)}, bf16[16,768]{1,0:T(8,128)(2,1)S(1)}, u32[]{:S(2)}, u32[]{:S(2)}) collective-permute-start(bf16[16,768]{1,0:T(8,128)(2,1)S(1)} %slice.11), channel_id=1, source_target_pairs={{1,0},{2,1},{3,2},{4,3},{5,4},{6,5},{7,6},{8,7},{9,8},{10,9},{11,1... | collective-permute-start | bytes 73736 | tf_op jit(solution)/shard_map/ppermute | solution.py:606
  21.0 20.5 %all-to-all-start = ((f32[8,16,128]{2,1,0:T(8,128)}), f32[8,16,128]{2,1,0:T(8,128)S(1)}, u32[]{:S(2)}, u32[]{:S(2)}) async-start(f32[8,16,128]{2,1,0:T(8,128)} %broadcast_in_dim.4), calls=%async_computation | async-start | bytes 131072 | tf_op jit(solution)/shard_map/all_to_all | solution.py:611
  25.8 95.9 %all-reduce.2.cloned.1.call-start = ((), (), s32[]{:S(2)}) async-start(), calls=%async_computation.2 | async-start | bytes 4718592 | tf_op jit(solution)/shard_map/psum | solution.py:627
  27.7 0.6 copy-start.11
  27.7 0.6 copy-start.12
  28.3 0.6 copy-start.13
  41.5 12.6 %copy-start.9 = (f32[8,16,128]{2,1,0:T(8,128)}, f32[8,16,128]{2,1,0:T(8,128)S(1)}, u32[]{:S(2)}) copy-start(f32[8,16,128]{2,1,0:T(8,128)S(1)} %all-to-all-done.tables_ref) | copy-start | bytes 196612
  41.5 2.6 collective-permute-start.3
  44.1 0.9 copy-start.17
  54.1 135.2 %all-gather.9.cloned.1.call-start = ((), (), s32[]{:S(2)}) async-start(), calls=%async_computation.4 | async-start | bytes 7077888 | tf_op jit(solution)/shard_map/all_gather | solution.py:540
  105.3 4.2 %collective-permute-start.7 = (bf16[2,8,16,2304]{3,2,1,0:T(8,128)(2,1)}, bf16[2,8,16,2304]{3,2,1,0:T(8,128)(2,1)S(1)}, u32[]{:S(2)}, u32[]{:S(2)}) collective-permute-start(bf16[2,8,16,2304]{3,2,1,0:T(8,128)(2,1)} %get-tuple-element.76), channel_id=1, source_target_pairs={{0,16},{16,0},{32,48},{48,32},{64,80},{80,64},{96,112},{112,96},{1... | collective-permute-start | bytes 3538952 | tf_op jit(solution)/shard_map/ppermute | solution.py:526
  106.0 6.1 %collective-permute-start.8 = (bf16[2,8,16,2304]{3,2,1,0:T(8,128)(2,1)}, bf16[2,8,16,2304]{3,2,1,0:T(8,128)(2,1)}, u32[]{:S(2)}, u32[]{:S(2)}) collective-permute-start(bf16[2,8,16,2304]{3,2,1,0:T(8,128)(2,1)} %get-tuple-element.78), channel_id=1, source_target_pairs={{0,16},{16,0},{32,48},{48,32},{64,80},{80,64},{96,112},{112,96},{1... | collective-permute-start | bytes 3538952 | tf_op jit(solution)/shard_map/ppermute | solution.py:526
  106.1 15.6 %collective-permute-start.5 = (bf16[2,8,16,2304]{3,2,1,0:T(8,128)(2,1)}, bf16[2,8,16,2304]{3,2,1,0:T(8,128)(2,1)S(1)}, u32[]{:S(2)}, u32[]{:S(2)}) collective-permute-start(bf16[2,8,16,2304]{3,2,1,0:T(8,128)(2,1)} %get-tuple-element.73), channel_id=1, source_target_pairs={{0,16},{16,0},{32,48},{48,32},{64,80},{80,64},{96,112},{112,96},{1... | collective-permute-start | bytes 3538952 | tf_op jit(solution)/shard_map/ppermute | solution.py:526
  106.5 15.2 %collective-permute-start.6 = (bf16[2,8,16,2304]{3,2,1,0:T(8,128)(2,1)}, bf16[2,8,16,2304]{3,2,1,0:T(8,128)(2,1)S(1)}, u32[]{:S(2)}, u32[]{:S(2)}) collective-permute-start(bf16[2,8,16,2304]{3,2,1,0:T(8,128)(2,1)} %get-tuple-element.74), channel_id=1, source_target_pairs={{0,16},{16,0},{32,48},{48,32},{64,80},{80,64},{96,112},{112,96},{1... | collective-permute-start | bytes 3538952 | tf_op jit(solution)/shard_map/ppermute | solution.py:526
  109.5 2.6 copy-start.7
  121.7 1.1 copy-start.4
  121.7 1.4 copy-start.3
  123.1 164.5 %all-gather.11.cloned.1.call-start = ((), (), s32[]{:S(2)}) async-start(), calls=%async_computation.5 | async-start | bytes 7077888 | tf_op jit(solution)/shard_map/all_gather | solution.py:540
  123.1 5.1 %collective-permute-start.9 = (bf16[512,2304]{1,0:T(8,128)(2,1)}, bf16[512,2304]{1,0:T(8,128)(2,1)S(1)}, u32[]{:S(2)}, u32[]{:S(2)}) collective-permute-start(bf16[512,2304]{1,0:T(8,128)(2,1)} %all-reduce.2.cloned.1.call-done.refs_0_), channel_id=1, source_target_pairs={{0,16},{16,0},{32,48},{48,32},{64,80},{80,64},{96,112},{112,96},{1... | collective-permute-start | bytes 7077896 | tf_op jit(solution)/shard_map/ppermute | solution.py:526
  128.3 1.4 copy-start.6
  138.3 27.6 %collective-permute-start.10 = (bf16[8,32,2304]{2,1,0:T(8,128)(2,1)}, bf16[8,32,2304]{2,1,0:T(8,128)(2,1)S(1)}, u32[]{:S(2)}, u32[]{:S(2)}) collective-permute-start(bf16[8,32,2304]{2,1,0:T(8,128)(2,1)} %get-tuple-element.85), channel_id=1, source_target_pairs={{0,1},{1,0},{2,3},{3,2},{4,5},{5,4},{6,7},{7,6},{8,9},{9,8},{10,11... | collective-permute-start | bytes 3538952 | tf_op jit(solution)/shard_map/ppermute | solution.py:526
  139.5 28.4 %collective-permute-start.11 = (bf16[8,32,2304]{2,1,0:T(8,128)(2,1)}, bf16[8,32,2304]{2,1,0:T(8,128)(2,1)}, u32[]{:S(2)}, u32[]{:S(2)}) collective-permute-start(bf16[8,32,2304]{2,1,0:T(8,128)(2,1)} %get-tuple-element.87), channel_id=1, source_target_pairs={{0,3},{1,2},{2,1},{3,0},{4,7},{5,6},{6,5},{7,4},{8,11},{9,10},{10,... | collective-permute-start | bytes 3538952 | tf_op jit(solution)/shard_map/ppermute | solution.py:526
  141.3 26.9 %collective-permute-start.12 = (bf16[8,32,2304]{2,1,0:T(8,128)(2,1)}, bf16[8,32,2304]{2,1,0:T(8,128)(2,1)}, u32[]{:S(2)}, u32[]{:S(2)}) collective-permute-start(bf16[8,32,2304]{2,1,0:T(8,128)(2,1)} %get-tuple-element.89), channel_id=1, source_target_pairs={{0,4},{1,5},{2,6},{3,7},{4,0},{5,1},{6,2},{7,3},{8,12},{9,13},{10,... | collective-permute-start | bytes 3538952 | tf_op jit(solution)/shard_map/ppermute | solution.py:526
  142.6 27.8 %collective-permute-start.13 = (bf16[8,32,2304]{2,1,0:T(8,128)(2,1)}, bf16[8,32,2304]{2,1,0:T(8,128)(2,1)}, u32[]{:S(2)}, u32[]{:S(2)}) collective-permute-start(bf16[8,32,2304]{2,1,0:T(8,128)(2,1)} %get-tuple-element.91), channel_id=1, source_target_pairs={{0,12},{1,13},{2,14},{3,15},{4,8},{5,9},{6,10},{7,11},{8,4},{9,5},... | collective-permute-start | bytes 3538952 | tf_op jit(solution)/shard_map/ppermute | solution.py:526
  144.5 54.3 %collective-permute-start.15 = (bf16[4,8,16,2304]{3,2,1,0:T(8,128)(2,1)}, bf16[4,8,16,2304]{3,2,1,0:T(8,128)(2,1)S(1)}, u32[]{:S(2)}, u32[]{:S(2)}) collective-permute-start(bf16[4,8,16,2304]{3,2,1,0:T(8,128)(2,1)} %get-tuple-element.98), channel_id=1, source_target_pairs={{0,32},{16,48},{32,0},{48,16},{64,96},{80,112},{96,64},{112,80},{1... | collective-permute-start | bytes 7077896 | tf_op jit(solution)/shard_map/ppermute | solution.py:526
  165.9 4.4 %copy-start.2 = (bf16[8,32,2304]{2,1,0:T(8,128)(2,1)}, bf16[8,32,2304]{2,1,0:T(8,128)(2,1)S(1)}, u32[]{:S(2)}) copy-start(bf16[8,32,2304]{2,1,0:T(8,128)(2,1)S(1)} %collective-permute-done.10.refs_1_) | copy-start | bytes 3538948
  193.1 5.7 %copy-start.5 = (bf16[8,32,2304]{2,1,0:T(8,128)(2,1)S(1)}, bf16[8,32,2304]{2,1,0:T(8,128)(2,1)}, u32[]{:S(2)}) copy-start(bf16[8,32,2304]{2,1,0:T(8,128)(2,1)} %get-tuple-element.109.refs_6_) | copy-start | bytes 3538948
  193.1 28.3 %collective-permute-start.14 = (bf16[8,32,2304]{2,1,0:T(8,128)(2,1)}, bf16[8,32,2304]{2,1,0:T(8,128)(2,1)}, u32[]{:S(2)}, u32[]{:S(2)}) collective-permute-start(bf16[8,32,2304]{2,1,0:T(8,128)(2,1)} %get-tuple-element.92.refs_3_), channel_id=1, source_target_pairs={{0,3},{1,2},{2,1},{3,0},{4,7},{5,6},{6,5},{7,4},{8,11},{9,10},{10,... | collective-permute-start | bytes 3538952 | tf_op jit(solution)/shard_map/ppermute | solution.py:526
  195.6 26.7 %collective-permute-start.16 = (bf16[8,32,2304]{2,1,0:T(8,128)(2,1)}, bf16[8,32,2304]{2,1,0:T(8,128)(2,1)}, u32[]{:S(2)}, u32[]{:S(2)}) collective-permute-start(bf16[8,32,2304]{2,1,0:T(8,128)(2,1)} %get-tuple-element.107.refs_4_), channel_id=1, source_target_pairs={{0,4},{1,5},{2,6},{3,7},{4,0},{5,1},{6,2},{7,3},{8,12},{9,13},{10,... | collective-permute-start | bytes 3538952 | tf_op jit(solution)/shard_map/ppermute | solution.py:526
  196.9 27.7 %collective-permute-start.17 = (bf16[8,32,2304]{2,1,0:T(8,128)(2,1)}, bf16[8,32,2304]{2,1,0:T(8,128)(2,1)}, u32[]{:S(2)}, u32[]{:S(2)}) collective-permute-start(bf16[8,32,2304]{2,1,0:T(8,128)(2,1)} %get-tuple-element.108.refs_5_), channel_id=1, source_target_pairs={{0,12},{1,13},{2,14},{3,15},{4,8},{5,9},{6,10},{7,11},{8,4},{9,5},... | collective-permute-start | bytes 3538952 | tf_op jit(solution)/shard_map/ppermute | solution.py:526
  198.8 26.0 %collective-permute-start.18 = (bf16[8,32,2304]{2,1,0:T(8,128)(2,1)S(1)}, bf16[8,32,2304]{2,1,0:T(8,128)(2,1)}, u32[]{:S(2)}, u32[]{:S(2)}) collective-permute-start(bf16[8,32,2304]{2,1,0:T(8,128)(2,1)S(1)} %copy-done.5), channel_id=1, source_target_pairs={{0,1},{1,0},{2,3},{3,2},{4,5},{5,4},{6,7},{7,6},{8,9},{9,8},{10,11... | collective-permute-start | bytes 3538952 | tf_op jit(solution)/shard_map/ppermute | solution.py:526
  198.8 1.4 copy-start.1
  204.3 74.2 %collective-permute-start.27 = (bf16[4,8,16,2304]{3,2,1,0:T(8,128)(2,1)}, bf16[4,8,16,2304]{3,2,1,0:T(8,128)(2,1)S(1)}, u32[]{:S(2)}, u32[]{:S(2)}) collective-permute-start(bf16[4,8,16,2304]{3,2,1,0:T(8,128)(2,1)} %merge_rows.11), channel_id=1, source_target_pairs={{0,96},{16,112},{32,64},{48,80},{64,32},{80,48},{96,0},{112,16},{1... | collective-permute-start | bytes 7077896 | tf_op jit(solution)/shard_map/ppermute | solution.py:526
  229.9 25.7 %collective-permute-start.19 = (bf16[8,32,2304]{2,1,0:T(8,128)(2,1)}, bf16[8,32,2304]{2,1,0:T(8,128)(2,1)S(1)}, u32[]{:S(2)}, u32[]{:S(2)}) collective-permute-start(bf16[8,32,2304]{2,1,0:T(8,128)(2,1)} %get-tuple-element.110), channel_id=1, source_target_pairs={{0,4},{1,5},{2,6},{3,7},{4,0},{5,1},{6,2},{7,3},{8,12},{9,13},{10,... | collective-permute-start | bytes 3538952 | tf_op jit(solution)/shard_map/ppermute | solution.py:526
  230.3 26.2 %collective-permute-start.20 = (bf16[8,32,2304]{2,1,0:T(8,128)(2,1)}, bf16[8,32,2304]{2,1,0:T(8,128)(2,1)}, u32[]{:S(2)}, u32[]{:S(2)}) collective-permute-start(bf16[8,32,2304]{2,1,0:T(8,128)(2,1)} %get-tuple-element.111), channel_id=1, source_target_pairs={{0,12},{1,13},{2,14},{3,15},{4,8},{5,9},{6,10},{7,11},{8,4},{9,5},... | collective-permute-start | bytes 3538952 | tf_op jit(solution)/shard_map/ppermute | solution.py:526
  231.8 25.2 %collective-permute-start.21 = (bf16[8,32,2304]{2,1,0:T(8,128)(2,1)}, bf16[8,32,2304]{2,1,0:T(8,128)(2,1)}, u32[]{:S(2)}, u32[]{:S(2)}) collective-permute-start(bf16[8,32,2304]{2,1,0:T(8,128)(2,1)} %get-tuple-element.112), channel_id=1, source_target_pairs={{0,1},{1,0},{2,3},{3,2},{4,5},{5,4},{6,7},{7,6},{8,9},{9,8},{10,11... | collective-permute-start | bytes 3538952 | tf_op jit(solution)/shard_map/ppermute | solution.py:526
  231.8 26.2 %collective-permute-start.22 = (bf16[8,32,2304]{2,1,0:T(8,128)(2,1)}, bf16[8,32,2304]{2,1,0:T(8,128)(2,1)}, u32[]{:S(2)}, u32[]{:S(2)}) collective-permute-start(bf16[8,32,2304]{2,1,0:T(8,128)(2,1)} %get-tuple-element.113), channel_id=1, source_target_pairs={{0,3},{1,2},{2,1},{3,0},{4,7},{5,6},{6,5},{7,4},{8,11},{9,10},{10,... | collective-permute-start | bytes 3538952 | tf_op jit(solution)/shard_map/ppermute | solution.py:526
  232.6 43.2 %all-to-all-start.1 = ((bf16[8,128,768]{2,1,0:T(8,128)(2,1)}), bf16[8,128,768]{2,1,0:T(8,128)(2,1)}, u32[]{:S(2)}, u32[]{:S(2)}) async-start(bf16[8,128,768]{2,1,0:T(8,128)(2,1)} %bitcast.21), calls=%async_computation.1 | async-start | bytes 3145728 | tf_op jit(solution)/shard_map/all_to_all | solution.py:653
  255.6 2.4 copy-start.8
  263.1 32.3 %collective-permute-start.23 = (bf16[8,32,2304]{2,1,0:T(8,128)(2,1)}, bf16[8,32,2304]{2,1,0:T(8,128)(2,1)S(1)}, u32[]{:S(2)}, u32[]{:S(2)}) collective-permute-start(bf16[8,32,2304]{2,1,0:T(8,128)(2,1)} %get-tuple-element.118), channel_id=1, source_target_pairs={{0,12},{1,13},{2,14},{3,15},{4,8},{5,9},{6,10},{7,11},{8,4},{9,5},... | collective-permute-start | bytes 3538952 | tf_op jit(solution)/shard_map/ppermute | solution.py:526
  263.9 31.5 %collective-permute-start.24 = (bf16[8,32,2304]{2,1,0:T(8,128)(2,1)}, bf16[8,32,2304]{2,1,0:T(8,128)(2,1)}, u32[]{:S(2)}, u32[]{:S(2)}) collective-permute-start(bf16[8,32,2304]{2,1,0:T(8,128)(2,1)} %get-tuple-element.119), channel_id=1, source_target_pairs={{0,1},{1,0},{2,3},{3,2},{4,5},{5,4},{6,7},{7,6},{8,9},{9,8},{10,11... | collective-permute-start | bytes 3538952 | tf_op jit(solution)/shard_map/ppermute | solution.py:526
  264.1 31.3 %collective-permute-start.25 = (bf16[8,32,2304]{2,1,0:T(8,128)(2,1)}, bf16[8,32,2304]{2,1,0:T(8,128)(2,1)}, u32[]{:S(2)}, u32[]{:S(2)}) collective-permute-start(bf16[8,32,2304]{2,1,0:T(8,128)(2,1)} %get-tuple-element.120), channel_id=1, source_target_pairs={{0,3},{1,2},{2,1},{3,0},{4,7},{5,6},{6,5},{7,4},{8,11},{9,10},{10,... | collective-permute-start | bytes 3538952 | tf_op jit(solution)/shard_map/ppermute | solution.py:526
  266.4 29.1 %collective-permute-start.26 = (bf16[8,32,2304]{2,1,0:T(8,128)(2,1)}, bf16[8,32,2304]{2,1,0:T(8,128)(2,1)}, u32[]{:S(2)}, u32[]{:S(2)}) collective-permute-start(bf16[8,32,2304]{2,1,0:T(8,128)(2,1)} %get-tuple-element.121), channel_id=1, source_target_pairs={{0,4},{1,5},{2,6},{3,7},{4,0},{5,1},{6,2},{7,3},{8,12},{9,13},{10,... | collective-permute-start | bytes 3538952 | tf_op jit(solution)/shard_map/ppermute | solution.py:526
  278.5 1.4 copy-start
  295.5 1.0 copy-start.16
Sparse Core Ops, SparseCore 0:
  11.7 81.3 all-gather.6
Sparse Core Ops, SparseCore 1:
  54.2 67.5 all-reduce.1
  123.2 66.0 all-gather.8
  193.2 78.3 all-gather.10

commit v6 on v5

--- a/solution.py
+++ b/solution.py
@@ -11,7 +11,7 @@
 F32 = jnp.float32
 HALO = 16
 MIB = 1024 * 1024
-VMEM_LIMIT = 60 * MIB
+VMEM_LIMIT = 127 * MIB // 2
 EXTRA = 128
 
 
@@ -266,15 +266,9 @@
                 buffer[quarter, index, core * capacity : (core + 1) * capacity] = picked[
                     index * capacity : (index + 1) * capacity
                 ]
-        for part in range(2):
-            at = 2 * quarter + part
-            copy = pltpu.make_async_copy(
-                buffer.at[quarter, pl.ds(part * count // 2, count // 2)],
-                out_refs[at],
-                sems.at[at],
-            )
-            copy.start()
-            copies.append(copy)
+        copy = pltpu.make_async_copy(buffer.at[quarter], out_refs[quarter], sems.at[quarter])
+        copy.start()
+        copies.append(copy)
     for copy in copies:
         copy.wait()
 
@@ -283,7 +277,7 @@
     dim = flows[0].shape[1]
     rows, count = 2 * capacity, len(turns[0])
     whole = lambda array: pl.BlockSpec(array.shape, lambda i, p: (0,) * array.ndim)
-    outs = 2 * len(turns)
+    outs = len(turns)
     return pl.pallas_call(
         functools.partial(pick_grad_kernel, per_token, capacity, n_exp, turns),
         grid_spec=pltpu.PrefetchScalarGridSpec(
@@ -296,7 +290,7 @@
                 pltpu.SemaphoreType.DMA((outs,)),
             ],
         ),
-        out_shape=[jax.ShapeDtypeStruct((count // 2, rows, dim), BF16)] * outs,
+        out_shape=[jax.ShapeDtypeStruct((count, rows, dim), BF16)] * outs,
         compiler_params=pltpu.CompilerParams(vmem_limit_bytes=VMEM_LIMIT),
         cost_estimate=call_cost(
             2 * len(turns) * count * rows * tables.shape[2] * dim,
@@ -323,8 +317,8 @@
     sig = jax.nn.sigmoid(gate)
     silu = gate * sig
     act_ref[...] = (silu * up).astype(BF16).T
-    gate_ref[...] = up * sig * (1.0 + gate * (1.0 - sig))
-    up_ref[...] = silu
+    gate_ref[...] = (up * sig * (1.0 + gate * (1.0 - sig))).astype(BF16)
+    up_ref[...] = silu.astype(BF16)
 
 
 def expert_forward(pieces, weight, hidden, shifts, parts, part, before):
@@ -358,8 +352,8 @@
         out_shape=[
             jax.ShapeDtypeStruct((dim, total), BF16),
             jax.ShapeDtypeStruct((hidden, total), BF16),
-            jax.ShapeDtypeStruct((total, hidden), F32),
-            jax.ShapeDtypeStruct((total, hidden), F32),
+            jax.ShapeDtypeStruct((total, hidden), BF16),
+            jax.ShapeDtypeStruct((total, hidden), BF16),
         ],
         input_output_aliases={sources + 2 + i: i for i in range(len(before))},
         compiler_params=pltpu.CompilerParams(vmem_limit_bytes=VMEM_LIMIT),
@@ -405,8 +399,8 @@
     def _():
         where = pl.ds(pl.multiple_of(step * tile, tile), tile)
         act_grad = jnp.dot(grads_all[where], weight_ref[...], preferred_element_type=F32)
-        hidden_all[where, :hidden] = (act_grad * gate_ref[...]).astype(BF16)
-        hidden_all[where, hidden:] = (act_grad * up_ref[...]).astype(BF16)
+        hidden_all[where, :hidden] = (act_grad * gate_ref[...].astype(F32)).astype(BF16)
+        hidden_all[where, hidden:] = (act_grad * up_ref[...].astype(F32)).astype(BF16)
 
     @pl.when(step >= row_steps)
     def _():
@@ -607,8 +601,6 @@
     weight_far = swap(qkv_weight, "seq", 1)
 
     table = jnp.concatenate([routes.astype(F32), route_weights], 1).T
-    tables = jnp.broadcast_to(table[None], (n_seq,) + table.shape)
-    tables = lax.all_to_all(tables, "seq", split_axis=0, concat_axis=0, tiled=True)
     normed = norm_rows(resid, norm_gain, routes.T)
     normed, conv_weight = lax.optimization_barrier((normed, conv_weight))
     exp_normed = lax.all_gather(normed, "exp")
@@ -620,12 +612,15 @@
     local_grad, local_keep, local_send = conv_back(
         place, qkv_in, low, high, qkv_grad, grad_high, ids.reshape(-1, 1), conv_weight, tokens
     )
-    local_send, tables = lax.optimization_barrier((local_send, tables))
     local_got = swap(local_send, "seq", 1)
     partial = project(place, local_keep, local_got, qkv_weight, weight_far, out_grad)
+    table, partial = lax.optimization_barrier((table, partial))
+    tables = jnp.broadcast_to(table[None], (n_seq,) + table.shape)
+    tables = lax.all_to_all(tables, "seq", split_axis=0, concat_axis=0, tiled=True)
     same_core = [[s for s in range(n_seq) if s % 2 == core] for core in range(2)]
     flow = lax.psum(partial, "seq", axis_index_groups=same_core)
 
+    exp_normed, tables = lax.optimization_barrier((exp_normed, tables))
     flips_a, flips_b = flips_of(0), flips_of(1)
     shifts = [(seq_index < seq_index ^ 2 * f).astype(jnp.int32) * 4 for f in flips_b]
     shifts = jnp.stack(shifts)
@@ -657,23 +652,30 @@
     quarters = len(flips)
     orders = [flips[k:] + flips[:k] for k in range(quarters)]
     bit_rows = [tuple((j >> (3 - b)) & 1 for b in range(4)) for j in range(n_exp)]
-    turns = tuple(tuple(mask_of(order, bits) for bits in bit_rows) for order in orders)
-    sends = pick_grad(place, tables, (flow, flow_far), turns, n_exp, per_token, capacity)
-
+    turns = [[mask_of(order, bits) for bits in bit_rows] for order in orders]
+    half = n_exp // 2
+    flows = (flow, flow_far)
+    sends = pick_grad(
+        place, tables, flows, [t[half:] for t in turns], n_exp, per_token, capacity
+    )
+    keeps = pick_grad(
+        place, tables, flows, [t[:half] for t in turns], n_exp, per_token, capacity
+    )
     streams = range(quarters)
-    keeps = [sends[2 * k] for k in streams]
-    firsts = [swap(sends[2 * k + 1], "exp", orders[k][0]) for k in streams]
+    firsts = [swap(sends[k], "exp", orders[k][0]) for k in streams]
     messages = merge(shifts, [second_parts(keeps[k], firsts[k]) for k in streams])
     seconds = [swap(messages[k], "exp", orders[k][1]) for k in streams]
+    thirds_out = merge(shifts, [third_parts(keeps[k], firsts[k], seconds[k]) for k in streams])
+    thirds = [swap(thirds_out[k], "exp", orders[k][2]) for k in streams]
     (message_a,) = merge(
         shifts,
         [[(keep_a, (1,), None), (far_a, (1,), None), (first_a, (1, 3), None)]],
-        messages,
+        thirds_out,
     )
     (message_b,) = merge(
         shifts,
         [[(keep_b, (1,), None), (far_b, (1,), None), (first_b, (1, 3), 0)]],
-        messages,
+        thirds_out,
     )
     second_a = swap(message_a, "seq", 2 * flips_a[1])
     second_b = swap_gather(message_b, "seq", 2 * flips_b[1])
@@ -683,8 +685,6 @@
         [(second_a, i, None) for i in range(4)],
         [(second_b, i, 1) for i in range(4)],
     ]
-    messages = merge(shifts, [third_parts(keeps[k], firsts[k], seconds[k]) for k in streams])
-    thirds = [swap(messages[k], "exp", orders[k][2]) for k in streams]
     results = ()
     for part, pieces in enumerate(calls):
         results = expert_forward(

time: 335 us -> 351 us (1.048)
  blocking collectives: 0 us -> 9.59 us
  local copies, waits for them, and re-layouts: 16 us -> 7.36 us
  waiting for transfers between devices: 127 us -> 135 us
  starting transfers between devices: 39.4 us -> 43.9 us
    all_to_all x1, waiting for transfers between devices: 9.41 us -> 25.1 us  [per_device(): lax.all_to_all(local_grad, 'seq', split_axis=0, concat_axis=1, tiled=True)]
    all_gather x2, waiting for transfers between devices: 13.8 us -> 0.04 us  [swap_gather(): both = lax.all_gather(array, axis, axis_index_groups=groups)]
    ppermute x25, waiting for transfers between devices: 60.2 us -> 71.8 us  [swap(): return lax.ppermute(array, axis, [(i, i ^ flip) for i in range(count)])]
    all_to_all x0 -> x1, blocking collectives: none -> 9.59 us  [per_device(): lax.all_to_all(tables, 'seq', split_axis=0, concat_axis=0, tiled=True)]
    all_to_all x1, starting transfers between devices: 7.25 us -> 16.1 us  [per_device(): lax.all_to_all(local_grad, 'seq', split_axis=0, concat_axis=1, tiled=True)]
    unnamed x36 -> x12, local copies, waits for them, and re-layouts: 8.64 us -> 0.62 us
    all_gather x1, waiting for transfers between devices: 38.9 us -> 33.3 us  [per_device(): exp_normed = lax.all_gather(normed, 'exp')]
    all_to_all x1 -> x0, starting transfers between devices: 4.77 us -> none  [per_device(): lax.all_to_all(tables, 'seq', split_axis=0, concat_axis=0, tiled=True)]
  transfers between devices with their start and end apart: 34 -> 33, of which waited for: 19 -> 16; matrix products, arithmetic and copies ran while one was open for 2% -> 2% of each run, Pallas kernels for 31% -> 30%
where the time goes in v6:
time: 351 us; the launch traced here: 349 us
  Pallas kernels  137 us (39%)
  waiting for transfers between devices  135 us (38%)
  starting transfers between devices  43.9 us (13%)
  between operations  15.9 us (5%)
  blocking collectives  9.59 us (3%)
  local copies, waits for them, and re-layouts  7.36 us (2%)
    ppermute x25, waiting for transfers between devices, swap(): return lax.ppermute(array, axis, [(i, i ^ flip) for i in range(count)])  71.8 us
    all_gather x1, waiting for transfers between devices, per_device(): exp_normed = lax.all_gather(normed, 'exp')  33.3 us
    pallas_call x4, Pallas kernels, expert_forward(): pl.pallas_call(functools.partial(forward_kernel, sources), grid_spec=pltp...  30.6 us
    pallas_call x1, Pallas kernels, expert_backward(): pl.pallas_call(functools.partial(backward_kernel, places, len(arrays)), g...  29.1 us
    pallas_call x6, Pallas kernels, merge(): pl.pallas_call(functools.partial(merge_kernel, tuple(plans), len(arrays))...  27.6 us
    all_to_all x1, waiting for transfers between devices, per_device(): lax.all_to_all(local_grad, 'seq', split_axis=0, concat_axis=1, tiled=True)  25.1 us
    ppermute x25, starting transfers between devices, swap(): return lax.ppermute(array, axis, [(i, i ^ flip) for i in range(count)])  21.9 us
    all_to_all x1, starting transfers between devices, per_device(): lax.all_to_all(local_grad, 'seq', split_axis=0, concat_axis=1, tiled=True)  16.1 us
  transfers between devices with their start and end apart: 33, of which 16 were waited for; matrix products, arithmetic and copies ran while one was open for 2% of the time, Pallas kernels for 30%

profile of v6, /device:TPU:1, one launch (start us, length us, event | category | flops | bytes accessed | tf_op | source)
XLA Modules:
  0.0 349.3 jit_solution(8279109763261912861)
XLA Ops:
  8.1 1.3 reshape.21.gain_ref
  9.4 2.2 norm_rows.1
  11.6 1.5 collective-permute-start.4
  13.1 0.8 fusion
  13.9 3.2 collective-permute-start
  17.0 1.3 collective-permute-start.1
  18.3 0.7 slice.11
  19.1 1.3 collective-permute-start.2
  20.4 0.6 pad_add_fusion.place_ref
  21.0 0.1 concatenate.7
  21.2 1.0 reshape.29.ids_ref
  22.3 2.0 collective-permute-done.2.grad_high_ref
  24.3 0.6 copy-done.3
  24.9 12.8 %conv_back.1 = (bf16[1024,768]{1,0:T(8,128)(2,1)}, bf16[512,768]{1,0:T(8,128)(2,1)}, bf16[512,768]{1,0:T(8,128)(2,1)}) custom-call(s32[2]{0:T(128)} %pad_add_fusion.place_ref, bf16[1024,768]{1,0:T(8,128)(2,1)} %in_ref.1, bf16[16,768]{1,0:T(8,128)(2,1)} %copy-done.1, bf16[16,768]{1,0:T(8,128)(2,1)} %copy-done.2, bf16[1024,768]{1,0:T(8,128)(2,1)} %grad_ref.1, ...), custom_call_target="tpu_custom_call" | custom-call | flops 31457280 | bytes 6291456 | tf_op jit(solution)/shard_map/conv_back/pallas_call | solution.py:107
  37.6 1.3 collective-permute-start.3
  38.9 2.2 collective-permute-done.3.other_ref
  41.2 8.9 %project.1 = bf16[512,2304]{1,0:T(8,128)(2,1)} custom-call(s32[2]{0:T(128)} %pad_add_fusion.place_ref, bf16[512,768]{1,0:T(8,128)(2,1)} %get-tuple-element.71.own_ref, bf16[512,768]{1,0:T(8,128)(2,1)} %collective-permute-done.3.other_ref, bf16[768,2304]{1,0:T(8,128)(2,1)} %own_weight.1, bf16[768,2304]{1,0:T(8,128)(2,1)} %collective-permute-done.4.other_weight, ...), custom_call_target="tpu_custom_call" | custom-call | flops 3623878656 | bytes 11010048 | tf_op jit(solution)/shard_map/project/pallas_call | solution.py:157
  50.2 9.6 %all_to_all.24.tables_ref = f32[8,16,128]{2,1,0:T(8,128)} all-to-all(f32[8,16,128]{2,1,0:T(8,128)S(1)} %broadcast_in_dim.4), channel_id=1, replica_groups=mesh['seq'=8,'exp'=16] {'seq'}, dimensions={0} | all-to-all | bytes 131072 | tf_op jit(solution)/shard_map/all_to_all | solution.py:619
  59.8 33.3 %all-gather.7.cloned.1.call-done = bf16[2048,2432]{1,0:T(8,128)(2,1)} async-done(((bf16[128,2432]{1,0:T(8,128)(2,1)}), bf16[2048,2432]{1,0:T(8,128)(2,1)}) %all-gather.7.cloned.1.call-update) | async-done | bytes 9961488 | tf_op jit(solution)/shard_map/all_gather | solution.py:606
  93.1 12.3 %pick_norm.1 = (bf16[2,8,16,2304]{3,2,1,0:T(8,128)(2,1)}, bf16[2,8,16,2304]{3,2,1,0:T(8,128)(2,1)}, bf16[2,8,16,2304]{3,2,1,0:T(8,128)(2,1)}, bf16[2,8,16,2304]{...) custom-call(s32[2]{0:T(128)} %pad_add_fusion.place_ref, ...), custom_call_target="tpu_custom_call" | custom-call | flops 1207959552 | bytes 18874368 | tf_op jit(solution)/shard_map/pick_norm/pallas_call | solution.py:219
  105.4 0.7 collective-permute-start.7
  106.2 0.4 collective-permute-start.5
  106.7 0.7 pad_add_fusion.1.shift_ref.refs_0_
  107.4 1.5 collective-permute-done.7.refs_1_
  108.9 1.7 collective-permute-done.8.refs_3_
  110.6 4.6 %merge_rows.6 = (bf16[4,8,16,2304]{3,2,1,0:T(8,128)(2,1)}, bf16[4,8,16,2304]{3,2,1,0:T(8,128)(2,1)}) custom-call(s32[2]{0:T(128)} %pad_add_fusion.1.shift_ref.refs_0_, bf16[2,8,16,2304]{3,2,1,0:T(8,128)(2,1)} %get-tuple-element.79.refs_0_, bf16[2,8,16,2304]{3,2,1,0:T(8,128)(2,1)} %collective-permute-done.7.refs_1_, ...), custom_call_target="tpu_custom_call" | custom-call | bytes 9437184 | tf_op jit(solution)/shard_map/merge_rows/pallas_call | solution.py:498
  115.2 2.4 all-reduce.2.cloned.1.call-done.refs_0_
  117.6 0.8 collective-permute-start.9
  118.5 4.4 %collective-permute-done.9.refs_1_ = bf16[512,2304]{1,0:T(8,128)(2,1)} collective-permute-done((bf16[512,2304]{1,0:T(8,128)(2,1)}, bf16[512,2304]{1,0:T(8,128)(2,1)}, u32[]{:S(2)}, u32[]{:S(2)}) %collective-permute-start.9) | collective-permute-done | bytes 2359328 | tf_op jit(solution)/shard_map/ppermute | solution.py:520
  122.9 6.5 %pick_grad.3 = (bf16[8,32,2304]{2,1,0:T(8,128)(2,1)}, bf16[8,32,2304]{2,1,0:T(8,128)(2,1)}, bf16[8,32,2304]{2,1,0:T(8,128)(2,1)}, bf16[8,32,2304]{2,1,0:T(8,128)(2,1)}) custom-call(s32[2]{0:T(128)} %pad_add_fusion.place_ref, f32[8,16,128]{2,1,0:T(8,128)} %all_to_all.24.tables_ref, bf16[512,2304]{1,0:T(8,128)(2,1)} %all-reduce.2.cloned.1.call-done.refs_0_, ...), custom_call_target="tpu_custom_call" | custom-call | flops 603979776 | bytes 9437184 | tf_op jit(solution)/shard_map/pick_grad/pallas_call | solution.py:281
  129.4 1.3 collective-permute-start.10
  130.7 1.8 collective-permute-start.11
  132.5 1.3 collective-permute-start.12
  133.7 1.9 collective-permute-start.13
  135.7 6.5 %pick_grad.2 = (bf16[8,32,2304]{2,1,0:T(8,128)(2,1)}, bf16[8,32,2304]{2,1,0:T(8,128)(2,1)}, bf16[8,32,2304]{2,1,0:T(8,128)(2,1)}, bf16[8,32,2304]{2,1,0:T(8,128)(2,1)}) custom-call(s32[2]{0:T(128)} %pad_add_fusion.place_ref, f32[8,16,128]{2,1,0:T(8,128)} %all_to_all.24.tables_ref, bf16[512,2304]{1,0:T(8,128)(2,1)} %all-reduce.2.cloned.1.call-done.refs_0_, ...), custom_call_target="tpu_custom_call" | custom-call | flops 603979776 | bytes 9437184 | tf_op jit(solution)/shard_map/pick_grad/pallas_call | solution.py:281
  142.1 14.9 %collective-permute-done.10.refs_1_ = bf16[8,32,2304]{2,1,0:T(8,128)(2,1)} collective-permute-done((bf16[8,32,2304]{2,1,0:T(8,128)(2,1)}, bf16[8,32,2304]{2,1,0:T(8,128)(2,1)}, u32[]{:S(2)}, u32[]{:S(2)}) %collective-permute-start.10) | collective-permute-done | bytes 1179680 | tf_op jit(solution)/shard_map/ppermute | solution.py:520
  157.0 2.0 collective-permute-done.11.refs_3_.refs_4_.refs_5_.refs_6_
  159.1 0.3 collective-permute-done.12.refs_5_.refs_7_.refs_9_.refs_11_
  159.3 2.2 collective-permute-done.13.refs_7_.refs_10_.refs_13_.refs_16_
  161.5 5.2 %merge_rows.7 = (bf16[8,32,2304]{2,1,0:T(8,128)(2,1)}, bf16[8,32,2304]{2,1,0:T(8,128)(2,1)}, bf16[8,32,2304]{2,1,0:T(8,128)(2,1)}, bf16[8,32,2304]{2,1,0:T(8,128)(2,1)}) custom-call(s32[2]{0:T(128)} %pad_add_fusion.1.shift_ref.refs_0_, bf16[8,32,2304]{2,1,0:T(8,128)(2,1)} %get-tuple-element.88.refs_0_, bf16[8,32,2304]{2,1,0:T(8,128)(2,1)} %collective-permute-done.10.refs_1_, ...), custom_call_target="tpu_custom_call" | custom-call | bytes 9437184 | tf_op jit(solution)/shard_map/merge_rows/pallas_call | solution.py:498
  166.7 1.0 collective-permute-start.14
  167.7 1.9 collective-permute-start.17
  169.6 24.0 %collective-permute-done.14.refs_2_ = bf16[8,32,2304]{2,1,0:T(8,128)(2,1)} collective-permute-done((bf16[8,32,2304]{2,1,0:T(8,128)(2,1)}, bf16[8,32,2304]{2,1,0:T(8,128)(2,1)}, u32[]{:S(2)}, u32[]{:S(2)}) %collective-permute-start.14) | collective-permute-done | bytes 1179680 | tf_op jit(solution)/shard_map/ppermute | solution.py:520
  193.6 0.6 collective-permute-done.17.refs_8_.refs_10_.refs_12_
  194.3 0.4 collective-permute-done.18.refs_11_.refs_14_.refs_17_
  194.7 5.1 %merge_rows.8 = (bf16[8,32,2304]{2,1,0:T(8,128)(2,1)}, bf16[8,32,2304]{2,1,0:T(8,128)(2,1)}, bf16[8,32,2304]{2,1,0:T(8,128)(2,1)}, bf16[8,32,2304]{2,1,0:T(8,128)(2,1)}) custom-call(s32[2]{0:T(128)} %pad_add_fusion.1.shift_ref.refs_0_, bf16[8,32,2304]{2,1,0:T(8,128)(2,1)} %get-tuple-element.88.refs_0_, bf16[8,32,2304]{2,1,0:T(8,128)(2,1)} %collective-permute-done.10.refs_1_, ...), custom_call_target="tpu_custom_call" | custom-call | bytes 9437184 | tf_op jit(solution)/shard_map/merge_rows/pallas_call | solution.py:498
  199.9 3.7 %merge_rows.10 = bf16[4,8,16,2304]{3,2,1,0:T(8,128)(2,1)} custom-call(s32[2]{0:T(128)} %pad_add_fusion.1.shift_ref.refs_0_, bf16[2,8,16,2304]{3,2,1,0:T(8,128)(2,1)} %get-tuple-element.97.refs_1_.refs_0_, bf16[2,8,16,2304]{3,2,1,0:T(8,128)(2,1)} %collective-permute-done.6.refs_2_.refs_1_, ...), custom_call_target="tpu_custom_call" | custom-call | bytes 4718592 | tf_op jit(solution)/shard_map/merge_rows/pallas_call | solution.py:498
  203.6 17.5 %collective-permute-done.15.refs_3_.refs_4_.refs_2_ = bf16[4,8,16,2304]{3,2,1,0:T(8,128)(2,1)} collective-permute-done((bf16[4,8,16,2304]{3,2,1,0:T(8,128)(2,1)}, bf16[4,8,16,2304]{3,2,1,0:T(8,128)(2,1)}, u32[]{:S(2)}, u32[]{:S(2)}) %collective-permute-start.15) | collective-permute-done | bytes 2359328 | tf_op jit(solution)/shard_map/ppermute | solution.py:520
  221.1 3.7 %merge_rows.11 = bf16[4,8,16,2304]{3,2,1,0:T(8,128)(2,1)} custom-call(s32[2]{0:T(128)} %pad_add_fusion.1.shift_ref.refs_0_, bf16[2,8,16,2304]{3,2,1,0:T(8,128)(2,1)} %get-tuple-element.100.refs_1_.refs_0_, bf16[2,8,16,2304]{3,2,1,0:T(8,128)(2,1)} %collective-permute-done.5.refs_2_.refs_1_, ...), custom_call_target="tpu_custom_call" | custom-call | bytes 4718592 | tf_op jit(solution)/shard_map/merge_rows/pallas_call | solution.py:498
  225.0 0.3 collective-permute-start.19
  225.3 0.6 collective-permute-start.20
  225.9 1.2 collective-permute-start.21
  227.1 1.8 collective-permute-start.22
  228.9 16.1 %all-to-all-start.1 = ((bf16[8,128,768]{2,1,0:T(8,128)(2,1)}), bf16[8,128,768]{2,1,0:T(8,128)(2,1)}, u32[]{:S(2)}, u32[]{:S(2)}) async-start(bf16[8,128,768]{2,1,0:T(8,128)(2,1)} %bitcast.21), calls=%async_computation.1 | async-start | bytes 3145728 | tf_op jit(solution)/shard_map/all_to_all | solution.py:648
  244.9 7.6 %expert_forward.4 = (bf16[2304,2048]{1,0:T(8,128)(2,1)}, bf16[512,2048]{1,0:T(8,128)(2,1)}, bf16[2048,512]{1,0:T(8,128)(2,1)}, bf16[2048,512]{1,0:T(8,128)(2,1)}) custom-call(s32[2]{0:T(128)} %pad_add_fusion.1.shift_ref.refs_0_, bf16[2,8,16,2304]{3,2,1,0:T(8,128)(2,1)} %get-tuple-element.100.refs_1_.refs_0_, ...), custom_call_target="tpu_custom_call" | custom-call | flops 2415919104 | bytes 7340032 | tf_op jit(solution)/shard_map/expert_forward/pallas_call | solution.py:341
  252.5 7.7 %expert_forward.5 = (bf16[2304,2048]{1,0:T(8,128)(2,1)}, bf16[512,2048]{1,0:T(8,128)(2,1)}, bf16[2048,512]{1,0:T(8,128)(2,1)}, bf16[2048,512]{1,0:T(8,128)(2,1)}) custom-call(s32[2]{0:T(128)} %pad_add_fusion.1.shift_ref.refs_0_, ...), custom_call_target="tpu_custom_call", output_to_operand_aliasing={{0}: (6, {}), {1}: (7, {}), {2}: (8, {}), {3}: (9, {})} | custom-call | flops 2415919104 | bytes 7340032 | tf_op jit(solution)/shard_map/expert_forward/pallas_call | solution.py:341
  260.3 5.2 %merge_rows.9 = (bf16[8,32,2304]{2,1,0:T(8,128)(2,1)}, bf16[8,32,2304]{2,1,0:T(8,128)(2,1)}, bf16[8,32,2304]{2,1,0:T(8,128)(2,1)}, bf16[8,32,2304]{2,1,0:T(8,128)(2,1)}) custom-call(s32[2]{0:T(128)} %pad_add_fusion.1.shift_ref.refs_0_, bf16[8,32,2304]{2,1,0:T(8,128)(2,1)} %get-tuple-element.88.refs_0_, bf16[8,32,2304]{2,1,0:T(8,128)(2,1)} %collective-permute-done.10.refs_1_, ...), custom_call_target="tpu_custom_call" | custom-call | bytes 9437184 | tf_op jit(solution)/shard_map/merge_rows/pallas_call | solution.py:498
  265.4 3.0 collective-permute-start.23
  268.5 0.9 collective-permute-start.25
  269.4 25.1 %all-to-all-done.1 = bf16[8,128,768]{2,1,0:T(8,128)(2,1)} async-done(((bf16[8,128,768]{2,1,0:T(8,128)(2,1)}), bf16[8,128,768]{2,1,0:T(8,128)(2,1)}, u32[]{:S(2)}, u32[]{:S(2)}) %all-to-all-start.1) | async-done | bytes 1572896 | tf_op jit(solution)/shard_map/all_to_all | solution.py:648
  294.5 2.7 copy.30
  297.2 7.6 %expert_forward.6 = (bf16[2304,2048]{1,0:T(8,128)(2,1)}, bf16[512,2048]{1,0:T(8,128)(2,1)}, bf16[2048,512]{1,0:T(8,128)(2,1)}, bf16[2048,512]{1,0:T(8,128)(2,1)}) custom-call(s32[2]{0:T(128)} %pad_add_fusion.1.shift_ref.refs_0_, ...), custom_call_target="tpu_custom_call", output_to_operand_aliasing={{0}: (6, {}), {1}: (7, {}), {2}: (8, {}), {3}: (9, {})} | custom-call | flops 2415919104 | bytes 7340032 | tf_op jit(solution)/shard_map/expert_forward/pallas_call | solution.py:341
  304.9 7.7 %expert_forward.7 = (bf16[2304,2048]{1,0:T(8,128)(2,1)}, bf16[512,2048]{1,0:T(8,128)(2,1)}, bf16[2048,512]{1,0:T(8,128)(2,1)}, bf16[2048,512]{1,0:T(8,128)(2,1)}) custom-call(s32[2]{0:T(128)} %pad_add_fusion.1.shift_ref.refs_0_, ...), custom_call_target="tpu_custom_call", output_to_operand_aliasing={{0}: (6, {}), {1}: (7, {}), {2}: (8, {}), {3}: (9, {})} | custom-call | flops 2415919104 | bytes 7340032 | tf_op jit(solution)/shard_map/expert_forward/pallas_call | solution.py:341
  312.6 29.1 %expert_backward.1 = bf16[2304,1536]{1,0:T(8,128)(2,1)} custom-call(bf16[8,32,2304]{2,1,0:T(8,128)(2,1)} %get-tuple-element.88.refs_0_, bf16[8,32,2304]{2,1,0:T(8,128)(2,1)} %collective-permute-done.10.refs_1_, bf16[8,32,2304]{2,1,0:T(8,128)(2,1)} %collective-permute-done.14.refs_2_, bf16[8,32,2304]{2,1,0:T(8,128)(2,1)} %collective-permute-done.19.refs_3_, ...), custom_call_target="tpu_custom_call" | custom-call | flops 19327352832 | bytes 39845888 | tf_op jit(solution)/shard_map/expert_backward/pallas_call | solution.py:424
  (49 shorter events, 0.7 us)
Async XLA Ops:
  8.0 13.0 %copy-start = (s32[16384]{0:T(1024)S(1)}, s32[16384]{0:T(1024)}, u32[]{:S(2)}) copy-start(s32[16384]{0:T(1024)} %param.14) | copy-start | bytes 196612
  8.0 85.0 %all-gather.7.cloned.1.call-start = ((), (), s32[]{:S(2)}) async-start(), calls=%async_computation.3 | async-start | bytes 10584064 | tf_op jit(solution)/shard_map/all_gather | solution.py:606
  11.5 106.1 %all-reduce.2.cloned.1.call-start = ((), (), s32[]{:S(2)}) async-start(), calls=%async_computation.2 | async-start | bytes 4718592 | tf_op jit(solution)/shard_map/psum | solution.py:621
  11.6 29.6 %collective-permute-start.4 = (bf16[768,2304]{1,0:T(8,128)(2,1)}, bf16[768,2304]{1,0:T(8,128)(2,1)}, u32[]{:S(2)}, u32[]{:S(2)}) collective-permute-start(bf16[768,2304]{1,0:T(8,128)(2,1)} %own_weight.1), channel_id=1, source_target_pairs={{0,16},{16,0},{32,48},{48,32},{64,80},{80,64},{96,112},{112,96},{1... | collective-permute-start | bytes 10616840 | tf_op jit(solution)/shard_map/ppermute | solution.py:520
  13.9 8.4 %collective-permute-start = (bf16[16,768]{1,0:T(8,128)(2,1)S(1)}, bf16[16,768]{1,0:T(8,128)(2,1)S(1)}, u32[]{:S(2)}, u32[]{:S(2)}) collective-permute-start(bf16[16,768]{1,0:T(8,128)(2,1)S(1)} %get-tuple-element.139), channel_id=1, source_target_pairs={{0,1},{1,2},{2,3},{3,4},{4,5},{5,6},{6,7},{7,8},{8,9},{9,10},{10,1... | collective-permute-start | bytes 73736 | tf_op jit(solution)/shard_map/ppermute | solution.py:598
  17.0 5.2 %collective-permute-start.1 = (bf16[16,768]{1,0:T(8,128)(2,1)S(1)}, bf16[16,768]{1,0:T(8,128)(2,1)S(1)}, u32[]{:S(2)}, u32[]{:S(2)}) collective-permute-start(bf16[16,768]{1,0:T(8,128)(2,1)S(1)} %get-tuple-element.138), channel_id=1, source_target_pairs={{1,0},{2,1},{3,2},{4,3},{5,4},{6,5},{7,6},{8,7},{9,8},{10,9},{11,1... | collective-permute-start | bytes 73736 | tf_op jit(solution)/shard_map/ppermute | solution.py:599
  19.1 5.2 %collective-permute-start.2 = (bf16[16,768]{1,0:T(8,128)(2,1)S(1)}, bf16[16,768]{1,0:T(8,128)(2,1)S(1)}, u32[]{:S(2)}, u32[]{:S(2)}) collective-permute-start(bf16[16,768]{1,0:T(8,128)(2,1)S(1)} %slice.11), channel_id=1, source_target_pairs={{1,0},{2,1},{3,2},{4,3},{5,4},{6,5},{7,6},{8,7},{9,8},{10,9},{11,1... | collective-permute-start | bytes 73736 | tf_op jit(solution)/shard_map/ppermute | solution.py:600
  22.2 16.7 %copy-start.4 = (s32[128,8]{0,1:T(8,128)S(1)}, s32[128,8]{0,1:T(8,128)}, u32[]{:S(2)}) copy-start(s32[128,8]{0,1:T(8,128)} %param.19) | copy-start | bytes 12292
  22.2 16.7 %copy-start.5 = (f32[128,8]{0,1:T(8,128)S(1)}, f32[128,8]{0,1:T(8,128)}, u32[]{:S(2)}) copy-start(f32[128,8]{0,1:T(8,128)} %param.20) | copy-start | bytes 12292
  22.2 2.0 copy-start.1
  22.2 2.0 copy-start.2
  24.3 0.6 copy-start.3
  37.6 3.5 %collective-permute-start.3 = (bf16[512,768]{1,0:T(8,128)(2,1)}, bf16[512,768]{1,0:T(8,128)(2,1)}, u32[]{:S(2)}, u32[]{:S(2)}) collective-permute-start(bf16[512,768]{1,0:T(8,128)(2,1)} %get-tuple-element.72), channel_id=1, source_target_pairs={{0,16},{16,0},{32,48},{48,32},{64,80},{80,64},{96,112},{112,96},{1... | collective-permute-start | bytes 2359304 | tf_op jit(solution)/shard_map/ppermute | solution.py:520
  50.1 149.8 %all-gather.9.cloned.1.call-start = ((), (), s32[]{:S(2)}) async-start(), calls=%async_computation.4 | async-start | bytes 7077888 | tf_op jit(solution)/shard_map/all_gather | solution.py:534
  105.4 3.5 %collective-permute-start.7 = (bf16[2,8,16,2304]{3,2,1,0:T(8,128)(2,1)}, bf16[2,8,16,2304]{3,2,1,0:T(8,128)(2,1)}, u32[]{:S(2)}, u32[]{:S(2)}) collective-permute-start(bf16[2,8,16,2304]{3,2,1,0:T(8,128)(2,1)} %get-tuple-element.80), channel_id=1, source_target_pairs={{0,16},{16,0},{32,48},{48,32},{64,80},{80,64},{96,112},{112,96},{1... | collective-permute-start | bytes 3538952 | tf_op jit(solution)/shard_map/ppermute | solution.py:520
  106.1 4.5 %collective-permute-start.8 = (bf16[2,8,16,2304]{3,2,1,0:T(8,128)(2,1)}, bf16[2,8,16,2304]{3,2,1,0:T(8,128)(2,1)}, u32[]{:S(2)}, u32[]{:S(2)}) collective-permute-start(bf16[2,8,16,2304]{3,2,1,0:T(8,128)(2,1)} %get-tuple-element.82), channel_id=1, source_target_pairs={{0,16},{16,0},{32,48},{48,32},{64,80},{80,64},{96,112},{112,96},{1... | collective-permute-start | bytes 3538952 | tf_op jit(solution)/shard_map/ppermute | solution.py:520
  106.2 11.5 %collective-permute-start.5 = (bf16[2,8,16,2304]{3,2,1,0:T(8,128)(2,1)}, bf16[2,8,16,2304]{3,2,1,0:T(8,128)(2,1)}, u32[]{:S(2)}, u32[]{:S(2)}) collective-permute-start(bf16[2,8,16,2304]{3,2,1,0:T(8,128)(2,1)} %get-tuple-element.77), channel_id=1, source_target_pairs={{0,16},{16,0},{32,48},{48,32},{64,80},{80,64},{96,112},{112,96},{1... | collective-permute-start | bytes 3538952 | tf_op jit(solution)/shard_map/ppermute | solution.py:520
  106.6 11.0 %collective-permute-start.6 = (bf16[2,8,16,2304]{3,2,1,0:T(8,128)(2,1)}, bf16[2,8,16,2304]{3,2,1,0:T(8,128)(2,1)}, u32[]{:S(2)}, u32[]{:S(2)}) collective-permute-start(bf16[2,8,16,2304]{3,2,1,0:T(8,128)(2,1)} %get-tuple-element.78), channel_id=1, source_target_pairs={{0,16},{16,0},{32,48},{48,32},{64,80},{80,64},{96,112},{112,96},{1... | collective-permute-start | bytes 3538952 | tf_op jit(solution)/shard_map/ppermute | solution.py:520
  117.6 5.3 %collective-permute-start.9 = (bf16[512,2304]{1,0:T(8,128)(2,1)}, bf16[512,2304]{1,0:T(8,128)(2,1)}, u32[]{:S(2)}, u32[]{:S(2)}) collective-permute-start(bf16[512,2304]{1,0:T(8,128)(2,1)} %all-reduce.2.cloned.1.call-done.refs_0_), channel_id=1, source_target_pairs={{0,16},{16,0},{32,48},{48,32},{64,80},{80,64},{96,112},{112,96},{1... | collective-permute-start | bytes 7077896 | tf_op jit(solution)/shard_map/ppermute | solution.py:520
  118.4 186.4 %all-gather.11.cloned.1.call-start = ((), (), s32[]{:S(2)}) async-start(), calls=%async_computation.5 | async-start | bytes 7077888 | tf_op jit(solution)/shard_map/all_gather | solution.py:534
  129.4 27.6 %collective-permute-start.10 = (bf16[8,32,2304]{2,1,0:T(8,128)(2,1)}, bf16[8,32,2304]{2,1,0:T(8,128)(2,1)}, u32[]{:S(2)}, u32[]{:S(2)}) collective-permute-start(bf16[8,32,2304]{2,1,0:T(8,128)(2,1)} %get-tuple-element.89), channel_id=1, source_target_pairs={{0,1},{1,0},{2,3},{3,2},{4,5},{5,4},{6,7},{7,6},{8,9},{9,8},{10,11... | collective-permute-start | bytes 3538952 | tf_op jit(solution)/shard_map/ppermute | solution.py:520
  130.7 28.4 %collective-permute-start.11 = (bf16[8,32,2304]{2,1,0:T(8,128)(2,1)}, bf16[8,32,2304]{2,1,0:T(8,128)(2,1)}, u32[]{:S(2)}, u32[]{:S(2)}) collective-permute-start(bf16[8,32,2304]{2,1,0:T(8,128)(2,1)} %get-tuple-element.91), channel_id=1, source_target_pairs={{0,3},{1,2},{2,1},{3,0},{4,7},{5,6},{6,5},{7,4},{8,11},{9,10},{10,... | collective-permute-start | bytes 3538952 | tf_op jit(solution)/shard_map/ppermute | solution.py:520
  132.5 26.9 %collective-permute-start.12 = (bf16[8,32,2304]{2,1,0:T(8,128)(2,1)}, bf16[8,32,2304]{2,1,0:T(8,128)(2,1)}, u32[]{:S(2)}, u32[]{:S(2)}) collective-permute-start(bf16[8,32,2304]{2,1,0:T(8,128)(2,1)} %get-tuple-element.93), channel_id=1, source_target_pairs={{0,4},{1,5},{2,6},{3,7},{4,0},{5,1},{6,2},{7,3},{8,12},{9,13},{10,... | collective-permute-start | bytes 3538952 | tf_op jit(solution)/shard_map/ppermute | solution.py:520
  133.7 27.8 %collective-permute-start.13 = (bf16[8,32,2304]{2,1,0:T(8,128)(2,1)}, bf16[8,32,2304]{2,1,0:T(8,128)(2,1)}, u32[]{:S(2)}, u32[]{:S(2)}) collective-permute-start(bf16[8,32,2304]{2,1,0:T(8,128)(2,1)} %get-tuple-element.95), channel_id=1, source_target_pairs={{0,12},{1,13},{2,14},{3,15},{4,8},{5,9},{6,10},{7,11},{8,4},{9,5},... | collective-permute-start | bytes 3538952 | tf_op jit(solution)/shard_map/ppermute | solution.py:520
  166.7 26.9 %collective-permute-start.14 = (bf16[8,32,2304]{2,1,0:T(8,128)(2,1)}, bf16[8,32,2304]{2,1,0:T(8,128)(2,1)}, u32[]{:S(2)}, u32[]{:S(2)}) collective-permute-start(bf16[8,32,2304]{2,1,0:T(8,128)(2,1)} %get-tuple-element.96), channel_id=1, source_target_pairs={{0,3},{1,2},{2,1},{3,0},{4,7},{5,6},{6,5},{7,4},{8,11},{9,10},{10,... | collective-permute-start | bytes 3538952 | tf_op jit(solution)/shard_map/ppermute | solution.py:520
  167.7 25.9 %collective-permute-start.16 = (bf16[8,32,2304]{2,1,0:T(8,128)(2,1)}, bf16[8,32,2304]{2,1,0:T(8,128)(2,1)}, u32[]{:S(2)}, u32[]{:S(2)}) collective-permute-start(bf16[8,32,2304]{2,1,0:T(8,128)(2,1)} %get-tuple-element.111), channel_id=1, source_target_pairs={{0,4},{1,5},{2,6},{3,7},{4,0},{5,1},{6,2},{7,3},{8,12},{9,13},{10,... | collective-permute-start | bytes 3538952 | tf_op jit(solution)/shard_map/ppermute | solution.py:520
  167.7 26.6 %collective-permute-start.17 = (bf16[8,32,2304]{2,1,0:T(8,128)(2,1)}, bf16[8,32,2304]{2,1,0:T(8,128)(2,1)}, u32[]{:S(2)}, u32[]{:S(2)}) collective-permute-start(bf16[8,32,2304]{2,1,0:T(8,128)(2,1)} %get-tuple-element.112), channel_id=1, source_target_pairs={{0,12},{1,13},{2,14},{3,15},{4,8},{5,9},{6,10},{7,11},{8,4},{9,5},... | collective-permute-start | bytes 3538952 | tf_op jit(solution)/shard_map/ppermute | solution.py:520
  169.6 25.1 %collective-permute-start.18 = (bf16[8,32,2304]{2,1,0:T(8,128)(2,1)}, bf16[8,32,2304]{2,1,0:T(8,128)(2,1)}, u32[]{:S(2)}, u32[]{:S(2)}) collective-permute-start(bf16[8,32,2304]{2,1,0:T(8,128)(2,1)} %get-tuple-element.113), channel_id=1, source_target_pairs={{0,1},{1,0},{2,3},{3,2},{4,5},{5,4},{6,7},{7,6},{8,9},{9,8},{10,11... | collective-permute-start | bytes 3538952 | tf_op jit(solution)/shard_map/ppermute | solution.py:520
  169.6 51.5 %collective-permute-start.15 = (bf16[4,8,16,2304]{3,2,1,0:T(8,128)(2,1)}, bf16[4,8,16,2304]{3,2,1,0:T(8,128)(2,1)}, u32[]{:S(2)}, u32[]{:S(2)}) collective-permute-start(bf16[4,8,16,2304]{3,2,1,0:T(8,128)(2,1)} %get-tuple-element.102), channel_id=1, source_target_pairs={{0,32},{16,48},{32,0},{48,16},{64,96},{80,112},{96,64},{112,80},{1... | collective-permute-start | bytes 7077896 | tf_op jit(solution)/shard_map/ppermute | solution.py:520
  224.9 72.3 %collective-permute-start.27 = (bf16[4,8,16,2304]{3,2,1,0:T(8,128)(2,1)}, bf16[4,8,16,2304]{3,2,1,0:T(8,128)(2,1)}, u32[]{:S(2)}, u32[]{:S(2)}) collective-permute-start(bf16[4,8,16,2304]{3,2,1,0:T(8,128)(2,1)} %merge_rows.11), channel_id=1, source_target_pairs={{0,96},{16,112},{32,64},{48,80},{64,32},{80,48},{96,0},{112,16},{1... | collective-permute-start | bytes 7077896 | tf_op jit(solution)/shard_map/ppermute | solution.py:520
  225.0 35.3 %collective-permute-start.19 = (bf16[8,32,2304]{2,1,0:T(8,128)(2,1)}, bf16[8,32,2304]{2,1,0:T(8,128)(2,1)}, u32[]{:S(2)}, u32[]{:S(2)}) collective-permute-start(bf16[8,32,2304]{2,1,0:T(8,128)(2,1)} %get-tuple-element.114.refs_3_), channel_id=1, source_target_pairs={{0,4},{1,5},{2,6},{3,7},{4,0},{5,1},{6,2},{7,3},{8,12},{9,13},{10,... | collective-permute-start | bytes 3538952 | tf_op jit(solution)/shard_map/ppermute | solution.py:520
  225.3 35.0 %collective-permute-start.20 = (bf16[8,32,2304]{2,1,0:T(8,128)(2,1)}, bf16[8,32,2304]{2,1,0:T(8,128)(2,1)}, u32[]{:S(2)}, u32[]{:S(2)}) collective-permute-start(bf16[8,32,2304]{2,1,0:T(8,128)(2,1)} %get-tuple-element.115.refs_4_), channel_id=1, source_target_pairs={{0,12},{1,13},{2,14},{3,15},{4,8},{5,9},{6,10},{7,11},{8,4},{9,5},... | collective-permute-start | bytes 3538952 | tf_op jit(solution)/shard_map/ppermute | solution.py:520
  225.9 34.4 %collective-permute-start.21 = (bf16[8,32,2304]{2,1,0:T(8,128)(2,1)}, bf16[8,32,2304]{2,1,0:T(8,128)(2,1)}, u32[]{:S(2)}, u32[]{:S(2)}) collective-permute-start(bf16[8,32,2304]{2,1,0:T(8,128)(2,1)} %get-tuple-element.116.refs_5_), channel_id=1, source_target_pairs={{0,1},{1,0},{2,3},{3,2},{4,5},{5,4},{6,7},{7,6},{8,9},{9,8},{10,11... | collective-permute-start | bytes 3538952 | tf_op jit(solution)/shard_map/ppermute | solution.py:520
  227.1 33.2 %collective-permute-start.22 = (bf16[8,32,2304]{2,1,0:T(8,128)(2,1)}, bf16[8,32,2304]{2,1,0:T(8,128)(2,1)}, u32[]{:S(2)}, u32[]{:S(2)}) collective-permute-start(bf16[8,32,2304]{2,1,0:T(8,128)(2,1)} %get-tuple-element.117.refs_6_), channel_id=1, source_target_pairs={{0,3},{1,2},{2,1},{3,0},{4,7},{5,6},{6,5},{7,4},{8,11},{9,10},{10,... | collective-permute-start | bytes 3538952 | tf_op jit(solution)/shard_map/ppermute | solution.py:520
  228.9 65.6 %all-to-all-start.1 = ((bf16[8,128,768]{2,1,0:T(8,128)(2,1)}), bf16[8,128,768]{2,1,0:T(8,128)(2,1)}, u32[]{:S(2)}, u32[]{:S(2)}) async-start(bf16[8,128,768]{2,1,0:T(8,128)(2,1)} %bitcast.21), calls=%async_computation.1 | async-start | bytes 3145728 | tf_op jit(solution)/shard_map/all_to_all | solution.py:648
  265.4 47.1 %collective-permute-start.23 = (bf16[8,32,2304]{2,1,0:T(8,128)(2,1)}, bf16[8,32,2304]{2,1,0:T(8,128)(2,1)}, u32[]{:S(2)}, u32[]{:S(2)}) collective-permute-start(bf16[8,32,2304]{2,1,0:T(8,128)(2,1)} %get-tuple-element.122), channel_id=1, source_target_pairs={{0,12},{1,13},{2,14},{3,15},{4,8},{5,9},{6,10},{7,11},{8,4},{9,5},... | collective-permute-start | bytes 3538952 | tf_op jit(solution)/shard_map/ppermute | solution.py:520
  268.5 44.1 %collective-permute-start.24 = (bf16[8,32,2304]{2,1,0:T(8,128)(2,1)}, bf16[8,32,2304]{2,1,0:T(8,128)(2,1)}, u32[]{:S(2)}, u32[]{:S(2)}) collective-permute-start(bf16[8,32,2304]{2,1,0:T(8,128)(2,1)} %get-tuple-element.123), channel_id=1, source_target_pairs={{0,1},{1,0},{2,3},{3,2},{4,5},{5,4},{6,7},{7,6},{8,9},{9,8},{10,11... | collective-permute-start | bytes 3538952 | tf_op jit(solution)/shard_map/ppermute | solution.py:520
  268.5 44.1 %collective-permute-start.25 = (bf16[8,32,2304]{2,1,0:T(8,128)(2,1)}, bf16[8,32,2304]{2,1,0:T(8,128)(2,1)}, u32[]{:S(2)}, u32[]{:S(2)}) collective-permute-start(bf16[8,32,2304]{2,1,0:T(8,128)(2,1)} %get-tuple-element.124), channel_id=1, source_target_pairs={{0,3},{1,2},{2,1},{3,0},{4,7},{5,6},{6,5},{7,4},{8,11},{9,10},{10,... | collective-permute-start | bytes 3538952 | tf_op jit(solution)/shard_map/ppermute | solution.py:520
  269.4 43.2 %collective-permute-start.26 = (bf16[8,32,2304]{2,1,0:T(8,128)(2,1)}, bf16[8,32,2304]{2,1,0:T(8,128)(2,1)}, u32[]{:S(2)}, u32[]{:S(2)}) collective-permute-start(bf16[8,32,2304]{2,1,0:T(8,128)(2,1)} %get-tuple-element.125), channel_id=1, source_target_pairs={{0,4},{1,5},{2,6},{3,7},{4,0},{5,1},{6,2},{7,3},{8,12},{9,13},{10,... | collective-permute-start | bytes 3538952 | tf_op jit(solution)/shard_map/ppermute | solution.py:520
Sparse Core Ops, SparseCore 0:
  11.7 81.3 all-gather.6
Sparse Core Ops, SparseCore 1:
  50.2 67.4 all-reduce.1
  119.2 66.0 all-gather.8
  203.7 86.9 all-gather.10

commit v7 on v6

--- a/solution.py
+++ b/solution.py
@@ -234,8 +234,8 @@
     )(place, *[rows] * halves)
 
 
-def pick_grad_kernel(per_token, capacity, n_exp, turns, place_ref, tables_ref, *refs):
-    flow_refs, out_refs = refs[:2], refs[2:-2]
+def pick_grad_kernel(per_token, capacity, n_exp, turns, cores, place_ref, tables_ref, *refs):
+    flow_refs, out_refs = refs[: len(cores)], refs[-2 - len(turns) : -2]
     buffer, sems = refs[-2:]
     tokens = tables_ref.shape[2]
     copies = []
@@ -248,7 +248,7 @@
             ]
         )
         first = pl.multiple_of(((place_ref[0] >> 1) ^ quarter) * tokens, tokens)
-        for core in range(2):
+        for spot, core in enumerate(cores):
             table = tables_ref[place_ref[0] ^ (2 * quarter + core)]
             names = table[:per_token].astype(jnp.int32)
             picker, match = slot_picker(names, own, capacity)
@@ -259,45 +259,49 @@
             scales = jnp.sum(picker * scale[:, None, :], axis=2, keepdims=True)
             picker = picker.reshape(count * capacity, tokens).astype(BF16)
             picked = jnp.dot(
-                picker, flow_refs[core][pl.ds(first, tokens)], preferred_element_type=F32
+                picker, flow_refs[spot][pl.ds(first, tokens)], preferred_element_type=F32
             )
             picked = (picked * scales.reshape(count * capacity, 1)).astype(BF16)
-            for index in range(count):
-                buffer[quarter, index, core * capacity : (core + 1) * capacity] = picked[
-                    index * capacity : (index + 1) * capacity
-                ]
-        copy = pltpu.make_async_copy(buffer.at[quarter], out_refs[quarter], sems.at[quarter])
-        copy.start()
-        copies.append(copy)
+            buffer[quarter, spot] = picked.reshape(count, capacity, -1)
+            at = quarter * len(cores) + spot
+            copy = pltpu.make_async_copy(
+                buffer.at[quarter, spot],
+                out_refs[quarter].at[:, pl.ds(core * capacity, capacity)],
+                sems.at[at],
+            )
+            copy.start()
+            copies.append(copy)
     for copy in copies:
         copy.wait()
 
 
-def pick_grad(place, tables, flows, turns, n_exp, per_token, capacity):
+def pick_grad(place, tables, flows, cores, turns, n_exp, per_token, capacity, before=()):
     dim = flows[0].shape[1]
     rows, count = 2 * capacity, len(turns[0])
     whole = lambda array: pl.BlockSpec(array.shape, lambda i, p: (0,) * array.ndim)
+    any_spec = pl.BlockSpec(memory_space=pl.ANY)
     outs = len(turns)
     return pl.pallas_call(
-        functools.partial(pick_grad_kernel, per_token, capacity, n_exp, turns),
+        functools.partial(pick_grad_kernel, per_token, capacity, n_exp, turns, cores),
         grid_spec=pltpu.PrefetchScalarGridSpec(
             num_scalar_prefetch=1,
             grid=(1,),
-            in_specs=[whole(tables), whole(flows[0]), whole(flows[1])],
-            out_specs=[pl.BlockSpec(memory_space=pl.ANY)] * outs,
+            in_specs=[whole(tables)] + [whole(flow) for flow in flows] + [any_spec] * len(before),
+            out_specs=[any_spec] * outs,
             scratch_shapes=[
-                pltpu.VMEM((len(turns), count, rows, dim), BF16),
-                pltpu.SemaphoreType.DMA((outs,)),
+                pltpu.VMEM((outs, len(cores), count, capacity, dim), BF16),
+                pltpu.SemaphoreType.DMA((outs * len(cores),)),
             ],
         ),
         out_shape=[jax.ShapeDtypeStruct((count, rows, dim), BF16)] * outs,
+        input_output_aliases={2 + len(flows) + i: i for i in range(len(before))},
         compiler_params=pltpu.CompilerParams(vmem_limit_bytes=VMEM_LIMIT),
         cost_estimate=call_cost(
-            2 * len(turns) * count * rows * tables.shape[2] * dim,
-            4 * dim * (flows[0].shape[0] + len(turns) * count * rows // 2),
+            2 * outs * count * capacity * len(cores) * tables.shape[2] * dim,
+            2 * dim * len(cores) * (flows[0].shape[0] + outs * count * capacity),
         ),
         name="pick_grad",
-    )(place, tables, *flows)
+    )(place, tables, *flows, *before)
 
 
 def forward_kernel(sources, *refs):
@@ -622,7 +626,9 @@
 
     exp_normed, tables = lax.optimization_barrier((exp_normed, tables))
     flips_a, flips_b = flips_of(0), flips_of(1)
-    shifts = [(seq_index < seq_index ^ 2 * f).astype(jnp.int32) * 4 for f in flips_b]
+    shifts = [
+        (seq_index < seq_index ^ 2 * f).astype(jnp.int32) * 4 for f in flips_b
+    ]
     shifts = jnp.stack(shifts)
     turns = []
     for near in (flips_a, flips_b):
@@ -644,8 +650,10 @@
     flow, far_a, far_b, message_b, local_grad = lax.optimization_barrier(
         (flow, far_a, far_b, message_b, local_grad)
     )
+    qkv_parts = local_grad.reshape(n_seq, tokens, width)
+    qkv_parts = lax.all_to_all(qkv_parts, "seq", split_axis=0, concat_axis=0, tiled=True)
+    qkv_in_grad = qkv_parts.swapaxes(0, 1).reshape(tokens, n_seq * width)
     first_b = swap_gather(message_b, "seq", 2 * flips_b[0])
-    qkv_in_grad = lax.all_to_all(local_grad, "seq", split_axis=0, concat_axis=1, tiled=True)
     flow_far = swap(flow, "seq", 1)
 
     flips = (1, 3, 4, 12)
@@ -654,29 +662,28 @@
     bit_rows = [tuple((j >> (3 - b)) & 1 for b in range(4)) for j in range(n_exp)]
     turns = [[mask_of(order, bits) for bits in bit_rows] for order in orders]
     half = n_exp // 2
-    flows = (flow, flow_far)
-    sends = pick_grad(
-        place, tables, flows, [t[half:] for t in turns], n_exp, per_token, capacity
-    )
+    late = [t[half:] for t in turns]
+    sends = pick_grad(place, tables, [flow], (0,), late, n_exp, per_token, capacity)
+    sends = pick_grad(place, tables, [flow_far], (1,), late, n_exp, per_token, capacity, sends)
+    early = [t[:half] for t in turns]
     keeps = pick_grad(
-        place, tables, flows, [t[:half] for t in turns], n_exp, per_token, capacity
+        place, tables, [flow, flow_far], (0, 1), early, n_exp, per_token, capacity
     )
     streams = range(quarters)
     firsts = [swap(sends[k], "exp", orders[k][0]) for k in streams]
-    messages = merge(shifts, [second_parts(keeps[k], firsts[k]) for k in streams])
+    messages = merge(shifts, [second_parts(keeps[k], firsts[k]) for k in streams], [first_a])
     seconds = [swap(messages[k], "exp", orders[k][1]) for k in streams]
-    thirds_out = merge(shifts, [third_parts(keeps[k], firsts[k], seconds[k]) for k in streams])
+    messages = merge(
+        shifts,
+        [third_parts(keeps[k], firsts[k], seconds[k]) for k in streams]
+        + [
+            [(keep_a, (1,), None), (far_a, (1,), None), (first_a, (1, 3), None)],
+            [(keep_b, (1,), None), (far_b, (1,), None), (first_b, (1, 3), 0)],
+        ],
+        [qkv_parts],
+    )
+    thirds_out, (message_a, message_b) = messages[:quarters], messages[quarters:]
     thirds = [swap(thirds_out[k], "exp", orders[k][2]) for k in streams]
-    (message_a,) = merge(
-        shifts,
-        [[(keep_a, (1,), None), (far_a, (1,), None), (first_a, (1, 3), None)]],
-        thirds_out,
-    )
-    (message_b,) = merge(
-        shifts,
-        [[(keep_b, (1,), None), (far_b, (1,), None), (first_b, (1, 3), 0)]],
-        thirds_out,
-    )
     second_a = swap(message_a, "seq", 2 * flips_a[1])
     second_b = swap_gather(message_b, "seq", 2 * flips_b[1])
     calls = [

time: 351 us -> 325 us (0.926)
  waiting for transfers between devices: 135 us -> 121 us
  starting transfers between devices: 43.9 us -> 33.5 us
    all_to_all x1, waiting for transfers between devices: 25.1 us -> 6.3 us  [per_device(): lax.all_to_all(qkv_parts, 'seq', split_axis=0, concat_axis=0, tiled=True)]
    all_to_all x1, starting transfers between devices: 16.1 us -> 5.54 us  [per_device(): lax.all_to_all(qkv_parts, 'seq', split_axis=0, concat_axis=0, tiled=True)]
    pallas_call x6 -> x4, Pallas kernels: 27.6 us -> 23.4 us  [merge(): pl.pallas_call(functools.partial(merge_kernel, tuple(plans), len(arrays))...]
    all_gather x2, waiting for transfers between devices: 0.04 us -> 4.24 us  [swap_gather(): both = lax.all_gather(array, axis, axis_index_groups=groups)]
    pallas_call x2 -> x3, Pallas kernels: 13 us -> 15.5 us  [pick_grad(): pl.pallas_call(functools.partial(pick_grad_kernel, per_token, capacity, n...]
  transfers between devices with their start and end apart: 33 -> 33, of which waited for: 16 -> 18; matrix products, arithmetic and copies ran while one was open for 2% -> 2% of each run, Pallas kernels for 30% -> 29%
where the time goes in v7:
time: 325 us; the launch traced here: 324 us
  Pallas kernels  135 us (42%)
  waiting for transfers between devices  121 us (37%)
  starting transfers between devices  33.5 us (10%)
  between operations  15.9 us (5%)
  blocking collectives  9.59 us (3%)
  local copies, waits for them, and re-layouts  8.13 us (3%)
    ppermute x25, waiting for transfers between devices, swap(): return lax.ppermute(array, axis, [(i, i ^ flip) for i in range(count)])  72.6 us
    all_gather x1, waiting for transfers between devices, per_device(): exp_normed = lax.all_gather(normed, 'exp')  33.3 us
    pallas_call x4, Pallas kernels, expert_forward(): pl.pallas_call(functools.partial(forward_kernel, sources), grid_spec=pltp...  31 us
    pallas_call x1, Pallas kernels, expert_backward(): pl.pallas_call(functools.partial(backward_kernel, places, len(arrays)), g...  29.1 us
    pallas_call x4, Pallas kernels, merge(): pl.pallas_call(functools.partial(merge_kernel, tuple(plans), len(arrays))...  23.4 us
    ppermute x25, starting transfers between devices, swap(): return lax.ppermute(array, axis, [(i, i ^ flip) for i in range(count)])  22.1 us
    pallas_call x3, Pallas kernels, pick_grad(): pl.pallas_call(functools.partial(pick_grad_kernel, per_token, capacity, n...  15.5 us
    pallas_call x1, Pallas kernels, conv_back(): pl.pallas_call(functools.partial(conv_kernel, tile), grid_spec=pltpu.Pref...  12.8 us
  transfers between devices with their start and end apart: 33, of which 18 were waited for; matrix products, arithmetic and copies ran while one was open for 2% of the time, Pallas kernels for 29%

profile of v7, /device:TPU:1, one launch (start us, length us, event | category | flops | bytes accessed | tf_op | source)
XLA Modules:
  0.0 324.5 jit_solution(17539591363343530991)
XLA Ops:
  8.1 1.3 reshape.24.gain_ref
  9.4 2.2 norm_rows.1
  11.6 1.5 collective-permute-start.4
  13.1 0.8 fusion
  13.9 3.2 collective-permute-start
  17.0 1.3 collective-permute-start.1
  18.3 0.7 slice.11
  19.1 1.3 collective-permute-start.2
  20.4 0.6 pad_add_fusion.place_ref
  21.2 1.0 reshape.34.ids_ref
  22.2 2.0 collective-permute-done.2.grad_high_ref
  24.3 0.6 copy-done.3
  24.9 12.8 %conv_back.1 = (bf16[1024,768]{1,0:T(8,128)(2,1)}, bf16[512,768]{1,0:T(8,128)(2,1)}, bf16[512,768]{1,0:T(8,128)(2,1)}) custom-call(s32[2]{0:T(128)} %pad_add_fusion.place_ref, bf16[1024,768]{1,0:T(8,128)(2,1)} %in_ref.1, bf16[16,768]{1,0:T(8,128)(2,1)} %copy-done.1, bf16[16,768]{1,0:T(8,128)(2,1)} %copy-done.2, bf16[1024,768]{1,0:T(8,128)(2,1)} %grad_ref.1, ...), custom_call_target="tpu_custom_call" | custom-call | flops 31457280 | bytes 6291456 | tf_op jit(solution)/shard_map/conv_back/pallas_call | solution.py:107
  37.7 1.3 collective-permute-start.3
  38.9 2.2 collective-permute-done.3.other_ref
  41.2 8.9 %project.1 = bf16[512,2304]{1,0:T(8,128)(2,1)} custom-call(s32[2]{0:T(128)} %pad_add_fusion.place_ref, bf16[512,768]{1,0:T(8,128)(2,1)} %get-tuple-element.77.own_ref, bf16[512,768]{1,0:T(8,128)(2,1)} %collective-permute-done.3.other_ref, bf16[768,2304]{1,0:T(8,128)(2,1)} %own_weight.1, bf16[768,2304]{1,0:T(8,128)(2,1)} %collective-permute-done.4.other_weight, ...), custom_call_target="tpu_custom_call" | custom-call | flops 3623878656 | bytes 11010048 | tf_op jit(solution)/shard_map/project/pallas_call | solution.py:157
  50.2 9.6 %all_to_all.10.tables_ref = f32[8,16,128]{2,1,0:T(8,128)} all-to-all(f32[8,16,128]{2,1,0:T(8,128)S(1)} %broadcast_in_dim.4), channel_id=1, replica_groups=mesh['seq'=8,'exp'=16] {'seq'}, dimensions={0} | all-to-all | bytes 131072 | tf_op jit(solution)/shard_map/all_to_all | solution.py:623
  59.8 33.3 %all-gather.7.cloned.1.call-done = bf16[2048,2432]{1,0:T(8,128)(2,1)} async-done(((bf16[128,2432]{1,0:T(8,128)(2,1)}), bf16[2048,2432]{1,0:T(8,128)(2,1)}) %all-gather.7.cloned.1.call-update) | async-done | bytes 9961488 | tf_op jit(solution)/shard_map/all_gather | solution.py:610
  93.1 12.3 %pick_norm.1 = (bf16[2,8,16,2304]{3,2,1,0:T(8,128)(2,1)}, bf16[2,8,16,2304]{3,2,1,0:T(8,128)(2,1)}, bf16[2,8,16,2304]{3,2,1,0:T(8,128)(2,1)}, bf16[2,8,16,2304]{...) custom-call(s32[2]{0:T(128)} %pad_add_fusion.place_ref, ...), custom_call_target="tpu_custom_call" | custom-call | flops 1207959552 | bytes 18874368 | tf_op jit(solution)/shard_map/pick_norm/pallas_call | solution.py:219
  105.4 0.7 collective-permute-start.7
  106.2 0.4 collective-permute-start.5
  106.7 0.6 pad_add_fusion.1.shift_ref.refs_0_
  107.3 1.6 collective-permute-done.7.refs_1_
  108.9 1.7 collective-permute-done.8.refs_3_
  110.6 4.6 %merge_rows.4 = (bf16[4,8,16,2304]{3,2,1,0:T(8,128)(2,1)}, bf16[4,8,16,2304]{3,2,1,0:T(8,128)(2,1)}) custom-call(s32[2]{0:T(128)} %pad_add_fusion.1.shift_ref.refs_0_, bf16[2,8,16,2304]{3,2,1,0:T(8,128)(2,1)} %get-tuple-element.85.refs_0_, bf16[2,8,16,2304]{3,2,1,0:T(8,128)(2,1)} %collective-permute-done.7.refs_1_, ...), custom_call_target="tpu_custom_call" | custom-call | bytes 9437184 | tf_op jit(solution)/shard_map/merge_rows/pallas_call | solution.py:502
  115.2 2.4 all-reduce.2.cloned.1.call-done.refs_0_
  117.7 0.8 collective-permute-start.9
  118.6 4.5 %pick_grad.4 = (bf16[8,32,2304]{2,1,0:T(8,128)(2,1)}, bf16[8,32,2304]{2,1,0:T(8,128)(2,1)}, bf16[8,32,2304]{2,1,0:T(8,128)(2,1)}, bf16[8,32,2304]{2,1,0:T(8,128)(2,1)}) custom-call(s32[2]{0:T(128)} %pad_add_fusion.place_ref, f32[8,16,128]{2,1,0:T(8,128)} %all_to_all.10.tables_ref, bf16[512,2304]{1,0:T(8,128)(2,1)} %all-reduce.2.cloned.1.call-done.refs_0_), custom_call_target="tpu_custom_call" | custom-call | flops 301989888 | bytes 4718592 | tf_op jit(solution)/shard_map/pick_grad/pallas_call | solution.py:284
  123.2 4.6 %pick_grad.5 = (bf16[8,32,2304]{2,1,0:T(8,128)(2,1)}, bf16[8,32,2304]{2,1,0:T(8,128)(2,1)}, bf16[8,32,2304]{2,1,0:T(8,128)(2,1)}, bf16[8,32,2304]{2,1,0:T(8,128)(2,1)}) custom-call(s32[2]{0:T(128)} %pad_add_fusion.place_ref, f32[8,16,128]{2,1,0:T(8,128)} %all_to_all.10.tables_ref, ...), custom_call_target="tpu_custom_call", output_to_operand_aliasing={{0}: (3, {}), {1}: (4, {}), {2}: (5, {}), {3}: (6, {})} | custom-call | flops 301989888 | bytes 4718592 | tf_op jit(solution)/shard_map/pick_grad/pallas_call | solution.py:284
  127.8 1.3 collective-permute-start.10
  129.1 1.8 collective-permute-start.11
  130.8 1.2 collective-permute-start.12
  132.0 1.9 collective-permute-start.13
  133.9 5.5 %all-to-all-start.1 = ((bf16[8,128,768]{2,1,0:T(8,128)(2,1)}), bf16[8,128,768]{2,1,0:T(8,128)(2,1)}, u32[]{:S(2)}, u32[]{:S(2)}) async-start(bf16[8,128,768]{2,1,0:T(8,128)(2,1)} %bitcast.21), calls=%async_computation.1 | async-start | bytes 3145728 | tf_op jit(solution)/shard_map/all_to_all | solution.py:654
  139.5 6.3 %pick_grad.3 = (bf16[8,32,2304]{2,1,0:T(8,128)(2,1)}, bf16[8,32,2304]{2,1,0:T(8,128)(2,1)}, bf16[8,32,2304]{2,1,0:T(8,128)(2,1)}, bf16[8,32,2304]{2,1,0:T(8,128)(2,1)}) custom-call(s32[2]{0:T(128)} %pad_add_fusion.place_ref, f32[8,16,128]{2,1,0:T(8,128)} %all_to_all.10.tables_ref, bf16[512,2304]{1,0:T(8,128)(2,1)} %all-reduce.2.cloned.1.call-done.refs_0_, ...), custom_call_target="tpu_custom_call" | custom-call | flops 603979776 | bytes 9437184 | tf_op jit(solution)/shard_map/pick_grad/pallas_call | solution.py:284
  145.8 25.9 %collective-permute-done.14.refs_8_.refs_3_.refs_4_.refs_14_ = bf16[4,8,16,2304]{3,2,1,0:T(8,128)(2,1)} collective-permute-done((bf16[4,8,16,2304]{3,2,1,0:T(8,128)(2,1)}, bf16[4,8,16,2304]{3,2,1,0:T(8,128)(2,1)}, u32[]{:S(2)}, u32[]{:S(2)}) %collective-permute-start.14) | collective-permute-done | bytes 2359328 | tf_op jit(solution)/shard_map/ppermute | solution.py:524
  171.8 5.2 %merge_rows.5 = (bf16[8,32,2304]{2,1,0:T(8,128)(2,1)}, bf16[8,32,2304]{2,1,0:T(8,128)(2,1)}, bf16[8,32,2304]{2,1,0:T(8,128)(2,1)}, bf16[8,32,2304]{2,1,0:T(8,128)(2,1)}) custom-call(s32[2]{0:T(128)} %pad_add_fusion.1.shift_ref.refs_0_, bf16[8,32,2304]{2,1,0:T(8,128)(2,1)} %get-tuple-element.94.refs_0_, bf16[8,32,2304]{2,1,0:T(8,128)(2,1)} %collective-permute-done.10.refs_1_, ...), custom_call_target="tpu_custom_call" | custom-call | bytes 9437184 | tf_op jit(solution)/shard_map/merge_rows/pallas_call | solution.py:502
  176.9 2.5 collective-permute-start.15
  179.4 1.3 collective-permute-start.16
  180.7 1.9 collective-permute-start.17
  182.6 6.3 %all-to-all-done.1.refs_18_ = bf16[8,128,768]{2,1,0:T(8,128)(2,1)} async-done(((bf16[8,128,768]{2,1,0:T(8,128)(2,1)}), bf16[8,128,768]{2,1,0:T(8,128)(2,1)}, u32[]{:S(2)}, u32[]{:S(2)}) %all-to-all-start.1) | async-done | bytes 1572896 | tf_op jit(solution)/shard_map/all_to_all | solution.py:654
  188.9 15.9 %collective-permute-done.15.refs_2_ = bf16[8,32,2304]{2,1,0:T(8,128)(2,1)} collective-permute-done((bf16[8,32,2304]{2,1,0:T(8,128)(2,1)}, bf16[8,32,2304]{2,1,0:T(8,128)(2,1)}, u32[]{:S(2)}, u32[]{:S(2)}) %collective-permute-start.15) | collective-permute-done | bytes 1179680 | tf_op jit(solution)/shard_map/ppermute | solution.py:524
  204.8 0.9 collective-permute-done.16.refs_5_.refs_6_.refs_7_
  205.8 2.2 collective-permute-done.17.refs_8_.refs_10_.refs_12_
  208.0 0.4 collective-permute-done.18.refs_11_.refs_14_.refs_17_
  208.4 8.4 %merge_rows.6 = (bf16[8,32,2304]{2,1,0:T(8,128)(2,1)}, bf16[8,32,2304]{2,1,0:T(8,128)(2,1)}, bf16[8,32,2304]{2,1,0:T(8,128)(2,1)}, bf16[8,32,2304]{2,1,0:T(8,128...) custom-call(s32[2]{0:T(128)} %pad_add_fusion.1.shift_ref.refs_0_, ...), custom_call_target="tpu_custom_call" | custom-call | bytes 18874368 | tf_op jit(solution)/shard_map/merge_rows/pallas_call | solution.py:502
  216.8 0.6 collective-permute-start.27
  217.8 1.1 collective-permute-start.20
  219.0 0.8 collective-permute-start.22
  219.8 7.6 %expert_forward.4 = (bf16[2304,2048]{1,0:T(8,128)(2,1)}, bf16[512,2048]{1,0:T(8,128)(2,1)}, bf16[2048,512]{1,0:T(8,128)(2,1)}, bf16[2048,512]{1,0:T(8,128)(2,1)}) custom-call(s32[2]{0:T(128)} %pad_add_fusion.1.shift_ref.refs_0_, bf16[2,8,16,2304]{3,2,1,0:T(8,128)(2,1)} %get-tuple-element.111.refs_1_.refs_12_, ...), custom_call_target="tpu_custom_call" | custom-call | flops 2415919104 | bytes 7340032 | tf_op jit(solution)/shard_map/expert_forward/pallas_call | solution.py:345
  227.4 8.2 %expert_forward.5 = (bf16[2304,2048]{1,0:T(8,128)(2,1)}, bf16[512,2048]{1,0:T(8,128)(2,1)}, bf16[2048,512]{1,0:T(8,128)(2,1)}, bf16[2048,512]{1,0:T(8,128)(2,1)}) custom-call(s32[2]{0:T(128)} %pad_add_fusion.1.shift_ref.refs_0_, ...), custom_call_target="tpu_custom_call", output_to_operand_aliasing={{0}: (6, {}), {1}: (7, {}), {2}: (8, {}), {3}: (9, {})} | custom-call | flops 2415919104 | bytes 7340032 | tf_op jit(solution)/shard_map/expert_forward/pallas_call | solution.py:345
  235.6 6.4 %collective-permute-done.19.refs_3_ = bf16[8,32,2304]{2,1,0:T(8,128)(2,1)} collective-permute-done((bf16[8,32,2304]{2,1,0:T(8,128)(2,1)}, bf16[8,32,2304]{2,1,0:T(8,128)(2,1)}, u32[]{:S(2)}, u32[]{:S(2)}) %collective-permute-start.19) | collective-permute-done | bytes 1179680 | tf_op jit(solution)/shard_map/ppermute | solution.py:524
  242.0 1.3 collective-permute-done.20.refs_7_.refs_8_
  243.5 0.9 collective-permute-done.22.refs_15_.refs_18_
  244.4 5.2 %merge_rows.7 = (bf16[8,32,2304]{2,1,0:T(8,128)(2,1)}, bf16[8,32,2304]{2,1,0:T(8,128)(2,1)}, bf16[8,32,2304]{2,1,0:T(8,128)(2,1)}, bf16[8,32,2304]{2,1,0:T(8,128)(2,1)}) custom-call(s32[2]{0:T(128)} %pad_add_fusion.1.shift_ref.refs_0_, bf16[8,32,2304]{2,1,0:T(8,128)(2,1)} %get-tuple-element.94.refs_0_, bf16[8,32,2304]{2,1,0:T(8,128)(2,1)} %collective-permute-done.10.refs_1_, ...), custom_call_target="tpu_custom_call" | custom-call | bytes 9437184 | tf_op jit(solution)/shard_map/merge_rows/pallas_call | solution.py:502
  249.6 1.2 collective-permute-start.23
  251.0 0.9 collective-permute-start.25
  251.9 1.9 copy.33
  253.8 1.6 copy.34
  255.3 12.9 %collective-permute-done.27.refs_1_.refs_2_.refs_3_.refs_4_ = bf16[4,8,16,2304]{3,2,1,0:T(8,128)(2,1)} collective-permute-done((bf16[4,8,16,2304]{3,2,1,0:T(8,128)(2,1)}, bf16[4,8,16,2304]{3,2,1,0:T(8,128)(2,1)}, u32[]{:S(2)}, u32[]{:S(2)}) %collective-permute-start.27) | collective-permute-done | bytes 2359328 | tf_op jit(solution)/shard_map/ppermute | solution.py:524
  268.3 7.6 %expert_forward.6 = (bf16[2304,2048]{1,0:T(8,128)(2,1)}, bf16[512,2048]{1,0:T(8,128)(2,1)}, bf16[2048,512]{1,0:T(8,128)(2,1)}, bf16[2048,512]{1,0:T(8,128)(2,1)}) custom-call(s32[2]{0:T(128)} %pad_add_fusion.1.shift_ref.refs_0_, ...), custom_call_target="tpu_custom_call", output_to_operand_aliasing={{0}: (6, {}), {1}: (7, {}), {2}: (8, {}), {3}: (9, {})} | custom-call | flops 2415919104 | bytes 7340032 | tf_op jit(solution)/shard_map/expert_forward/pallas_call | solution.py:345
  275.9 4.2 %all-gather.11.cloned.1.call-done.refs_1_.refs_2_.refs_3_.refs_4_ = bf16[8,8,16,2304]{3,2,1,0:T(8,128)(2,1)} async-done(((bf16[4,8,16,2304]{3,2,1,0:T(8,128)(2,1)}), bf16[8,8,16,2304]{3,2,1,0:T(8,128)(2,1)}) %all-gather.11.cloned.1.call-update) | async-done | bytes 4718608 | tf_op jit(solution)/shard_map/all_gather | solution.py:538
  280.1 7.6 %expert_forward.7 = (bf16[2304,2048]{1,0:T(8,128)(2,1)}, bf16[512,2048]{1,0:T(8,128)(2,1)}, bf16[2048,512]{1,0:T(8,128)(2,1)}, bf16[2048,512]{1,0:T(8,128)(2,1)}) custom-call(s32[2]{0:T(128)} %pad_add_fusion.1.shift_ref.refs_0_, ...), custom_call_target="tpu_custom_call", output_to_operand_aliasing={{0}: (6, {}), {1}: (7, {}), {2}: (8, {}), {3}: (9, {})} | custom-call | flops 2415919104 | bytes 7340032 | tf_op jit(solution)/shard_map/expert_forward/pallas_call | solution.py:345
  287.7 29.1 %expert_backward.1 = bf16[2304,1536]{1,0:T(8,128)(2,1)} custom-call(bf16[8,32,2304]{2,1,0:T(8,128)(2,1)} %get-tuple-element.94.refs_0_, bf16[8,32,2304]{2,1,0:T(8,128)(2,1)} %collective-permute-done.10.refs_1_, bf16[8,32,2304]{2,1,0:T(8,128)(2,1)} %collective-permute-done.15.refs_2_, bf16[8,32,2304]{2,1,0:T(8,128)(2,1)} %collective-permute-done.19.refs_3_, ...), custom_call_target="tpu_custom_call" | custom-call | flops 19327352832 | bytes 39845888 | tf_op jit(solution)/shard_map/expert_backward/pallas_call | solution.py:428
  (49 shorter events, 1.5 us)
Async XLA Ops:
  8.0 13.0 %copy-start = (s32[16384]{0:T(1024)S(1)}, s32[16384]{0:T(1024)}, u32[]{:S(2)}) copy-start(s32[16384]{0:T(1024)} %param.14) | copy-start | bytes 196612
  8.0 85.0 %all-gather.7.cloned.1.call-start = ((), (), s32[]{:S(2)}) async-start(), calls=%async_computation.3 | async-start | bytes 10584064 | tf_op jit(solution)/shard_map/all_gather | solution.py:610
  11.5 106.1 %all-reduce.2.cloned.1.call-start = ((), (), s32[]{:S(2)}) async-start(), calls=%async_computation.2 | async-start | bytes 4718592 | tf_op jit(solution)/shard_map/psum | solution.py:625
  11.6 29.6 %collective-permute-start.4 = (bf16[768,2304]{1,0:T(8,128)(2,1)}, bf16[768,2304]{1,0:T(8,128)(2,1)}, u32[]{:S(2)}, u32[]{:S(2)}) collective-permute-start(bf16[768,2304]{1,0:T(8,128)(2,1)} %own_weight.1), channel_id=1, source_target_pairs={{0,16},{16,0},{32,48},{48,32},{64,80},{80,64},{96,112},{112,96},{1... | collective-permute-start | bytes 10616840 | tf_op jit(solution)/shard_map/ppermute | solution.py:524
  13.9 8.4 %collective-permute-start = (bf16[16,768]{1,0:T(8,128)(2,1)S(1)}, bf16[16,768]{1,0:T(8,128)(2,1)S(1)}, u32[]{:S(2)}, u32[]{:S(2)}) collective-permute-start(bf16[16,768]{1,0:T(8,128)(2,1)S(1)} %get-tuple-element.155), channel_id=1, source_target_pairs={{0,1},{1,2},{2,3},{3,4},{4,5},{5,6},{6,7},{7,8},{8,9},{9,10},{10,1... | collective-permute-start | bytes 73736 | tf_op jit(solution)/shard_map/ppermute | solution.py:602
  17.0 5.2 %collective-permute-start.1 = (bf16[16,768]{1,0:T(8,128)(2,1)S(1)}, bf16[16,768]{1,0:T(8,128)(2,1)S(1)}, u32[]{:S(2)}, u32[]{:S(2)}) collective-permute-start(bf16[16,768]{1,0:T(8,128)(2,1)S(1)} %get-tuple-element.154), channel_id=1, source_target_pairs={{1,0},{2,1},{3,2},{4,3},{5,4},{6,5},{7,6},{8,7},{9,8},{10,9},{11,1... | collective-permute-start | bytes 73736 | tf_op jit(solution)/shard_map/ppermute | solution.py:603
  19.1 5.2 %collective-permute-start.2 = (bf16[16,768]{1,0:T(8,128)(2,1)S(1)}, bf16[16,768]{1,0:T(8,128)(2,1)S(1)}, u32[]{:S(2)}, u32[]{:S(2)}) collective-permute-start(bf16[16,768]{1,0:T(8,128)(2,1)S(1)} %slice.11), channel_id=1, source_target_pairs={{1,0},{2,1},{3,2},{4,3},{5,4},{6,5},{7,6},{8,7},{9,8},{10,9},{11,1... | collective-permute-start | bytes 73736 | tf_op jit(solution)/shard_map/ppermute | solution.py:604
  22.2 16.7 %copy-start.4 = (s32[128,8]{0,1:T(8,128)S(1)}, s32[128,8]{0,1:T(8,128)}, u32[]{:S(2)}) copy-start(s32[128,8]{0,1:T(8,128)} %param.19) | copy-start | bytes 12292
  22.2 16.7 %copy-start.5 = (f32[128,8]{0,1:T(8,128)S(1)}, f32[128,8]{0,1:T(8,128)}, u32[]{:S(2)}) copy-start(f32[128,8]{0,1:T(8,128)} %param.20) | copy-start | bytes 12292
  22.2 2.1 copy-start.1
  22.2 2.1 copy-start.2
  24.3 0.6 copy-start.3
  37.7 3.5 %collective-permute-start.3 = (bf16[512,768]{1,0:T(8,128)(2,1)}, bf16[512,768]{1,0:T(8,128)(2,1)}, u32[]{:S(2)}, u32[]{:S(2)}) collective-permute-start(bf16[512,768]{1,0:T(8,128)(2,1)} %get-tuple-element.78), channel_id=1, source_target_pairs={{0,16},{16,0},{32,48},{48,32},{64,80},{80,64},{96,112},{112,96},{1... | collective-permute-start | bytes 2359304 | tf_op jit(solution)/shard_map/ppermute | solution.py:524
  50.1 154.7 %all-gather.9.cloned.1.call-start = ((), (), s32[]{:S(2)}) async-start(), calls=%async_computation.4 | async-start | bytes 7077888 | tf_op jit(solution)/shard_map/all_gather | solution.py:538
  105.4 3.5 %collective-permute-start.7 = (bf16[2,8,16,2304]{3,2,1,0:T(8,128)(2,1)}, bf16[2,8,16,2304]{3,2,1,0:T(8,128)(2,1)}, u32[]{:S(2)}, u32[]{:S(2)}) collective-permute-start(bf16[2,8,16,2304]{3,2,1,0:T(8,128)(2,1)} %get-tuple-element.86), channel_id=1, source_target_pairs={{0,16},{16,0},{32,48},{48,32},{64,80},{80,64},{96,112},{112,96},{1... | collective-permute-start | bytes 3538952 | tf_op jit(solution)/shard_map/ppermute | solution.py:524
  106.1 4.5 %collective-permute-start.8 = (bf16[2,8,16,2304]{3,2,1,0:T(8,128)(2,1)}, bf16[2,8,16,2304]{3,2,1,0:T(8,128)(2,1)}, u32[]{:S(2)}, u32[]{:S(2)}) collective-permute-start(bf16[2,8,16,2304]{3,2,1,0:T(8,128)(2,1)} %get-tuple-element.88), channel_id=1, source_target_pairs={{0,16},{16,0},{32,48},{48,32},{64,80},{80,64},{96,112},{112,96},{1... | collective-permute-start | bytes 3538952 | tf_op jit(solution)/shard_map/ppermute | solution.py:524
  106.2 11.5 %collective-permute-start.5 = (bf16[2,8,16,2304]{3,2,1,0:T(8,128)(2,1)}, bf16[2,8,16,2304]{3,2,1,0:T(8,128)(2,1)}, u32[]{:S(2)}, u32[]{:S(2)}) collective-permute-start(bf16[2,8,16,2304]{3,2,1,0:T(8,128)(2,1)} %get-tuple-element.83), channel_id=1, source_target_pairs={{0,16},{16,0},{32,48},{48,32},{64,80},{80,64},{96,112},{112,96},{1... | collective-permute-start | bytes 3538952 | tf_op jit(solution)/shard_map/ppermute | solution.py:524
  106.6 11.1 %collective-permute-start.6 = (bf16[2,8,16,2304]{3,2,1,0:T(8,128)(2,1)}, bf16[2,8,16,2304]{3,2,1,0:T(8,128)(2,1)}, u32[]{:S(2)}, u32[]{:S(2)}) collective-permute-start(bf16[2,8,16,2304]{3,2,1,0:T(8,128)(2,1)} %get-tuple-element.84), channel_id=1, source_target_pairs={{0,16},{16,0},{32,48},{48,32},{64,80},{80,64},{96,112},{112,96},{1... | collective-permute-start | bytes 3538952 | tf_op jit(solution)/shard_map/ppermute | solution.py:524
  117.7 5.5 %collective-permute-start.9 = (bf16[512,2304]{1,0:T(8,128)(2,1)}, bf16[512,2304]{1,0:T(8,128)(2,1)}, u32[]{:S(2)}, u32[]{:S(2)}) collective-permute-start(bf16[512,2304]{1,0:T(8,128)(2,1)} %all-reduce.2.cloned.1.call-done.refs_0_), channel_id=1, source_target_pairs={{0,16},{16,0},{32,48},{48,32},{64,80},{80,64},{96,112},{112,96},{1... | collective-permute-start | bytes 7077896 | tf_op jit(solution)/shard_map/ppermute | solution.py:524
  118.5 53.3 %collective-permute-start.14 = (bf16[4,8,16,2304]{3,2,1,0:T(8,128)(2,1)}, bf16[4,8,16,2304]{3,2,1,0:T(8,128)(2,1)}, u32[]{:S(2)}, u32[]{:S(2)}) collective-permute-start(bf16[4,8,16,2304]{3,2,1,0:T(8,128)(2,1)} %get-tuple-element.106), channel_id=1, source_target_pairs={{0,32},{16,48},{32,0},{48,16},{64,96},{80,112},{96,64},{112,80},{1... | collective-permute-start | bytes 7077896 | tf_op jit(solution)/shard_map/ppermute | solution.py:524
  127.8 44.0 %collective-permute-start.10 = (bf16[8,32,2304]{2,1,0:T(8,128)(2,1)}, bf16[8,32,2304]{2,1,0:T(8,128)(2,1)}, u32[]{:S(2)}, u32[]{:S(2)}) collective-permute-start(bf16[8,32,2304]{2,1,0:T(8,128)(2,1)} %get-tuple-element.99), channel_id=1, source_target_pairs={{0,1},{1,0},{2,3},{3,2},{4,5},{5,4},{6,7},{7,6},{8,9},{9,8},{10,11... | collective-permute-start | bytes 3538952 | tf_op jit(solution)/shard_map/ppermute | solution.py:524
  129.1 42.7 %collective-permute-start.11 = (bf16[8,32,2304]{2,1,0:T(8,128)(2,1)}, bf16[8,32,2304]{2,1,0:T(8,128)(2,1)}, u32[]{:S(2)}, u32[]{:S(2)}) collective-permute-start(bf16[8,32,2304]{2,1,0:T(8,128)(2,1)} %get-tuple-element.101), channel_id=1, source_target_pairs={{0,3},{1,2},{2,1},{3,0},{4,7},{5,6},{6,5},{7,4},{8,11},{9,10},{10,... | collective-permute-start | bytes 3538952 | tf_op jit(solution)/shard_map/ppermute | solution.py:524
  130.8 40.9 %collective-permute-start.12 = (bf16[8,32,2304]{2,1,0:T(8,128)(2,1)}, bf16[8,32,2304]{2,1,0:T(8,128)(2,1)}, u32[]{:S(2)}, u32[]{:S(2)}) collective-permute-start(bf16[8,32,2304]{2,1,0:T(8,128)(2,1)} %get-tuple-element.103), channel_id=1, source_target_pairs={{0,4},{1,5},{2,6},{3,7},{4,0},{5,1},{6,2},{7,3},{8,12},{9,13},{10,... | collective-permute-start | bytes 3538952 | tf_op jit(solution)/shard_map/ppermute | solution.py:524
  132.0 39.7 %collective-permute-start.13 = (bf16[8,32,2304]{2,1,0:T(8,128)(2,1)}, bf16[8,32,2304]{2,1,0:T(8,128)(2,1)}, u32[]{:S(2)}, u32[]{:S(2)}) collective-permute-start(bf16[8,32,2304]{2,1,0:T(8,128)(2,1)} %get-tuple-element.105), channel_id=1, source_target_pairs={{0,12},{1,13},{2,14},{3,15},{4,8},{5,9},{6,10},{7,11},{8,4},{9,5},... | collective-permute-start | bytes 3538952 | tf_op jit(solution)/shard_map/ppermute | solution.py:524
  133.9 55.0 %all-to-all-start.1 = ((bf16[8,128,768]{2,1,0:T(8,128)(2,1)}), bf16[8,128,768]{2,1,0:T(8,128)(2,1)}, u32[]{:S(2)}, u32[]{:S(2)}) async-start(bf16[8,128,768]{2,1,0:T(8,128)(2,1)} %bitcast.21), calls=%async_computation.1 | async-start | bytes 3145728 | tf_op jit(solution)/shard_map/all_to_all | solution.py:654
  139.5 140.7 %all-gather.11.cloned.1.call-start = ((), (), s32[]{:S(2)}) async-start(), calls=%async_computation.5 | async-start | bytes 7077888 | tf_op jit(solution)/shard_map/all_gather | solution.py:538
  176.9 27.9 %collective-permute-start.15 = (bf16[8,32,2304]{2,1,0:T(8,128)(2,1)}, bf16[8,32,2304]{2,1,0:T(8,128)(2,1)}, u32[]{:S(2)}, u32[]{:S(2)}) collective-permute-start(bf16[8,32,2304]{2,1,0:T(8,128)(2,1)} %get-tuple-element.107), channel_id=1, source_target_pairs={{0,3},{1,2},{2,1},{3,0},{4,7},{5,6},{6,5},{7,4},{8,11},{9,10},{10,... | collective-permute-start | bytes 3538952 | tf_op jit(solution)/shard_map/ppermute | solution.py:524
  179.4 26.3 %collective-permute-start.16 = (bf16[8,32,2304]{2,1,0:T(8,128)(2,1)}, bf16[8,32,2304]{2,1,0:T(8,128)(2,1)}, u32[]{:S(2)}, u32[]{:S(2)}) collective-permute-start(bf16[8,32,2304]{2,1,0:T(8,128)(2,1)} %get-tuple-element.121), channel_id=1, source_target_pairs={{0,4},{1,5},{2,6},{3,7},{4,0},{5,1},{6,2},{7,3},{8,12},{9,13},{10,... | collective-permute-start | bytes 3538952 | tf_op jit(solution)/shard_map/ppermute | solution.py:524
  180.7 27.3 %collective-permute-start.17 = (bf16[8,32,2304]{2,1,0:T(8,128)(2,1)}, bf16[8,32,2304]{2,1,0:T(8,128)(2,1)}, u32[]{:S(2)}, u32[]{:S(2)}) collective-permute-start(bf16[8,32,2304]{2,1,0:T(8,128)(2,1)} %get-tuple-element.122), channel_id=1, source_target_pairs={{0,12},{1,13},{2,14},{3,15},{4,8},{5,9},{6,10},{7,11},{8,4},{9,5},... | collective-permute-start | bytes 3538952 | tf_op jit(solution)/shard_map/ppermute | solution.py:524
  182.6 25.8 %collective-permute-start.18 = (bf16[8,32,2304]{2,1,0:T(8,128)(2,1)}, bf16[8,32,2304]{2,1,0:T(8,128)(2,1)}, u32[]{:S(2)}, u32[]{:S(2)}) collective-permute-start(bf16[8,32,2304]{2,1,0:T(8,128)(2,1)} %get-tuple-element.123), channel_id=1, source_target_pairs={{0,1},{1,0},{2,3},{3,2},{4,5},{5,4},{6,7},{7,6},{8,9},{9,8},{10,11... | collective-permute-start | bytes 3538952 | tf_op jit(solution)/shard_map/ppermute | solution.py:524
  216.8 51.4 %collective-permute-start.27 = (bf16[4,8,16,2304]{3,2,1,0:T(8,128)(2,1)}, bf16[4,8,16,2304]{3,2,1,0:T(8,128)(2,1)}, u32[]{:S(2)}, u32[]{:S(2)}) collective-permute-start(bf16[4,8,16,2304]{3,2,1,0:T(8,128)(2,1)} %get-tuple-element.137), channel_id=1, source_target_pairs={{0,96},{16,112},{32,64},{48,80},{64,32},{80,48},{96,0},{112,16},{1... | collective-permute-start | bytes 7077896 | tf_op jit(solution)/shard_map/ppermute | solution.py:524
  217.5 24.6 %collective-permute-start.19 = (bf16[8,32,2304]{2,1,0:T(8,128)(2,1)}, bf16[8,32,2304]{2,1,0:T(8,128)(2,1)}, u32[]{:S(2)}, u32[]{:S(2)}) collective-permute-start(bf16[8,32,2304]{2,1,0:T(8,128)(2,1)} %get-tuple-element.124), channel_id=1, source_target_pairs={{0,4},{1,5},{2,6},{3,7},{4,0},{5,1},{6,2},{7,3},{8,12},{9,13},{10,... | collective-permute-start | bytes 3538952 | tf_op jit(solution)/shard_map/ppermute | solution.py:524
  217.8 25.5 %collective-permute-start.20 = (bf16[8,32,2304]{2,1,0:T(8,128)(2,1)}, bf16[8,32,2304]{2,1,0:T(8,128)(2,1)}, u32[]{:S(2)}, u32[]{:S(2)}) collective-permute-start(bf16[8,32,2304]{2,1,0:T(8,128)(2,1)} %get-tuple-element.125), channel_id=1, source_target_pairs={{0,12},{1,13},{2,14},{3,15},{4,8},{5,9},{6,10},{7,11},{8,4},{9,5},... | collective-permute-start | bytes 3538952 | tf_op jit(solution)/shard_map/ppermute | solution.py:524
  219.0 24.5 %collective-permute-start.21 = (bf16[8,32,2304]{2,1,0:T(8,128)(2,1)}, bf16[8,32,2304]{2,1,0:T(8,128)(2,1)}, u32[]{:S(2)}, u32[]{:S(2)}) collective-permute-start(bf16[8,32,2304]{2,1,0:T(8,128)(2,1)} %get-tuple-element.126), channel_id=1, source_target_pairs={{0,1},{1,0},{2,3},{3,2},{4,5},{5,4},{6,7},{7,6},{8,9},{9,8},{10,11... | collective-permute-start | bytes 3538952 | tf_op jit(solution)/shard_map/ppermute | solution.py:524
  219.0 25.4 %collective-permute-start.22 = (bf16[8,32,2304]{2,1,0:T(8,128)(2,1)}, bf16[8,32,2304]{2,1,0:T(8,128)(2,1)}, u32[]{:S(2)}, u32[]{:S(2)}) collective-permute-start(bf16[8,32,2304]{2,1,0:T(8,128)(2,1)} %get-tuple-element.127), channel_id=1, source_target_pairs={{0,3},{1,2},{2,1},{3,0},{4,7},{5,6},{6,5},{7,4},{8,11},{9,10},{10,... | collective-permute-start | bytes 3538952 | tf_op jit(solution)/shard_map/ppermute | solution.py:524
  249.6 38.1 %collective-permute-start.23 = (bf16[8,32,2304]{2,1,0:T(8,128)(2,1)}, bf16[8,32,2304]{2,1,0:T(8,128)(2,1)}, u32[]{:S(2)}, u32[]{:S(2)}) collective-permute-start(bf16[8,32,2304]{2,1,0:T(8,128)(2,1)} %get-tuple-element.132), channel_id=1, source_target_pairs={{0,12},{1,13},{2,14},{3,15},{4,8},{5,9},{6,10},{7,11},{8,4},{9,5},... | collective-permute-start | bytes 3538952 | tf_op jit(solution)/shard_map/ppermute | solution.py:524
  250.8 36.9 %collective-permute-start.24 = (bf16[8,32,2304]{2,1,0:T(8,128)(2,1)}, bf16[8,32,2304]{2,1,0:T(8,128)(2,1)}, u32[]{:S(2)}, u32[]{:S(2)}) collective-permute-start(bf16[8,32,2304]{2,1,0:T(8,128)(2,1)} %get-tuple-element.133), channel_id=1, source_target_pairs={{0,1},{1,0},{2,3},{3,2},{4,5},{5,4},{6,7},{7,6},{8,9},{9,8},{10,11... | collective-permute-start | bytes 3538952 | tf_op jit(solution)/shard_map/ppermute | solution.py:524
  251.0 36.7 %collective-permute-start.25 = (bf16[8,32,2304]{2,1,0:T(8,128)(2,1)}, bf16[8,32,2304]{2,1,0:T(8,128)(2,1)}, u32[]{:S(2)}, u32[]{:S(2)}) collective-permute-start(bf16[8,32,2304]{2,1,0:T(8,128)(2,1)} %get-tuple-element.134), channel_id=1, source_target_pairs={{0,3},{1,2},{2,1},{3,0},{4,7},{5,6},{6,5},{7,4},{8,11},{9,10},{10,... | collective-permute-start | bytes 3538952 | tf_op jit(solution)/shard_map/ppermute | solution.py:524
  251.9 35.9 %collective-permute-start.26 = (bf16[8,32,2304]{2,1,0:T(8,128)(2,1)}, bf16[8,32,2304]{2,1,0:T(8,128)(2,1)}, u32[]{:S(2)}, u32[]{:S(2)}) collective-permute-start(bf16[8,32,2304]{2,1,0:T(8,128)(2,1)} %get-tuple-element.135), channel_id=1, source_target_pairs={{0,4},{1,5},{2,6},{3,7},{4,0},{5,1},{6,2},{7,3},{8,12},{9,13},{10,... | collective-permute-start | bytes 3538952 | tf_op jit(solution)/shard_map/ppermute | solution.py:524
Sparse Core Ops, SparseCore 0:
  11.7 81.3 all-gather.6
Sparse Core Ops, SparseCore 1:
  50.2 67.4 all-reduce.1
  119.2 82.9 all-gather.8
  216.9 63.1 all-gather.10

commit v8 on v7

--- a/solution.py
+++ b/solution.py
@@ -647,13 +647,7 @@
     )
     first_a = swap(message_a, "seq", 2 * flips_a[0])
     far_a, far_b = swap(keep_far_a, "seq", 1), swap(keep_far_b, "seq", 1)
-    flow, far_a, far_b, message_b, local_grad = lax.optimization_barrier(
-        (flow, far_a, far_b, message_b, local_grad)
-    )
-    qkv_parts = local_grad.reshape(n_seq, tokens, width)
-    qkv_parts = lax.all_to_all(qkv_parts, "seq", split_axis=0, concat_axis=0, tiled=True)
-    qkv_in_grad = qkv_parts.swapaxes(0, 1).reshape(tokens, n_seq * width)
-    first_b = swap_gather(message_b, "seq", 2 * flips_b[0])
+    flow, far_a, far_b, message_b = lax.optimization_barrier((flow, far_a, far_b, message_b))
     flow_far = swap(flow, "seq", 1)
 
     flips = (1, 3, 4, 12)
@@ -673,6 +667,11 @@
     firsts = [swap(sends[k], "exp", orders[k][0]) for k in streams]
     messages = merge(shifts, [second_parts(keeps[k], firsts[k]) for k in streams], [first_a])
     seconds = [swap(messages[k], "exp", orders[k][1]) for k in streams]
+    firsts, local_grad = lax.optimization_barrier((firsts, local_grad))
+    qkv_parts = local_grad.reshape(n_seq, tokens, width)
+    qkv_parts = lax.all_to_all(qkv_parts, "seq", split_axis=0, concat_axis=0, tiled=True)
+    qkv_in_grad = qkv_parts.swapaxes(0, 1).reshape(tokens, n_seq * width)
+    first_b = swap_gather(message_b, "seq", 2 * flips_b[0])
     messages = merge(
         shifts,
         [third_parts(keeps[k], firsts[k], seconds[k]) for k in streams]

time: 325 us -> 326 us (level)
  starting transfers between devices: 33.5 us -> 37.2 us
    all_to_all x1, waiting for transfers between devices: 6.3 us -> 0.01 us  [per_device(): lax.all_to_all(qkv_parts, 'seq', split_axis=0, concat_axis=0, tiled=True)]
where the time goes in v8:
time: 326 us; the launch traced here: 325 us
  Pallas kernels  135 us (41%)
  waiting for transfers between devices  118 us (36%)
  starting transfers between devices  37.2 us (11%)
  between operations  15.9 us (5%)
  blocking collectives  9.59 us (3%)
  local copies, waits for them, and re-layouts  8.13 us (2%)
    ppermute x25, waiting for transfers between devices, swap(): return lax.ppermute(array, axis, [(i, i ^ flip) for i in range(count)])  75 us
    all_gather x1, waiting for transfers between devices, per_device(): exp_normed = lax.all_gather(normed, 'exp')  33.3 us
    pallas_call x4, Pallas kernels, expert_forward(): pl.pallas_call(functools.partial(forward_kernel, sources), grid_spec=pltp...  31.2 us
    pallas_call x1, Pallas kernels, expert_backward(): pl.pallas_call(functools.partial(backward_kernel, places, len(arrays)), g...  29.1 us
    ppermute x25, starting transfers between devices, swap(): return lax.ppermute(array, axis, [(i, i ^ flip) for i in range(count)])  25.1 us
    pallas_call x4, Pallas kernels, merge(): pl.pallas_call(functools.partial(merge_kernel, tuple(plans), len(arrays))...  23.4 us
    pallas_call x3, Pallas kernels, pick_grad(): pl.pallas_call(functools.partial(pick_grad_kernel, per_token, capacity, n...  15.5 us
    pallas_call x1, Pallas kernels, conv_back(): pl.pallas_call(functools.partial(conv_kernel, tile), grid_spec=pltpu.Pref...  12.8 us
  transfers between devices with their start and end apart: 33, of which 18 were waited for; matrix products, arithmetic and copies ran while one was open for 2% of the time, Pallas kernels for 29%

profile of v8, /device:TPU:1, one launch (start us, length us, event | category | flops | bytes accessed | tf_op | source)
XLA Modules:
  0.0 325.4 jit_solution(6250885411642194692)
XLA Ops:
  8.1 1.3 reshape.23.gain_ref
  9.4 2.2 norm_rows.1
  11.6 1.5 collective-permute-start.4
  13.1 0.8 fusion
  13.9 3.2 collective-permute-start
  17.0 1.3 collective-permute-start.1
  18.3 0.7 slice.11
  19.1 1.3 collective-permute-start.2
  20.4 0.6 pad_add_fusion.place_ref
  21.2 1.0 reshape.34.ids_ref
  22.2 2.0 collective-permute-done.2.grad_high_ref
  24.3 0.6 copy-done.3
  24.9 12.8 %conv_back.1 = (bf16[1024,768]{1,0:T(8,128)(2,1)}, bf16[512,768]{1,0:T(8,128)(2,1)}, bf16[512,768]{1,0:T(8,128)(2,1)}) custom-call(s32[2]{0:T(128)} %pad_add_fusion.place_ref, bf16[1024,768]{1,0:T(8,128)(2,1)} %in_ref.1, bf16[16,768]{1,0:T(8,128)(2,1)} %copy-done.1, bf16[16,768]{1,0:T(8,128)(2,1)} %copy-done.2, bf16[1024,768]{1,0:T(8,128)(2,1)} %grad_ref.1, ...), custom_call_target="tpu_custom_call" | custom-call | flops 31457280 | bytes 6291456 | tf_op jit(solution)/shard_map/conv_back/pallas_call | solution.py:107
  37.7 1.3 collective-permute-start.3
  38.9 2.2 collective-permute-done.3.other_ref
  41.2 8.9 %project.1 = bf16[512,2304]{1,0:T(8,128)(2,1)} custom-call(s32[2]{0:T(128)} %pad_add_fusion.place_ref, bf16[512,768]{1,0:T(8,128)(2,1)} %get-tuple-element.82.own_ref, bf16[512,768]{1,0:T(8,128)(2,1)} %collective-permute-done.3.other_ref, bf16[768,2304]{1,0:T(8,128)(2,1)} %own_weight.1, bf16[768,2304]{1,0:T(8,128)(2,1)} %collective-permute-done.4.other_weight, ...), custom_call_target="tpu_custom_call" | custom-call | flops 3623878656 | bytes 11010048 | tf_op jit(solution)/shard_map/project/pallas_call | solution.py:157
  50.2 9.6 %all_to_all.10.tables_ref = f32[8,16,128]{2,1,0:T(8,128)} all-to-all(f32[8,16,128]{2,1,0:T(8,128)S(1)} %broadcast_in_dim.4), channel_id=1, replica_groups=mesh['seq'=8,'exp'=16] {'seq'}, dimensions={0} | all-to-all | bytes 131072 | tf_op jit(solution)/shard_map/all_to_all | solution.py:623
  59.8 33.3 %all-gather.7.cloned.1.call-done = bf16[2048,2432]{1,0:T(8,128)(2,1)} async-done(((bf16[128,2432]{1,0:T(8,128)(2,1)}), bf16[2048,2432]{1,0:T(8,128)(2,1)}) %all-gather.7.cloned.1.call-update) | async-done | bytes 9961488 | tf_op jit(solution)/shard_map/all_gather | solution.py:610
  93.1 12.3 %pick_norm.1 = (bf16[2,8,16,2304]{3,2,1,0:T(8,128)(2,1)}, bf16[2,8,16,2304]{3,2,1,0:T(8,128)(2,1)}, bf16[2,8,16,2304]{3,2,1,0:T(8,128)(2,1)}, bf16[2,8,16,2304]{...) custom-call(s32[2]{0:T(128)} %pad_add_fusion.place_ref, ...), custom_call_target="tpu_custom_call" | custom-call | flops 1207959552 | bytes 18874368 | tf_op jit(solution)/shard_map/pick_norm/pallas_call | solution.py:219
  105.4 0.7 collective-permute-start.7
  106.2 0.4 collective-permute-start.5
  106.7 0.6 pad_add_fusion.1.shift_ref.refs_0_
  107.3 1.6 collective-permute-done.7.refs_1_
  108.9 1.7 collective-permute-done.8.refs_3_
  110.6 4.6 %merge_rows.4 = (bf16[4,8,16,2304]{3,2,1,0:T(8,128)(2,1)}, bf16[4,8,16,2304]{3,2,1,0:T(8,128)(2,1)}) custom-call(s32[2]{0:T(128)} %pad_add_fusion.1.shift_ref.refs_0_, bf16[2,8,16,2304]{3,2,1,0:T(8,128)(2,1)} %get-tuple-element.90.refs_0_, bf16[2,8,16,2304]{3,2,1,0:T(8,128)(2,1)} %collective-permute-done.7.refs_1_, ...), custom_call_target="tpu_custom_call" | custom-call | bytes 9437184 | tf_op jit(solution)/shard_map/merge_rows/pallas_call | solution.py:502
  115.2 2.4 all-reduce.2.cloned.1.call-done.refs_0_
  117.7 0.8 collective-permute-start.9
  118.6 4.5 %pick_grad.3 = (bf16[8,32,2304]{2,1,0:T(8,128)(2,1)}, bf16[8,32,2304]{2,1,0:T(8,128)(2,1)}, bf16[8,32,2304]{2,1,0:T(8,128)(2,1)}, bf16[8,32,2304]{2,1,0:T(8,128)(2,1)}) custom-call(s32[2]{0:T(128)} %pad_add_fusion.place_ref, f32[8,16,128]{2,1,0:T(8,128)} %all_to_all.10.tables_ref, bf16[512,2304]{1,0:T(8,128)(2,1)} %all-reduce.2.cloned.1.call-done.refs_0_), custom_call_target="tpu_custom_call" | custom-call | flops 301989888 | bytes 4718592 | tf_op jit(solution)/shard_map/pick_grad/pallas_call | solution.py:284
  123.2 4.6 %pick_grad.4 = (bf16[8,32,2304]{2,1,0:T(8,128)(2,1)}, bf16[8,32,2304]{2,1,0:T(8,128)(2,1)}, bf16[8,32,2304]{2,1,0:T(8,128)(2,1)}, bf16[8,32,2304]{2,1,0:T(8,128)(2,1)}) custom-call(s32[2]{0:T(128)} %pad_add_fusion.place_ref, f32[8,16,128]{2,1,0:T(8,128)} %all_to_all.10.tables_ref, ...), custom_call_target="tpu_custom_call", output_to_operand_aliasing={{0}: (3, {}), {1}: (4, {}), {2}: (5, {}), {3}: (6, {})} | custom-call | flops 301989888 | bytes 4718592 | tf_op jit(solution)/shard_map/pick_grad/pallas_call | solution.py:284
  127.8 1.3 collective-permute-start.10
  129.1 1.8 collective-permute-start.11
  130.8 1.2 collective-permute-start.12
  132.0 1.9 collective-permute-start.13
  133.9 21.5 %collective-permute-done.10.refs_1_ = bf16[8,32,2304]{2,1,0:T(8,128)(2,1)} collective-permute-done((bf16[8,32,2304]{2,1,0:T(8,128)(2,1)}, bf16[8,32,2304]{2,1,0:T(8,128)(2,1)}, u32[]{:S(2)}, u32[]{:S(2)}) %collective-permute-start.10) | collective-permute-done | bytes 1179680 | tf_op jit(solution)/shard_map/ppermute | solution.py:524
  155.4 2.1 collective-permute-done.11.refs_3_.refs_4_.refs_5_.refs_6_
  157.8 2.1 collective-permute-done.13.refs_7_.refs_10_.refs_13_.refs_16_
  159.9 6.2 %all-to-all-start.1 = ((bf16[8,128,768]{2,1,0:T(8,128)(2,1)}), bf16[8,128,768]{2,1,0:T(8,128)(2,1)}, u32[]{:S(2)}, u32[]{:S(2)}) async-start(bf16[8,128,768]{2,1,0:T(8,128)(2,1)} %bitcast.21), calls=%async_computation.1 | async-start | bytes 3145728 | tf_op jit(solution)/shard_map/all_to_all | solution.py:672
  166.1 6.4 %pick_grad.5 = (bf16[8,32,2304]{2,1,0:T(8,128)(2,1)}, bf16[8,32,2304]{2,1,0:T(8,128)(2,1)}, bf16[8,32,2304]{2,1,0:T(8,128)(2,1)}, bf16[8,32,2304]{2,1,0:T(8,128)(2,1)}) custom-call(s32[2]{0:T(128)} %pad_add_fusion.place_ref, f32[8,16,128]{2,1,0:T(8,128)} %all_to_all.10.tables_ref, bf16[512,2304]{1,0:T(8,128)(2,1)} %all-reduce.2.cloned.1.call-done.refs_0_, ...), custom_call_target="tpu_custom_call" | custom-call | flops 603979776 | bytes 9437184 | tf_op jit(solution)/shard_map/pick_grad/pallas_call | solution.py:284
  172.5 5.2 %merge_rows.5 = (bf16[8,32,2304]{2,1,0:T(8,128)(2,1)}, bf16[8,32,2304]{2,1,0:T(8,128)(2,1)}, bf16[8,32,2304]{2,1,0:T(8,128)(2,1)}, bf16[8,32,2304]{2,1,0:T(8,128)(2,1)}) custom-call(s32[2]{0:T(128)} %pad_add_fusion.1.shift_ref.refs_0_, bf16[8,32,2304]{2,1,0:T(8,128)(2,1)} %get-tuple-element.106.refs_0_, ...), custom_call_target="tpu_custom_call" | custom-call | bytes 9437184 | tf_op jit(solution)/shard_map/merge_rows/pallas_call | solution.py:502
  177.7 1.7 collective-permute-start.15
  179.4 1.3 collective-permute-start.16
  180.7 1.9 collective-permute-start.17
  182.6 23.9 %collective-permute-done.15.refs_2_ = bf16[8,32,2304]{2,1,0:T(8,128)(2,1)} collective-permute-done((bf16[8,32,2304]{2,1,0:T(8,128)(2,1)}, bf16[8,32,2304]{2,1,0:T(8,128)(2,1)}, u32[]{:S(2)}, u32[]{:S(2)}) %collective-permute-start.15) | collective-permute-done | bytes 1179680 | tf_op jit(solution)/shard_map/ppermute | solution.py:524
  206.4 1.5 collective-permute-done.17.refs_8_.refs_10_.refs_12_
  208.3 8.4 %merge_rows.6 = (bf16[8,32,2304]{2,1,0:T(8,128)(2,1)}, bf16[8,32,2304]{2,1,0:T(8,128)(2,1)}, bf16[8,32,2304]{2,1,0:T(8,128)(2,1)}, bf16[8,32,2304]{2,1,0:T(8,128...) custom-call(s32[2]{0:T(128)} %pad_add_fusion.1.shift_ref.refs_0_, ...), custom_call_target="tpu_custom_call" | custom-call | bytes 18874368 | tf_op jit(solution)/shard_map/merge_rows/pallas_call | solution.py:502
  216.8 0.9 collective-permute-start.27
  217.7 1.1 collective-permute-start.19
  218.9 1.1 collective-permute-start.20
  220.3 1.8 collective-permute-start.22
  222.1 7.8 %expert_forward.4 = (bf16[2304,2048]{1,0:T(8,128)(2,1)}, bf16[512,2048]{1,0:T(8,128)(2,1)}, bf16[2048,512]{1,0:T(8,128)(2,1)}, bf16[2048,512]{1,0:T(8,128)(2,1)}) custom-call(s32[2]{0:T(128)} %pad_add_fusion.1.shift_ref.refs_0_, bf16[2,8,16,2304]{3,2,1,0:T(8,128)(2,1)} %get-tuple-element.116.refs_1_.refs_12_, ...), custom_call_target="tpu_custom_call" | custom-call | flops 2415919104 | bytes 7340032 | tf_op jit(solution)/shard_map/expert_forward/pallas_call | solution.py:345
  229.9 8.2 %expert_forward.5 = (bf16[2304,2048]{1,0:T(8,128)(2,1)}, bf16[512,2048]{1,0:T(8,128)(2,1)}, bf16[2048,512]{1,0:T(8,128)(2,1)}, bf16[2048,512]{1,0:T(8,128)(2,1)}) custom-call(s32[2]{0:T(128)} %pad_add_fusion.1.shift_ref.refs_0_, ...), custom_call_target="tpu_custom_call", output_to_operand_aliasing={{0}: (6, {}), {1}: (7, {}), {2}: (8, {}), {3}: (9, {})} | custom-call | flops 2415919104 | bytes 7340032 | tf_op jit(solution)/shard_map/expert_forward/pallas_call | solution.py:345
  238.1 4.5 %collective-permute-done.19.refs_3_ = bf16[8,32,2304]{2,1,0:T(8,128)(2,1)} collective-permute-done((bf16[8,32,2304]{2,1,0:T(8,128)(2,1)}, bf16[8,32,2304]{2,1,0:T(8,128)(2,1)}, u32[]{:S(2)}, u32[]{:S(2)}) %collective-permute-start.19) | collective-permute-done | bytes 1179680 | tf_op jit(solution)/shard_map/ppermute | solution.py:524
  242.6 2.4 collective-permute-done.20.refs_7_.refs_8_
  244.9 1.4 collective-permute-done.22.refs_15_.refs_18_
  246.3 5.2 %merge_rows.7 = (bf16[8,32,2304]{2,1,0:T(8,128)(2,1)}, bf16[8,32,2304]{2,1,0:T(8,128)(2,1)}, bf16[8,32,2304]{2,1,0:T(8,128)(2,1)}, bf16[8,32,2304]{2,1,0:T(8,128)(2,1)}) custom-call(s32[2]{0:T(128)} %pad_add_fusion.1.shift_ref.refs_0_, bf16[8,32,2304]{2,1,0:T(8,128)(2,1)} %get-tuple-element.106.refs_0_, ...), custom_call_target="tpu_custom_call" | custom-call | bytes 9437184 | tf_op jit(solution)/shard_map/merge_rows/pallas_call | solution.py:502
  251.5 0.9 collective-permute-start.23
  252.6 2.7 collective-permute-start.25
  255.2 1.9 copy.33
  257.2 1.6 copy.34
  258.7 9.5 %collective-permute-done.27.refs_1_.refs_2_.refs_3_.refs_4_ = bf16[4,8,16,2304]{3,2,1,0:T(8,128)(2,1)} collective-permute-done((bf16[4,8,16,2304]{3,2,1,0:T(8,128)(2,1)}, bf16[4,8,16,2304]{3,2,1,0:T(8,128)(2,1)}, u32[]{:S(2)}, u32[]{:S(2)}) %collective-permute-start.27) | collective-permute-done | bytes 2359328 | tf_op jit(solution)/shard_map/ppermute | solution.py:524
  268.2 7.6 %expert_forward.6 = (bf16[2304,2048]{1,0:T(8,128)(2,1)}, bf16[512,2048]{1,0:T(8,128)(2,1)}, bf16[2048,512]{1,0:T(8,128)(2,1)}, bf16[2048,512]{1,0:T(8,128)(2,1)}) custom-call(s32[2]{0:T(128)} %pad_add_fusion.1.shift_ref.refs_0_, ...), custom_call_target="tpu_custom_call", output_to_operand_aliasing={{0}: (6, {}), {1}: (7, {}), {2}: (8, {}), {3}: (9, {})} | custom-call | flops 2415919104 | bytes 7340032 | tf_op jit(solution)/shard_map/expert_forward/pallas_call | solution.py:345
  275.9 5.2 %all-gather.11.cloned.1.call-done.refs_1_.refs_2_.refs_3_.refs_4_ = bf16[8,8,16,2304]{3,2,1,0:T(8,128)(2,1)} async-done(((bf16[4,8,16,2304]{3,2,1,0:T(8,128)(2,1)}), bf16[8,8,16,2304]{3,2,1,0:T(8,128)(2,1)}) %all-gather.11.cloned.1.call-update) | async-done | bytes 4718608 | tf_op jit(solution)/shard_map/all_gather | solution.py:538
  281.1 7.6 %expert_forward.7 = (bf16[2304,2048]{1,0:T(8,128)(2,1)}, bf16[512,2048]{1,0:T(8,128)(2,1)}, bf16[2048,512]{1,0:T(8,128)(2,1)}, bf16[2048,512]{1,0:T(8,128)(2,1)}) custom-call(s32[2]{0:T(128)} %pad_add_fusion.1.shift_ref.refs_0_, ...), custom_call_target="tpu_custom_call", output_to_operand_aliasing={{0}: (6, {}), {1}: (7, {}), {2}: (8, {}), {3}: (9, {})} | custom-call | flops 2415919104 | bytes 7340032 | tf_op jit(solution)/shard_map/expert_forward/pallas_call | solution.py:345
  288.7 29.1 %expert_backward.1 = bf16[2304,1536]{1,0:T(8,128)(2,1)} custom-call(bf16[8,32,2304]{2,1,0:T(8,128)(2,1)} %get-tuple-element.106.refs_0_, bf16[8,32,2304]{2,1,0:T(8,128)(2,1)} %collective-permute-done.10.refs_1_, bf16[8,32,2304]{2,1,0:T(8,128)(2,1)} %collective-permute-done.15.refs_2_, bf16[8,32,2304]{2,1,0:T(8,128)(2,1)} %collective-permute-done.19.refs_3_, ...), custom_call_target="tpu_custom_call" | custom-call | flops 19327352832 | bytes 39845888 | tf_op jit(solution)/shard_map/expert_backward/pallas_call | solution.py:428
  (49 shorter events, 1.9 us)
Async XLA Ops:
  8.0 13.0 %copy-start = (s32[16384]{0:T(1024)S(1)}, s32[16384]{0:T(1024)}, u32[]{:S(2)}) copy-start(s32[16384]{0:T(1024)} %param.14) | copy-start | bytes 196612
  8.0 85.0 %all-gather.7.cloned.1.call-start = ((), (), s32[]{:S(2)}) async-start(), calls=%async_computation.3 | async-start | bytes 10584064 | tf_op jit(solution)/shard_map/all_gather | solution.py:610
  11.5 106.1 %all-reduce.2.cloned.1.call-start = ((), (), s32[]{:S(2)}) async-start(), calls=%async_computation.2 | async-start | bytes 4718592 | tf_op jit(solution)/shard_map/psum | solution.py:625
  11.6 29.6 %collective-permute-start.4 = (bf16[768,2304]{1,0:T(8,128)(2,1)}, bf16[768,2304]{1,0:T(8,128)(2,1)}, u32[]{:S(2)}, u32[]{:S(2)}) collective-permute-start(bf16[768,2304]{1,0:T(8,128)(2,1)} %own_weight.1), channel_id=1, source_target_pairs={{0,16},{16,0},{32,48},{48,32},{64,80},{80,64},{96,112},{112,96},{1... | collective-permute-start | bytes 10616840 | tf_op jit(solution)/shard_map/ppermute | solution.py:524
  13.9 8.4 %collective-permute-start = (bf16[16,768]{1,0:T(8,128)(2,1)S(1)}, bf16[16,768]{1,0:T(8,128)(2,1)S(1)}, u32[]{:S(2)}, u32[]{:S(2)}) collective-permute-start(bf16[16,768]{1,0:T(8,128)(2,1)S(1)} %get-tuple-element.163), channel_id=1, source_target_pairs={{0,1},{1,2},{2,3},{3,4},{4,5},{5,6},{6,7},{7,8},{8,9},{9,10},{10,1... | collective-permute-start | bytes 73736 | tf_op jit(solution)/shard_map/ppermute | solution.py:602
  17.0 5.2 %collective-permute-start.1 = (bf16[16,768]{1,0:T(8,128)(2,1)S(1)}, bf16[16,768]{1,0:T(8,128)(2,1)S(1)}, u32[]{:S(2)}, u32[]{:S(2)}) collective-permute-start(bf16[16,768]{1,0:T(8,128)(2,1)S(1)} %get-tuple-element.162), channel_id=1, source_target_pairs={{1,0},{2,1},{3,2},{4,3},{5,4},{6,5},{7,6},{8,7},{9,8},{10,9},{11,1... | collective-permute-start | bytes 73736 | tf_op jit(solution)/shard_map/ppermute | solution.py:603
  19.1 5.2 %collective-permute-start.2 = (bf16[16,768]{1,0:T(8,128)(2,1)S(1)}, bf16[16,768]{1,0:T(8,128)(2,1)S(1)}, u32[]{:S(2)}, u32[]{:S(2)}) collective-permute-start(bf16[16,768]{1,0:T(8,128)(2,1)S(1)} %slice.11), channel_id=1, source_target_pairs={{1,0},{2,1},{3,2},{4,3},{5,4},{6,5},{7,6},{8,7},{9,8},{10,9},{11,1... | collective-permute-start | bytes 73736 | tf_op jit(solution)/shard_map/ppermute | solution.py:604
  22.2 16.7 %copy-start.4 = (s32[128,8]{0,1:T(8,128)S(1)}, s32[128,8]{0,1:T(8,128)}, u32[]{:S(2)}) copy-start(s32[128,8]{0,1:T(8,128)} %param.19) | copy-start | bytes 12292
  22.2 16.7 %copy-start.5 = (f32[128,8]{0,1:T(8,128)S(1)}, f32[128,8]{0,1:T(8,128)}, u32[]{:S(2)}) copy-start(f32[128,8]{0,1:T(8,128)} %param.20) | copy-start | bytes 12292
  22.2 2.1 copy-start.1
  22.2 2.1 copy-start.2
  24.3 0.6 copy-start.3
  37.7 3.5 %collective-permute-start.3 = (bf16[512,768]{1,0:T(8,128)(2,1)}, bf16[512,768]{1,0:T(8,128)(2,1)}, u32[]{:S(2)}, u32[]{:S(2)}) collective-permute-start(bf16[512,768]{1,0:T(8,128)(2,1)} %get-tuple-element.83), channel_id=1, source_target_pairs={{0,16},{16,0},{32,48},{48,32},{64,80},{80,64},{96,112},{112,96},{1... | collective-permute-start | bytes 2359304 | tf_op jit(solution)/shard_map/ppermute | solution.py:524
  50.1 156.3 %all-gather.9.cloned.1.call-start = ((), (), s32[]{:S(2)}) async-start(), calls=%async_computation.4 | async-start | bytes 7077888 | tf_op jit(solution)/shard_map/all_gather | solution.py:538
  105.4 3.5 %collective-permute-start.7 = (bf16[2,8,16,2304]{3,2,1,0:T(8,128)(2,1)}, bf16[2,8,16,2304]{3,2,1,0:T(8,128)(2,1)}, u32[]{:S(2)}, u32[]{:S(2)}) collective-permute-start(bf16[2,8,16,2304]{3,2,1,0:T(8,128)(2,1)} %get-tuple-element.91), channel_id=1, source_target_pairs={{0,16},{16,0},{32,48},{48,32},{64,80},{80,64},{96,112},{112,96},{1... | collective-permute-start | bytes 3538952 | tf_op jit(solution)/shard_map/ppermute | solution.py:524
  106.1 4.5 %collective-permute-start.8 = (bf16[2,8,16,2304]{3,2,1,0:T(8,128)(2,1)}, bf16[2,8,16,2304]{3,2,1,0:T(8,128)(2,1)}, u32[]{:S(2)}, u32[]{:S(2)}) collective-permute-start(bf16[2,8,16,2304]{3,2,1,0:T(8,128)(2,1)} %get-tuple-element.93), channel_id=1, source_target_pairs={{0,16},{16,0},{32,48},{48,32},{64,80},{80,64},{96,112},{112,96},{1... | collective-permute-start | bytes 3538952 | tf_op jit(solution)/shard_map/ppermute | solution.py:524
  106.2 11.5 %collective-permute-start.5 = (bf16[2,8,16,2304]{3,2,1,0:T(8,128)(2,1)}, bf16[2,8,16,2304]{3,2,1,0:T(8,128)(2,1)}, u32[]{:S(2)}, u32[]{:S(2)}) collective-permute-start(bf16[2,8,16,2304]{3,2,1,0:T(8,128)(2,1)} %get-tuple-element.88), channel_id=1, source_target_pairs={{0,16},{16,0},{32,48},{48,32},{64,80},{80,64},{96,112},{112,96},{1... | collective-permute-start | bytes 3538952 | tf_op jit(solution)/shard_map/ppermute | solution.py:524
  106.6 11.1 %collective-permute-start.6 = (bf16[2,8,16,2304]{3,2,1,0:T(8,128)(2,1)}, bf16[2,8,16,2304]{3,2,1,0:T(8,128)(2,1)}, u32[]{:S(2)}, u32[]{:S(2)}) collective-permute-start(bf16[2,8,16,2304]{3,2,1,0:T(8,128)(2,1)} %get-tuple-element.89), channel_id=1, source_target_pairs={{0,16},{16,0},{32,48},{48,32},{64,80},{80,64},{96,112},{112,96},{1... | collective-permute-start | bytes 3538952 | tf_op jit(solution)/shard_map/ppermute | solution.py:524
  117.7 5.5 %collective-permute-start.9 = (bf16[512,2304]{1,0:T(8,128)(2,1)}, bf16[512,2304]{1,0:T(8,128)(2,1)}, u32[]{:S(2)}, u32[]{:S(2)}) collective-permute-start(bf16[512,2304]{1,0:T(8,128)(2,1)} %all-reduce.2.cloned.1.call-done.refs_0_), channel_id=1, source_target_pairs={{0,16},{16,0},{32,48},{48,32},{64,80},{80,64},{96,112},{112,96},{1... | collective-permute-start | bytes 7077896 | tf_op jit(solution)/shard_map/ppermute | solution.py:524
  118.5 54.0 %collective-permute-start.14 = (bf16[4,8,16,2304]{3,2,1,0:T(8,128)(2,1)}, bf16[4,8,16,2304]{3,2,1,0:T(8,128)(2,1)}, u32[]{:S(2)}, u32[]{:S(2)}) collective-permute-start(bf16[4,8,16,2304]{3,2,1,0:T(8,128)(2,1)} %get-tuple-element.111), channel_id=1, source_target_pairs={{0,32},{16,48},{32,0},{48,16},{64,96},{80,112},{96,64},{112,80},{1... | collective-permute-start | bytes 7077896 | tf_op jit(solution)/shard_map/ppermute | solution.py:524
  127.8 27.7 %collective-permute-start.10 = (bf16[8,32,2304]{2,1,0:T(8,128)(2,1)}, bf16[8,32,2304]{2,1,0:T(8,128)(2,1)}, u32[]{:S(2)}, u32[]{:S(2)}) collective-permute-start(bf16[8,32,2304]{2,1,0:T(8,128)(2,1)} %get-tuple-element.100), channel_id=1, source_target_pairs={{0,1},{1,0},{2,3},{3,2},{4,5},{5,4},{6,7},{7,6},{8,9},{9,8},{10,11... | collective-permute-start | bytes 3538952 | tf_op jit(solution)/shard_map/ppermute | solution.py:524
  129.1 28.5 %collective-permute-start.11 = (bf16[8,32,2304]{2,1,0:T(8,128)(2,1)}, bf16[8,32,2304]{2,1,0:T(8,128)(2,1)}, u32[]{:S(2)}, u32[]{:S(2)}) collective-permute-start(bf16[8,32,2304]{2,1,0:T(8,128)(2,1)} %get-tuple-element.101), channel_id=1, source_target_pairs={{0,3},{1,2},{2,1},{3,0},{4,7},{5,6},{6,5},{7,4},{8,11},{9,10},{10,... | collective-permute-start | bytes 3538952 | tf_op jit(solution)/shard_map/ppermute | solution.py:524
  130.8 26.9 %collective-permute-start.12 = (bf16[8,32,2304]{2,1,0:T(8,128)(2,1)}, bf16[8,32,2304]{2,1,0:T(8,128)(2,1)}, u32[]{:S(2)}, u32[]{:S(2)}) collective-permute-start(bf16[8,32,2304]{2,1,0:T(8,128)(2,1)} %get-tuple-element.102), channel_id=1, source_target_pairs={{0,4},{1,5},{2,6},{3,7},{4,0},{5,1},{6,2},{7,3},{8,12},{9,13},{10,... | collective-permute-start | bytes 3538952 | tf_op jit(solution)/shard_map/ppermute | solution.py:524
  132.0 27.9 %collective-permute-start.13 = (bf16[8,32,2304]{2,1,0:T(8,128)(2,1)}, bf16[8,32,2304]{2,1,0:T(8,128)(2,1)}, u32[]{:S(2)}, u32[]{:S(2)}) collective-permute-start(bf16[8,32,2304]{2,1,0:T(8,128)(2,1)} %get-tuple-element.103), channel_id=1, source_target_pairs={{0,12},{1,13},{2,14},{3,15},{4,8},{5,9},{6,10},{7,11},{8,4},{9,5},... | collective-permute-start | bytes 3538952 | tf_op jit(solution)/shard_map/ppermute | solution.py:524
  159.9 48.4 %all-to-all-start.1 = ((bf16[8,128,768]{2,1,0:T(8,128)(2,1)}), bf16[8,128,768]{2,1,0:T(8,128)(2,1)}, u32[]{:S(2)}, u32[]{:S(2)}) async-start(bf16[8,128,768]{2,1,0:T(8,128)(2,1)} %bitcast.21), calls=%async_computation.1 | async-start | bytes 3145728 | tf_op jit(solution)/shard_map/all_to_all | solution.py:672
  166.1 115.0 %all-gather.11.cloned.1.call-start = ((), (), s32[]{:S(2)}) async-start(), calls=%async_computation.5 | async-start | bytes 7077888 | tf_op jit(solution)/shard_map/all_gather | solution.py:538
  177.7 28.8 %collective-permute-start.15 = (bf16[8,32,2304]{2,1,0:T(8,128)(2,1)}, bf16[8,32,2304]{2,1,0:T(8,128)(2,1)}, u32[]{:S(2)}, u32[]{:S(2)}) collective-permute-start(bf16[8,32,2304]{2,1,0:T(8,128)(2,1)} %get-tuple-element.112), channel_id=1, source_target_pairs={{0,3},{1,2},{2,1},{3,0},{4,7},{5,6},{6,5},{7,4},{8,11},{9,10},{10,... | collective-permute-start | bytes 3538952 | tf_op jit(solution)/shard_map/ppermute | solution.py:524
  179.4 27.0 %collective-permute-start.16 = (bf16[8,32,2304]{2,1,0:T(8,128)(2,1)}, bf16[8,32,2304]{2,1,0:T(8,128)(2,1)}, u32[]{:S(2)}, u32[]{:S(2)}) collective-permute-start(bf16[8,32,2304]{2,1,0:T(8,128)(2,1)} %get-tuple-element.127), channel_id=1, source_target_pairs={{0,4},{1,5},{2,6},{3,7},{4,0},{5,1},{6,2},{7,3},{8,12},{9,13},{10,... | collective-permute-start | bytes 3538952 | tf_op jit(solution)/shard_map/ppermute | solution.py:524
  180.7 27.3 %collective-permute-start.17 = (bf16[8,32,2304]{2,1,0:T(8,128)(2,1)}, bf16[8,32,2304]{2,1,0:T(8,128)(2,1)}, u32[]{:S(2)}, u32[]{:S(2)}) collective-permute-start(bf16[8,32,2304]{2,1,0:T(8,128)(2,1)} %get-tuple-element.129), channel_id=1, source_target_pairs={{0,12},{1,13},{2,14},{3,15},{4,8},{5,9},{6,10},{7,11},{8,4},{9,5},... | collective-permute-start | bytes 3538952 | tf_op jit(solution)/shard_map/ppermute | solution.py:524
  182.6 25.8 %collective-permute-start.18 = (bf16[8,32,2304]{2,1,0:T(8,128)(2,1)}, bf16[8,32,2304]{2,1,0:T(8,128)(2,1)}, u32[]{:S(2)}, u32[]{:S(2)}) collective-permute-start(bf16[8,32,2304]{2,1,0:T(8,128)(2,1)} %get-tuple-element.131), channel_id=1, source_target_pairs={{0,1},{1,0},{2,3},{3,2},{4,5},{5,4},{6,7},{7,6},{8,9},{9,8},{10,11... | collective-permute-start | bytes 3538952 | tf_op jit(solution)/shard_map/ppermute | solution.py:524
  216.8 51.4 %collective-permute-start.27 = (bf16[4,8,16,2304]{3,2,1,0:T(8,128)(2,1)}, bf16[4,8,16,2304]{3,2,1,0:T(8,128)(2,1)}, u32[]{:S(2)}, u32[]{:S(2)}) collective-permute-start(bf16[4,8,16,2304]{3,2,1,0:T(8,128)(2,1)} %get-tuple-element.145), channel_id=1, source_target_pairs={{0,96},{16,112},{32,64},{48,80},{64,32},{80,48},{96,0},{112,16},{1... | collective-permute-start | bytes 7077896 | tf_op jit(solution)/shard_map/ppermute | solution.py:524
  217.7 24.8 %collective-permute-start.19 = (bf16[8,32,2304]{2,1,0:T(8,128)(2,1)}, bf16[8,32,2304]{2,1,0:T(8,128)(2,1)}, u32[]{:S(2)}, u32[]{:S(2)}) collective-permute-start(bf16[8,32,2304]{2,1,0:T(8,128)(2,1)} %get-tuple-element.132), channel_id=1, source_target_pairs={{0,4},{1,5},{2,6},{3,7},{4,0},{5,1},{6,2},{7,3},{8,12},{9,13},{10,... | collective-permute-start | bytes 3538952 | tf_op jit(solution)/shard_map/ppermute | solution.py:524
  218.9 26.0 %collective-permute-start.20 = (bf16[8,32,2304]{2,1,0:T(8,128)(2,1)}, bf16[8,32,2304]{2,1,0:T(8,128)(2,1)}, u32[]{:S(2)}, u32[]{:S(2)}) collective-permute-start(bf16[8,32,2304]{2,1,0:T(8,128)(2,1)} %get-tuple-element.133), channel_id=1, source_target_pairs={{0,12},{1,13},{2,14},{3,15},{4,8},{5,9},{6,10},{7,11},{8,4},{9,5},... | collective-permute-start | bytes 3538952 | tf_op jit(solution)/shard_map/ppermute | solution.py:524
  220.0 24.9 %collective-permute-start.21 = (bf16[8,32,2304]{2,1,0:T(8,128)(2,1)}, bf16[8,32,2304]{2,1,0:T(8,128)(2,1)}, u32[]{:S(2)}, u32[]{:S(2)}) collective-permute-start(bf16[8,32,2304]{2,1,0:T(8,128)(2,1)} %get-tuple-element.134), channel_id=1, source_target_pairs={{0,1},{1,0},{2,3},{3,2},{4,5},{5,4},{6,7},{7,6},{8,9},{9,8},{10,11... | collective-permute-start | bytes 3538952 | tf_op jit(solution)/shard_map/ppermute | solution.py:524
  220.3 26.0 %collective-permute-start.22 = (bf16[8,32,2304]{2,1,0:T(8,128)(2,1)}, bf16[8,32,2304]{2,1,0:T(8,128)(2,1)}, u32[]{:S(2)}, u32[]{:S(2)}) collective-permute-start(bf16[8,32,2304]{2,1,0:T(8,128)(2,1)} %get-tuple-element.135), channel_id=1, source_target_pairs={{0,3},{1,2},{2,1},{3,0},{4,7},{5,6},{6,5},{7,4},{8,11},{9,10},{10,... | collective-permute-start | bytes 3538952 | tf_op jit(solution)/shard_map/ppermute | solution.py:524
  251.5 37.2 %collective-permute-start.23 = (bf16[8,32,2304]{2,1,0:T(8,128)(2,1)}, bf16[8,32,2304]{2,1,0:T(8,128)(2,1)}, u32[]{:S(2)}, u32[]{:S(2)}) collective-permute-start(bf16[8,32,2304]{2,1,0:T(8,128)(2,1)} %get-tuple-element.140), channel_id=1, source_target_pairs={{0,12},{1,13},{2,14},{3,15},{4,8},{5,9},{6,10},{7,11},{8,4},{9,5},... | collective-permute-start | bytes 3538952 | tf_op jit(solution)/shard_map/ppermute | solution.py:524
  252.4 36.3 %collective-permute-start.24 = (bf16[8,32,2304]{2,1,0:T(8,128)(2,1)}, bf16[8,32,2304]{2,1,0:T(8,128)(2,1)}, u32[]{:S(2)}, u32[]{:S(2)}) collective-permute-start(bf16[8,32,2304]{2,1,0:T(8,128)(2,1)} %get-tuple-element.141), channel_id=1, source_target_pairs={{0,1},{1,0},{2,3},{3,2},{4,5},{5,4},{6,7},{7,6},{8,9},{9,8},{10,11... | collective-permute-start | bytes 3538952 | tf_op jit(solution)/shard_map/ppermute | solution.py:524
  252.6 36.1 %collective-permute-start.25 = (bf16[8,32,2304]{2,1,0:T(8,128)(2,1)}, bf16[8,32,2304]{2,1,0:T(8,128)(2,1)}, u32[]{:S(2)}, u32[]{:S(2)}) collective-permute-start(bf16[8,32,2304]{2,1,0:T(8,128)(2,1)} %get-tuple-element.142), channel_id=1, source_target_pairs={{0,3},{1,2},{2,1},{3,0},{4,7},{5,6},{6,5},{7,4},{8,11},{9,10},{10,... | collective-permute-start | bytes 3538952 | tf_op jit(solution)/shard_map/ppermute | solution.py:524
  255.2 33.5 %collective-permute-start.26 = (bf16[8,32,2304]{2,1,0:T(8,128)(2,1)}, bf16[8,32,2304]{2,1,0:T(8,128)(2,1)}, u32[]{:S(2)}, u32[]{:S(2)}) collective-permute-start(bf16[8,32,2304]{2,1,0:T(8,128)(2,1)} %get-tuple-element.143), channel_id=1, source_target_pairs={{0,4},{1,5},{2,6},{3,7},{4,0},{5,1},{6,2},{7,3},{8,12},{9,13},{10,... | collective-permute-start | bytes 3538952 | tf_op jit(solution)/shard_map/ppermute | solution.py:524
Sparse Core Ops, SparseCore 0:
  11.7 81.3 all-gather.6
Sparse Core Ops, SparseCore 1:
  50.2 67.4 all-reduce.1
  119.2 82.9 all-gather.8
  216.9 64.1 all-gather.10

commit v9 on v7

--- a/solution.py
+++ b/solution.py
@@ -151,7 +151,7 @@
 def project(place, own, other, own_weight, other_weight, out_grad):
     rows, width = own.shape
     dim = own_weight.shape[1]
-    tile = dim // 3
+    tile = dim // 9
     whole = pl.BlockSpec((rows, width), lambda i, p: (0, 0))
     columns = lambda size: pl.BlockSpec((size, tile), lambda i, p: (0, i))
     return pl.pallas_call(

time: 325 us -> 328 us (level)
  transfers between devices with their start and end apart: 33 -> 33, of which waited for: 18 -> 18; matrix products, arithmetic and copies ran while one was open for 2% -> 2% of each run, Pallas kernels for 29% -> 30%
where the time goes in v9:
time: 328 us; the launch traced here: 327 us
  Pallas kernels  138 us (42%)
  waiting for transfers between devices  121 us (37%)
  starting transfers between devices  33.5 us (10%)
  between operations  15.9 us (5%)
  blocking collectives  9.59 us (3%)
  local copies, waits for them, and re-layouts  8.13 us (2%)
    ppermute x25, waiting for transfers between devices, swap(): return lax.ppermute(array, axis, [(i, i ^ flip) for i in range(count)])  72.6 us
    pallas_call x4, Pallas kernels, expert_forward(): pl.pallas_call(functools.partial(forward_kernel, sources), grid_spec=pltp...  31 us
    all_gather x1, waiting for transfers between devices, per_device(): exp_normed = lax.all_gather(normed, 'exp')  30.7 us
    pallas_call x1, Pallas kernels, expert_backward(): pl.pallas_call(functools.partial(backward_kernel, places, len(arrays)), g...  29.1 us
    pallas_call x4, Pallas kernels, merge(): pl.pallas_call(functools.partial(merge_kernel, tuple(plans), len(arrays))...  23.4 us
    ppermute x25, starting transfers between devices, swap(): return lax.ppermute(array, axis, [(i, i ^ flip) for i in range(count)])  22 us
    pallas_call x3, Pallas kernels, pick_grad(): pl.pallas_call(functools.partial(pick_grad_kernel, per_token, capacity, n...  15.5 us
    pallas_call x1, Pallas kernels, conv_back(): pl.pallas_call(functools.partial(conv_kernel, tile), grid_spec=pltpu.Pref...  12.8 us
  transfers between devices with their start and end apart: 33, of which 18 were waited for; matrix products, arithmetic and copies ran while one was open for 2% of the time, Pallas kernels for 30%

profile of v9, /device:TPU:1, one launch (start us, length us, event | category | flops | bytes accessed | tf_op | source)
XLA Modules:
  0.0 326.7 jit_solution(9162707891655108007)
XLA Ops:
  8.1 1.3 reshape.24.gain_ref
  9.4 2.2 norm_rows.1
  11.6 1.5 collective-permute-start.4
  13.1 0.8 fusion
  13.9 3.2 collective-permute-start
  17.0 1.3 collective-permute-start.1
  18.3 0.7 slice.11
  19.1 1.3 collective-permute-start.2
  20.4 0.6 pad_add_fusion.place_ref
  21.2 1.0 reshape.34.ids_ref
  22.2 2.0 collective-permute-done.2.grad_high_ref
  24.3 0.6 copy-done.3
  24.9 12.8 %conv_back.1 = (bf16[1024,768]{1,0:T(8,128)(2,1)}, bf16[512,768]{1,0:T(8,128)(2,1)}, bf16[512,768]{1,0:T(8,128)(2,1)}) custom-call(s32[2]{0:T(128)} %pad_add_fusion.place_ref, bf16[1024,768]{1,0:T(8,128)(2,1)} %in_ref.1, bf16[16,768]{1,0:T(8,128)(2,1)} %copy-done.1, bf16[16,768]{1,0:T(8,128)(2,1)} %copy-done.2, bf16[1024,768]{1,0:T(8,128)(2,1)} %grad_ref.1, ...), custom_call_target="tpu_custom_call" | custom-call | flops 31457280 | bytes 6291456 | tf_op jit(solution)/shard_map/conv_back/pallas_call | solution.py:107
  37.7 1.3 collective-permute-start.3
  38.9 2.2 collective-permute-done.3.other_ref
  41.2 11.5 %project.1 = bf16[512,2304]{1,0:T(8,128)(2,1)} custom-call(s32[2]{0:T(128)} %pad_add_fusion.place_ref, bf16[512,768]{1,0:T(8,128)(2,1)} %get-tuple-element.77.own_ref, bf16[512,768]{1,0:T(8,128)(2,1)} %collective-permute-done.3.other_ref, bf16[768,2304]{1,0:T(8,128)(2,1)} %own_weight.1, bf16[768,2304]{1,0:T(8,128)(2,1)} %collective-permute-done.4.other_weight, ...), custom_call_target="tpu_custom_call" | custom-call | flops 3623878656 | bytes 11010048 | tf_op jit(solution)/shard_map/project/pallas_call | solution.py:157
  52.7 9.6 %all_to_all.10.tables_ref = f32[8,16,128]{2,1,0:T(8,128)} all-to-all(f32[8,16,128]{2,1,0:T(8,128)S(1)} %broadcast_in_dim.4), channel_id=1, replica_groups=mesh['seq'=8,'exp'=16] {'seq'}, dimensions={0} | all-to-all | bytes 131072 | tf_op jit(solution)/shard_map/all_to_all | solution.py:623
  62.3 30.7 %all-gather.7.cloned.1.call-done = bf16[2048,2432]{1,0:T(8,128)(2,1)} async-done(((bf16[128,2432]{1,0:T(8,128)(2,1)}), bf16[2048,2432]{1,0:T(8,128)(2,1)}) %all-gather.7.cloned.1.call-update) | async-done | bytes 9961488 | tf_op jit(solution)/shard_map/all_gather | solution.py:610
  93.1 12.3 %pick_norm.1 = (bf16[2,8,16,2304]{3,2,1,0:T(8,128)(2,1)}, bf16[2,8,16,2304]{3,2,1,0:T(8,128)(2,1)}, bf16[2,8,16,2304]{3,2,1,0:T(8,128)(2,1)}, bf16[2,8,16,2304]{...) custom-call(s32[2]{0:T(128)} %pad_add_fusion.place_ref, ...), custom_call_target="tpu_custom_call" | custom-call | flops 1207959552 | bytes 18874368 | tf_op jit(solution)/shard_map/pick_norm/pallas_call | solution.py:219
  105.3 0.7 collective-permute-start.7
  106.1 0.4 collective-permute-start.5
  106.6 0.6 pad_add_fusion.1.shift_ref.refs_0_
  107.2 1.6 collective-permute-done.7.refs_1_
  108.9 1.7 collective-permute-done.8.refs_3_
  110.5 4.6 %merge_rows.4 = (bf16[4,8,16,2304]{3,2,1,0:T(8,128)(2,1)}, bf16[4,8,16,2304]{3,2,1,0:T(8,128)(2,1)}) custom-call(s32[2]{0:T(128)} %pad_add_fusion.1.shift_ref.refs_0_, bf16[2,8,16,2304]{3,2,1,0:T(8,128)(2,1)} %get-tuple-element.85.refs_0_, bf16[2,8,16,2304]{3,2,1,0:T(8,128)(2,1)} %collective-permute-done.7.refs_1_, ...), custom_call_target="tpu_custom_call" | custom-call | bytes 9437184 | tf_op jit(solution)/shard_map/merge_rows/pallas_call | solution.py:502
  115.2 4.8 %all-reduce.2.cloned.1.call-done.refs_0_ = bf16[512,2304]{1,0:T(8,128)(2,1)} async-done(((bf16[512,2304]{1,0:T(8,128)(2,1)}), bf16[512,2304]{1,0:T(8,128)(2,1)}) %all-reduce.2.cloned.1.call-update) | async-done | bytes 2359312 | tf_op jit(solution)/shard_map/psum | solution.py:625
  119.9 0.8 collective-permute-start.9
  120.8 4.5 %pick_grad.4 = (bf16[8,32,2304]{2,1,0:T(8,128)(2,1)}, bf16[8,32,2304]{2,1,0:T(8,128)(2,1)}, bf16[8,32,2304]{2,1,0:T(8,128)(2,1)}, bf16[8,32,2304]{2,1,0:T(8,128)(2,1)}) custom-call(s32[2]{0:T(128)} %pad_add_fusion.place_ref, f32[8,16,128]{2,1,0:T(8,128)} %all_to_all.10.tables_ref, bf16[512,2304]{1,0:T(8,128)(2,1)} %all-reduce.2.cloned.1.call-done.refs_0_), custom_call_target="tpu_custom_call" | custom-call | flops 301989888 | bytes 4718592 | tf_op jit(solution)/shard_map/pick_grad/pallas_call | solution.py:284
  125.4 4.6 %pick_grad.5 = (bf16[8,32,2304]{2,1,0:T(8,128)(2,1)}, bf16[8,32,2304]{2,1,0:T(8,128)(2,1)}, bf16[8,32,2304]{2,1,0:T(8,128)(2,1)}, bf16[8,32,2304]{2,1,0:T(8,128)(2,1)}) custom-call(s32[2]{0:T(128)} %pad_add_fusion.place_ref, f32[8,16,128]{2,1,0:T(8,128)} %all_to_all.10.tables_ref, ...), custom_call_target="tpu_custom_call", output_to_operand_aliasing={{0}: (3, {}), {1}: (4, {}), {2}: (5, {}), {3}: (6, {})} | custom-call | flops 301989888 | bytes 4718592 | tf_op jit(solution)/shard_map/pick_grad/pallas_call | solution.py:284
  130.0 1.3 collective-permute-start.10
  131.2 1.8 collective-permute-start.11
  133.1 1.3 collective-permute-start.12
  134.4 1.8 collective-permute-start.13
  136.2 5.6 %all-to-all-start.1 = ((bf16[8,128,768]{2,1,0:T(8,128)(2,1)}), bf16[8,128,768]{2,1,0:T(8,128)(2,1)}, u32[]{:S(2)}, u32[]{:S(2)}) async-start(bf16[8,128,768]{2,1,0:T(8,128)(2,1)} %bitcast.21), calls=%async_computation.1 | async-start | bytes 3145728 | tf_op jit(solution)/shard_map/all_to_all | solution.py:654
  141.8 6.3 %pick_grad.3 = (bf16[8,32,2304]{2,1,0:T(8,128)(2,1)}, bf16[8,32,2304]{2,1,0:T(8,128)(2,1)}, bf16[8,32,2304]{2,1,0:T(8,128)(2,1)}, bf16[8,32,2304]{2,1,0:T(8,128)(2,1)}) custom-call(s32[2]{0:T(128)} %pad_add_fusion.place_ref, f32[8,16,128]{2,1,0:T(8,128)} %all_to_all.10.tables_ref, bf16[512,2304]{1,0:T(8,128)(2,1)} %all-reduce.2.cloned.1.call-done.refs_0_, ...), custom_call_target="tpu_custom_call" | custom-call | flops 603979776 | bytes 9437184 | tf_op jit(solution)/shard_map/pick_grad/pallas_call | solution.py:284
  148.1 25.9 %collective-permute-done.14.refs_8_.refs_3_.refs_4_.refs_14_ = bf16[4,8,16,2304]{3,2,1,0:T(8,128)(2,1)} collective-permute-done((bf16[4,8,16,2304]{3,2,1,0:T(8,128)(2,1)}, bf16[4,8,16,2304]{3,2,1,0:T(8,128)(2,1)}, u32[]{:S(2)}, u32[]{:S(2)}) %collective-permute-start.14) | collective-permute-done | bytes 2359328 | tf_op jit(solution)/shard_map/ppermute | solution.py:524
  174.0 5.2 %merge_rows.5 = (bf16[8,32,2304]{2,1,0:T(8,128)(2,1)}, bf16[8,32,2304]{2,1,0:T(8,128)(2,1)}, bf16[8,32,2304]{2,1,0:T(8,128)(2,1)}, bf16[8,32,2304]{2,1,0:T(8,128)(2,1)}) custom-call(s32[2]{0:T(128)} %pad_add_fusion.1.shift_ref.refs_0_, bf16[8,32,2304]{2,1,0:T(8,128)(2,1)} %get-tuple-element.94.refs_0_, bf16[8,32,2304]{2,1,0:T(8,128)(2,1)} %collective-permute-done.10.refs_1_, ...), custom_call_target="tpu_custom_call" | custom-call | bytes 9437184 | tf_op jit(solution)/shard_map/merge_rows/pallas_call | solution.py:502
  179.2 2.5 collective-permute-start.15
  181.7 1.3 collective-permute-start.16
  183.0 1.8 collective-permute-start.17
  184.9 6.3 %all-to-all-done.1.refs_18_ = bf16[8,128,768]{2,1,0:T(8,128)(2,1)} async-done(((bf16[8,128,768]{2,1,0:T(8,128)(2,1)}), bf16[8,128,768]{2,1,0:T(8,128)(2,1)}, u32[]{:S(2)}, u32[]{:S(2)}) %all-to-all-start.1) | async-done | bytes 1572896 | tf_op jit(solution)/shard_map/all_to_all | solution.py:654
  191.2 15.9 %collective-permute-done.15.refs_2_ = bf16[8,32,2304]{2,1,0:T(8,128)(2,1)} collective-permute-done((bf16[8,32,2304]{2,1,0:T(8,128)(2,1)}, bf16[8,32,2304]{2,1,0:T(8,128)(2,1)}, u32[]{:S(2)}, u32[]{:S(2)}) %collective-permute-start.15) | collective-permute-done | bytes 1179680 | tf_op jit(solution)/shard_map/ppermute | solution.py:524
  207.1 0.9 collective-permute-done.16.refs_5_.refs_6_.refs_7_
  208.0 2.2 collective-permute-done.17.refs_8_.refs_10_.refs_12_
  210.6 8.4 %merge_rows.6 = (bf16[8,32,2304]{2,1,0:T(8,128)(2,1)}, bf16[8,32,2304]{2,1,0:T(8,128)(2,1)}, bf16[8,32,2304]{2,1,0:T(8,128)(2,1)}, bf16[8,32,2304]{2,1,0:T(8,128...) custom-call(s32[2]{0:T(128)} %pad_add_fusion.1.shift_ref.refs_0_, ...), custom_call_target="tpu_custom_call" | custom-call | bytes 18874368 | tf_op jit(solution)/shard_map/merge_rows/pallas_call | solution.py:502
  219.1 0.6 collective-permute-start.27
  219.7 0.4 collective-permute-start.19
  220.1 1.1 collective-permute-start.20
  221.2 0.8 collective-permute-start.22
  222.1 7.6 %expert_forward.4 = (bf16[2304,2048]{1,0:T(8,128)(2,1)}, bf16[512,2048]{1,0:T(8,128)(2,1)}, bf16[2048,512]{1,0:T(8,128)(2,1)}, bf16[2048,512]{1,0:T(8,128)(2,1)}) custom-call(s32[2]{0:T(128)} %pad_add_fusion.1.shift_ref.refs_0_, bf16[2,8,16,2304]{3,2,1,0:T(8,128)(2,1)} %get-tuple-element.111.refs_1_.refs_12_, ...), custom_call_target="tpu_custom_call" | custom-call | flops 2415919104 | bytes 7340032 | tf_op jit(solution)/shard_map/expert_forward/pallas_call | solution.py:345
  229.7 8.2 %expert_forward.5 = (bf16[2304,2048]{1,0:T(8,128)(2,1)}, bf16[512,2048]{1,0:T(8,128)(2,1)}, bf16[2048,512]{1,0:T(8,128)(2,1)}, bf16[2048,512]{1,0:T(8,128)(2,1)}) custom-call(s32[2]{0:T(128)} %pad_add_fusion.1.shift_ref.refs_0_, ...), custom_call_target="tpu_custom_call", output_to_operand_aliasing={{0}: (6, {}), {1}: (7, {}), {2}: (8, {}), {3}: (9, {})} | custom-call | flops 2415919104 | bytes 7340032 | tf_op jit(solution)/shard_map/expert_forward/pallas_call | solution.py:345
  237.9 6.4 %collective-permute-done.19.refs_3_ = bf16[8,32,2304]{2,1,0:T(8,128)(2,1)} collective-permute-done((bf16[8,32,2304]{2,1,0:T(8,128)(2,1)}, bf16[8,32,2304]{2,1,0:T(8,128)(2,1)}, u32[]{:S(2)}, u32[]{:S(2)}) %collective-permute-start.19) | collective-permute-done | bytes 1179680 | tf_op jit(solution)/shard_map/ppermute | solution.py:524
  244.3 1.3 collective-permute-done.20.refs_7_.refs_8_
  245.8 0.9 collective-permute-done.22.refs_15_.refs_18_
  246.7 5.2 %merge_rows.7 = (bf16[8,32,2304]{2,1,0:T(8,128)(2,1)}, bf16[8,32,2304]{2,1,0:T(8,128)(2,1)}, bf16[8,32,2304]{2,1,0:T(8,128)(2,1)}, bf16[8,32,2304]{2,1,0:T(8,128)(2,1)}) custom-call(s32[2]{0:T(128)} %pad_add_fusion.1.shift_ref.refs_0_, bf16[8,32,2304]{2,1,0:T(8,128)(2,1)} %get-tuple-element.94.refs_0_, bf16[8,32,2304]{2,1,0:T(8,128)(2,1)} %collective-permute-done.10.refs_1_, ...), custom_call_target="tpu_custom_call" | custom-call | bytes 9437184 | tf_op jit(solution)/shard_map/merge_rows/pallas_call | solution.py:502
  251.9 1.2 collective-permute-start.23
  253.2 0.9 collective-permute-start.25
  254.1 1.9 copy.33
  256.0 1.6 copy.34
  257.6 12.9 %collective-permute-done.27.refs_1_.refs_2_.refs_3_.refs_4_ = bf16[4,8,16,2304]{3,2,1,0:T(8,128)(2,1)} collective-permute-done((bf16[4,8,16,2304]{3,2,1,0:T(8,128)(2,1)}, bf16[4,8,16,2304]{3,2,1,0:T(8,128)(2,1)}, u32[]{:S(2)}, u32[]{:S(2)}) %collective-permute-start.27) | collective-permute-done | bytes 2359328 | tf_op jit(solution)/shard_map/ppermute | solution.py:524
  270.5 7.6 %expert_forward.6 = (bf16[2304,2048]{1,0:T(8,128)(2,1)}, bf16[512,2048]{1,0:T(8,128)(2,1)}, bf16[2048,512]{1,0:T(8,128)(2,1)}, bf16[2048,512]{1,0:T(8,128)(2,1)}) custom-call(s32[2]{0:T(128)} %pad_add_fusion.1.shift_ref.refs_0_, ...), custom_call_target="tpu_custom_call", output_to_operand_aliasing={{0}: (6, {}), {1}: (7, {}), {2}: (8, {}), {3}: (9, {})} | custom-call | flops 2415919104 | bytes 7340032 | tf_op jit(solution)/shard_map/expert_forward/pallas_call | solution.py:345
  278.2 4.2 %all-gather.11.cloned.1.call-done.refs_1_.refs_2_.refs_3_.refs_4_ = bf16[8,8,16,2304]{3,2,1,0:T(8,128)(2,1)} async-done(((bf16[4,8,16,2304]{3,2,1,0:T(8,128)(2,1)}), bf16[8,8,16,2304]{3,2,1,0:T(8,128)(2,1)}) %all-gather.11.cloned.1.call-update) | async-done | bytes 4718608 | tf_op jit(solution)/shard_map/all_gather | solution.py:538
  282.4 7.6 %expert_forward.7 = (bf16[2304,2048]{1,0:T(8,128)(2,1)}, bf16[512,2048]{1,0:T(8,128)(2,1)}, bf16[2048,512]{1,0:T(8,128)(2,1)}, bf16[2048,512]{1,0:T(8,128)(2,1)}) custom-call(s32[2]{0:T(128)} %pad_add_fusion.1.shift_ref.refs_0_, ...), custom_call_target="tpu_custom_call", output_to_operand_aliasing={{0}: (6, {}), {1}: (7, {}), {2}: (8, {}), {3}: (9, {})} | custom-call | flops 2415919104 | bytes 7340032 | tf_op jit(solution)/shard_map/expert_forward/pallas_call | solution.py:345
  290.0 29.1 %expert_backward.1 = bf16[2304,1536]{1,0:T(8,128)(2,1)} custom-call(bf16[8,32,2304]{2,1,0:T(8,128)(2,1)} %get-tuple-element.94.refs_0_, bf16[8,32,2304]{2,1,0:T(8,128)(2,1)} %collective-permute-done.10.refs_1_, bf16[8,32,2304]{2,1,0:T(8,128)(2,1)} %collective-permute-done.15.refs_2_, bf16[8,32,2304]{2,1,0:T(8,128)(2,1)} %collective-permute-done.19.refs_3_, ...), custom_call_target="tpu_custom_call" | custom-call | flops 19327352832 | bytes 39845888 | tf_op jit(solution)/shard_map/expert_backward/pallas_call | solution.py:428
  (49 shorter events, 1.4 us)
Async XLA Ops:
  8.0 13.0 %copy-start = (s32[16384]{0:T(1024)S(1)}, s32[16384]{0:T(1024)}, u32[]{:S(2)}) copy-start(s32[16384]{0:T(1024)} %param.14) | copy-start | bytes 196612
  8.0 85.0 %all-gather.7.cloned.1.call-start = ((), (), s32[]{:S(2)}) async-start(), calls=%async_computation.3 | async-start | bytes 10584064 | tf_op jit(solution)/shard_map/all_gather | solution.py:610
  11.5 108.4 %all-reduce.2.cloned.1.call-start = ((), (), s32[]{:S(2)}) async-start(), calls=%async_computation.2 | async-start | bytes 4718592 | tf_op jit(solution)/shard_map/psum | solution.py:625
  11.6 29.6 %collective-permute-start.4 = (bf16[768,2304]{1,0:T(8,128)(2,1)}, bf16[768,2304]{1,0:T(8,128)(2,1)}, u32[]{:S(2)}, u32[]{:S(2)}) collective-permute-start(bf16[768,2304]{1,0:T(8,128)(2,1)} %own_weight.1), channel_id=1, source_target_pairs={{0,16},{16,0},{32,48},{48,32},{64,80},{80,64},{96,112},{112,96},{1... | collective-permute-start | bytes 10616840 | tf_op jit(solution)/shard_map/ppermute | solution.py:524
  13.9 8.4 %collective-permute-start = (bf16[16,768]{1,0:T(8,128)(2,1)S(1)}, bf16[16,768]{1,0:T(8,128)(2,1)S(1)}, u32[]{:S(2)}, u32[]{:S(2)}) collective-permute-start(bf16[16,768]{1,0:T(8,128)(2,1)S(1)} %get-tuple-element.155), channel_id=1, source_target_pairs={{0,1},{1,2},{2,3},{3,4},{4,5},{5,6},{6,7},{7,8},{8,9},{9,10},{10,1... | collective-permute-start | bytes 73736 | tf_op jit(solution)/shard_map/ppermute | solution.py:602
  17.0 5.2 %collective-permute-start.1 = (bf16[16,768]{1,0:T(8,128)(2,1)S(1)}, bf16[16,768]{1,0:T(8,128)(2,1)S(1)}, u32[]{:S(2)}, u32[]{:S(2)}) collective-permute-start(bf16[16,768]{1,0:T(8,128)(2,1)S(1)} %get-tuple-element.154), channel_id=1, source_target_pairs={{1,0},{2,1},{3,2},{4,3},{5,4},{6,5},{7,6},{8,7},{9,8},{10,9},{11,1... | collective-permute-start | bytes 73736 | tf_op jit(solution)/shard_map/ppermute | solution.py:603
  19.1 5.2 %collective-permute-start.2 = (bf16[16,768]{1,0:T(8,128)(2,1)S(1)}, bf16[16,768]{1,0:T(8,128)(2,1)S(1)}, u32[]{:S(2)}, u32[]{:S(2)}) collective-permute-start(bf16[16,768]{1,0:T(8,128)(2,1)S(1)} %slice.11), channel_id=1, source_target_pairs={{1,0},{2,1},{3,2},{4,3},{5,4},{6,5},{7,6},{8,7},{9,8},{10,9},{11,1... | collective-permute-start | bytes 73736 | tf_op jit(solution)/shard_map/ppermute | solution.py:604
  22.2 16.7 %copy-start.4 = (s32[128,8]{0,1:T(8,128)S(1)}, s32[128,8]{0,1:T(8,128)}, u32[]{:S(2)}) copy-start(s32[128,8]{0,1:T(8,128)} %param.19) | copy-start | bytes 12292
  22.2 16.7 %copy-start.5 = (f32[128,8]{0,1:T(8,128)S(1)}, f32[128,8]{0,1:T(8,128)}, u32[]{:S(2)}) copy-start(f32[128,8]{0,1:T(8,128)} %param.20) | copy-start | bytes 12292
  22.2 2.1 copy-start.1
  22.2 2.1 copy-start.2
  24.3 0.6 copy-start.3
  37.7 3.5 %collective-permute-start.3 = (bf16[512,768]{1,0:T(8,128)(2,1)}, bf16[512,768]{1,0:T(8,128)(2,1)}, u32[]{:S(2)}, u32[]{:S(2)}) collective-permute-start(bf16[512,768]{1,0:T(8,128)(2,1)} %get-tuple-element.78), channel_id=1, source_target_pairs={{0,16},{16,0},{32,48},{48,32},{64,80},{80,64},{96,112},{112,96},{1... | collective-permute-start | bytes 2359304 | tf_op jit(solution)/shard_map/ppermute | solution.py:524
  52.7 154.4 %all-gather.9.cloned.1.call-start = ((), (), s32[]{:S(2)}) async-start(), calls=%async_computation.4 | async-start | bytes 7077888 | tf_op jit(solution)/shard_map/all_gather | solution.py:538
  105.3 3.5 %collective-permute-start.7 = (bf16[2,8,16,2304]{3,2,1,0:T(8,128)(2,1)}, bf16[2,8,16,2304]{3,2,1,0:T(8,128)(2,1)}, u32[]{:S(2)}, u32[]{:S(2)}) collective-permute-start(bf16[2,8,16,2304]{3,2,1,0:T(8,128)(2,1)} %get-tuple-element.86), channel_id=1, source_target_pairs={{0,16},{16,0},{32,48},{48,32},{64,80},{80,64},{96,112},{112,96},{1... | collective-permute-start | bytes 3538952 | tf_op jit(solution)/shard_map/ppermute | solution.py:524
  106.0 4.5 %collective-permute-start.8 = (bf16[2,8,16,2304]{3,2,1,0:T(8,128)(2,1)}, bf16[2,8,16,2304]{3,2,1,0:T(8,128)(2,1)}, u32[]{:S(2)}, u32[]{:S(2)}) collective-permute-start(bf16[2,8,16,2304]{3,2,1,0:T(8,128)(2,1)} %get-tuple-element.88), channel_id=1, source_target_pairs={{0,16},{16,0},{32,48},{48,32},{64,80},{80,64},{96,112},{112,96},{1... | collective-permute-start | bytes 3538952 | tf_op jit(solution)/shard_map/ppermute | solution.py:524
  106.1 13.8 %collective-permute-start.5 = (bf16[2,8,16,2304]{3,2,1,0:T(8,128)(2,1)}, bf16[2,8,16,2304]{3,2,1,0:T(8,128)(2,1)}, u32[]{:S(2)}, u32[]{:S(2)}) collective-permute-start(bf16[2,8,16,2304]{3,2,1,0:T(8,128)(2,1)} %get-tuple-element.83), channel_id=1, source_target_pairs={{0,16},{16,0},{32,48},{48,32},{64,80},{80,64},{96,112},{112,96},{1... | collective-permute-start | bytes 3538952 | tf_op jit(solution)/shard_map/ppermute | solution.py:524
  106.5 13.4 %collective-permute-start.6 = (bf16[2,8,16,2304]{3,2,1,0:T(8,128)(2,1)}, bf16[2,8,16,2304]{3,2,1,0:T(8,128)(2,1)}, u32[]{:S(2)}, u32[]{:S(2)}) collective-permute-start(bf16[2,8,16,2304]{3,2,1,0:T(8,128)(2,1)} %get-tuple-element.84), channel_id=1, source_target_pairs={{0,16},{16,0},{32,48},{48,32},{64,80},{80,64},{96,112},{112,96},{1... | collective-permute-start | bytes 3538952 | tf_op jit(solution)/shard_map/ppermute | solution.py:524
  119.9 5.4 %collective-permute-start.9 = (bf16[512,2304]{1,0:T(8,128)(2,1)}, bf16[512,2304]{1,0:T(8,128)(2,1)}, u32[]{:S(2)}, u32[]{:S(2)}) collective-permute-start(bf16[512,2304]{1,0:T(8,128)(2,1)} %all-reduce.2.cloned.1.call-done.refs_0_), channel_id=1, source_target_pairs={{0,16},{16,0},{32,48},{48,32},{64,80},{80,64},{96,112},{112,96},{1... | collective-permute-start | bytes 7077896 | tf_op jit(solution)/shard_map/ppermute | solution.py:524
  120.7 53.3 %collective-permute-start.14 = (bf16[4,8,16,2304]{3,2,1,0:T(8,128)(2,1)}, bf16[4,8,16,2304]{3,2,1,0:T(8,128)(2,1)}, u32[]{:S(2)}, u32[]{:S(2)}) collective-permute-start(bf16[4,8,16,2304]{3,2,1,0:T(8,128)(2,1)} %get-tuple-element.106), channel_id=1, source_target_pairs={{0,32},{16,48},{32,0},{48,16},{64,96},{80,112},{96,64},{112,80},{1... | collective-permute-start | bytes 7077896 | tf_op jit(solution)/shard_map/ppermute | solution.py:524
  130.0 44.0 %collective-permute-start.10 = (bf16[8,32,2304]{2,1,0:T(8,128)(2,1)}, bf16[8,32,2304]{2,1,0:T(8,128)(2,1)}, u32[]{:S(2)}, u32[]{:S(2)}) collective-permute-start(bf16[8,32,2304]{2,1,0:T(8,128)(2,1)} %get-tuple-element.99), channel_id=1, source_target_pairs={{0,1},{1,0},{2,3},{3,2},{4,5},{5,4},{6,7},{7,6},{8,9},{9,8},{10,11... | collective-permute-start | bytes 3538952 | tf_op jit(solution)/shard_map/ppermute | solution.py:524
  131.2 42.8 %collective-permute-start.11 = (bf16[8,32,2304]{2,1,0:T(8,128)(2,1)}, bf16[8,32,2304]{2,1,0:T(8,128)(2,1)}, u32[]{:S(2)}, u32[]{:S(2)}) collective-permute-start(bf16[8,32,2304]{2,1,0:T(8,128)(2,1)} %get-tuple-element.101), channel_id=1, source_target_pairs={{0,3},{1,2},{2,1},{3,0},{4,7},{5,6},{6,5},{7,4},{8,11},{9,10},{10,... | collective-permute-start | bytes 3538952 | tf_op jit(solution)/shard_map/ppermute | solution.py:524
  133.1 41.0 %collective-permute-start.12 = (bf16[8,32,2304]{2,1,0:T(8,128)(2,1)}, bf16[8,32,2304]{2,1,0:T(8,128)(2,1)}, u32[]{:S(2)}, u32[]{:S(2)}) collective-permute-start(bf16[8,32,2304]{2,1,0:T(8,128)(2,1)} %get-tuple-element.103), channel_id=1, source_target_pairs={{0,4},{1,5},{2,6},{3,7},{4,0},{5,1},{6,2},{7,3},{8,12},{9,13},{10,... | collective-permute-start | bytes 3538952 | tf_op jit(solution)/shard_map/ppermute | solution.py:524
  134.4 39.6 %collective-permute-start.13 = (bf16[8,32,2304]{2,1,0:T(8,128)(2,1)}, bf16[8,32,2304]{2,1,0:T(8,128)(2,1)}, u32[]{:S(2)}, u32[]{:S(2)}) collective-permute-start(bf16[8,32,2304]{2,1,0:T(8,128)(2,1)} %get-tuple-element.105), channel_id=1, source_target_pairs={{0,12},{1,13},{2,14},{3,15},{4,8},{5,9},{6,10},{7,11},{8,4},{9,5},... | collective-permute-start | bytes 3538952 | tf_op jit(solution)/shard_map/ppermute | solution.py:524
  136.2 55.0 %all-to-all-start.1 = ((bf16[8,128,768]{2,1,0:T(8,128)(2,1)}), bf16[8,128,768]{2,1,0:T(8,128)(2,1)}, u32[]{:S(2)}, u32[]{:S(2)}) async-start(bf16[8,128,768]{2,1,0:T(8,128)(2,1)} %bitcast.21), calls=%async_computation.1 | async-start | bytes 3145728 | tf_op jit(solution)/shard_map/all_to_all | solution.py:654
  141.7 140.6 %all-gather.11.cloned.1.call-start = ((), (), s32[]{:S(2)}) async-start(), calls=%async_computation.5 | async-start | bytes 7077888 | tf_op jit(solution)/shard_map/all_gather | solution.py:538
  179.2 27.9 %collective-permute-start.15 = (bf16[8,32,2304]{2,1,0:T(8,128)(2,1)}, bf16[8,32,2304]{2,1,0:T(8,128)(2,1)}, u32[]{:S(2)}, u32[]{:S(2)}) collective-permute-start(bf16[8,32,2304]{2,1,0:T(8,128)(2,1)} %get-tuple-element.107), channel_id=1, source_target_pairs={{0,3},{1,2},{2,1},{3,0},{4,7},{5,6},{6,5},{7,4},{8,11},{9,10},{10,... | collective-permute-start | bytes 3538952 | tf_op jit(solution)/shard_map/ppermute | solution.py:524
  181.7 26.3 %collective-permute-start.16 = (bf16[8,32,2304]{2,1,0:T(8,128)(2,1)}, bf16[8,32,2304]{2,1,0:T(8,128)(2,1)}, u32[]{:S(2)}, u32[]{:S(2)}) collective-permute-start(bf16[8,32,2304]{2,1,0:T(8,128)(2,1)} %get-tuple-element.121), channel_id=1, source_target_pairs={{0,4},{1,5},{2,6},{3,7},{4,0},{5,1},{6,2},{7,3},{8,12},{9,13},{10,... | collective-permute-start | bytes 3538952 | tf_op jit(solution)/shard_map/ppermute | solution.py:524
  183.0 27.3 %collective-permute-start.17 = (bf16[8,32,2304]{2,1,0:T(8,128)(2,1)}, bf16[8,32,2304]{2,1,0:T(8,128)(2,1)}, u32[]{:S(2)}, u32[]{:S(2)}) collective-permute-start(bf16[8,32,2304]{2,1,0:T(8,128)(2,1)} %get-tuple-element.122), channel_id=1, source_target_pairs={{0,12},{1,13},{2,14},{3,15},{4,8},{5,9},{6,10},{7,11},{8,4},{9,5},... | collective-permute-start | bytes 3538952 | tf_op jit(solution)/shard_map/ppermute | solution.py:524
  184.9 25.8 %collective-permute-start.18 = (bf16[8,32,2304]{2,1,0:T(8,128)(2,1)}, bf16[8,32,2304]{2,1,0:T(8,128)(2,1)}, u32[]{:S(2)}, u32[]{:S(2)}) collective-permute-start(bf16[8,32,2304]{2,1,0:T(8,128)(2,1)} %get-tuple-element.123), channel_id=1, source_target_pairs={{0,1},{1,0},{2,3},{3,2},{4,5},{5,4},{6,7},{7,6},{8,9},{9,8},{10,11... | collective-permute-start | bytes 3538952 | tf_op jit(solution)/shard_map/ppermute | solution.py:524
  219.1 51.4 %collective-permute-start.27 = (bf16[4,8,16,2304]{3,2,1,0:T(8,128)(2,1)}, bf16[4,8,16,2304]{3,2,1,0:T(8,128)(2,1)}, u32[]{:S(2)}, u32[]{:S(2)}) collective-permute-start(bf16[4,8,16,2304]{3,2,1,0:T(8,128)(2,1)} %get-tuple-element.137), channel_id=1, source_target_pairs={{0,96},{16,112},{32,64},{48,80},{64,32},{80,48},{96,0},{112,16},{1... | collective-permute-start | bytes 7077896 | tf_op jit(solution)/shard_map/ppermute | solution.py:524
  219.7 24.6 %collective-permute-start.19 = (bf16[8,32,2304]{2,1,0:T(8,128)(2,1)}, bf16[8,32,2304]{2,1,0:T(8,128)(2,1)}, u32[]{:S(2)}, u32[]{:S(2)}) collective-permute-start(bf16[8,32,2304]{2,1,0:T(8,128)(2,1)} %get-tuple-element.124), channel_id=1, source_target_pairs={{0,4},{1,5},{2,6},{3,7},{4,0},{5,1},{6,2},{7,3},{8,12},{9,13},{10,... | collective-permute-start | bytes 3538952 | tf_op jit(solution)/shard_map/ppermute | solution.py:524
  220.1 25.5 %collective-permute-start.20 = (bf16[8,32,2304]{2,1,0:T(8,128)(2,1)}, bf16[8,32,2304]{2,1,0:T(8,128)(2,1)}, u32[]{:S(2)}, u32[]{:S(2)}) collective-permute-start(bf16[8,32,2304]{2,1,0:T(8,128)(2,1)} %get-tuple-element.125), channel_id=1, source_target_pairs={{0,12},{1,13},{2,14},{3,15},{4,8},{5,9},{6,10},{7,11},{8,4},{9,5},... | collective-permute-start | bytes 3538952 | tf_op jit(solution)/shard_map/ppermute | solution.py:524
  221.2 24.5 %collective-permute-start.21 = (bf16[8,32,2304]{2,1,0:T(8,128)(2,1)}, bf16[8,32,2304]{2,1,0:T(8,128)(2,1)}, u32[]{:S(2)}, u32[]{:S(2)}) collective-permute-start(bf16[8,32,2304]{2,1,0:T(8,128)(2,1)} %get-tuple-element.126), channel_id=1, source_target_pairs={{0,1},{1,0},{2,3},{3,2},{4,5},{5,4},{6,7},{7,6},{8,9},{9,8},{10,11... | collective-permute-start | bytes 3538952 | tf_op jit(solution)/shard_map/ppermute | solution.py:524
  221.2 25.4 %collective-permute-start.22 = (bf16[8,32,2304]{2,1,0:T(8,128)(2,1)}, bf16[8,32,2304]{2,1,0:T(8,128)(2,1)}, u32[]{:S(2)}, u32[]{:S(2)}) collective-permute-start(bf16[8,32,2304]{2,1,0:T(8,128)(2,1)} %get-tuple-element.127), channel_id=1, source_target_pairs={{0,3},{1,2},{2,1},{3,0},{4,7},{5,6},{6,5},{7,4},{8,11},{9,10},{10,... | collective-permute-start | bytes 3538952 | tf_op jit(solution)/shard_map/ppermute | solution.py:524
  251.9 38.1 %collective-permute-start.23 = (bf16[8,32,2304]{2,1,0:T(8,128)(2,1)}, bf16[8,32,2304]{2,1,0:T(8,128)(2,1)}, u32[]{:S(2)}, u32[]{:S(2)}) collective-permute-start(bf16[8,32,2304]{2,1,0:T(8,128)(2,1)} %get-tuple-element.132), channel_id=1, source_target_pairs={{0,12},{1,13},{2,14},{3,15},{4,8},{5,9},{6,10},{7,11},{8,4},{9,5},... | collective-permute-start | bytes 3538952 | tf_op jit(solution)/shard_map/ppermute | solution.py:524
  253.0 36.9 %collective-permute-start.24 = (bf16[8,32,2304]{2,1,0:T(8,128)(2,1)}, bf16[8,32,2304]{2,1,0:T(8,128)(2,1)}, u32[]{:S(2)}, u32[]{:S(2)}) collective-permute-start(bf16[8,32,2304]{2,1,0:T(8,128)(2,1)} %get-tuple-element.133), channel_id=1, source_target_pairs={{0,1},{1,0},{2,3},{3,2},{4,5},{5,4},{6,7},{7,6},{8,9},{9,8},{10,11... | collective-permute-start | bytes 3538952 | tf_op jit(solution)/shard_map/ppermute | solution.py:524
  253.2 36.8 %collective-permute-start.25 = (bf16[8,32,2304]{2,1,0:T(8,128)(2,1)}, bf16[8,32,2304]{2,1,0:T(8,128)(2,1)}, u32[]{:S(2)}, u32[]{:S(2)}) collective-permute-start(bf16[8,32,2304]{2,1,0:T(8,128)(2,1)} %get-tuple-element.134), channel_id=1, source_target_pairs={{0,3},{1,2},{2,1},{3,0},{4,7},{5,6},{6,5},{7,4},{8,11},{9,10},{10,... | collective-permute-start | bytes 3538952 | tf_op jit(solution)/shard_map/ppermute | solution.py:524
  254.1 35.9 %collective-permute-start.26 = (bf16[8,32,2304]{2,1,0:T(8,128)(2,1)}, bf16[8,32,2304]{2,1,0:T(8,128)(2,1)}, u32[]{:S(2)}, u32[]{:S(2)}) collective-permute-start(bf16[8,32,2304]{2,1,0:T(8,128)(2,1)} %get-tuple-element.135), channel_id=1, source_target_pairs={{0,4},{1,5},{2,6},{3,7},{4,0},{5,1},{6,2},{7,3},{8,12},{9,13},{10,... | collective-permute-start | bytes 3538952 | tf_op jit(solution)/shard_map/ppermute | solution.py:524
Sparse Core Ops, SparseCore 0:
  11.7 81.3 all-gather.6
Sparse Core Ops, SparseCore 1:
  52.8 67.1 all-reduce.1
  121.4 82.9 all-gather.8
  219.2 63.1 all-gather.10
